TPU v7x, 256 devices: a whole 4x4x8 slice. The times are simulated.
256 devices in a mesh: dp: 8 (over y, core), label: 32 (over z, x).
Axes of the slice: x: 4, y: 4, z: 8, core: 2. Of those that a mesh axis runs over, the one named last changes fastest.
Arguments:
- embed: bfloat16 [16384, 768], P(('dp', 'label')), may hold values from -6 to 6
- cluster_weight: bfloat16 [512, 768], P('label'), may hold values from -0.21875 to 0.21875
- leaf_weight: bfloat16 [512, 32, 768], P('label'), may hold values from -0.21875 to 0.21875
- match_instance: int32 [8, 32, 32, 96], P('dp', 'label'), may hold values from 0 to 63
- match_cluster: int32 [8, 32, 32, 96], P('dp', 'label'), may hold values from 0 to 15
- match_count: int32 [8, 32, 32], P('dp', 'label'), may hold values from 24 to 96, as said below
- prefix: bfloat16 [8, 32, 32, 96], P('dp', 'label'), may hold values from 0.099609375 to 1
- targets: bfloat16 [8, 32, 32, 96, 32], P('dp', 'label'), may hold values from 0 to 1
Outputs:
- grad_embed: float32 [16384, 768], P(('dp', 'label'))
- grad_cluster: float32 [512, 768], P('label')
- grad_leaf: float32 [512, 32, 768], P('label', 'dp')
Inputs may be any that keep to these rules, and one draw needn't show every extreme that they name: `match_count`: valid slots from one device to one owner; in each dp group one owner receives 96 valid slots from every device. Slots past the count hold arbitrary in-range indices.
All inputs are finite; a program needn't handle non-finite values.
Results may differ from a plain program's by a relative error of at most 0.0065.
Values may be sent and summed in bfloat16 or wider, within the bound.
No kernel may reach another device: no remote copies, remote signals or barrier semaphores. Data moves between devices by JAX's collectives and lax.ppermute only.
A program may use at most 128 MiB of HBM per device.

v0:
```python
import jax
import jax.numpy as jnp
from jax import lax
from jax.sharding import PartitionSpec as P


def owner_terms(rows, clus_ids, alpha, want, cluster_weight, leaf_weight):
    clusters_here, kids, width = leaf_weight.shape
    slot_total = rows.shape[0]
    tile_size = 128
    tile_total = -(-slot_total // tile_size) + clusters_here
    padded_total = tile_total * tile_size
    select = (clus_ids[:, None] == jnp.arange(clusters_here, dtype=jnp.int32)[None, :]).astype(
        jnp.int32
    )
    member_count = jnp.sum(select, axis=0)
    rank_table = jnp.cumsum(select, axis=0) - 1
    slot_rank = jnp.sum(select * rank_table, axis=1)
    tiles_each = (member_count + tile_size - 1) // tile_size
    tile_end = jnp.cumsum(tiles_each)
    tile_begin = tile_end - tiles_each
    slot_dest = jnp.sum(select * tile_begin[None, :], axis=1) * tile_size + slot_rank
    tile_iota = jnp.arange(tile_total, dtype=jnp.int32)
    tile_cluster = jnp.minimum(
        jnp.sum((tile_iota[:, None] >= tile_end[None, :]).astype(jnp.int32), axis=1),
        clusters_here - 1,
    )
    tile_rows = jnp.zeros((padded_total, width), rows.dtype).at[slot_dest].set(rows)
    tile_rows = tile_rows.reshape(tile_total, tile_size, width)
    tile_alpha = (
        jnp.zeros((padded_total,), alpha.dtype)
        .at[slot_dest]
        .set(alpha)
        .reshape(tile_total, tile_size)
    )
    tile_want = (
        jnp.zeros((padded_total, kids), want.dtype)
        .at[slot_dest]
        .set(want)
        .reshape(tile_total, tile_size, kids)
    )
    tile_leaf = jnp.take(leaf_weight, tile_cluster, axis=0)
    tile_upper = jnp.take(cluster_weight, tile_cluster, axis=0)
    z1 = jnp.einsum("trd,td->tr", tile_rows, tile_upper, preferred_element_type=jnp.float32)
    z2 = jnp.einsum("trd,tkd->trk", tile_rows, tile_leaf, preferred_element_type=jnp.float32)
    s1 = jax.nn.sigmoid(z1)
    s2 = jax.nn.sigmoid(z2)
    a = tile_alpha.astype(jnp.float32)
    resid = (a * s1)[..., None] * s2 - tile_want.astype(jnp.float32)
    dz2 = (resid * (a * s1)[..., None] * s2 * (1.0 - s2)).astype(jnp.bfloat16)
    dz1 = (jnp.sum(resid * a[..., None] * s2, axis=2) * s1 * (1.0 - s1)).astype(jnp.bfloat16)
    tile_grad = jnp.einsum("trk,tkd->trd", dz2, tile_leaf, preferred_element_type=jnp.float32)
    tile_grad = (
        tile_grad + dz1.astype(jnp.float32)[..., None] * tile_upper.astype(jnp.float32)[:, None, :]
    )
    grad_rows = jnp.take(tile_grad.reshape(padded_total, width), slot_dest, axis=0)
    leaf_tiles = jnp.einsum("trk,trd->tkd", dz2, tile_rows, preferred_element_type=jnp.float32)
    upper_tiles = jnp.einsum("tr,trd->td", dz1, tile_rows, preferred_element_type=jnp.float32)
    tile_onehot = (
        tile_cluster[:, None] == jnp.arange(clusters_here, dtype=jnp.int32)[None, :]
    ).astype(jnp.float32)
    leaf_grad = jnp.einsum("tc,tkd->ckd", tile_onehot, leaf_tiles, precision=lax.Precision.HIGHEST)
    cluster_grad = jnp.einsum(
        "tc,td->cd", tile_onehot, upper_tiles, precision=lax.Precision.HIGHEST
    )
    return (grad_rows, leaf_grad, cluster_grad)


def shards(
    embed, cluster_weight, leaf_weight, match_instance, match_cluster, match_count, prefix, targets
):
    inst_dev, width = embed.shape
    kids = leaf_weight.shape[1]
    owners = lax.axis_size("label")
    capacity = match_instance.shape[-1]
    inst_ids = match_instance.reshape(owners, capacity)
    clus_ids = match_cluster.reshape(owners, capacity)
    counts = match_count.reshape(owners)
    valid = jnp.arange(capacity, dtype=jnp.int32)[None, :] < counts[:, None]
    nothing = jnp.zeros((), jnp.bfloat16)
    alpha = jnp.where(valid, prefix.reshape(owners, capacity), nothing)
    want = jnp.where(valid[:, :, None], targets.reshape(owners, capacity, kids), nothing)
    outgoing = jnp.take(embed, inst_ids.reshape(-1), axis=0).reshape(owners, capacity, width)
    arrived, got_clus, got_alpha, got_want = (
        lax.all_to_all(outgoing, "label", split_axis=0, concat_axis=0, tiled=True),
        lax.all_to_all(clus_ids, "label", split_axis=0, concat_axis=0, tiled=True),
        lax.all_to_all(alpha, "label", split_axis=0, concat_axis=0, tiled=True),
        lax.all_to_all(want, "label", split_axis=0, concat_axis=0, tiled=True),
    )
    rows = arrived.reshape(-1, width)
    grad_rows, leaf_grad, cluster_grad = owner_terms(
        rows,
        got_clus.reshape(-1),
        got_alpha.reshape(-1),
        got_want.reshape(-1, kids),
        cluster_weight,
        leaf_weight,
    )
    instance_iota = jnp.arange(inst_dev, dtype=jnp.int32)
    returned = lax.all_to_all(
        grad_rows.reshape(owners, capacity, width), "label", split_axis=0, concat_axis=0, tiled=True
    )
    onehot = (inst_ids.reshape(-1)[:, None] == instance_iota[None, :]).astype(jnp.float32)
    grad_embed = lax.dot_general(
        onehot,
        returned.reshape(-1, width),
        (((0,), (0,)), ((), ())),
        precision=lax.Precision.HIGHEST,
        preferred_element_type=jnp.float32,
    )
    leaf_total = lax.psum_scatter(leaf_grad, "dp", scatter_dimension=1, tiled=True)
    cluster_total = lax.psum(cluster_grad, "dp")
    return (grad_embed, cluster_total, leaf_total)


def solution(mesh):
    in_specs = (
        P(("dp", "label"), None),
        P("label", None),
        P("label", None, None),
        P("dp", "label", None, None),
        P("dp", "label", None, None),
        P("dp", "label", None),
        P("dp", "label", None, None),
        P("dp", "label", None, None, None),
    )
    out_specs = (P(("dp", "label"), None), P("label", None), P("label", "dp", None))
    return jax.shard_map(shards, mesh=mesh, in_specs=in_specs, out_specs=out_specs, check_vma=False)
```

profile of v0, /device:TPU:24, one launch (start us, length us, event | category | flops | bytes accessed | tf_op | source)
XLA Modules:
  0.0 463.0 jit_solution(12268088137134991952)
XLA Ops:
  8.7 11.3 %all-to-all-start.1 = ((bf16[32,1,96]{2,1,0:T(2,128)(2,1)}), bf16[32,1,96]{2,1,0:T(2,128)(2,1)S(1)}, u32[]{:S(2)}, u32[]{:S(2)}) async-start(bf16[32,1,96]{2,1,0:T(2,128)(2,1)} %copy.48), calls=%async_computation.1 | async-start | bytes 32768 | tf_op jit(solution)/shard_map/all_to_all | solution.py:87
  23.3 6.4 %all-to-all-done.1 = bf16[32,1,96]{2,1,0:T(2,128)(2,1)S(1)} async-done(((bf16[32,1,96]{2,1,0:T(2,128)(2,1)}), bf16[32,1,96]{2,1,0:T(2,128)(2,1)S(1)}, u32[]{:S(2)}, u32[]{:S(2)}) %all-to-all-start.1) | async-done | bytes 6176 | tf_op jit(solution)/shard_map/all_to_all | solution.py:87
  34.2 13.6 %gather_fusion = bf16[3072,768]{1,0:T(8,128)(2,1)} fusion(bf16[64,768]{1,0:T(8,128)(2,1)S(1)} %copy-done.2, s32[3072]{0:T(1024)S(1)} %broadcast_clamp_fusion.1), kind=kCustom, calls=%fused_computation | custom fusion | bytes 9449472 | tf_op jit(solution)/shard_map/jit(_take)/gather | solution.py:83
  47.9 9.8 %all-to-all-start.3 = ((bf16[32,96,32]{1,2,0:T(8,128)(2,1)}), bf16[32,96,32]{1,2,0:T(8,128)(2,1)S(1)}, u32[]{:S(2)}, u32[]{:S(2)}) async-start(bf16[32,96,32]{1,2,0:T(8,128)(2,1)} %bitcast_select_fusion), calls=%async_computation.3 | async-start | bytes 524288 | tf_op jit(solution)/shard_map/all_to_all | solution.py:88
  57.6 5.7 %broadcast_select_fusion.1 = bf16[32,96,768]{2,1,0:T(8,128)(2,1)} fusion(bf16[32,96,768]{2,1,0:T(8,128)(2,1)} %bitcast.92, pred[32,96]{1,0:T(8,128)(4,1)S(1)} %compare_and_fusion), kind=kLoop, calls=%fused_computation.9 | loop fusion | flops 2359296 | bytes 9440256 | tf_op jit(solution)/shard_map/jit(_take)/select_n | solution.py:83
  63.4 6.0 %all-to-all-done.3 = bf16[32,96,32]{1,2,0:T(8,128)(2,1)S(1)} async-done(((bf16[32,96,32]{1,2,0:T(8,128)(2,1)}), bf16[32,96,32]{1,2,0:T(8,128)(2,1)S(1)}, u32[]{:S(2)}, u32[]{:S(2)}) %all-to-all-start.3) | async-done | bytes 196640 | tf_op jit(solution)/shard_map/all_to_all | solution.py:88
  69.4 4.9 %all-to-all-start.2 = ((bf16[32,96,768]{2,1,0:T(8,128)(2,1)}), bf16[32,96,768]{2,1,0:T(8,128)(2,1)}, u32[]{:S(2)}, u32[]{:S(2)}) async-start(bf16[32,96,768]{2,1,0:T(8,128)(2,1)} %broadcast_select_fusion.1), calls=%async_computation.2 | async-start | bytes 9437184 | tf_op jit(solution)/shard_map/all_to_all | solution.py:85
  76.2 4.6 reduce-window.18
  83.2 21.6 %scatter_custom_fusion = bf16[5120]{0:T(1024)(128)(2,1)S(1)} fusion(s32[3072]{0:T(1024)S(1)} %bitcast.100, bf16[3072]{0:T(1024)(128)(2,1)S(1)} %reshape.403, bf16[]{:T(256)} %constant.94.clone.1), kind=kCustom, calls=%fused_computation.68 | custom fusion | bytes 10242 | tf_op jit(solution)/shard_map/scatter | solution.py:33
  105.3 9.5 %scatter_custom_fusion.2 = bf16[5120,32]{1,0:T(8,128)(2,1)} fusion(s32[3072]{0:T(1024)S(1)} %bitcast.102, bf16[3072,32]{1,0:T(8,128)(2,1)S(1)} %bitcast.94, bf16[]{:T(256)} %constant.94.clone.1), kind=kCustom, calls=%fused_computation.26 | custom fusion | bytes 327682 | tf_op jit(solution)/shard_map/scatter | solution.py:39
  116.4 60.5 %all-to-all-done.2 = bf16[32,96,768]{2,1,0:T(8,128)(2,1)} async-done(((bf16[32,96,768]{2,1,0:T(8,128)(2,1)}), bf16[32,96,768]{2,1,0:T(8,128)(2,1)}, u32[]{:S(2)}, u32[]{:S(2)}) %all-to-all-start.2) | async-done | bytes 4718624 | tf_op jit(solution)/shard_map/all_to_all | solution.py:85
  176.9 19.2 %scatter_custom_fusion.1 = bf16[5120,768]{1,0:T(8,128)(2,1)} fusion(s32[3072]{0:T(1024)S(1)} %bitcast.103, bf16[3072,768]{1,0:T(8,128)(2,1)} %bitcast.11, bf16[]{:T(256)} %constant.94.clone.1), kind=kCustom, calls=%fused_computation.12 | custom fusion | bytes 7864832 | tf_op jit(solution)/shard_map/scatter | solution.py:28
  196.1 5.5 %fusion.17 = f32[40,1,128]{2,1,0:T(1,128)S(1)} fusion(bf16[40,128,768]{2,1,0:T(8,128)(2,1)} %bitcast.87, bf16[40,768,1]{1,0,2:T(8,128)(2,1)S(1)} %get-tuple-element.31), kind=kOutput, calls=%fused_computation.42 | convolution fusion | flops 7864320 | bytes 7946240 | tf_op jit(solution)/shard_map/trd,td->tr/dot_general | solution.py:44
  204.4 7.0 %multiply_add_fusion = f32[40,128,768]{2,1,0:T(8,128)} fusion(bf16[40,128,32]{1,2,0:T(8,128)(2,1)S(1)} %get-tuple-element.29, f32[40,768]{1,0:T(8,128)S(1)} %get-tuple-element.30, f32[40,128]{1,0:T(8,128)S(1)} %get-tuple-element.26, bf16[40,32,768]{2,1,0:T(8,128)(2,1)S(1)} %gather_fusion.2, pred[40]{0:T(512)(128)(4,1)S(1)} %compare_and_fusion.2), kind=kOutput, calls=%fused_computation.7 | convolution fusion | flops 260505600 | bytes 18165800 | tf_op jit(solution)/shard_map/trk,tkd->trd/dot_general | solution.py:52
  211.4 20.9 %gather_fusion.3 = f32[3072,768]{1,0:T(8,128)} fusion(f32[5120,768]{1,0:T(8,128)} %bitcast.86, s32[3072]{0:T(1024)S(1)} %broadcast_clamp_fusion), kind=kCustom, calls=%fused_computation.3 | custom fusion | bytes 18886656 | tf_op jit(solution)/shard_map/jit(_take)/gather | solution.py:56
  232.3 6.4 %broadcast_select_fusion = f32[32,96,768]{2,1,0:T(8,128)} fusion(f32[32,96,768]{2,1,0:T(8,128)} %bitcast.91, pred[32,96]{1,0:T(8,128)(4,1)S(1)} %compare_and_fusion.1), kind=kLoop, calls=%fused_computation.8 | loop fusion | flops 2359296 | bytes 18877440 | tf_op jit(solution)/shard_map/jit(_take)/select_n | solution.py:56
  238.7 6.9 %all-to-all-start.4 = ((f32[32,96,768]{2,1,0:T(8,128)}), f32[32,96,768]{2,1,0:T(8,128)}, u32[]{:S(2)}, u32[]{:S(2)}) async-start(f32[32,96,768]{2,1,0:T(8,128)} %broadcast_select_fusion), calls=%async_computation.4 | async-start | bytes 18874368 | tf_op jit(solution)/shard_map/all_to_all | solution.py:100
  245.8 4.4 fusion.36
  250.2 4.8 %fusion = f32[16,32,768]{2,0,1:T(8,128)} fusion(f32[40,32,768]{2,1,0:T(8,128)S(1)} %fusion.36, s32[40]{0:T(128)S(1)} %broadcast_minimum_fusion), kind=kOutput, calls=%fused_computation.10 | convolution fusion | flops 188744320 | bytes 5505184 | tf_op jit(solution)/shard_map/tc,tkd->ckd/dot_general | solution.py:62
  255.1 4.4 fusion.21
  259.7 22.7 %psum.7 = f32[16,768]{1,0:T(8,128)} all-reduce(f32[16,768]{1,0:T(8,128)S(1)} %fusion.14), channel_id=1, replica_groups=mesh['dp'=8,'label'=32] {'dp'}, use_global_device_ids=true, to_apply=%region_11.12 | all-reduce | flops 12288 | bytes 98304 | tf_op jit(solution)/shard_map/psum | solution.py:112
  282.4 6.9 %reduce-scatter.2.cloned.1.call-done = f32[16,4,768]{2,0,1:T(8,128)} async-done(((f32[16,32,768]{2,0,1:T(8,128)}), f32[16,4,768]{2,0,1:T(8,128)}) %reduce-scatter.2.cloned.1.call-update) | async-done | bytes 196624 | tf_op jit(solution)/shard_map/reduce_scatter | solution.py:111
  291.0 156.9 %all-to-all-done.4 = f32[32,96,768]{2,1,0:T(8,128)} async-done(((f32[32,96,768]{2,1,0:T(8,128)}), f32[32,96,768]{2,1,0:T(8,128)}, u32[]{:S(2)}, u32[]{:S(2)}) %all-to-all-start.4) | async-done | bytes 9437216 | tf_op jit(solution)/shard_map/all_to_all | solution.py:100
  448.0 8.2 %fusion.4 = f32[64,768]{1,0:T(8,128)} fusion(f32[3072,768]{1,0:T(8,128)} %bitcast.23, s32[3072]{0:T(1024)S(1)} %eq.55), kind=kOutput, calls=%fused_computation.16 | convolution fusion | flops 1812135936 | bytes 9646080 | tf_op jit(solution)/shard_map/dot_general | solution.py:104
  (63 shorter events, 20.6 us)
Async XLA Ops:
  7.2 75.4 %copy-start = (bf16[16,32,768]{2,1,0:T(8,128)(2,1)S(1)}, bf16[16,32,768]{2,1,0:T(8,128)(2,1)}, u32[]{:S(2)}) copy-start(bf16[16,32,768]{2,1,0:T(8,128)(2,1)} %param.10) | copy-start | bytes 2359300
  7.2 27.0 %copy-start.2 = (bf16[64,768]{1,0:T(8,128)(2,1)S(1)}, bf16[64,768]{1,0:T(8,128)(2,1)}, u32[]{:S(2)}) copy-start(bf16[64,768]{1,0:T(8,128)(2,1)} %param.8) | copy-start | bytes 294916
  8.7 21.0 %all-to-all-start.1 = ((bf16[32,1,96]{2,1,0:T(2,128)(2,1)}), bf16[32,1,96]{2,1,0:T(2,128)(2,1)S(1)}, u32[]{:S(2)}, u32[]{:S(2)}) async-start(bf16[32,1,96]{2,1,0:T(2,128)(2,1)} %copy.48), calls=%async_computation.1 | async-start | bytes 32768 | tf_op jit(solution)/shard_map/all_to_all | solution.py:87
  29.7 18.2 %all-to-all-start = ((s32[32,1,96]{2,1,0:T(1,128)}), s32[32,1,96]{2,1,0:T(1,128)S(1)}, u32[]{:S(2)}, u32[]{:S(2)}) async-start(s32[32,1,96]{2,1,0:T(1,128)} %bitcast.106), calls=%async_computation | async-start | bytes 32768 | tf_op jit(solution)/shard_map/all_to_all | solution.py:86
  47.9 21.5 %all-to-all-start.3 = ((bf16[32,96,32]{1,2,0:T(8,128)(2,1)}), bf16[32,96,32]{1,2,0:T(8,128)(2,1)S(1)}, u32[]{:S(2)}, u32[]{:S(2)}) async-start(bf16[32,96,32]{1,2,0:T(8,128)(2,1)} %bitcast_select_fusion), calls=%async_computation.3 | async-start | bytes 524288 | tf_op jit(solution)/shard_map/all_to_all | solution.py:88
  63.4 18.5 %copy-start.4 = (bf16[16,768]{1,0:T(8,128)(2,1)S(1)}, bf16[16,768]{1,0:T(8,128)(2,1)}, u32[]{:S(2)}) copy-start(bf16[16,768]{1,0:T(8,128)(2,1)} %param.9) | copy-start | bytes 73732
  69.4 107.5 %all-to-all-start.2 = ((bf16[32,96,768]{2,1,0:T(8,128)(2,1)}), bf16[32,96,768]{2,1,0:T(8,128)(2,1)}, u32[]{:S(2)}, u32[]{:S(2)}) async-start(bf16[32,96,768]{2,1,0:T(8,128)(2,1)} %broadcast_select_fusion.1), calls=%async_computation.2 | async-start | bytes 9437184 | tf_op jit(solution)/shard_map/all_to_all | solution.py:85
  196.1 5.5 %copy-start.3 = (bf16[5120,768]{1,0:T(8,128)(2,1)S(1)}, bf16[5120,768]{1,0:T(8,128)(2,1)}, u32[]{:S(2)}) copy-start(bf16[5120,768]{1,0:T(8,128)(2,1)} %scatter_custom_fusion.1) | copy-start | bytes 23592964
  238.7 209.3 %all-to-all-start.4 = ((f32[32,96,768]{2,1,0:T(8,128)}), f32[32,96,768]{2,1,0:T(8,128)}, u32[]{:S(2)}, u32[]{:S(2)}) async-start(f32[32,96,768]{2,1,0:T(8,128)} %broadcast_select_fusion), calls=%async_computation.4 | async-start | bytes 18874368 | tf_op jit(solution)/shard_map/all_to_all | solution.py:100
  245.5 43.8 %reduce-scatter.2.cloned.1.call-start = ((), (), s32[]{:S(2)}) async-start(), calls=%async_computation.6 | async-start | bytes 1769472 | tf_op jit(solution)/shard_map/reduce_scatter | solution.py:111
  250.2 4.8 %copy-start.5 = (s32[1,1,32,96]{3,2,1,0:T(8,128)S(1)}, s32[1,1,32,96]{3,2,1,0:T(8,128)}, u32[]{:S(2)}) copy-start(s32[1,1,32,96]{3,2,1,0:T(8,128)} %param.11) | copy-start | bytes 36868
  448.0 8.2 %copy-start.1 = (bf16[16,32,768]{2,1,0:T(8,128)(2,1)S(1)}, bf16[16,32,768]{2,1,0:T(8,128)(2,1)}, u32[]{:S(2)}) copy-start(bf16[16,32,768]{2,1,0:T(8,128)(2,1)} %param.10) | copy-start | bytes 2359300
Sparse Core Ops, SparseCore 0:
  255.2 34.0 reduce-scatter.1
where the time goes:
time: 467 us; the launch traced here: 463 us
  waiting for transfers between devices  237 us (51%)
  local copies, waits for them, and re-layouts  92.6 us (20%)
  matrix products  37.1 us (8%)
  starting transfers between devices  36.9 us (8%)
  blocking collectives  22.7 us (5%)
  other arithmetic  22.5 us (5%)
  between operations  14.3 us (3%)
    all_to_all x1, waiting for transfers between devices, shards(): lax.all_to_all(grad_rows.reshape(owners, capacity, width), 'label', split...  157 us
    all_to_all x1, waiting for transfers between devices, shards(): lax.all_to_all(outgoing, 'label', split_axis=0, concat_axis=0, tiled=True)  60.5 us
    psum x1, blocking collectives, shards(): cluster_total = lax.psum(cluster_grad, 'dp')  22.7 us
    scatter x1, local copies, waits for them, and re-layouts, owner_terms(): tile_alpha = jnp.zeros((padded_total,), alpha.dtype).at[slot_dest].set(al...  21.6 us
    gather x1, local copies, waits for them, and re-layouts, owner_terms(): jnp.take(tile_grad.reshape(padded_total, width), slot_dest, axis=0)  20.9 us
    scatter x1, local copies, waits for them, and re-layouts, owner_terms(): jnp.zeros((padded_total, width), rows.dtype).at[slot_dest].set(rows)  19.2 us
    gather x1, local copies, waits for them, and re-layouts, shards(): jnp.take(embed, inst_ids.reshape(-1), axis=0)  13.6 us
    all_to_all x1, starting transfers between devices, shards(): lax.all_to_all(alpha, 'label', split_axis=0, concat_axis=0, tiled=True)  11.3 us
  transfers between devices with their start and end apart: 6, of which 5 were waited for; matrix products, arithmetic and copies ran while one was open for 17% of the time, Pallas kernels for 0%

commit v1 on v0

v1 whole, which is shorter than its diff:
```python
import jax
import jax.numpy as jnp
from jax import lax
from jax.experimental import pallas as pl
from jax.experimental.pallas import tpu as pltpu
from jax.sharding import Mesh, PartitionSpec as P

BF16 = jnp.bfloat16
F32 = jnp.float32
NY, NC, NZ, NX = 4, 2, 8, 4
SIZE = {"y": NY, "core": NC, "z": NZ, "x": NX}
INST, D, KIDS, CL = 64, 768, 32, 16
ROWS = INST * NZ
WIDE = (KIDS + 1) * CL
PART = 17 * CL
NT = (((1,), (1,)), ((), ()))
NN = (((1,), (0,)), ((), ()))
TN = (((0,), (0,)), ((), ()))
VMEM = pl.BlockSpec(memory_space=pltpu.VMEM)
PARAMS = pltpu.CompilerParams(vmem_limit_bytes=40 * 1024 * 1024)


def dot(a, b, dims):
    return lax.dot_general(a, b, dims, preferred_element_type=F32)


def shift(x, axis, by):
    n = SIZE[axis]
    return lax.ppermute(x, axis, [(i, (i + by) % n) for i in range(n)])


def slot_kernel(slots, ay, wide):
    lane_row = lax.broadcasted_iota(jnp.int32, (256, 128), 0)
    cluster_row = lax.broadcasted_iota(jnp.int32, (CL, 128), 0)
    left = []
    for q in range(4):
        side = slots[q, 0].astype(F32)
        alpha = side[KIDS : KIDS + 1]
        inst = side[KIDS + 1 : KIDS + 2].astype(jnp.int32)
        clus = side[KIDS + 2 : KIDS + 3].astype(jnp.int32)
        left.append(jnp.where(lane_row == inst + q * INST, alpha, 0.0).astype(BF16))
        member = cluster_row == clus
        for k in range(KIDS + 1):
            wide[k * CL : k * CL + CL, q * 128 : q * 128 + 128] = jnp.where(
                member, side[k : k + 1], 0.0
            ).astype(BF16)
    ay[0] = dot(wide[...], jnp.concatenate(left, axis=1), NT)


def sum_slots(slots):
    return pl.pallas_call(
        slot_kernel,
        grid=(NX, 2),
        out_shape=jax.ShapeDtypeStruct((NX, WIDE, ROWS), F32),
        in_specs=[pl.BlockSpec((4, 1, 40, 128), lambda o, g: (g, o, 0, 0))],
        out_specs=pl.BlockSpec((1, WIDE, 256), lambda o, g: (o, 0, g)),
        scratch_shapes=[pltpu.VMEM((WIDE, 512), BF16)],
        compiler_params=PARAMS,
    )(slots)


def first_kernel(place, e, w, a, b, c, d, ao, bo, co, do, ay, give, top, dzs, wall, z):
    r = pl.program_id(0)
    core = place[1]
    mine = pl.multiple_of(core * 256, 256)
    other = pl.multiple_of((1 - core) * 256, 256)

    @pl.when(r == 0)
    def _():
        wall[0] = w[...]
        for at, near, far in ((1, a, ao), (3, b, bo)):
            wall[at, pl.ds(mine, PART)] = near[...]
            wall[at, pl.ds(other, PART)] = far[...]
        wall[2, pl.ds(mine, 144)] = c[...]
        wall[2, pl.ds(pl.multiple_of(mine + 144, 16), 128)] = d[...]
        wall[2, pl.ds(other, 144)] = co[...]
        wall[2, pl.ds(pl.multiple_of(other + 144, 16), 128)] = do[...]

    z[...] = dot(wall[r], e[...], NT)
    s1 = jax.nn.sigmoid(z[KIDS * CL :])
    s1a = s1 * ay[0, KIDS * CL :]
    total = jnp.zeros((CL, ROWS), F32)
    for k in range(KIDS):
        at = pl.ds(k * CL, CL)
        s2 = jax.nn.sigmoid(z[at])
        t = s2 * (s1a * s2 - ay[0, at])
        total = total + t
        dzs[0, at] = (s1 * (1.0 - s2) * t).astype(BF16)
    dzs[0, KIDS * CL :] = (total * s1 * (1.0 - s1)).astype(BF16)
    out = dot(dzs[0, pl.ds(other, 256)], e[...], NN).astype(BF16)
    for y in range(NY):
        give[y, 0] = out[y * 64 : y * 64 + 64]
    top[0] = dot(dzs[0, KIDS * CL :], e[...], NN)


def first_terms(place, e, w, pieces, ay):
    def owner(r, place):
        return lax.rem(place[0] - r + NX, NX)

    return pl.pallas_call(
        first_kernel,
        grid_spec=pltpu.PrefetchScalarGridSpec(
            num_scalar_prefetch=1,
            grid=(NX,),
            in_specs=[VMEM] * (2 + len(pieces))
            + [pl.BlockSpec((1, WIDE, ROWS), lambda r, p: (owner(r, p), 0, 0))],
            out_specs=[
                pl.BlockSpec((NY, 1, 64, D), lambda r, p: (0, owner(r, p), 0, 0)),
                pl.BlockSpec((1, CL, D), lambda r, p: (owner(r, p), 0, 0)),
                pl.BlockSpec((1, WIDE, ROWS), lambda r, p: (r, 0, 0)),
                VMEM,
            ],
            scratch_shapes=[pltpu.VMEM((WIDE, ROWS), F32)],
        ),
        out_shape=(
            jax.ShapeDtypeStruct((NY, NX, 64, D), BF16),
            jax.ShapeDtypeStruct((NX, CL, D), F32),
            jax.ShapeDtypeStruct((NX, WIDE, ROWS), BF16),
            jax.ShapeDtypeStruct((NX, WIDE, D), BF16),
        ),
        compiler_params=PARAMS,
    )(place, e, w, *pieces, ay)


def second_kernel(place, e, dzs, wall, back, own, keep, ge):
    x, core, zz = place[0], place[1], place[2]
    ge[...] = dot(dzs[0], wall[0], TN)
    for r in range(1, NX):
        ge[...] += dot(dzs[r], wall[r], TN)
    for d in range(NZ):
        at = lax.rem(zz + d, NZ) * INST
        block = ge[pl.ds(pl.multiple_of(at, INST), INST)]
        if d == 0:
            own[...] = block
        else:
            back[d - 1] = block.astype(BF16)
    mine = pl.multiple_of(core * 256, 256)
    for r in range(NX):
        out = dot(dzs[r, pl.ds(mine, 256)], e[...], NN)
        to = lax.rem(x - r + NX, NX)
        for y in range(NY):
            keep[y, to] = out[y * 64 : y * 64 + 64]


def second_terms(place, e, dzs, wall):
    return pl.pallas_call(
        second_kernel,
        out_shape=(
            jax.ShapeDtypeStruct((NZ - 1, INST, D), BF16),
            jax.ShapeDtypeStruct((INST, D), F32),
            jax.ShapeDtypeStruct((NY, NX, 64, D), F32),
        ),
        in_specs=[pl.BlockSpec(memory_space=pltpu.SMEM)] + [VMEM] * 3,
        out_specs=[VMEM] * 3,
        scratch_shapes=[pltpu.VMEM((ROWS, D), F32)],
        compiler_params=PARAMS,
    )(place, e, dzs, wall)


def shards(e, cw, lw, inst, clus, counts, prefix, targets):
    iz, ix, ic = lax.axis_index("z"), lax.axis_index("x"), lax.axis_index("core")
    place = jnp.stack([ix, ic, iz]).astype(jnp.int32)

    with jax.named_scope("rows"):
        rows = lax.all_gather(e, "z", axis=0, tiled=True)

    with jax.named_scope("weights"):
        leaf = lw.reshape(CL, NY, NC, 4, D).transpose(2, 1, 3, 0, 4).reshape(KIDS * CL, D)
        w = jnp.concatenate([leaf, cw], axis=0)
        part = lax.dynamic_slice_in_dim(w, ic * 256, PART, 0)
        a, b = shift(part, "x", 1), shift(part, "x", -1)
        c, d = shift(a[:144], "x", 1), shift(b[144:], "x", -1)
        pieces = [a, b, c, d]
        pieces += [shift(p, "core", 1) for p in pieces]

    with jax.named_scope("slots"):
        cap = prefix.shape[-1]
        owners = NZ * NX
        inst, clus = inst.reshape(owners, 1, cap), clus.reshape(owners, 1, cap)
        valid = jnp.arange(cap, dtype=jnp.int32)[None, None, :] < counts.reshape(owners, 1, 1)
        nothing = jnp.zeros((), BF16)
        alpha = jnp.where(valid, prefix.reshape(owners, 1, cap), nothing)
        want = targets.reshape(owners, cap, NY, NC, 4).transpose(0, 3, 2, 4, 1)
        want = jnp.where(valid, want.reshape(owners, KIDS, cap), nothing)
        side = jnp.concatenate([want, alpha, inst.astype(BF16), clus.astype(BF16)], axis=1)
        side = jnp.pad(side, ((0, 0), (0, 5), (0, 128 - cap))).reshape(NZ, NX, 40, 128)
        slots = lax.all_to_all(side, "z", 0, 0, tiled=True)
    ay = sum_slots(slots)

    give, top, dzs, wall = first_terms(place, rows, w, pieces, ay)
    with jax.named_scope("weights_core"):
        got = shift(give, "core", 1)
        top = top + shift(top, "core", 1)
    back, own, keep = second_terms(place, rows, dzs, wall)

    with jax.named_scope("weights_back"):
        summed = (keep + got.astype(F32)).astype(BF16)
        tops = jnp.broadcast_to(top.astype(BF16)[None], (NY, NX, CL, D))
        out = jnp.concatenate([summed, tops], axis=2).reshape(NY * NX, 64 + CL, D)
        out = lax.all_to_all(out, ("y", "x"), 0, 0, tiled=True)
        out = jnp.sum(out.astype(F32), axis=0)
        grad_leaf = jnp.swapaxes(out[:64].reshape(4, CL, D), 0, 1)
        grad_cluster = out[64:]

    with jax.named_scope("rows_back"):
        grad_embed = own
        for d in (1, 7, 2, 6, 3, 5, 4):
            grad_embed = grad_embed + shift(back[d - 1], "z", d).astype(F32)
    return grad_embed, grad_cluster, grad_leaf


def solution(mesh):
    fine = Mesh(mesh.devices.reshape(NY, NC, NZ, NX), ("y", "core", "z", "x"))
    dp, label = ("y", "core"), ("z", "x")
    every = dp + label
    in_specs = (
        P(every, None),
        P(label, None),
        P(label, None, None),
        P(dp, label, None, None),
        P(dp, label, None, None),
        P(dp, label, None),
        P(dp, label, None, None),
        P(dp, label, None, None, None),
    )
    out_specs = (P(every, None), P(label, None), P(label, dp, None))
    return jax.shard_map(shards, mesh=fine, in_specs=in_specs, out_specs=out_specs, check_vma=False)
```

time: 467 us -> 115 us (0.25)
  waiting for transfers between devices: 237 us -> 13 us
  local copies, waits for them, and re-layouts: 92.6 us -> 6.8 us
  matrix products: 37.1 us -> 0 us
  Pallas kernels: 0 us -> 15.8 us
  other arithmetic: 22.5 us -> 7.1 us
  between operations: 14.3 us -> 0.97 us
  blocking collectives: 22.7 us -> 29.3 us
    all_to_all x5 -> x2, waiting for transfers between devices: 230 us -> 7.27 us  [the longest x1 7.27 us: shards(): out = lax.all_to_all(out, ('y', 'x'), 0, 0, tiled=True)]
    scatter x4 -> x0, local copies, waits for them, and re-layouts: 51.8 us -> none  [the longest x1 21.6 us: owner_terms(): tile_alpha = jnp.zeros((padded_total,), alpha.dtype).at[slot_dest].set(al...]
    dot_general x8 -> x0, matrix products: 37.1 us -> none  [the longest x1 8.15 us: shards(): lax.dot_general(onehot, returned.reshape(-1, width), (((0,), (0,)), ((),...]
    gather x4 -> x0, local copies, waits for them, and re-layouts: 35.9 us -> none  [the longest x1 20.9 us: owner_terms(): jnp.take(tile_grad.reshape(padded_total, width), slot_dest, axis=0)]
    all_gather x0 -> x1, blocking collectives: none -> 29.3 us  [shards(): rows = lax.all_gather(e, 'z', axis=0, tiled=True)]
    ppermute x0 -> x17, starting transfers between devices: none -> 24 us  [shift(): return lax.ppermute(x, axis, [(i, (i + by) % n) for i in range(n)])]
    psum x1 -> x0, blocking collectives: 22.7 us -> none  [shards(): cluster_total = lax.psum(cluster_grad, 'dp')]
    all_to_all x5 -> x2, starting transfers between devices: 36.7 us -> 16 us  [the longest x1 8.47 us: shards(): slots = lax.all_to_all(side, 'z', 0, 0, tiled=True)]
  transfers between devices with their start and end apart: 6 -> 19, of which waited for: 5 -> 4; matrix products, arithmetic and copies ran while one was open for 17% -> 3% of each run, Pallas kernels for 0% -> 7%
where the time goes in v1:
time: 115 us; the launch traced here: 113 us
  starting transfers between devices  40 us (35%)
  blocking collectives  29.3 us (25%)
  Pallas kernels  15.8 us (14%)
  waiting for transfers between devices  13 us (11%)
  other arithmetic  7.1 us (6%)
  local copies, waits for them, and re-layouts  6.8 us (6%)
    all_gather x1, blocking collectives, shards(): rows = lax.all_gather(e, 'z', axis=0, tiled=True)  29.3 us
    ppermute x17, starting transfers between devices, shift(): return lax.ppermute(x, axis, [(i, (i + by) % n) for i in range(n)])  24 us
    all_to_all x1, starting transfers between devices, shards(): slots = lax.all_to_all(side, 'z', 0, 0, tiled=True)  8.47 us
    pallas_call x1, Pallas kernels, first_terms(): pl.pallas_call(first_kernel, grid_spec=pltpu.PrefetchScalarGridSpec(num_s...  8.14 us
    all_to_all x1, starting transfers between devices, shards(): out = lax.all_to_all(out, ('y', 'x'), 0, 0, tiled=True)  7.49 us
    all_to_all x1, waiting for transfers between devices, shards(): out = lax.all_to_all(out, ('y', 'x'), 0, 0, tiled=True)  7.27 us
    ppermute x17, waiting for transfers between devices, shift(): return lax.ppermute(x, axis, [(i, (i + by) % n) for i in range(n)])  5.77 us
    pallas_call x1, Pallas kernels, second_terms(): pl.pallas_call(second_kernel, out_shape=(jax.ShapeDtypeStruct((NZ - 1, IN...  4.07 us
  transfers between devices with their start and end apart: 19, of which 4 were waited for; matrix products, arithmetic and copies ran while one was open for 3% of the time, Pallas kernels for 7%

profile of v1, /device:TPU:24, one launch (start us, length us, event | category | flops | bytes accessed | tf_op | source)
XLA Modules:
  0.0 112.9 jit_solution(8872143479149659301)
XLA Ops:
  0.7 1.7 %reshape.131 = bf16[16,4,2,4,768]{4,3,2,1,0:T(4,128)(2,1)S(1)} reshape(bf16[16,32,768]{2,1,0:T(8,128)(2,1)} %param.10) | data formatting | bytes 1572864 | tf_op jit(solution)/shard_map/weights/reshape | solution.py:168
  2.9 0.9 copy-done.1
  4.0 2.8 %collective-permute-start.1 = (bf16[272,768]{1,0:T(8,128)(2,1)S(1)}, bf16[272,768]{1,0:T(8,128)(2,1)S(1)}, u32[]{:S(2)}, u32[]{:S(2)}) collective-permute-start(bf16[272,768]{1,0:T(8,128)(2,1)S(1)} %fusion.5), channel_id=1, source_target_pairs={{0,3},{1,0},{2,1},{3,2},{4,7},{5,4},{6,5},{7,6},{8,11},{9,8},{10,9... | collective-permute-start | bytes 1253384 | tf_op jit(solution)/shard_map/weights/ppermute | solution.py:29
  7.3 1.0 fusion.9
  8.3 8.5 %all-to-all-start = ((bf16[8,4,40,128]{3,2,1,0:T(8,128)(2,1)}), bf16[8,4,40,128]{3,2,1,0:T(8,128)(2,1)S(1)}, u32[]{:S(2)}, u32[]{:S(2)}) async-start(bf16[8,4,40,128]{3,2,1,0:T(8,128)(2,1)} %bitcast.12), calls=%async_computation | async-start | bytes 655360 | tf_op jit(solution)/shard_map/slots/all_to_all | solution.py:187
  16.8 3.3 %collective-permute-start.3 = (bf16[128,768]{1,0:T(8,128)(2,1)S(1)}, bf16[128,768]{1,0:T(8,128)(2,1)}, u32[]{:S(2)}, u32[]{:S(2)}) collective-permute-start(bf16[128,768]{1,0:T(8,128)(2,1)S(1)} %slice.45), channel_id=1, source_target_pairs={{0,3},{1,0},{2,1},{3,2},{4,7},{5,4},{6,5},{7,6},{8,11},{9,8},{10,9... | collective-permute-start | bytes 589832 | tf_op jit(solution)/shard_map/weights/ppermute | solution.py:29
  20.8 29.3 %all_gather.3.e = bf16[512,768]{1,0:T(8,128)(2,1)S(1)} all-gather(bf16[64,768]{1,0:T(8,128)(2,1)S(1)} %copy-done.3), channel_id=1, replica_groups=mesh['y'=4,'core'=2,'z'=8,'x'=4] {'z'}, dimensions={0}, use_global_device_ids=true | all-gather | bytes 884736 | tf_op jit(solution)/shard_map/rows/all_gather | solution.py:165
  50.7 1.2 %pad_maximum_fusion.1.w = bf16[528,768]{1,0:T(8,128)(2,1)S(1)} fusion(bf16[16,768]{1,0:T(8,128)(2,1)S(1)} %copy-done.4, bf16[512,768]{1,0:T(8,128)(2,1)} %bitcast.37), kind=kLoop, calls=%fused_computation.4 | loop fusion | flops 1622016 | bytes 1622016 | tf_op jit(solution)/shard_map/weights/concatenate | solution.py:169
  51.9 3.5 %shard_map.103.ay = f32[4,528,512]{2,1,0:T(8,128)S(1)} custom-call(bf16[8,4,40,128]{3,2,1,0:T(8,128)(2,1)S(1)} %all-to-all-done.slots), custom_call_target="tpu_custom_call" | custom-call | tf_op jit(solution)/shard_map/pallas_call | solution.py:51
  55.5 2.0 %copy-done = f32[4,528,512]{2,1,0:T(8,128)} copy-done((f32[4,528,512]{2,1,0:T(8,128)}, f32[4,528,512]{2,1,0:T(8,128)S(1)}, u32[]{:S(2)}) %copy-start) | copy-done | bytes 4325400
  57.5 8.1 %shard_map.104 = (bf16[4,4,64,768]{3,2,1,0:T(8,128)(2,1)S(1)}, f32[4,16,768]{2,1,0:T(8,128)S(1)}, bf16[4,528,512]{2,1,0:T(8,128)(2,1)S(1)}, bf16[4,528,768]{2,1,0:T(8,128)(2,1)S(1)}) custom-call(s32[3]{0:T(128)S(1)} %pad_add_fusion.place, bf16[512,768]{1,0:T(8,128)(2,1)S(1)} %all_gather.3.e, bf16[528,768]{1,0:T(8,128)(2,1)S(1)} %pad_maximum_fusion.1.w, ...), custom_call_target="tpu_custom_call" | custom-call | tf_op jit(solution)/shard_map/pallas_call | solution.py:100
  66.2 4.1 %shard_map.105 = (bf16[7,64,768]{2,1,0:T(8,128)(2,1)S(1)}, f32[64,768]{1,0:T(8,128)S(1)}, f32[4,4,64,768]{3,2,1,0:T(8,128)S(1)}) custom-call(s32[3]{0:T(128)S(1)} %pad_add_fusion.place, bf16[512,768]{1,0:T(8,128)(2,1)S(1)} %all_gather.3.e, bf16[4,528,512]{2,1,0:T(8,128)(2,1)S(1)} %get-tuple-element.10.dzs, bf16[4,528,768]{2,1,0:T(8,128)(2,1)S(1)} %get-tuple-element.11.wall), custom_call_target="tpu_custom_call" | custom-call | tf_op jit(solution)/shard_map/pallas_call | solution.py:146
  70.8 1.4 %pad_maximum_fusion = bf16[4,4,80,768]{3,2,1,0:T(8,128)(2,1)} fusion(bf16[4,4,16,768]{3,2,1,0:T(8,128)(2,1)S(1)} %broadcast_in_dim.26, bf16[4,4,64,768]{3,2,1,0:T(8,128)(2,1)S(1)} %add_convert_fusion), kind=kLoop, calls=%fused_computation.2 | loop fusion | flops 3932160 | bytes 3932160 | tf_op jit(solution)/shard_map/weights_back/concatenate | solution.py:199
  72.2 7.5 %all-to-all-start.1 = ((bf16[16,80,768]{2,1,0:T(8,128)(2,1)}), bf16[16,80,768]{2,1,0:T(8,128)(2,1)}, u32[]{:S(2)}, u32[]{:S(2)}) async-start(bf16[16,80,768]{2,1,0:T(8,128)(2,1)} %bitcast.20), calls=%async_computation.1 | async-start | bytes 3932160 | tf_op jit(solution)/shard_map/weights_back/all_to_all | solution.py:200
  79.8 0.8 collective-permute-start.8
  80.6 2.7 %collective-permute-start.14 = (bf16[64,768]{1,0:T(8,128)(2,1)S(1)}, bf16[64,768]{1,0:T(8,128)(2,1)S(1)}, u32[]{:S(2)}, u32[]{:S(2)}) collective-permute-start(bf16[64,768]{1,0:T(8,128)(2,1)S(1)} %get-tuple-element.21), channel_id=1, source_target_pairs={{0,16},{4,20},{8,24},{12,28},{16,0},{20,4},{24,8},{28,12},{1,17},{... | collective-permute-start | bytes 294920 | tf_op jit(solution)/shard_map/rows_back/ppermute | solution.py:29
  83.3 2.8 %collective-permute-start.13 = (bf16[64,768]{1,0:T(8,128)(2,1)S(1)}, bf16[64,768]{1,0:T(8,128)(2,1)S(1)}, u32[]{:S(2)}, u32[]{:S(2)}) collective-permute-start(bf16[64,768]{1,0:T(8,128)(2,1)S(1)} %get-tuple-element.22), channel_id=1, source_target_pairs={{0,20},{4,24},{8,28},{12,0},{16,4},{20,8},{24,12},{28,16},{1,21},{... | collective-permute-start | bytes 294920 | tf_op jit(solution)/shard_map/rows_back/ppermute | solution.py:29
  86.1 1.0 collective-permute-start.12
  87.1 3.5 %collective-permute-start.11 = (bf16[64,768]{1,0:T(8,128)(2,1)S(1)}, bf16[64,768]{1,0:T(8,128)(2,1)S(1)}, u32[]{:S(2)}, u32[]{:S(2)}) collective-permute-start(bf16[64,768]{1,0:T(8,128)(2,1)S(1)} %get-tuple-element.24), channel_id=1, source_target_pairs={{0,24},{4,28},{8,0},{12,4},{16,8},{20,12},{24,16},{28,20},{1,25},{... | collective-permute-start | bytes 294920 | tf_op jit(solution)/shard_map/rows_back/ppermute | solution.py:29
  90.7 5.2 %collective-permute-start.9 = (bf16[64,768]{1,0:T(8,128)(2,1)S(1)}, bf16[64,768]{1,0:T(8,128)(2,1)S(1)}, u32[]{:S(2)}, u32[]{:S(2)}) collective-permute-start(bf16[64,768]{1,0:T(8,128)(2,1)S(1)} %get-tuple-element.26), channel_id=1, source_target_pairs={{0,28},{4,0},{8,4},{12,8},{16,12},{20,16},{24,20},{28,24},{1,29},{... | collective-permute-start | bytes 294920 | tf_op jit(solution)/shard_map/rows_back/ppermute | solution.py:29
  96.2 3.3 %collective-permute-done.12 = bf16[64,768]{1,0:T(8,128)(2,1)S(1)} collective-permute-done((bf16[64,768]{1,0:T(8,128)(2,1)S(1)}, bf16[64,768]{1,0:T(8,128)(2,1)S(1)}, u32[]{:S(2)}, u32[]{:S(2)}) %collective-permute-start.12) | collective-permute-done | bytes 98336 | tf_op jit(solution)/shard_map/rows_back/ppermute | solution.py:29
  99.5 2.0 %collective-permute-done.11 = bf16[64,768]{1,0:T(8,128)(2,1)S(1)} collective-permute-done((bf16[64,768]{1,0:T(8,128)(2,1)S(1)}, bf16[64,768]{1,0:T(8,128)(2,1)S(1)}, u32[]{:S(2)}, u32[]{:S(2)}) %collective-permute-start.11) | collective-permute-done | bytes 98336 | tf_op jit(solution)/shard_map/rows_back/ppermute | solution.py:29
  102.4 7.3 %all-to-all-done.1 = bf16[16,80,768]{2,1,0:T(8,128)(2,1)} async-done(((bf16[16,80,768]{2,1,0:T(8,128)(2,1)}), bf16[16,80,768]{2,1,0:T(8,128)(2,1)}, u32[]{:S(2)}, u32[]{:S(2)}) %all-to-all-start.1) | async-done | bytes 1966112 | tf_op jit(solution)/shard_map/weights_back/all_to_all | solution.py:200
  109.6 1.8 %convert_reduce_fusion = f32[80,768]{1,0:T(8,128)S(1)} fusion(bf16[16,80,768]{2,1,0:T(8,128)(2,1)} %all-to-all-done.1), kind=kLoop, calls=%fused_computation | loop fusion | flops 1904640 | bytes 2211840 | tf_op jit(solution)/shard_map/weights_back/reduce_sum | solution.py:201
  (63 shorter events, 6.0 us)
Async XLA Ops:
  0.6 6.2 %copy-start.5 = (s32[1,1,32,96]{3,2,1,0:T(8,128)S(1)}, s32[1,1,32,96]{3,2,1,0:T(8,128)}, u32[]{:S(2)}) copy-start(s32[1,1,32,96]{3,2,1,0:T(8,128)} %param.11) | copy-start | bytes 36868
  0.7 6.2 %copy-start.7 = (bf16[1,1,32,96]{3,2,1,0:T(8,128)(2,1)S(1)}, bf16[1,1,32,96]{3,2,1,0:T(8,128)(2,1)}, u32[]{:S(2)}) copy-start(bf16[1,1,32,96]{3,2,1,0:T(8,128)(2,1)} %param.14) | copy-start | bytes 18436
  0.7 6.2 %copy-start.8 = (s32[1,1,32]{2,1,0:T(1,128)S(1)}, s32[1,1,32]{2,1,0:T(1,128)}, u32[]{:S(2)}) copy-start(s32[1,1,32]{2,1,0:T(1,128)} %param.13) | copy-start | bytes 388
  0.7 6.5 %copy-start.2 = (bf16[1,1,32,96,32]{3,4,2,1,0:T(8,128)(2,1)S(1)}, bf16[1,1,32,96,32]{3,4,2,1,0:T(8,128)(2,1)}, u32[]{:S(2)}) copy-start(bf16[1,1,32,96,32]{3,4,2,1,0:T(8,128)(2,1)} %param.15) | copy-start | bytes 589828
  4.0 16.8 %copy-start.3 = (bf16[64,768]{1,0:T(8,128)(2,1)S(1)}, bf16[64,768]{1,0:T(8,128)(2,1)}, u32[]{:S(2)}) copy-start(bf16[64,768]{1,0:T(8,128)(2,1)} %param.8) | copy-start | bytes 294916
  4.0 12.7 %collective-permute-start.1 = (bf16[272,768]{1,0:T(8,128)(2,1)S(1)}, bf16[272,768]{1,0:T(8,128)(2,1)S(1)}, u32[]{:S(2)}, u32[]{:S(2)}) collective-permute-start(bf16[272,768]{1,0:T(8,128)(2,1)S(1)} %fusion.5), channel_id=1, source_target_pairs={{0,3},{1,0},{2,1},{3,2},{4,7},{5,4},{6,5},{7,6},{8,11},{9,8},{10,9... | collective-permute-start | bytes 1253384 | tf_op jit(solution)/shard_map/weights/ppermute | solution.py:29
  6.9 13.2 %collective-permute-start = (bf16[272,768]{1,0:T(8,128)(2,1)S(1)}, bf16[272,768]{1,0:T(8,128)(2,1)S(1)}, u32[]{:S(2)}, u32[]{:S(2)}) collective-permute-start(bf16[272,768]{1,0:T(8,128)(2,1)S(1)} %fusion.5), channel_id=1, source_target_pairs={{0,1},{1,2},{2,3},{3,0},{4,5},{5,6},{6,7},{7,4},{8,9},{9,10},{10,1... | collective-permute-start | bytes 1253384 | tf_op jit(solution)/shard_map/weights/ppermute | solution.py:29
  8.3 43.6 %all-to-all-start = ((bf16[8,4,40,128]{3,2,1,0:T(8,128)(2,1)}), bf16[8,4,40,128]{3,2,1,0:T(8,128)(2,1)S(1)}, u32[]{:S(2)}, u32[]{:S(2)}) async-start(bf16[8,4,40,128]{3,2,1,0:T(8,128)(2,1)} %bitcast.12), calls=%async_computation | async-start | bytes 655360 | tf_op jit(solution)/shard_map/slots/all_to_all | solution.py:187
  16.8 33.3 %collective-permute-start.3 = (bf16[128,768]{1,0:T(8,128)(2,1)S(1)}, bf16[128,768]{1,0:T(8,128)(2,1)}, u32[]{:S(2)}, u32[]{:S(2)}) collective-permute-start(bf16[128,768]{1,0:T(8,128)(2,1)S(1)} %slice.45), channel_id=1, source_target_pairs={{0,3},{1,0},{2,1},{3,2},{4,7},{5,4},{6,5},{7,6},{8,11},{9,8},{10,9... | collective-permute-start | bytes 589832 | tf_op jit(solution)/shard_map/weights/ppermute | solution.py:29
  20.1 30.0 %collective-permute-start.2 = (bf16[144,768]{1,0:T(8,128)(2,1)S(1)}, bf16[144,768]{1,0:T(8,128)(2,1)S(1)}, u32[]{:S(2)}, u32[]{:S(2)}) collective-permute-start(bf16[144,768]{1,0:T(8,128)(2,1)S(1)} %slice.44), channel_id=1, source_target_pairs={{0,1},{1,2},{2,3},{3,0},{4,5},{5,6},{6,7},{7,4},{8,9},{9,10},{10,1... | collective-permute-start | bytes 663560 | tf_op jit(solution)/shard_map/weights/ppermute | solution.py:29
  20.2 37.3 %collective-permute-start.5 = (bf16[272,768]{1,0:T(8,128)(2,1)S(1)}, bf16[272,768]{1,0:T(8,128)(2,1)S(1)}, u32[]{:S(2)}, u32[]{:S(2)}) collective-permute-start(bf16[272,768]{1,0:T(8,128)(2,1)S(1)} %collective-permute-done.1.b), channel_id=1, source_target_pairs={{0,32},{32,0},{1,33},{33,1},{2,34},{34,2},{3,35},{35,3},{4,36},{36... | collective-permute-start | bytes 1253384 | tf_op jit(solution)/shard_map/weights/ppermute | solution.py:29
  20.3 37.2 %collective-permute-start.4 = (bf16[272,768]{1,0:T(8,128)(2,1)S(1)}, bf16[272,768]{1,0:T(8,128)(2,1)}, u32[]{:S(2)}, u32[]{:S(2)}) collective-permute-start(bf16[272,768]{1,0:T(8,128)(2,1)S(1)} %collective-permute-done.a), channel_id=1, source_target_pairs={{0,32},{32,0},{1,33},{33,1},{2,34},{34,2},{3,35},{35,3},{4,36},{36... | collective-permute-start | bytes 1253384 | tf_op jit(solution)/shard_map/weights/ppermute | solution.py:29
  50.1 7.4 %collective-permute-start.7 = (bf16[128,768]{1,0:T(8,128)(2,1)}, bf16[128,768]{1,0:T(8,128)(2,1)}, u32[]{:S(2)}, u32[]{:S(2)}) collective-permute-start(bf16[128,768]{1,0:T(8,128)(2,1)} %collective-permute-done.3.d), channel_id=1, source_target_pairs={{0,32},{32,0},{1,33},{33,1},{2,34},{34,2},{3,35},{35,3},{4,36},{36... | collective-permute-start | bytes 589832 | tf_op jit(solution)/shard_map/weights/ppermute | solution.py:29
  50.1 7.4 %collective-permute-start.6 = (bf16[144,768]{1,0:T(8,128)(2,1)S(1)}, bf16[144,768]{1,0:T(8,128)(2,1)}, u32[]{:S(2)}, u32[]{:S(2)}) collective-permute-start(bf16[144,768]{1,0:T(8,128)(2,1)S(1)} %collective-permute-done.2.c), channel_id=1, source_target_pairs={{0,32},{32,0},{1,33},{33,1},{2,34},{34,2},{3,35},{35,3},{4,36},{36... | collective-permute-start | bytes 663560 | tf_op jit(solution)/shard_map/weights/ppermute | solution.py:29
  65.6 4.7 %collective-permute-start.15 = (bf16[4,4,64,768]{3,2,1,0:T(8,128)(2,1)S(1)}, bf16[4,4,64,768]{3,2,1,0:T(8,128)(2,1)S(1)}, u32[]{:S(2)}, u32[]{:S(2)}) collective-permute-start(bf16[4,4,64,768]{3,2,1,0:T(8,128)(2,1)S(1)} %get-tuple-element.15), channel_id=1, source_target_pairs={{0,32},{32,0},{1,33},{33,1},{2,34},{34,2},{3,35},{35,3},{4,36},{36... | collective-permute-start | bytes 4718600 | tf_op jit(solution)/shard_map/weights_core/ppermute | solution.py:29
  65.8 4.5 %collective-permute-start.16 = (f32[4,16,768]{2,1,0:T(8,128)S(1)}, f32[4,16,768]{2,1,0:T(8,128)S(1)}, u32[]{:S(2)}, u32[]{:S(2)}) collective-permute-start(f32[4,16,768]{2,1,0:T(8,128)S(1)} %get-tuple-element.16), channel_id=1, source_target_pairs={{0,32},{32,0},{1,33},{33,1},{2,34},{34,2},{3,35},{35,3},{4,36},{36... | collective-permute-start | bytes 589832 | tf_op jit(solution)/shard_map/weights_core/ppermute | solution.py:29
  72.2 37.4 %all-to-all-start.1 = ((bf16[16,80,768]{2,1,0:T(8,128)(2,1)}), bf16[16,80,768]{2,1,0:T(8,128)(2,1)}, u32[]{:S(2)}, u32[]{:S(2)}) async-start(bf16[16,80,768]{2,1,0:T(8,128)(2,1)} %bitcast.20), calls=%async_computation.1 | async-start | bytes 3932160 | tf_op jit(solution)/shard_map/weights_back/all_to_all | solution.py:200
  79.8 10.9 %collective-permute-start.8 = (bf16[64,768]{1,0:T(8,128)(2,1)S(1)}, bf16[64,768]{1,0:T(8,128)(2,1)S(1)}, u32[]{:S(2)}, u32[]{:S(2)}) collective-permute-start(bf16[64,768]{1,0:T(8,128)(2,1)S(1)} %get-tuple-element.20), channel_id=1, source_target_pairs={{0,4},{4,8},{8,12},{12,16},{16,20},{20,24},{24,28},{28,0},{1,5},{5... | collective-permute-start | bytes 294920 | tf_op jit(solution)/shard_map/rows_back/ppermute | solution.py:29
  80.6 10.1 %collective-permute-start.14 = (bf16[64,768]{1,0:T(8,128)(2,1)S(1)}, bf16[64,768]{1,0:T(8,128)(2,1)S(1)}, u32[]{:S(2)}, u32[]{:S(2)}) collective-permute-start(bf16[64,768]{1,0:T(8,128)(2,1)S(1)} %get-tuple-element.21), channel_id=1, source_target_pairs={{0,16},{4,20},{8,24},{12,28},{16,0},{20,4},{24,8},{28,12},{1,17},{... | collective-permute-start | bytes 294920 | tf_op jit(solution)/shard_map/rows_back/ppermute | solution.py:29
  83.3 12.9 %collective-permute-start.13 = (bf16[64,768]{1,0:T(8,128)(2,1)S(1)}, bf16[64,768]{1,0:T(8,128)(2,1)S(1)}, u32[]{:S(2)}, u32[]{:S(2)}) collective-permute-start(bf16[64,768]{1,0:T(8,128)(2,1)S(1)} %get-tuple-element.22), channel_id=1, source_target_pairs={{0,20},{4,24},{8,28},{12,0},{16,4},{20,8},{24,12},{28,16},{1,21},{... | collective-permute-start | bytes 294920 | tf_op jit(solution)/shard_map/rows_back/ppermute | solution.py:29
  86.1 13.4 %collective-permute-start.12 = (bf16[64,768]{1,0:T(8,128)(2,1)S(1)}, bf16[64,768]{1,0:T(8,128)(2,1)S(1)}, u32[]{:S(2)}, u32[]{:S(2)}) collective-permute-start(bf16[64,768]{1,0:T(8,128)(2,1)S(1)} %get-tuple-element.23), channel_id=1, source_target_pairs={{0,12},{4,16},{8,20},{12,24},{16,28},{20,0},{24,4},{28,8},{1,13},{... | collective-permute-start | bytes 294920 | tf_op jit(solution)/shard_map/rows_back/ppermute | solution.py:29
  87.1 14.4 %collective-permute-start.11 = (bf16[64,768]{1,0:T(8,128)(2,1)S(1)}, bf16[64,768]{1,0:T(8,128)(2,1)S(1)}, u32[]{:S(2)}, u32[]{:S(2)}) collective-permute-start(bf16[64,768]{1,0:T(8,128)(2,1)S(1)} %get-tuple-element.24), channel_id=1, source_target_pairs={{0,24},{4,28},{8,0},{12,4},{16,8},{20,12},{24,16},{28,20},{1,25},{... | collective-permute-start | bytes 294920 | tf_op jit(solution)/shard_map/rows_back/ppermute | solution.py:29
  90.7 10.9 %collective-permute-start.10 = (bf16[64,768]{1,0:T(8,128)(2,1)S(1)}, bf16[64,768]{1,0:T(8,128)(2,1)S(1)}, u32[]{:S(2)}, u32[]{:S(2)}) collective-permute-start(bf16[64,768]{1,0:T(8,128)(2,1)S(1)} %get-tuple-element.25), channel_id=1, source_target_pairs={{0,8},{4,12},{8,16},{12,20},{16,24},{20,28},{24,0},{28,4},{1,9},{5... | collective-permute-start | bytes 294920 | tf_op jit(solution)/shard_map/rows_back/ppermute | solution.py:29
  90.7 10.9 %collective-permute-start.9 = (bf16[64,768]{1,0:T(8,128)(2,1)S(1)}, bf16[64,768]{1,0:T(8,128)(2,1)S(1)}, u32[]{:S(2)}, u32[]{:S(2)}) collective-permute-start(bf16[64,768]{1,0:T(8,128)(2,1)S(1)} %get-tuple-element.26), channel_id=1, source_target_pairs={{0,28},{4,0},{8,4},{12,8},{16,12},{20,16},{24,20},{28,24},{1,29},{... | collective-permute-start | bytes 294920 | tf_op jit(solution)/shard_map/rows_back/ppermute | solution.py:29
  (4 other events, 12.3 us)

commit v2 on v1

v2 whole, which is shorter than its diff:
```python
import functools

import jax
import jax.numpy as jnp
from jax import lax
from jax.experimental import pallas as pl
from jax.experimental.pallas import tpu as pltpu
from jax.sharding import Mesh, PartitionSpec as P

BF16 = jnp.bfloat16
F32 = jnp.float32
NY, NC, NZ, NX = 4, 2, 8, 4
SIZE = {"y": NY, "core": NC, "z": NZ, "x": NX}
INST, D, KIDS, CL = 64, 768, 32, 16
ROWS = INST * NZ
WIDE = (KIDS + 1) * CL
PART = 17 * CL
NT = (((1,), (1,)), ((), ()))
NN = (((1,), (0,)), ((), ()))
TN = (((0,), (0,)), ((), ()))
VMEM = pl.BlockSpec(memory_space=pltpu.VMEM)
SMEM = pl.BlockSpec(memory_space=pltpu.SMEM)
PARAMS = pltpu.CompilerParams(vmem_limit_bytes=40 * 1024 * 1024)


def dot(a, b, dims):
    return lax.dot_general(a, b, dims, preferred_element_type=F32)


def shift(x, axis, by):
    n = SIZE[axis]
    return lax.ppermute(x, axis, [(i, (i + by) % n) for i in range(n)])


def cost(flops):
    return pl.CostEstimate(flops=flops, bytes_accessed=1 << 20, transcendentals=0)


def slot_kernel(place, slots, ay, wide):
    x, z = place[0], place[2]
    lane_row = lax.broadcasted_iota(jnp.int32, (256, 128), 0)
    cluster_row = lax.broadcasted_iota(jnp.int32, (CL, 128), 0)

    def step(i, _):
        r, g = i // 2, lax.rem(i, 2)
        owner = lax.rem(x - r + NX, NX)
        left = []
        for q in range(4):
            side = slots[lax.rem(z - (g * 4 + q) + NZ, NZ), owner].astype(F32)
            alpha = side[KIDS : KIDS + 1]
            inst = side[KIDS + 1 : KIDS + 2].astype(jnp.int32)
            clus = side[KIDS + 2 : KIDS + 3].astype(jnp.int32)
            left.append(jnp.where(lane_row == inst + q * INST, alpha, 0.0).astype(BF16))
            member = cluster_row == clus
            for k in range(KIDS + 1):
                wide[k * CL : k * CL + CL, q * 128 : q * 128 + 128] = jnp.where(
                    member, side[k : k + 1], 0.0
                ).astype(BF16)
        ay[r, :, pl.ds(pl.multiple_of(g * 256, 256), 256)] = dot(
            wide[...], jnp.concatenate(left, axis=1), NT
        )
        return 0

    lax.fori_loop(0, 2 * NX, step, 0)


def sum_slots(place, slots):
    return pl.pallas_call(
        slot_kernel,
        out_shape=jax.ShapeDtypeStruct((NX, WIDE, ROWS), F32),
        in_specs=[SMEM, VMEM],
        out_specs=VMEM,
        scratch_shapes=[pltpu.VMEM((WIDE, 512), BF16)],
        compiler_params=PARAMS,
        cost_estimate=cost(2 * 10**9),
    )(place, slots)


def owner_kernel(r, n_e, n_w, place, *refs):
    core = place[1]
    blocks, refs = refs[:n_e], refs[n_e:]
    pieces, refs = refs[:n_w], refs[n_w:]
    ay, refs = refs[0], refs[1:]
    keep, give, dzs, refs = refs[0], refs[1], refs[2], refs[3:]
    z = refs[-1]
    mine = pl.multiple_of(core * 256, 256)
    other = pl.multiple_of((1 - core) * 256, 256)
    if n_e > 1:
        e = refs[0]
        for i in range(n_e):
            e[i * INST : i * INST + INST] = blocks[i][...]
    else:
        e = blocks[0]
    if n_w == 1:
        w = pieces[0]
    else:
        w = refs[-2]
        half = n_w // 2
        for base, part in ((mine, pieces[:half]), (other, pieces[half:])):
            at = 0
            for p in part:
                w[pl.ds(pl.multiple_of(base + at, 16), p.shape[0])] = p[...]
                at += p.shape[0]
    z[...] = dot(w[...], e[...], NT)
    s1 = jax.nn.sigmoid(z[KIDS * CL :])
    s1a = s1 * ay[r, KIDS * CL :]
    total = jnp.zeros((CL, ROWS), F32)
    for k in range(KIDS):
        at = pl.ds(k * CL, CL)
        s2 = jax.nn.sigmoid(z[at])
        t = s2 * (s1a * s2 - ay[r, at])
        total = total + t
        dzs[at] = (s1 * (1.0 - s2) * t).astype(BF16)
    dzs[KIDS * CL :] = (total * s1 * (1.0 - s1)).astype(BF16)
    top = dot(dzs[KIDS * CL :], e[...], NN).astype(BF16)
    give[:256] = dot(dzs[pl.ds(other, 256)], e[...], NN).astype(BF16)
    give[256:] = top
    keep[:256] = dot(dzs[pl.ds(mine, 256)], e[...], NN)
    keep[256:] = top.astype(F32)


def owner_terms(r, place, blocks, pieces, ay):
    n_e, n_w = len(blocks), len(pieces)
    out = [
        jax.ShapeDtypeStruct((PART, D), F32),
        jax.ShapeDtypeStruct((PART, D), BF16),
        jax.ShapeDtypeStruct((WIDE, ROWS), BF16),
    ]
    if n_e > 1:
        out.append(jax.ShapeDtypeStruct((ROWS, D), BF16))
    if n_w > 1:
        out.append(jax.ShapeDtypeStruct((WIDE, D), BF16))
    return pl.pallas_call(
        functools.partial(owner_kernel, r, n_e, n_w),
        out_shape=tuple(out),
        in_specs=[SMEM] + [VMEM] * (n_e + n_w + 1),
        out_specs=[VMEM] * len(out),
        scratch_shapes=[pltpu.VMEM((WIDE, ROWS), F32)],
        compiler_params=PARAMS,
        cost_estimate=cost(2 * 10**9),
    )(place, *blocks, *pieces, ay)


def rows_kernel(*refs):
    dzs, ws, back, own, ge = refs[:NX], refs[NX : 2 * NX], refs[-3], refs[-2], refs[-1]
    ge[...] = dot(dzs[0][...], ws[0][...], TN)
    for r in range(1, NX):
        ge[...] += dot(dzs[r][...], ws[r][...], TN)
    own[...] = ge[:INST]
    for d in range(1, NZ):
        back[d - 1] = ge[d * INST : d * INST + INST].astype(BF16)


def row_terms(dzs, ws):
    return pl.pallas_call(
        rows_kernel,
        out_shape=(
            jax.ShapeDtypeStruct((NZ - 1, INST, D), BF16),
            jax.ShapeDtypeStruct((INST, D), F32),
        ),
        in_specs=[VMEM] * (2 * NX),
        out_specs=[VMEM] * 2,
        scratch_shapes=[pltpu.VMEM((ROWS, D), F32)],
        compiler_params=PARAMS,
        cost_estimate=cost(2 * 10**9),
    )(*dzs, *ws)


def shards(e, cw, lw, inst, clus, counts, prefix, targets):
    ix, iy, iz = lax.axis_index("x"), lax.axis_index("y"), lax.axis_index("z")
    ic = lax.axis_index("core")
    place = jnp.stack([ix, ic, iz]).astype(jnp.int32)

    with jax.named_scope("rows"):
        e1, e7 = shift(e, "z", 1), shift(e, "z", -1)
        e2, e6 = shift(e1, "z", 1), shift(e7, "z", -1)
        e3, e5 = shift(e2, "z", 1), shift(e6, "z", -1)
        e4a, e4b = shift(e3[:32], "z", 1), shift(e5[32:], "z", -1)
        blocks = [e, e1, e2, e3, jnp.concatenate([e4a, e4b], axis=0), e5, e6, e7]

    with jax.named_scope("weights"):
        leaf = lw.reshape(CL, NY, NC, 4, D).transpose(2, 1, 3, 0, 4).reshape(KIDS * CL, D)
        w = jnp.concatenate([leaf, cw], axis=0)
        part = lax.dynamic_slice_in_dim(w, ic * 256, PART, 0)
        a, b = shift(part, "x", 1), shift(part, "x", -1)
        c, d = shift(a[:144], "x", 1), shift(b[144:], "x", -1)
        ao, bo, co, do = (shift(p, "core", 1) for p in (a, b, c, d))

    with jax.named_scope("slots"):
        cap = prefix.shape[-1]
        owners = NZ * NX
        inst, clus = inst.reshape(owners, 1, cap), clus.reshape(owners, 1, cap)
        valid = jnp.arange(cap, dtype=jnp.int32)[None, None, :] < counts.reshape(owners, 1, 1)
        nothing = jnp.zeros((), BF16)
        alpha = jnp.where(valid, prefix.reshape(owners, 1, cap), nothing)
        want = targets.reshape(owners, cap, NY, NC, 4).transpose(0, 3, 2, 4, 1)
        want = jnp.where(valid, want.reshape(owners, KIDS, cap), nothing)
        side = jnp.concatenate([want, alpha, inst.astype(BF16), clus.astype(BF16)], axis=1)
        side = jnp.pad(side, ((0, 0), (0, 5), (0, 128 - cap))).reshape(NZ, NX, 40, 128)
        slots = lax.all_to_all(side, "z", 0, 0, tiled=True)
    ay = sum_slots(place, slots)

    def settle(keep, give):
        return keep + shift(give, "core", 1).astype(F32)

    keep2, give2, dz2, rows, w2 = owner_terms(2, place, blocks, (c, d, co, do), ay)
    with jax.named_scope("weights_x"):
        t2 = settle(keep2, give2).astype(BF16)
        low, high = shift(t2[:144], "x", -1), shift(t2[144:], "x", 1)
    keep1, give1, dz1, w1 = owner_terms(1, place, (rows,), (a, ao), ay)
    keep3, give3, dz3, w3 = owner_terms(3, place, (rows,), (b, bo), ay)
    with jax.named_scope("weights_x"):
        t1 = settle(keep1, give1) + jnp.pad(low.astype(F32), ((0, 128), (0, 0)))
        t3 = settle(keep3, give3) + jnp.pad(high.astype(F32), ((144, 0), (0, 0)))
        t1, t3 = shift(t1.astype(BF16), "x", -1), shift(t3.astype(BF16), "x", 1)
    keep0, give0, dz0 = owner_terms(0, place, (rows,), (w,), ay)
    back, own = row_terms((dz0, dz1, dz2, dz3), (w, w1, w2, w3))

    with jax.named_scope("weights_y"):
        t0 = settle(keep0, give0) + t1.astype(F32) + t3.astype(F32)
        top = t0[256:].astype(BF16)

        def piece(d):
            return lax.dynamic_slice_in_dim(t0, lax.rem(iy + d, NY) * 64, 64, 0)

        got = [
            shift(jnp.concatenate([piece(d).astype(BF16), top], axis=0), "y", d).astype(F32)
            for d in (1, 3, 2)
        ]
        out = piece(0) + got[0][:64] + got[1][:64] + got[2][:64]
        grad_leaf = jnp.swapaxes(out.reshape(4, CL, D), 0, 1)
        even = lax.rem(iy, 2) == 0
        one, three, two = (g[64:] for g in got)
        near = jnp.where(even, three, one)
        far = jnp.where(even, one, three)
        grad_cluster = (top.astype(F32) + near) + (two + far)

    with jax.named_scope("rows_back"):
        grad_embed = own
        for d in (1, 7, 2, 6, 3, 5, 4):
            grad_embed = grad_embed + shift(back[d - 1], "z", -d).astype(F32)
    return grad_embed, grad_cluster, grad_leaf


def solution(mesh):
    fine = Mesh(mesh.devices.reshape(NY, NC, NZ, NX), ("y", "core", "z", "x"))
    dp, label = ("y", "core"), ("z", "x")
    every = dp + label
    in_specs = (
        P(every, None),
        P(label, None),
        P(label, None, None),
        P(dp, label, None, None),
        P(dp, label, None, None),
        P(dp, label, None),
        P(dp, label, None, None),
        P(dp, label, None, None, None),
    )
    out_specs = (P(every, None), P(label, None), P(label, dp, None))
    return jax.shard_map(shards, mesh=fine, in_specs=in_specs, out_specs=out_specs, check_vma=False)
```

time: 115 us -> 116 us (level)
  blocking collectives: 29.3 us -> 0 us
  starting transfers between devices: 40 us -> 54.7 us
  waiting for transfers between devices: 13 us -> 22.5 us
  local copies, waits for them, and re-layouts: 6.8 us -> 15.3 us
  other arithmetic: 7.1 us -> 4.87 us
    all_gather x1 -> x0, blocking collectives: 29.3 us -> none  [shards(): rows = lax.all_gather(e, 'z', axis=0, tiled=True)]
    ppermute x17 -> x34, starting transfers between devices: 24 us -> 46.2 us  [shift(): return lax.ppermute(x, axis, [(i, (i + by) % n) for i in range(n)])]
    ppermute x17 -> x34, waiting for transfers between devices: 5.77 us -> 22.5 us  [shift(): return lax.ppermute(x, axis, [(i, (i + by) % n) for i in range(n)])]
    unnamed x19 -> x52, local copies, waits for them, and re-layouts: 3.74 us -> 12.1 us
    all_to_all x1 -> x0, starting transfers between devices: 7.49 us -> none  [shards(): out = lax.all_to_all(out, ('y', 'x'), 0, 0, tiled=True)]
    all_to_all x1 -> x0, waiting for transfers between devices: 7.27 us -> none  [shards(): out = lax.all_to_all(out, ('y', 'x'), 0, 0, tiled=True)]
    reduce_sum x1 -> x0, other arithmetic: 1.85 us -> none  [shards(): out = jnp.sum(out.astype(F32), axis=0)]
    concatenate x1 -> x2, other arithmetic: 1.42 us -> 0.03 us  [the longest x1 0.02 us: shards(): jnp.concatenate([piece(d).astype(BF16), top], axis=0)]
  transfers between devices with their start and end apart: 19 -> 35, of which waited for: 4 -> 7; matrix products, arithmetic and copies ran while one was open for 3% -> 4% of each run, Pallas kernels for 7% -> 13%
where the time goes in v2:
time: 116 us; the launch traced here: 114 us
  starting transfers between devices  54.7 us (47%)
  waiting for transfers between devices  22.5 us (19%)
  local copies, waits for them, and re-layouts  15.3 us (13%)
  Pallas kernels  15.3 us (13%)
  other arithmetic  4.87 us (4%)
    ppermute x34, starting transfers between devices, shift(): return lax.ppermute(x, axis, [(i, (i + by) % n) for i in range(n)])  46.2 us
    ppermute x34, waiting for transfers between devices, shift(): return lax.ppermute(x, axis, [(i, (i + by) % n) for i in range(n)])  22.5 us
    unnamed x52, local copies, waits for them, and re-layouts  12.1 us
    pallas_call x4, Pallas kernels, owner_terms(): pl.pallas_call(functools.partial(owner_kernel, r, n_e, n_w), out_shape=tu...  8.87 us
    all_to_all x1, starting transfers between devices, shards(): slots = lax.all_to_all(side, 'z', 0, 0, tiled=True)  8.47 us
    pallas_call x1, Pallas kernels, sum_slots(): pl.pallas_call(slot_kernel, out_shape=jax.ShapeDtypeStruct((NX, WIDE, ROW...  3.82 us
    pallas_call x1, Pallas kernels, row_terms(): pl.pallas_call(rows_kernel, out_shape=(jax.ShapeDtypeStruct((NZ - 1, INST...  2.66 us
  transfers between devices with their start and end apart: 35, of which 7 were waited for; matrix products, arithmetic and copies ran while one was open for 4% of the time, Pallas kernels for 13%

profile of v2, /device:TPU:24, one launch (start us, length us, event | category | flops | bytes accessed | tf_op | source)
XLA Modules:
  0.0 113.9 jit_solution(12053583969895294371)
XLA Ops:
  4.7 1.7 %collective-permute-start.10 = (bf16[272,768]{1,0:T(8,128)(2,1)S(1)}, bf16[272,768]{1,0:T(8,128)(2,1)S(1)}, u32[]{:S(2)}, u32[]{:S(2)}) collective-permute-start(bf16[272,768]{1,0:T(8,128)(2,1)S(1)} %fusion.5), channel_id=1, source_target_pairs={{0,3},{1,0},{2,1},{3,2},{4,7},{5,4},{6,5},{7,6},{8,11},{9,8},{10,9... | collective-permute-start | bytes 1253384 | tf_op jit(solution)/shard_map/weights/ppermute | solution.py:32
  7.8 8.5 %all-to-all-start = ((bf16[8,4,40,128]{3,2,1,0:T(8,128)(2,1)}), bf16[8,4,40,128]{3,2,1,0:T(8,128)(2,1)S(1)}, u32[]{:S(2)}, u32[]{:S(2)}) async-start(bf16[8,4,40,128]{3,2,1,0:T(8,128)(2,1)} %bitcast.12), calls=%async_computation | async-start | bytes 655360 | tf_op jit(solution)/shard_map/slots/all_to_all | solution.py:200
  16.3 2.0 %collective-permute-start = (bf16[64,768]{1,0:T(8,128)(2,1)S(1)}, bf16[64,768]{1,0:T(8,128)(2,1)S(1)}, u32[]{:S(2)}, u32[]{:S(2)}) collective-permute-start(bf16[64,768]{1,0:T(8,128)(2,1)S(1)} %copy-done.2), channel_id=1, source_target_pairs={{0,4},{4,8},{8,12},{12,16},{16,20},{20,24},{24,28},{28,0},{1,5},{5... | collective-permute-start | bytes 294920 | tf_op jit(solution)/shard_map/rows/ppermute | solution.py:32
  19.6 8.4 %collective-permute-done.refs_1_ = bf16[64,768]{1,0:T(8,128)(2,1)S(1)} collective-permute-done((bf16[64,768]{1,0:T(8,128)(2,1)S(1)}, bf16[64,768]{1,0:T(8,128)(2,1)S(1)}, u32[]{:S(2)}, u32[]{:S(2)}) %collective-permute-start) | collective-permute-done | bytes 98336 | tf_op jit(solution)/shard_map/rows/ppermute | solution.py:32
  28.0 3.2 %collective-permute-start.5 = (bf16[64,768]{1,0:T(8,128)(2,1)S(1)}, bf16[64,768]{1,0:T(8,128)(2,1)S(1)}, u32[]{:S(2)}, u32[]{:S(2)}) collective-permute-start(bf16[64,768]{1,0:T(8,128)(2,1)S(1)} %collective-permute-done.4.refs_7_), channel_id=1, source_target_pairs={{0,28},{4,0},{8,4},{12,8},{16,12},{20,16},{24,20},{28,24},{1,29},{... | collective-permute-start | bytes 294920 | tf_op jit(solution)/shard_map/rows/ppermute | solution.py:32
  31.6 2.2 %collective-permute-done.1.refs_2_ = bf16[64,768]{1,0:T(8,128)(2,1)S(1)} collective-permute-done((bf16[64,768]{1,0:T(8,128)(2,1)S(1)}, bf16[64,768]{1,0:T(8,128)(2,1)S(1)}, u32[]{:S(2)}, u32[]{:S(2)}) %collective-permute-start.1) | collective-permute-done | bytes 98336 | tf_op jit(solution)/shard_map/rows/ppermute | solution.py:32
  33.8 3.2 %collective-permute-start.6 = (bf16[64,768]{1,0:T(8,128)(2,1)S(1)}, bf16[64,768]{1,0:T(8,128)(2,1)S(1)}, u32[]{:S(2)}, u32[]{:S(2)}) collective-permute-start(bf16[64,768]{1,0:T(8,128)(2,1)S(1)} %collective-permute-done.5.refs_6_), channel_id=1, source_target_pairs={{0,28},{4,0},{8,4},{12,8},{16,12},{20,16},{24,20},{28,24},{1,29},{... | collective-permute-start | bytes 294920 | tf_op jit(solution)/shard_map/rows/ppermute | solution.py:32
  39.7 3.4 %collective-permute-start.7 = (bf16[32,768]{1,0:T(8,128)(2,1)S(1)}, bf16[32,768]{1,0:T(8,128)(2,1)S(1)}, u32[]{:S(2)}, u32[]{:S(2)}) collective-permute-start(bf16[32,768]{1,0:T(8,128)(2,1)S(1)} %slice.82), channel_id=1, source_target_pairs={{0,28},{4,0},{8,4},{12,8},{16,12},{20,16},{24,20},{28,24},{1,29},{... | collective-permute-start | bytes 147464 | tf_op jit(solution)/shard_map/rows/ppermute | solution.py:32
  45.1 3.8 %shard_map.103.refs_12_.refs_2_.refs_3_ = f32[4,528,512]{2,1,0:T(8,128)S(1)} custom-call(s32[3]{0:T(128)S(1)} %pad_add_fusion.place, bf16[8,4,40,128]{3,2,1,0:T(8,128)(2,1)S(1)} %all-to-all-done.slots), custom_call_target="tpu_custom_call" | custom-call | flops 2000000000 | bytes 1048576 | tf_op jit(solution)/shard_map/pallas_call | solution.py:68
  54.2 2.2 %shard_map.104 = (f32[272,768]{1,0:T(8,128)S(1)}, bf16[272,768]{1,0:T(8,128)(2,1)S(1)}, bf16[528,512]{1,0:T(8,128)(2,1)S(1)}, bf16[512,768]{1,0:T(8,128)(2,1)S(1)}, bf16[528,768]{1,0:T(8,128)(2,1)S(1)}) custom-call(s32[3]{0:T(128)S(1)} %pad_add_fusion.place, bf16[64,768]{1,0:T(8,128)(2,1)S(1)} %copy-done.2, bf16[64,768]{1,0:T(8,128)(2,1)S(1)} %copy-done.4, ...), custom_call_target="tpu_custom_call" | custom-call | flops 2000000000 | bytes 1048576 | tf_op jit(solution)/shard_map/pallas_call | solution.py:133
  56.4 2.0 %copy-done.11 = f32[4,528,512]{2,1,0:T(8,128)} copy-done((f32[4,528,512]{2,1,0:T(8,128)}, f32[4,528,512]{2,1,0:T(8,128)S(1)}, u32[]{:S(2)}) %copy-start.11) | copy-done | bytes 4325400
  62.9 2.2 %copy-done.12 = f32[4,528,512]{2,1,0:T(8,128)S(1)} copy-done((f32[4,528,512]{2,1,0:T(8,128)S(1)}, f32[4,528,512]{2,1,0:T(8,128)}, u32[]{:S(2)}) %copy-start.12) | copy-done | bytes 4325400
  65.2 2.2 %shard_map.107 = (f32[272,768]{1,0:T(8,128)S(1)}, bf16[272,768]{1,0:T(8,128)(2,1)S(1)}, bf16[528,512]{1,0:T(8,128)(2,1)S(1)}, bf16[528,768]{1,0:T(8,128)(2,1)S(1)}) custom-call(s32[3]{0:T(128)S(1)} %pad_add_fusion.place, bf16[512,768]{1,0:T(8,128)(2,1)S(1)} %copy-done.16, bf16[272,768]{1,0:T(8,128)(2,1)S(1)} %collective-permute-done.10.refs_1_, ...), custom_call_target="tpu_custom_call" | custom-call | flops 2000000000 | bytes 1048576 | tf_op jit(solution)/shard_map/pallas_call | solution.py:133
  68.4 2.2 %shard_map.106 = (f32[272,768]{1,0:T(8,128)S(1)}, bf16[272,768]{1,0:T(8,128)(2,1)S(1)}, bf16[528,512]{1,0:T(8,128)(2,1)S(1)}, bf16[528,768]{1,0:T(8,128)(2,1)S(1)}) custom-call(s32[3]{0:T(128)S(1)} %pad_add_fusion.place, bf16[512,768]{1,0:T(8,128)(2,1)S(1)} %copy-done.16, bf16[272,768]{1,0:T(8,128)(2,1)S(1)} %collective-permute-done.8.refs_1_, ...), custom_call_target="tpu_custom_call" | custom-call | flops 2000000000 | bytes 1048576 | tf_op jit(solution)/shard_map/pallas_call | solution.py:133
  70.7 2.2 %shard_map.105 = (f32[272,768]{1,0:T(8,128)S(1)}, bf16[272,768]{1,0:T(8,128)(2,1)S(1)}, bf16[528,512]{1,0:T(8,128)(2,1)S(1)}) custom-call(s32[3]{0:T(128)S(1)} %pad_add_fusion.place, bf16[512,768]{1,0:T(8,128)(2,1)S(1)} %copy-done.16, bf16[528,768]{1,0:T(8,128)(2,1)S(1)} %pad_maximum_fusion.refs_1_.refs_4_, f32[4,528,512]{2,1,0:T(8,128)S(1)} %copy-done.12), custom_call_target="tpu_custom_call" | custom-call | flops 2000000000 | bytes 1048576 | tf_op jit(solution)/shard_map/pallas_call | solution.py:133
  73.6 3.0 %collective-permute-start.26 = (bf16[144,768]{1,0:T(8,128)(2,1)S(1)}, bf16[144,768]{1,0:T(8,128)(2,1)S(1)}, u32[]{:S(2)}, u32[]{:S(2)}) collective-permute-start(bf16[144,768]{1,0:T(8,128)(2,1)S(1)} %slice.85), channel_id=1, source_target_pairs={{0,3},{1,0},{2,1},{3,2},{4,7},{5,4},{6,5},{7,6},{8,11},{9,8},{10,9... | collective-permute-start | bytes 663560 | tf_op jit(solution)/shard_map/weights_x/ppermute | solution.py:32
  77.1 4.4 %collective-permute-done.26 = bf16[144,768]{1,0:T(8,128)(2,1)S(1)} collective-permute-done((bf16[144,768]{1,0:T(8,128)(2,1)S(1)}, bf16[144,768]{1,0:T(8,128)(2,1)S(1)}, u32[]{:S(2)}, u32[]{:S(2)}) %collective-permute-start.26) | collective-permute-done | bytes 221216 | tf_op jit(solution)/shard_map/weights_x/ppermute | solution.py:32
  81.6 3.8 %collective-permute-start.27 = (bf16[272,768]{1,0:T(8,128)(2,1)S(1)}, bf16[272,768]{1,0:T(8,128)(2,1)S(1)}, u32[]{:S(2)}, u32[]{:S(2)}) collective-permute-start(bf16[272,768]{1,0:T(8,128)(2,1)S(1)} %add_convert_fusion.1), channel_id=1, source_target_pairs={{0,3},{1,0},{2,1},{3,2},{4,7},{5,4},{6,5},{7,6},{8,11},{9,8},{10,9... | collective-permute-start | bytes 1253384 | tf_op jit(solution)/shard_map/weights_x/ppermute | solution.py:32
  85.4 2.7 %shard_map.108 = (bf16[7,64,768]{2,1,0:T(8,128)(2,1)S(1)}, f32[64,768]{1,0:T(8,128)S(1)}) custom-call(bf16[528,512]{1,0:T(8,128)(2,1)S(1)} %get-tuple-element.22.refs_0_, bf16[528,512]{1,0:T(8,128)(2,1)S(1)} %get-tuple-element.23.refs_1_, bf16[528,512]{1,0:T(8,128)(2,1)S(1)} %copy-done.18, bf16[528,512]{1,0:T(8,128)(2,1)S(1)} %get-tuple-element.25.refs_3_, ...), custom_call_target="tpu_custom_call" | custom-call | flops 2000000000 | bytes 1048576 | tf_op jit(solution)/shard_map/pallas_call | solution.py:155
  88.1 3.5 %collective-permute-start.16 = (bf16[64,768]{1,0:T(8,128)(2,1)S(1)}, bf16[64,768]{1,0:T(8,128)(2,1)S(1)}, u32[]{:S(2)}, u32[]{:S(2)}) collective-permute-start(bf16[64,768]{1,0:T(8,128)(2,1)S(1)} %get-tuple-element.42), channel_id=1, source_target_pairs={{0,28},{4,0},{8,4},{12,8},{16,12},{20,16},{24,20},{28,24},{1,29},{... | collective-permute-start | bytes 294920 | tf_op jit(solution)/shard_map/rows_back/ppermute | solution.py:32
  94.5 3.9 %collective-permute-start.20 = (bf16[64,768]{1,0:T(8,128)(2,1)S(1)}, bf16[64,768]{1,0:T(8,128)(2,1)S(1)}, u32[]{:S(2)}, u32[]{:S(2)}) collective-permute-start(bf16[64,768]{1,0:T(8,128)(2,1)S(1)} %get-tuple-element.45), channel_id=1, source_target_pairs={{0,20},{4,24},{8,28},{12,0},{16,4},{20,8},{24,12},{28,16},{1,21},{... | collective-permute-start | bytes 294920 | tf_op jit(solution)/shard_map/rows_back/ppermute | solution.py:32
  100.2 2.4 %collective-permute-start.22 = (bf16[64,768]{1,0:T(8,128)(2,1)S(1)}, bf16[64,768]{1,0:T(8,128)(2,1)S(1)}, u32[]{:S(2)}, u32[]{:S(2)}) collective-permute-start(bf16[64,768]{1,0:T(8,128)(2,1)S(1)} %get-tuple-element.43), channel_id=1, source_target_pairs={{0,16},{4,20},{8,24},{12,28},{16,0},{20,4},{24,8},{28,12},{1,17},{... | collective-permute-start | bytes 294920 | tf_op jit(solution)/shard_map/rows_back/ppermute | solution.py:32
  103.5 2.5 %collective-permute-start.32 = (bf16[80,768]{1,0:T(8,128)(2,1)S(1)}, bf16[80,768]{1,0:T(8,128)(2,1)S(1)}, u32[]{:S(2)}, u32[]{:S(2)}) collective-permute-start(bf16[80,768]{1,0:T(8,128)(2,1)S(1)} %get-tuple-element.50), channel_id=1, source_target_pairs={{0,64},{64,128},{128,192},{192,0},{1,65},{65,129},{129,193},{193,1... | collective-permute-start | bytes 368648 | tf_op jit(solution)/shard_map/weights_y/ppermute | solution.py:32
  106.0 4.1 %collective-permute-done.21 = bf16[64,768]{1,0:T(8,128)(2,1)S(1)} collective-permute-done((bf16[64,768]{1,0:T(8,128)(2,1)S(1)}, bf16[64,768]{1,0:T(8,128)(2,1)S(1)}, u32[]{:S(2)}, u32[]{:S(2)}) %collective-permute-start.21) | collective-permute-done | bytes 98336 | tf_op jit(solution)/shard_map/rows_back/ppermute | solution.py:32
  (141 shorter events, 32.9 us)
Async XLA Ops:
  3.1 28.1 %collective-permute-start.8 = (bf16[272,768]{1,0:T(8,128)(2,1)S(1)}, bf16[272,768]{1,0:T(8,128)(2,1)S(1)}, u32[]{:S(2)}, u32[]{:S(2)}) collective-permute-start(bf16[272,768]{1,0:T(8,128)(2,1)S(1)} %fusion.5), channel_id=1, source_target_pairs={{0,1},{1,2},{2,3},{3,0},{4,5},{5,6},{6,7},{7,4},{8,9},{9,10},{10,1... | collective-permute-start | bytes 1253384 | tf_op jit(solution)/shard_map/weights/ppermute | solution.py:32
  4.7 32.4 %collective-permute-start.10 = (bf16[272,768]{1,0:T(8,128)(2,1)S(1)}, bf16[272,768]{1,0:T(8,128)(2,1)S(1)}, u32[]{:S(2)}, u32[]{:S(2)}) collective-permute-start(bf16[272,768]{1,0:T(8,128)(2,1)S(1)} %fusion.5), channel_id=1, source_target_pairs={{0,3},{1,0},{2,1},{3,2},{4,7},{5,4},{6,5},{7,6},{8,11},{9,8},{10,9... | collective-permute-start | bytes 1253384 | tf_op jit(solution)/shard_map/weights/ppermute | solution.py:32
  7.8 37.3 %all-to-all-start = ((bf16[8,4,40,128]{3,2,1,0:T(8,128)(2,1)}), bf16[8,4,40,128]{3,2,1,0:T(8,128)(2,1)S(1)}, u32[]{:S(2)}, u32[]{:S(2)}) async-start(bf16[8,4,40,128]{3,2,1,0:T(8,128)(2,1)} %bitcast.12), calls=%async_computation | async-start | bytes 655360 | tf_op jit(solution)/shard_map/slots/all_to_all | solution.py:200
  16.3 11.7 %collective-permute-start = (bf16[64,768]{1,0:T(8,128)(2,1)S(1)}, bf16[64,768]{1,0:T(8,128)(2,1)S(1)}, u32[]{:S(2)}, u32[]{:S(2)}) collective-permute-start(bf16[64,768]{1,0:T(8,128)(2,1)S(1)} %copy-done.2), channel_id=1, source_target_pairs={{0,4},{4,8},{8,12},{12,16},{16,20},{20,24},{24,28},{28,0},{1,5},{5... | collective-permute-start | bytes 294920 | tf_op jit(solution)/shard_map/rows/ppermute | solution.py:32
  18.3 9.7 %collective-permute-start.4 = (bf16[64,768]{1,0:T(8,128)(2,1)S(1)}, bf16[64,768]{1,0:T(8,128)(2,1)S(1)}, u32[]{:S(2)}, u32[]{:S(2)}) collective-permute-start(bf16[64,768]{1,0:T(8,128)(2,1)S(1)} %copy-done.2), channel_id=1, source_target_pairs={{0,28},{4,0},{8,4},{12,8},{16,12},{20,16},{24,20},{28,24},{1,29},{... | collective-permute-start | bytes 294920 | tf_op jit(solution)/shard_map/rows/ppermute | solution.py:32
  31.2 12.0 %collective-permute-start.9 = (bf16[144,768]{1,0:T(8,128)(2,1)S(1)}, bf16[144,768]{1,0:T(8,128)(2,1)S(1)}, u32[]{:S(2)}, u32[]{:S(2)}) collective-permute-start(bf16[144,768]{1,0:T(8,128)(2,1)S(1)} %slice.83), channel_id=1, source_target_pairs={{0,1},{1,2},{2,3},{3,0},{4,5},{5,6},{6,7},{7,4},{8,9},{9,10},{10,1... | collective-permute-start | bytes 663560 | tf_op jit(solution)/shard_map/weights/ppermute | solution.py:32
  45.0 17.9 %collective-permute-start.15 = (bf16[272,768]{1,0:T(8,128)(2,1)S(1)}, bf16[272,768]{1,0:T(8,128)(2,1)S(1)}, u32[]{:S(2)}, u32[]{:S(2)}) collective-permute-start(bf16[272,768]{1,0:T(8,128)(2,1)S(1)} %collective-permute-done.10.refs_1_), channel_id=1, source_target_pairs={{0,32},{32,0},{1,33},{33,1},{2,34},{34,2},{3,35},{35,3},{4,36},{36... | collective-permute-start | bytes 1253384 | tf_op jit(solution)/shard_map/weights/ppermute | solution.py:32
  61.0 6.9 %collective-permute-start.25 = (bf16[272,768]{1,0:T(8,128)(2,1)S(1)}, bf16[272,768]{1,0:T(8,128)(2,1)S(1)}, u32[]{:S(2)}, u32[]{:S(2)}) collective-permute-start(bf16[272,768]{1,0:T(8,128)(2,1)S(1)} %get-tuple-element.36), channel_id=1, source_target_pairs={{0,32},{32,0},{1,33},{33,1},{2,34},{34,2},{3,35},{35,3},{4,36},{36... | collective-permute-start | bytes 1253384 | tf_op jit(solution)/shard_map/weights_x/ppermute | solution.py:32
  67.4 9.2 %collective-permute-start.28 = (bf16[272,768]{1,0:T(8,128)(2,1)S(1)}, bf16[272,768]{1,0:T(8,128)(2,1)S(1)}, u32[]{:S(2)}, u32[]{:S(2)}) collective-permute-start(bf16[272,768]{1,0:T(8,128)(2,1)S(1)} %get-tuple-element.38), channel_id=1, source_target_pairs={{0,32},{32,0},{1,33},{33,1},{2,34},{34,2},{3,35},{35,3},{4,36},{36... | collective-permute-start | bytes 1253384 | tf_op jit(solution)/shard_map/weights_x/ppermute | solution.py:32
  68.1 8.5 %collective-permute-start.29 = (bf16[128,768]{1,0:T(8,128)(2,1)S(1)}, bf16[128,768]{1,0:T(8,128)(2,1)S(1)}, u32[]{:S(2)}, u32[]{:S(2)}) collective-permute-start(bf16[128,768]{1,0:T(8,128)(2,1)S(1)} %slice.86), channel_id=1, source_target_pairs={{0,1},{1,2},{2,3},{3,0},{4,5},{5,6},{6,7},{7,4},{8,9},{9,10},{10,1... | collective-permute-start | bytes 589832 | tf_op jit(solution)/shard_map/weights_x/ppermute | solution.py:32
  70.6 6.4 %collective-permute-start.24 = (bf16[272,768]{1,0:T(8,128)(2,1)S(1)}, bf16[272,768]{1,0:T(8,128)(2,1)S(1)}, u32[]{:S(2)}, u32[]{:S(2)}) collective-permute-start(bf16[272,768]{1,0:T(8,128)(2,1)S(1)} %get-tuple-element.34), channel_id=1, source_target_pairs={{0,32},{32,0},{1,33},{33,1},{2,34},{34,2},{3,35},{35,3},{4,36},{36... | collective-permute-start | bytes 1253384 | tf_op jit(solution)/shard_map/weights_x/ppermute | solution.py:32
  73.0 18.6 %collective-permute-start.23 = (bf16[272,768]{1,0:T(8,128)(2,1)S(1)}, bf16[272,768]{1,0:T(8,128)(2,1)S(1)}, u32[]{:S(2)}, u32[]{:S(2)}) collective-permute-start(bf16[272,768]{1,0:T(8,128)(2,1)S(1)} %get-tuple-element.32), channel_id=1, source_target_pairs={{0,32},{32,0},{1,33},{33,1},{2,34},{34,2},{3,35},{35,3},{4,36},{36... | collective-permute-start | bytes 1253384 | tf_op jit(solution)/shard_map/weights_y/ppermute | solution.py:32
  73.6 7.9 %collective-permute-start.26 = (bf16[144,768]{1,0:T(8,128)(2,1)S(1)}, bf16[144,768]{1,0:T(8,128)(2,1)S(1)}, u32[]{:S(2)}, u32[]{:S(2)}) collective-permute-start(bf16[144,768]{1,0:T(8,128)(2,1)S(1)} %slice.85), channel_id=1, source_target_pairs={{0,3},{1,0},{2,1},{3,2},{4,7},{5,4},{6,5},{7,6},{8,11},{9,8},{10,9... | collective-permute-start | bytes 663560 | tf_op jit(solution)/shard_map/weights_x/ppermute | solution.py:32
  76.7 16.4 %collective-permute-start.30 = (bf16[272,768]{1,0:T(8,128)(2,1)S(1)}, bf16[272,768]{1,0:T(8,128)(2,1)S(1)}, u32[]{:S(2)}, u32[]{:S(2)}) collective-permute-start(bf16[272,768]{1,0:T(8,128)(2,1)S(1)} %add_convert_fusion), channel_id=1, source_target_pairs={{0,1},{1,2},{2,3},{3,0},{4,5},{5,6},{6,7},{7,4},{8,9},{9,10},{10,1... | collective-permute-start | bytes 1253384 | tf_op jit(solution)/shard_map/weights_x/ppermute | solution.py:32
  81.6 12.9 %collective-permute-start.27 = (bf16[272,768]{1,0:T(8,128)(2,1)S(1)}, bf16[272,768]{1,0:T(8,128)(2,1)S(1)}, u32[]{:S(2)}, u32[]{:S(2)}) collective-permute-start(bf16[272,768]{1,0:T(8,128)(2,1)S(1)} %add_convert_fusion.1), channel_id=1, source_target_pairs={{0,3},{1,0},{2,1},{3,2},{4,7},{5,4},{6,5},{7,6},{8,11},{9,8},{10,9... | collective-permute-start | bytes 1253384 | tf_op jit(solution)/shard_map/weights_x/ppermute | solution.py:32
  88.1 10.6 %collective-permute-start.16 = (bf16[64,768]{1,0:T(8,128)(2,1)S(1)}, bf16[64,768]{1,0:T(8,128)(2,1)S(1)}, u32[]{:S(2)}, u32[]{:S(2)}) collective-permute-start(bf16[64,768]{1,0:T(8,128)(2,1)S(1)} %get-tuple-element.42), channel_id=1, source_target_pairs={{0,28},{4,0},{8,4},{12,8},{16,12},{20,16},{24,20},{28,24},{1,29},{... | collective-permute-start | bytes 294920 | tf_op jit(solution)/shard_map/rows_back/ppermute | solution.py:32
  91.6 8.6 %collective-permute-start.17 = (bf16[64,768]{1,0:T(8,128)(2,1)S(1)}, bf16[64,768]{1,0:T(8,128)(2,1)S(1)}, u32[]{:S(2)}, u32[]{:S(2)}) collective-permute-start(bf16[64,768]{1,0:T(8,128)(2,1)S(1)} %get-tuple-element.48), channel_id=1, source_target_pairs={{0,4},{4,8},{8,12},{12,16},{16,20},{20,24},{24,28},{28,0},{1,5},{5... | collective-permute-start | bytes 294920 | tf_op jit(solution)/shard_map/rows_back/ppermute | solution.py:32
  91.6 11.1 %collective-permute-start.18 = (bf16[64,768]{1,0:T(8,128)(2,1)S(1)}, bf16[64,768]{1,0:T(8,128)(2,1)S(1)}, u32[]{:S(2)}, u32[]{:S(2)}) collective-permute-start(bf16[64,768]{1,0:T(8,128)(2,1)S(1)} %get-tuple-element.47), channel_id=1, source_target_pairs={{0,24},{4,28},{8,0},{12,4},{16,8},{20,12},{24,16},{28,20},{1,25},{... | collective-permute-start | bytes 294920 | tf_op jit(solution)/shard_map/rows_back/ppermute | solution.py:32
  93.2 10.3 %collective-permute-start.19 = (bf16[64,768]{1,0:T(8,128)(2,1)S(1)}, bf16[64,768]{1,0:T(8,128)(2,1)S(1)}, u32[]{:S(2)}, u32[]{:S(2)}) collective-permute-start(bf16[64,768]{1,0:T(8,128)(2,1)S(1)} %get-tuple-element.46), channel_id=1, source_target_pairs={{0,8},{4,12},{8,16},{12,20},{16,24},{20,28},{24,0},{28,4},{1,9},{5... | collective-permute-start | bytes 294920 | tf_op jit(solution)/shard_map/rows_back/ppermute | solution.py:32
  94.5 11.5 %collective-permute-start.20 = (bf16[64,768]{1,0:T(8,128)(2,1)S(1)}, bf16[64,768]{1,0:T(8,128)(2,1)S(1)}, u32[]{:S(2)}, u32[]{:S(2)}) collective-permute-start(bf16[64,768]{1,0:T(8,128)(2,1)S(1)} %get-tuple-element.45), channel_id=1, source_target_pairs={{0,20},{4,24},{8,28},{12,0},{16,4},{20,8},{24,12},{28,16},{1,21},{... | collective-permute-start | bytes 294920 | tf_op jit(solution)/shard_map/rows_back/ppermute | solution.py:32
  98.7 11.4 %collective-permute-start.21 = (bf16[64,768]{1,0:T(8,128)(2,1)S(1)}, bf16[64,768]{1,0:T(8,128)(2,1)S(1)}, u32[]{:S(2)}, u32[]{:S(2)}) collective-permute-start(bf16[64,768]{1,0:T(8,128)(2,1)S(1)} %get-tuple-element.44), channel_id=1, source_target_pairs={{0,12},{4,16},{8,20},{12,24},{16,28},{20,0},{24,4},{28,8},{1,13},{... | collective-permute-start | bytes 294920 | tf_op jit(solution)/shard_map/rows_back/ppermute | solution.py:32
  100.2 9.9 %collective-permute-start.22 = (bf16[64,768]{1,0:T(8,128)(2,1)S(1)}, bf16[64,768]{1,0:T(8,128)(2,1)S(1)}, u32[]{:S(2)}, u32[]{:S(2)}) collective-permute-start(bf16[64,768]{1,0:T(8,128)(2,1)S(1)} %get-tuple-element.43), channel_id=1, source_target_pairs={{0,16},{4,20},{8,24},{12,28},{16,0},{20,4},{24,8},{28,12},{1,17},{... | collective-permute-start | bytes 294920 | tf_op jit(solution)/shard_map/rows_back/ppermute | solution.py:32
  102.7 8.3 %collective-permute-start.31 = (bf16[80,768]{1,0:T(8,128)(2,1)S(1)}, bf16[80,768]{1,0:T(8,128)(2,1)S(1)}, u32[]{:S(2)}, u32[]{:S(2)}) collective-permute-start(bf16[80,768]{1,0:T(8,128)(2,1)S(1)} %get-tuple-element.49), channel_id=1, source_target_pairs={{0,192},{64,0},{128,64},{192,128},{1,193},{65,1},{129,65},{193,129... | collective-permute-start | bytes 368648 | tf_op jit(solution)/shard_map/weights_y/ppermute | solution.py:32
  103.5 7.5 %collective-permute-start.32 = (bf16[80,768]{1,0:T(8,128)(2,1)S(1)}, bf16[80,768]{1,0:T(8,128)(2,1)S(1)}, u32[]{:S(2)}, u32[]{:S(2)}) collective-permute-start(bf16[80,768]{1,0:T(8,128)(2,1)S(1)} %get-tuple-element.50), channel_id=1, source_target_pairs={{0,64},{64,128},{128,192},{192,0},{1,65},{65,129},{129,193},{193,1... | collective-permute-start | bytes 368648 | tf_op jit(solution)/shard_map/weights_y/ppermute | solution.py:32
  (37 other events, 193.8 us)

commit v3 on v2

v3 whole, which is shorter than its diff:
```python
import functools

import jax
import jax.numpy as jnp
from jax import lax
from jax.experimental import pallas as pl
from jax.experimental.pallas import tpu as pltpu
from jax.sharding import Mesh, PartitionSpec as P

BF16 = jnp.bfloat16
F32 = jnp.float32
NY, NC, NZ, NX = 4, 2, 8, 4
SIZE = {"y": NY, "core": NC, "z": NZ, "x": NX}
INST, D, KIDS, CL = 64, 768, 32, 16
ROWS = INST * NZ
WIDE = (KIDS + 1) * CL
TOP = 256
PART = 272
NT = (((1,), (1,)), ((), ()))
NN = (((1,), (0,)), ((), ()))
TN = (((0,), (0,)), ((), ()))
VMEM = pl.BlockSpec(memory_space=pltpu.VMEM)
SMEM = pl.BlockSpec(memory_space=pltpu.SMEM)


def dot(a, b, dims):
    return lax.dot_general(a, b, dims, preferred_element_type=F32)


def call(kernel, out, args, scratch=(), flops=10**8, **static):
    return pl.pallas_call(
        functools.partial(kernel, **static),
        out_shape=tuple(jax.ShapeDtypeStruct(s, t) for s, t in out),
        in_specs=[SMEM] + [VMEM] * (len(args) - 1),
        out_specs=(VMEM,) * len(out),
        scratch_shapes=[pltpu.VMEM(s, t) for s, t in scratch],
        compiler_params=pltpu.CompilerParams(vmem_limit_bytes=16 * 1024 * 1024),
        cost_estimate=pl.CostEstimate(flops=flops, bytes_accessed=1 << 20, transcendentals=0),
    )(*args)


def shift(x, axis, by):
    n = SIZE[axis]
    return lax.ppermute(x, axis, [(i, (i + by) % n) for i in range(n)])


def swap(x):
    return shift(x, "core", 1)


def turn(x, axis, by):
    n = SIZE[axis]
    pairs = [(i, (i + by) % n) for i in range(n)] + [(n + i, n + (i - by) % n) for i in range(n)]
    return lax.ppermute(x, ("core", axis), pairs)


def slot_kernel(place, slots, ay, wide):
    x, z, sign = place[0], place[2], 1 - 2 * place[1]
    lane_row = lax.broadcasted_iota(jnp.int32, (256, 128), 0)
    cluster_row = lax.broadcasted_iota(jnp.int32, (CL, 128), 0)

    def step(i, _):
        r, g = i // 2, lax.rem(i, 2)
        owner = lax.rem(x - sign * r + NX, NX)
        left = []
        for q in range(4):
            source = lax.rem(z - sign * (g * 4 + q) + NZ, NZ)
            side = slots[source, owner].astype(F32)
            alpha = side[KIDS : KIDS + 1]
            inst = side[KIDS + 1 : KIDS + 2].astype(jnp.int32)
            clus = side[KIDS + 2 : KIDS + 3].astype(jnp.int32)
            left.append(jnp.where(lane_row == inst + q * INST, alpha, 0.0).astype(BF16))
            member = cluster_row == clus
            for k in range(KIDS + 1):
                at = TOP if k == KIDS else k * CL + (CL if k * CL >= TOP else 0)
                wide[at : at + CL, q * 128 : q * 128 + 128] = jnp.where(
                    member, side[k : k + 1], 0.0
                ).astype(BF16)
        ay[r, :, pl.ds(pl.multiple_of(g * 256, 256), 256)] = dot(
            wide[...], jnp.concatenate(left, axis=1), NT
        )
        return 0

    lax.fori_loop(0, 2 * NX, step, 0)


def owner_kernel(place, *refs, r):
    core = place[1]
    if r == 2:
        blocks, (near, far, ay, a, b, dzs, e, w, z) = refs[:8], refs[8:]
        for d, (ref, lo) in enumerate(zip(blocks, (0,) * NZ)):
            e[d * INST : d * INST + INST] = ref[lo : lo + INST]
        w[pl.ds(pl.multiple_of(core * TOP, 16), PART)] = near[...]
        w[pl.ds(pl.multiple_of((1 - core) * TOP, 16), PART)] = far[...]
    elif r == 0:
        e, w, ay, a, b, dzs, z = refs
    else:
        e, w, ay, a, dzs, z = refs
    z[...] = dot(w[...], e[...], NT)
    top = pl.ds(TOP, CL)
    s1 = jax.nn.sigmoid(z[top])
    s1a = s1 * ay[r, top]
    total = jnp.zeros((CL, ROWS), F32)
    for k in range(KIDS + 1):
        if k * CL == TOP:
            continue
        at = pl.ds(k * CL, CL)
        s2 = jax.nn.sigmoid(z[at])
        t = s2 * (s1a * s2 - ay[r, at])
        total = total + t
        dzs[at] = (s1 * (1.0 - s2) * t).astype(BF16)
    dzs[top] = (total * s1 * (1.0 - s1)).astype(BF16)
    if r in (1, 3):
        a[...] = dot(dzs[...], e[...], NN).astype(a.dtype)
        return
    mine = pl.ds(pl.multiple_of(core * TOP, 16), PART)
    other = pl.ds(pl.multiple_of((1 - core) * TOP, 16), PART)
    b[...] = dot(dzs[other], e[...], NN).astype(BF16)
    a[...] = dot(dzs[mine], e[...], NN).astype(a.dtype)
    if r == 2:

        @pl.when(core == 0)
        def _():
            b[:CL] = jnp.zeros((CL, D), BF16)

        @pl.when(core == 1)
        def _():
            a[:CL] = jnp.zeros((CL, D), F32)


def rows_kernel(place, *refs):
    dzs, ws, (near, far, own, ge) = refs[:NX], refs[NX : 2 * NX], refs[2 * NX :]
    ge[...] = dot(dzs[0][...], ws[0][...], TN)
    for r in range(1, NX):
        ge[...] += dot(dzs[r][...], ws[r][...], TN)
    own[...] = ge[:INST]
    near[...] = ge[INST : 5 * INST].astype(BF16)
    for i, d in enumerate((7, 6, 5)):
        far[i * INST : i * INST + INST] = ge[d * INST : d * INST + INST].astype(BF16)


def pass_kernel(place, near, far, got, out, *, d):
    at = pl.ds((d - 1) * INST, INST)
    out[:INST] = (near[at].astype(F32) + got[:INST].astype(F32)).astype(BF16)
    if d == 3:
        out[INST:] = far[at]
    else:
        out[INST:] = (far[at].astype(F32) + got[INST:].astype(F32)).astype(BF16)


def merge_kernel(place, a, b, got, out, total):
    total[...] = a[...] + b[...].astype(F32)
    at = pl.ds(pl.multiple_of(place[1] * TOP, 16), PART)
    total[at] = total[at] + got[...].astype(F32)
    out[...] = total[...].astype(BF16)


def split_kernel(place, keep, give, mine, other, own, top, p1, p2, p3, total):
    core, y = place[1], place[3]
    at = pl.ds(pl.multiple_of(core * TOP, 16), PART)
    total[...] = (keep[...].astype(F32) + give[...].astype(F32)) + (
        mine[at].astype(F32) + other[...].astype(F32)
    )

    def piece(d):
        return total[pl.ds(pl.multiple_of(core * CL + lax.rem(y + d, NY) * 64, 16), 64)]

    own[...] = piece(0)
    cluster = total[pl.ds(pl.multiple_of((1 - core) * TOP, 16), CL)].astype(BF16)
    top[...] = cluster
    for d, p in ((1, p1), (2, p2), (3, p3)):
        p[:64] = piece(d).astype(BF16)
        p[64:] = cluster


def finish_kernel(place, own, top, g1, g2, g3, leaf, cluster):
    out = own[...] + g1[:64].astype(F32) + g2[:64].astype(F32) + g3[:64].astype(F32)
    for k in range(4):
        leaf[:, k, :] = out[k * CL : k * CL + CL]
    even = lax.rem(place[3], 2) == 0
    one, two, three = (g[64:].astype(F32) for g in (g1, g2, g3))
    near = jnp.where(even, three, one)
    far = jnp.where(even, one, three)
    cluster[...] = (top[...].astype(F32) + near) + (two + far)


def shards(e, cw, lw, inst, clus, counts, prefix, targets):
    iy, ic, iz, ix = (lax.axis_index(n) for n in ("y", "core", "z", "x"))
    place = jnp.stack([ix, ic, iz, iy]).astype(jnp.int32)

    with jax.named_scope("rows"):
        p1 = turn(jnp.concatenate([e, swap(e)], axis=0), "z", 1)
        p2 = turn(p1, "z", 1)
        p3 = turn(p2, "z", 1)
        p4 = turn(p3[:INST], "z", 1)
        q1, q2, q3 = (swap(p[INST:]) for p in (p1, p2, p3))
        blocks = (e, p1, p2, p3, p4, q3, q2, q1)

    with jax.named_scope("weights"):
        leaf = lw.reshape(CL, NY, NC, 4, D).transpose(2, 1, 3, 0, 4).reshape(2, TOP, D)
        w = jnp.concatenate([leaf[0], cw, leaf[1]], axis=0)
        v1 = turn(w, "x", 1)
        v2 = turn(lax.dynamic_slice_in_dim(v1, ic * TOP, PART, 0), "x", 1)
        u1, u2 = swap(v1), swap(v2)

    with jax.named_scope("slots"):
        counts, _ = lax.optimization_barrier((counts, p1))
        cap = prefix.shape[-1]
        owners = NZ * NX
        inst, clus = inst.reshape(owners, 1, cap), clus.reshape(owners, 1, cap)
        valid = jnp.arange(cap, dtype=jnp.int32)[None, None, :] < counts.reshape(owners, 1, 1)
        nothing = jnp.zeros((), BF16)
        alpha = jnp.where(valid, prefix.reshape(owners, 1, cap), nothing)
        want = targets.reshape(owners, cap, NY, NC, 4).transpose(0, 3, 2, 4, 1)
        want = jnp.where(valid, want.reshape(owners, KIDS, cap), nothing)
        side = jnp.concatenate([want, alpha, inst.astype(BF16), clus.astype(BF16)], axis=1)
        side = jnp.pad(side, ((0, 0), (0, 5), (0, 128 - cap))).reshape(NZ, NX, 40, 128)
        slots = lax.all_to_all(side, "z", 0, 0, tiled=True)
    (ay,) = call(
        slot_kernel, [((NX, WIDE, ROWS), F32)], (place, slots), [((WIDE, 512), BF16)], 2 * 10**9
    )

    wide, dzs = ((WIDE, D), BF16), ((WIDE, ROWS), BF16)
    half, half32 = ((PART, D), BF16), ((PART, D), F32)
    z = [((WIDE, ROWS), F32)]
    work = 2 * 10**9

    a2, b2, dz2, rows, w2 = call(
        owner_kernel,
        [half32, half, dzs, ((ROWS, D), BF16), wide],
        (place,) + blocks + (v2, u2, ay),
        z,
        work,
        r=2,
    )
    with jax.named_scope("weights_x"):
        t2 = turn((a2 + swap(b2).astype(F32)).astype(BF16), "x", -1)
    b3, dz3 = call(owner_kernel, [wide, dzs], (place, rows, u1, ay), z, work, r=3)
    with jax.named_scope("weights_x"):
        b3 = swap(b3)
    a1, dz1 = call(
        owner_kernel, [((WIDE, D), F32), dzs], (place, rows, v1, ay), z, work, r=1
    )
    with jax.named_scope("weights_x"):
        (t1,) = call(merge_kernel, [wide], (place, a1, b3, t2), [((WIDE, D), F32)])
        t1 = turn(t1, "x", -1)
    a0, b0, dz0 = call(owner_kernel, [half, half, dzs], (place, rows, w, ay), z, work, r=0)
    near, far, own = call(
        rows_kernel,
        [((4 * INST, D), BF16), ((3 * INST, D), BF16), ((INST, D), F32)],
        (place, dz0, dz1, dz2, dz3, w, v1, w2, u1),
        [((ROWS, D), F32)],
        work,
    )

    with jax.named_scope("rows_back"):
        far = swap(far)
        run = turn(near[3 * INST :], "z", -1)
        for d in (3, 2, 1):
            (run,) = call(pass_kernel, [((2 * INST, D), BF16)], (place, near, far, run), d=d)
            run = turn(run, "z", -1)
        grad_embed = own + run[:INST].astype(F32) + swap(run[INST:]).astype(F32)

    with jax.named_scope("weights_y"):
        b0 = swap(b0)
        other = swap(lax.dynamic_slice_in_dim(t1, (1 - ic) * TOP, PART, 0))
        send = ((80, D), BF16)
        mine, top, s1, s2, s3 = call(
            split_kernel,
            [((64, D), F32), ((CL, D), BF16), send, send, send],
            (place, a0, b0, t1, other),
            [((PART, D), F32)],
        )
        g1, g3, g2 = shift(s1, "y", 1), shift(s3, "y", 3), shift(s2, "y", 2)
        grad_leaf, grad_cluster = call(
            finish_kernel, [((CL, 4, D), F32), ((CL, D), F32)], (place, mine, top, g1, g2, g3)
        )
    return grad_embed, grad_cluster, grad_leaf


def solution(mesh):
    fine = Mesh(mesh.devices.reshape(NY, NC, NZ, NX), ("y", "core", "z", "x"))
    dp, label = ("y", "core"), ("z", "x")
    every = dp + label
    in_specs = (
        P(every, None),
        P(label, None),
        P(label, None, None),
        P(dp, label, None, None),
        P(dp, label, None, None),
        P(dp, label, None),
        P(dp, label, None, None),
        P(dp, label, None, None, None),
    )
    out_specs = (P(every, None), P(label, None), P(label, dp, None))
    return jax.shard_map(shards, mesh=fine, in_specs=in_specs, out_specs=out_specs, check_vma=False)
```

time: 116 us -> 111 us (0.957)
  waiting for transfers between devices: 22.5 us -> 43.4 us
  starting transfers between devices: 54.7 us -> 36.2 us
  local copies, waits for them, and re-layouts: 15.3 us -> 5.43 us
  Pallas kernels: 15.3 us -> 20.8 us
  other arithmetic: 4.87 us -> 2.09 us
    ppermute x34 -> x15, starting transfers between devices: 46.2 us -> 7.3 us  [shift(): return lax.ppermute(x, axis, [(i, (i + by) % n) for i in range(n)])]
    ppermute x0 -> x12, waiting for transfers between devices: none -> 36.6 us  [turn(): return lax.ppermute(x, ('core', axis), pairs)]
    ppermute x0 -> x12, starting transfers between devices: none -> 20.5 us  [turn(): return lax.ppermute(x, ('core', axis), pairs)]
    ppermute x34 -> x15, waiting for transfers between devices: 22.5 us -> 6.45 us  [shift(): return lax.ppermute(x, axis, [(i, (i + by) % n) for i in range(n)])]
    unnamed x52 -> x28, local copies, waits for them, and re-layouts: 12.1 us -> 0.87 us
    pallas_call x6 -> x12, Pallas kernels: 15.3 us -> 20.8 us  [call(): pl.pallas_call(functools.partial(kernel, **static), out_shape=tuple((jax....]
    concatenate x4 -> x2, other arithmetic: 1.53 us -> 0.07 us  [the longest x1 0.05 us: shards(): w = jnp.concatenate([leaf[0], cw, leaf[1]], axis=0)]
    slice x7 -> x6, local copies, waits for them, and re-layouts: 0.07 us -> 1.42 us  [the longest x3 1.33 us: shards(): q1, q2, q3 = (swap(p[INST:]) for p in (p1, p2, p3))]
  transfers between devices with their start and end apart: 35 -> 28, of which waited for: 7 -> 13; matrix products, arithmetic and copies ran while one was open for 4% -> 6% of each run, Pallas kernels for 13% -> 17%
where the time goes in v3:
time: 111 us; the launch traced here: 109 us
  waiting for transfers between devices  43.4 us (39%)
  starting transfers between devices  36.2 us (33%)
  Pallas kernels  20.8 us (19%)
  local copies, waits for them, and re-layouts  5.43 us (5%)
  other arithmetic  2.09 us (2%)
    ppermute x12, waiting for transfers between devices, turn(): return lax.ppermute(x, ('core', axis), pairs)  36.6 us
    pallas_call x12, Pallas kernels, call(): pl.pallas_call(functools.partial(kernel, **static), out_shape=tuple((jax....  20.8 us
    ppermute x12, starting transfers between devices, turn(): return lax.ppermute(x, ('core', axis), pairs)  20.5 us
    all_to_all x1, starting transfers between devices, shards(): slots = lax.all_to_all(side, 'z', 0, 0, tiled=True)  8.47 us
    ppermute x15, starting transfers between devices, shift(): return lax.ppermute(x, axis, [(i, (i + by) % n) for i in range(n)])  7.3 us
    ppermute x15, waiting for transfers between devices, shift(): return lax.ppermute(x, axis, [(i, (i + by) % n) for i in range(n)])  6.45 us
  transfers between devices with their start and end apart: 28, of which 13 were waited for; matrix products, arithmetic and copies ran while one was open for 6% of the time, Pallas kernels for 17%

profile of v3, /device:TPU:24, one launch (start us, length us, event | category | flops | bytes accessed | tf_op | source)
XLA Modules:
  0.0 109.0 jit_solution(1077780762439853081)
XLA Ops:
  5.0 2.0 %collective-permute-start.1 = (bf16[128,768]{1,0:T(8,128)(2,1)S(1)}, bf16[128,768]{1,0:T(8,128)(2,1)S(1)}, u32[]{:S(2)}, u32[]{:S(2)}) collective-permute-start(bf16[128,768]{1,0:T(8,128)(2,1)S(1)} %pad_maximum_fusion.1), channel_id=1, source_target_pairs={{0,4},{4,8},{8,12},{12,16},{16,20},{20,24},{24,28},{28,0},{32,60},... | collective-permute-start | bytes 589832 | tf_op jit(solution)/shard_map/rows/ppermute | solution.py:54
  7.0 7.6 %collective-permute-done.1.refs_1_ = bf16[128,768]{1,0:T(8,128)(2,1)S(1)} collective-permute-done((bf16[128,768]{1,0:T(8,128)(2,1)S(1)}, bf16[128,768]{1,0:T(8,128)(2,1)S(1)}, u32[]{:S(2)}, u32[]{:S(2)}) %collective-permute-start.1) | collective-permute-done | bytes 196640 | tf_op jit(solution)/shard_map/rows/ppermute | solution.py:54
  18.8 8.5 %all-to-all-start = ((bf16[8,4,40,128]{3,2,1,0:T(8,128)(2,1)}), bf16[8,4,40,128]{3,2,1,0:T(8,128)(2,1)S(1)}, u32[]{:S(2)}, u32[]{:S(2)}) async-start(bf16[8,4,40,128]{3,2,1,0:T(8,128)(2,1)} %bitcast.14), calls=%async_computation | async-start | bytes 655360 | tf_op jit(solution)/shard_map/slots/all_to_all | solution.py:218
  27.3 2.0 %collective-permute-start.3 = (bf16[128,768]{1,0:T(8,128)(2,1)S(1)}, bf16[128,768]{1,0:T(8,128)(2,1)S(1)}, u32[]{:S(2)}, u32[]{:S(2)}) collective-permute-start(bf16[128,768]{1,0:T(8,128)(2,1)S(1)} %collective-permute-done.2.refs_2_), channel_id=1, source_target_pairs={{0,4},{4,8},{8,12},{12,16},{16,20},{20,24},{24,28},{28,0},{32,60},... | collective-permute-start | bytes 589832 | tf_op jit(solution)/shard_map/rows/ppermute | solution.py:54
  29.3 2.2 %collective-permute-start.11 = (bf16[528,768]{1,0:T(8,128)(2,1)S(1)}, bf16[528,768]{1,0:T(8,128)(2,1)S(1)}, u32[]{:S(2)}, u32[]{:S(2)}) collective-permute-start(bf16[528,768]{1,0:T(8,128)(2,1)S(1)} %collective-permute-done.8.refs_1_.refs_5_), channel_id=1, source_target_pairs={{0,32},{32,0},{1,33},{33,1},{2,34},{34,2},{3,35},{35,3},{4,36},{36... | collective-permute-start | bytes 2433032 | tf_op jit(solution)/shard_map/weights/ppermute | solution.py:44
  32.9 7.7 %collective-permute-done.3.refs_3_ = bf16[128,768]{1,0:T(8,128)(2,1)S(1)} collective-permute-done((bf16[128,768]{1,0:T(8,128)(2,1)S(1)}, bf16[128,768]{1,0:T(8,128)(2,1)S(1)}, u32[]{:S(2)}, u32[]{:S(2)}) %collective-permute-start.3) | collective-permute-done | bytes 196640 | tf_op jit(solution)/shard_map/rows/ppermute | solution.py:54
  42.0 3.8 %shard_map.103.refs_10_.refs_2_ = f32[4,528,512]{2,1,0:T(8,128)S(1)} custom-call(s32[4]{0:T(128)S(1)} %pad_add_fusion.place, bf16[8,4,40,128]{3,2,1,0:T(8,128)(2,1)S(1)} %all-to-all-done.slots), custom_call_target="tpu_custom_call" | custom-call | flops 2000000000 | bytes 1048576 | tf_op jit(solution)/shard_map/pallas_call | solution.py:31
  47.5 2.8 %shard_map.104 = (f32[272,768]{1,0:T(8,128)S(1)}, bf16[272,768]{1,0:T(8,128)(2,1)S(1)}, bf16[528,512]{1,0:T(8,128)(2,1)S(1)}, bf16[512,768]{1,0:T(8,128)(2,1)S(1)}, bf16[528,768]{1,0:T(8,128)(2,1)S(1)}) custom-call(s32[4]{0:T(128)S(1)} %pad_add_fusion.place, bf16[64,768]{1,0:T(8,128)(2,1)S(1)} %copy-done.4, ...), custom_call_target="tpu_custom_call" | custom-call | flops 2000000000 | bytes 1048576 | tf_op jit(solution)/shard_map/pallas_call | solution.py:31
  50.6 2.0 %shard_map.107 = (bf16[528,768]{1,0:T(8,128)(2,1)S(1)}, bf16[528,512]{1,0:T(8,128)(2,1)S(1)}) custom-call(s32[4]{0:T(128)S(1)} %pad_add_fusion.place, bf16[512,768]{1,0:T(8,128)(2,1)S(1)} %get-tuple-element.27.refs_0_, bf16[528,768]{1,0:T(8,128)(2,1)S(1)} %collective-permute-done.11.refs_1_.refs_7_, f32[4,528,512]{2,1,0:T(8,128)S(1)} %shard_map.103.refs_10_.refs_2_), custom_call_target="tpu_custom_call" | custom-call | flops 2000000000 | bytes 1048576 | tf_op jit(solution)/shard_map/pallas_call | solution.py:31
  54.6 2.0 %shard_map.106 = (f32[528,768]{1,0:T(8,128)S(1)}, bf16[528,512]{1,0:T(8,128)(2,1)S(1)}) custom-call(s32[4]{0:T(128)S(1)} %pad_add_fusion.place, bf16[512,768]{1,0:T(8,128)(2,1)S(1)} %get-tuple-element.27.refs_0_, bf16[528,768]{1,0:T(8,128)(2,1)S(1)} %collective-permute-done.8.refs_1_.refs_5_, f32[4,528,512]{2,1,0:T(8,128)S(1)} %shard_map.103.refs_10_.refs_2_), custom_call_target="tpu_custom_call" | custom-call | flops 2000000000 | bytes 1048576 | tf_op jit(solution)/shard_map/pallas_call | solution.py:31
  56.6 4.8 %collective-permute-done.21.got = bf16[272,768]{1,0:T(8,128)(2,1)S(1)} collective-permute-done((bf16[272,768]{1,0:T(8,128)(2,1)S(1)}, bf16[272,768]{1,0:T(8,128)(2,1)S(1)}, u32[]{:S(2)}, u32[]{:S(2)}) %collective-permute-start.21) | collective-permute-done | bytes 417824 | tf_op jit(solution)/shard_map/weights_x/ppermute | solution.py:54
  62.3 2.5 %collective-permute-start.22 = (bf16[528,768]{1,0:T(8,128)(2,1)S(1)}, bf16[528,768]{1,0:T(8,128)(2,1)S(1)}, u32[]{:S(2)}, u32[]{:S(2)}) collective-permute-start(bf16[528,768]{1,0:T(8,128)(2,1)S(1)} %weights_x.1), channel_id=1, source_target_pairs={{0,3},{1,0},{2,1},{3,2},{32,33},{33,34},{34,35},{35,32},{4,7},{5,4... | collective-permute-start | bytes 2433032 | tf_op jit(solution)/shard_map/weights_x/ppermute | solution.py:54
  64.8 2.1 %shard_map.105 = (bf16[272,768]{1,0:T(8,128)(2,1)S(1)}, bf16[272,768]{1,0:T(8,128)(2,1)S(1)}, bf16[528,512]{1,0:T(8,128)(2,1)S(1)}) custom-call(s32[4]{0:T(128)S(1)} %pad_add_fusion.place, bf16[512,768]{1,0:T(8,128)(2,1)S(1)} %get-tuple-element.27.refs_0_, bf16[528,768]{1,0:T(8,128)(2,1)S(1)} %pad_maximum_fusion.refs_1_.refs_4_, ...), custom_call_target="tpu_custom_call" | custom-call | flops 2000000000 | bytes 1048576 | tf_op jit(solution)/shard_map/pallas_call | solution.py:31
  66.9 3.2 %shard_map.108 = (bf16[256,768]{1,0:T(8,128)(2,1)S(1)}, bf16[192,768]{1,0:T(8,128)(2,1)S(1)}, f32[64,768]{1,0:T(8,128)S(1)}) custom-call(s32[4]{0:T(128)S(1)} %pad_add_fusion.place, bf16[528,512]{1,0:T(8,128)(2,1)S(1)} %get-tuple-element.28.refs_0_, bf16[528,512]{1,0:T(8,128)(2,1)S(1)} %get-tuple-element.29.refs_1_, ...), custom_call_target="tpu_custom_call" | custom-call | flops 2000000000 | bytes 1048576 | tf_op jit(solution)/shard_map/pallas_call | solution.py:31
  71.9 3.6 %collective-permute-done.13.got = bf16[64,768]{1,0:T(8,128)(2,1)S(1)} collective-permute-done((bf16[64,768]{1,0:T(8,128)(2,1)S(1)}, bf16[64,768]{1,0:T(8,128)(2,1)S(1)}, u32[]{:S(2)}, u32[]{:S(2)}) %collective-permute-start.13) | collective-permute-done | bytes 98336 | tf_op jit(solution)/shard_map/rows_back/ppermute | solution.py:54
  76.1 2.3 %collective-permute-start.14 = (bf16[128,768]{1,0:T(8,128)(2,1)S(1)}, bf16[128,768]{1,0:T(8,128)(2,1)S(1)}, u32[]{:S(2)}, u32[]{:S(2)}) collective-permute-start(bf16[128,768]{1,0:T(8,128)(2,1)S(1)} %rows_back.3), channel_id=1, source_target_pairs={{0,28},{4,0},{8,4},{12,8},{16,12},{20,16},{24,20},{28,24},{32,36},... | collective-permute-start | bytes 589832 | tf_op jit(solution)/shard_map/rows_back/ppermute | solution.py:54
  78.4 3.4 %collective-permute-done.14.got = bf16[128,768]{1,0:T(8,128)(2,1)S(1)} collective-permute-done((bf16[128,768]{1,0:T(8,128)(2,1)S(1)}, bf16[128,768]{1,0:T(8,128)(2,1)S(1)}, u32[]{:S(2)}, u32[]{:S(2)}) %collective-permute-start.14) | collective-permute-done | bytes 196640 | tf_op jit(solution)/shard_map/rows_back/ppermute | solution.py:54
  82.4 3.5 %collective-permute-start.15 = (bf16[128,768]{1,0:T(8,128)(2,1)S(1)}, bf16[128,768]{1,0:T(8,128)(2,1)S(1)}, u32[]{:S(2)}, u32[]{:S(2)}) collective-permute-start(bf16[128,768]{1,0:T(8,128)(2,1)S(1)} %rows_back.4), channel_id=1, source_target_pairs={{0,28},{4,0},{8,4},{12,8},{16,12},{20,16},{24,20},{28,24},{32,36},... | collective-permute-start | bytes 589832 | tf_op jit(solution)/shard_map/rows_back/ppermute | solution.py:54
  86.3 2.8 %collective-permute-done.15.got = bf16[128,768]{1,0:T(8,128)(2,1)S(1)} collective-permute-done((bf16[128,768]{1,0:T(8,128)(2,1)S(1)}, bf16[128,768]{1,0:T(8,128)(2,1)S(1)}, u32[]{:S(2)}, u32[]{:S(2)}) %collective-permute-start.15) | collective-permute-done | bytes 196640 | tf_op jit(solution)/shard_map/rows_back/ppermute | solution.py:54
  89.7 3.8 %collective-permute-start.16 = (bf16[128,768]{1,0:T(8,128)(2,1)S(1)}, bf16[128,768]{1,0:T(8,128)(2,1)S(1)}, u32[]{:S(2)}, u32[]{:S(2)}) collective-permute-start(bf16[128,768]{1,0:T(8,128)(2,1)S(1)} %rows_back.5), channel_id=1, source_target_pairs={{0,28},{4,0},{8,4},{12,8},{16,12},{20,16},{24,20},{28,24},{32,36},... | collective-permute-start | bytes 589832 | tf_op jit(solution)/shard_map/rows_back/ppermute | solution.py:54
  93.5 3.2 %collective-permute-done.16 = bf16[128,768]{1,0:T(8,128)(2,1)S(1)} collective-permute-done((bf16[128,768]{1,0:T(8,128)(2,1)S(1)}, bf16[128,768]{1,0:T(8,128)(2,1)S(1)}, u32[]{:S(2)}, u32[]{:S(2)}) %collective-permute-start.16) | collective-permute-done | bytes 196640 | tf_op jit(solution)/shard_map/rows_back/ppermute | solution.py:54
  98.0 2.6 %collective-permute-start.25 = (bf16[80,768]{1,0:T(8,128)(2,1)S(1)}, bf16[80,768]{1,0:T(8,128)(2,1)S(1)}, u32[]{:S(2)}, u32[]{:S(2)}) collective-permute-start(bf16[80,768]{1,0:T(8,128)(2,1)S(1)} %get-tuple-element.45), channel_id=1, source_target_pairs={{0,128},{64,192},{128,0},{192,64},{1,129},{65,193},{129,1},{193,65... | collective-permute-start | bytes 368648 | tf_op jit(solution)/shard_map/weights_y/ppermute | solution.py:44
  101.3 2.6 %collective-permute-done.24.g1 = bf16[80,768]{1,0:T(8,128)(2,1)S(1)} collective-permute-done((bf16[80,768]{1,0:T(8,128)(2,1)S(1)}, bf16[80,768]{1,0:T(8,128)(2,1)S(1)}, u32[]{:S(2)}, u32[]{:S(2)}) %collective-permute-start.24) | collective-permute-done | bytes 122912 | tf_op jit(solution)/shard_map/weights_y/ppermute | solution.py:44
  105.7 2.1 %collective-permute-done.26.g3 = bf16[80,768]{1,0:T(8,128)(2,1)S(1)} collective-permute-done((bf16[80,768]{1,0:T(8,128)(2,1)S(1)}, bf16[80,768]{1,0:T(8,128)(2,1)S(1)}, u32[]{:S(2)}, u32[]{:S(2)}) %collective-permute-start.26) | collective-permute-done | bytes 122912 | tf_op jit(solution)/shard_map/weights_y/ppermute | solution.py:44
  (97 shorter events, 24.9 us)
Async XLA Ops:
  3.2 13.5 %collective-permute-start.8 = (bf16[528,768]{1,0:T(8,128)(2,1)S(1)}, bf16[528,768]{1,0:T(8,128)(2,1)S(1)}, u32[]{:S(2)}, u32[]{:S(2)}) collective-permute-start(bf16[528,768]{1,0:T(8,128)(2,1)S(1)} %pad_maximum_fusion.refs_1_.refs_4_), channel_id=1, source_target_pairs={{0,1},{1,2},{2,3},{3,0},{32,35},{33,32},{34,33},{35,34},{4,5},{5,6... | collective-permute-start | bytes 2433032 | tf_op jit(solution)/shard_map/weights/ppermute | solution.py:54
  5.0 9.6 %collective-permute-start.1 = (bf16[128,768]{1,0:T(8,128)(2,1)S(1)}, bf16[128,768]{1,0:T(8,128)(2,1)S(1)}, u32[]{:S(2)}, u32[]{:S(2)}) collective-permute-start(bf16[128,768]{1,0:T(8,128)(2,1)S(1)} %pad_maximum_fusion.1), channel_id=1, source_target_pairs={{0,4},{4,8},{8,12},{12,16},{16,20},{20,24},{24,28},{28,0},{32,60},... | collective-permute-start | bytes 589832 | tf_op jit(solution)/shard_map/rows/ppermute | solution.py:54
  14.7 12.7 %collective-permute-start.2 = (bf16[128,768]{1,0:T(8,128)(2,1)S(1)}, bf16[128,768]{1,0:T(8,128)(2,1)S(1)}, u32[]{:S(2)}, u32[]{:S(2)}) collective-permute-start(bf16[128,768]{1,0:T(8,128)(2,1)S(1)} %collective-permute-done.1.refs_1_), channel_id=1, source_target_pairs={{0,4},{4,8},{8,12},{12,16},{16,20},{20,24},{24,28},{28,0},{32,60},... | collective-permute-start | bytes 589832 | tf_op jit(solution)/shard_map/rows/ppermute | solution.py:54
  17.6 15.3 %collective-permute-start.9 = (bf16[272,768]{1,0:T(8,128)(2,1)}, bf16[272,768]{1,0:T(8,128)(2,1)}, u32[]{:S(2)}, u32[]{:S(2)}) collective-permute-start(bf16[272,768]{1,0:T(8,128)(2,1)} %constant_dynamic-slice_fusion.1), channel_id=1, source_target_pairs={{0,1},{1,2},{2,3},{3,0},{32,35},{33,32},{34,33},{35,34},{4,5},{5,6... | collective-permute-start | bytes 1253384 | tf_op jit(solution)/shard_map/weights/ppermute | solution.py:54
  18.8 23.1 %all-to-all-start = ((bf16[8,4,40,128]{3,2,1,0:T(8,128)(2,1)}), bf16[8,4,40,128]{3,2,1,0:T(8,128)(2,1)S(1)}, u32[]{:S(2)}, u32[]{:S(2)}) async-start(bf16[8,4,40,128]{3,2,1,0:T(8,128)(2,1)} %bitcast.14), calls=%async_computation | async-start | bytes 655360 | tf_op jit(solution)/shard_map/slots/all_to_all | solution.py:218
  27.3 13.3 %collective-permute-start.3 = (bf16[128,768]{1,0:T(8,128)(2,1)S(1)}, bf16[128,768]{1,0:T(8,128)(2,1)S(1)}, u32[]{:S(2)}, u32[]{:S(2)}) collective-permute-start(bf16[128,768]{1,0:T(8,128)(2,1)S(1)} %collective-permute-done.2.refs_2_), channel_id=1, source_target_pairs={{0,4},{4,8},{8,12},{12,16},{16,20},{20,24},{24,28},{28,0},{32,60},... | collective-permute-start | bytes 589832 | tf_op jit(solution)/shard_map/rows/ppermute | solution.py:54
  29.3 21.2 %collective-permute-start.11 = (bf16[528,768]{1,0:T(8,128)(2,1)S(1)}, bf16[528,768]{1,0:T(8,128)(2,1)S(1)}, u32[]{:S(2)}, u32[]{:S(2)}) collective-permute-start(bf16[528,768]{1,0:T(8,128)(2,1)S(1)} %collective-permute-done.8.refs_1_.refs_5_), channel_id=1, source_target_pairs={{0,32},{32,0},{1,33},{33,1},{2,34},{34,2},{3,35},{35,3},{4,36},{36... | collective-permute-start | bytes 2433032 | tf_op jit(solution)/shard_map/weights/ppermute | solution.py:44
  31.6 9.7 %collective-permute-start.7 = (bf16[64,768]{1,0:T(8,128)(2,1)S(1)}, bf16[64,768]{1,0:T(8,128)(2,1)S(1)}, u32[]{:S(2)}, u32[]{:S(2)}) collective-permute-start(bf16[64,768]{1,0:T(8,128)(2,1)S(1)} %slice.41), channel_id=1, source_target_pairs={{0,32},{32,0},{1,33},{33,1},{2,34},{34,2},{3,35},{35,3},{4,36},{36... | collective-permute-start | bytes 294920 | tf_op jit(solution)/shard_map/rows/ppermute | solution.py:44
  32.4 13.5 %collective-permute-start.6 = (bf16[64,768]{1,0:T(8,128)(2,1)}, bf16[64,768]{1,0:T(8,128)(2,1)}, u32[]{:S(2)}, u32[]{:S(2)}) collective-permute-start(bf16[64,768]{1,0:T(8,128)(2,1)} %slice.40), channel_id=1, source_target_pairs={{0,32},{32,0},{1,33},{33,1},{2,34},{34,2},{3,35},{35,3},{4,36},{36... | collective-permute-start | bytes 294920 | tf_op jit(solution)/shard_map/rows/ppermute | solution.py:44
  32.9 14.6 %collective-permute-start.10 = (bf16[272,768]{1,0:T(8,128)(2,1)}, bf16[272,768]{1,0:T(8,128)(2,1)}, u32[]{:S(2)}, u32[]{:S(2)}) collective-permute-start(bf16[272,768]{1,0:T(8,128)(2,1)} %collective-permute-done.9.refs_8_), channel_id=1, source_target_pairs={{0,32},{32,0},{1,33},{33,1},{2,34},{34,2},{3,35},{35,3},{4,36},{36... | collective-permute-start | bytes 1253384 | tf_op jit(solution)/shard_map/weights/ppermute | solution.py:44
  41.3 6.1 %collective-permute-start.4 = (bf16[64,768]{1,0:T(8,128)(2,1)}, bf16[64,768]{1,0:T(8,128)(2,1)}, u32[]{:S(2)}, u32[]{:S(2)}) collective-permute-start(bf16[64,768]{1,0:T(8,128)(2,1)} %get-tuple-element.52), channel_id=1, source_target_pairs={{0,4},{4,8},{8,12},{12,16},{16,20},{20,24},{24,28},{28,0},{32,60},... | collective-permute-start | bytes 294920 | tf_op jit(solution)/shard_map/rows/ppermute | solution.py:54
  41.3 6.1 %collective-permute-start.5 = (bf16[64,768]{1,0:T(8,128)(2,1)}, bf16[64,768]{1,0:T(8,128)(2,1)}, u32[]{:S(2)}, u32[]{:S(2)}) collective-permute-start(bf16[64,768]{1,0:T(8,128)(2,1)} %get-tuple-element.51), channel_id=1, source_target_pairs={{0,32},{32,0},{1,33},{33,1},{2,34},{34,2},{3,35},{35,3},{4,36},{36... | collective-permute-start | bytes 294920 | tf_op jit(solution)/shard_map/rows/ppermute | solution.py:44
  53.3 8.1 %collective-permute-start.21 = (bf16[272,768]{1,0:T(8,128)(2,1)S(1)}, bf16[272,768]{1,0:T(8,128)(2,1)S(1)}, u32[]{:S(2)}, u32[]{:S(2)}) collective-permute-start(bf16[272,768]{1,0:T(8,128)(2,1)S(1)} %add_convert_fusion), channel_id=1, source_target_pairs={{0,3},{1,0},{2,1},{3,2},{32,33},{33,34},{34,35},{35,32},{4,7},{5,4... | collective-permute-start | bytes 1253384 | tf_op jit(solution)/shard_map/weights_x/ppermute | solution.py:54
  62.3 23.7 %collective-permute-start.22 = (bf16[528,768]{1,0:T(8,128)(2,1)S(1)}, bf16[528,768]{1,0:T(8,128)(2,1)S(1)}, u32[]{:S(2)}, u32[]{:S(2)}) collective-permute-start(bf16[528,768]{1,0:T(8,128)(2,1)S(1)} %weights_x.1), channel_id=1, source_target_pairs={{0,3},{1,0},{2,1},{3,2},{32,33},{33,34},{34,35},{35,32},{4,7},{5,4... | collective-permute-start | bytes 2433032 | tf_op jit(solution)/shard_map/weights_x/ppermute | solution.py:54
  70.8 4.7 %collective-permute-start.12 = (bf16[192,768]{1,0:T(8,128)(2,1)S(1)}, bf16[192,768]{1,0:T(8,128)(2,1)S(1)}, u32[]{:S(2)}, u32[]{:S(2)}) collective-permute-start(bf16[192,768]{1,0:T(8,128)(2,1)S(1)} %get-tuple-element.35), channel_id=1, source_target_pairs={{0,32},{32,0},{1,33},{33,1},{2,34},{34,2},{3,35},{35,3},{4,36},{36... | collective-permute-start | bytes 884744 | tf_op jit(solution)/shard_map/rows_back/ppermute | solution.py:44
  70.8 4.7 %collective-permute-start.13 = (bf16[64,768]{1,0:T(8,128)(2,1)S(1)}, bf16[64,768]{1,0:T(8,128)(2,1)S(1)}, u32[]{:S(2)}, u32[]{:S(2)}) collective-permute-start(bf16[64,768]{1,0:T(8,128)(2,1)S(1)} %slice.35), channel_id=1, source_target_pairs={{0,28},{4,0},{8,4},{12,8},{16,12},{20,16},{24,20},{28,24},{32,36},... | collective-permute-start | bytes 294920 | tf_op jit(solution)/shard_map/rows_back/ppermute | solution.py:54
  76.1 5.7 %collective-permute-start.14 = (bf16[128,768]{1,0:T(8,128)(2,1)S(1)}, bf16[128,768]{1,0:T(8,128)(2,1)S(1)}, u32[]{:S(2)}, u32[]{:S(2)}) collective-permute-start(bf16[128,768]{1,0:T(8,128)(2,1)S(1)} %rows_back.3), channel_id=1, source_target_pairs={{0,28},{4,0},{8,4},{12,8},{16,12},{20,16},{24,20},{28,24},{32,36},... | collective-permute-start | bytes 589832 | tf_op jit(solution)/shard_map/rows_back/ppermute | solution.py:54
  78.4 18.3 %collective-permute-start.18 = (bf16[272,768]{1,0:T(8,128)(2,1)}, bf16[272,768]{1,0:T(8,128)(2,1)S(1)}, u32[]{:S(2)}, u32[]{:S(2)}) collective-permute-start(bf16[272,768]{1,0:T(8,128)(2,1)} %copy-done.7), channel_id=1, source_target_pairs={{0,32},{32,0},{1,33},{33,1},{2,34},{34,2},{3,35},{35,3},{4,36},{36... | collective-permute-start | bytes 1253384 | tf_op jit(solution)/shard_map/weights_y/ppermute | solution.py:44
  82.4 6.7 %collective-permute-start.15 = (bf16[128,768]{1,0:T(8,128)(2,1)S(1)}, bf16[128,768]{1,0:T(8,128)(2,1)S(1)}, u32[]{:S(2)}, u32[]{:S(2)}) collective-permute-start(bf16[128,768]{1,0:T(8,128)(2,1)S(1)} %rows_back.4), channel_id=1, source_target_pairs={{0,28},{4,0},{8,4},{12,8},{16,12},{20,16},{24,20},{28,24},{32,36},... | collective-permute-start | bytes 589832 | tf_op jit(solution)/shard_map/rows_back/ppermute | solution.py:54
  86.0 10.7 %collective-permute-start.23 = (bf16[272,768]{1,0:T(8,128)(2,1)S(1)}, bf16[272,768]{1,0:T(8,128)(2,1)S(1)}, u32[]{:S(2)}, u32[]{:S(2)}) collective-permute-start(bf16[272,768]{1,0:T(8,128)(2,1)S(1)} %constant_dynamic-slice_fusion), channel_id=1, source_target_pairs={{0,32},{32,0},{1,33},{33,1},{2,34},{34,2},{3,35},{35,3},{4,36},{36... | collective-permute-start | bytes 1253384 | tf_op jit(solution)/shard_map/weights_y/ppermute | solution.py:44
  89.7 7.0 %collective-permute-start.16 = (bf16[128,768]{1,0:T(8,128)(2,1)S(1)}, bf16[128,768]{1,0:T(8,128)(2,1)S(1)}, u32[]{:S(2)}, u32[]{:S(2)}) collective-permute-start(bf16[128,768]{1,0:T(8,128)(2,1)S(1)} %rows_back.5), channel_id=1, source_target_pairs={{0,28},{4,0},{8,4},{12,8},{16,12},{20,16},{24,20},{28,24},{32,36},... | collective-permute-start | bytes 589832 | tf_op jit(solution)/shard_map/rows_back/ppermute | solution.py:54
  97.7 6.2 %collective-permute-start.24 = (bf16[80,768]{1,0:T(8,128)(2,1)S(1)}, bf16[80,768]{1,0:T(8,128)(2,1)S(1)}, u32[]{:S(2)}, u32[]{:S(2)}) collective-permute-start(bf16[80,768]{1,0:T(8,128)(2,1)S(1)} %get-tuple-element.44), channel_id=1, source_target_pairs={{0,64},{64,128},{128,192},{192,0},{1,65},{65,129},{129,193},{193,1... | collective-permute-start | bytes 368648 | tf_op jit(solution)/shard_map/weights_y/ppermute | solution.py:44
  98.0 7.7 %collective-permute-start.25 = (bf16[80,768]{1,0:T(8,128)(2,1)S(1)}, bf16[80,768]{1,0:T(8,128)(2,1)S(1)}, u32[]{:S(2)}, u32[]{:S(2)}) collective-permute-start(bf16[80,768]{1,0:T(8,128)(2,1)S(1)} %get-tuple-element.45), channel_id=1, source_target_pairs={{0,128},{64,192},{128,0},{192,64},{1,129},{65,193},{129,1},{193,65... | collective-permute-start | bytes 368648 | tf_op jit(solution)/shard_map/weights_y/ppermute | solution.py:44
  100.6 7.1 %collective-permute-start.26 = (bf16[80,768]{1,0:T(8,128)(2,1)S(1)}, bf16[80,768]{1,0:T(8,128)(2,1)S(1)}, u32[]{:S(2)}, u32[]{:S(2)}) collective-permute-start(bf16[80,768]{1,0:T(8,128)(2,1)S(1)} %get-tuple-element.46), channel_id=1, source_target_pairs={{0,192},{64,0},{128,64},{192,128},{1,193},{65,1},{129,65},{193,129... | collective-permute-start | bytes 368648 | tf_op jit(solution)/shard_map/weights_y/ppermute | solution.py:44
  (18 other events, 116.3 us)

commit v4 on v3

--- a/solution.py
+++ b/solution.py
@@ -16,6 +16,7 @@
 WIDE = (KIDS + 1) * CL
 TOP = 256
 PART = 272
+CUT = 144
 NT = (((1,), (1,)), ((), ()))
 NN = (((1,), (0,)), ((), ()))
 TN = (((0,), (0,)), ((), ()))
@@ -27,7 +28,7 @@
     return lax.dot_general(a, b, dims, preferred_element_type=F32)
 
 
-def call(kernel, out, args, scratch=(), flops=10**8, **static):
+def call(kernel, out, args, scratch=(), **static):
     return pl.pallas_call(
         functools.partial(kernel, **static),
         out_shape=tuple(jax.ShapeDtypeStruct(s, t) for s, t in out),
@@ -35,7 +36,7 @@
         out_specs=(VMEM,) * len(out),
         scratch_shapes=[pltpu.VMEM(s, t) for s, t in scratch],
         compiler_params=pltpu.CompilerParams(vmem_limit_bytes=16 * 1024 * 1024),
-        cost_estimate=pl.CostEstimate(flops=flops, bytes_accessed=1 << 20, transcendentals=0),
+        cost_estimate=pl.CostEstimate(flops=2 * 10**9, bytes_accessed=1 << 20, transcendentals=0),
     )(*args)
 
 
@@ -61,7 +62,7 @@
 
     def step(i, _):
         r, g = i // 2, lax.rem(i, 2)
-        owner = lax.rem(x - sign * r + NX, NX)
+        owner = lax.rem(x - r + NX, NX)
         left = []
         for q in range(4):
             source = lax.rem(z - sign * (g * 4 + q) + NZ, NZ)
@@ -86,16 +87,21 @@
 
 def owner_kernel(place, *refs, r):
     core = place[1]
+    mine = pl.ds(pl.multiple_of(core * TOP, 16), PART)
+    other = pl.ds(pl.multiple_of((1 - core) * TOP, 16), PART)
     if r == 2:
-        blocks, (near, far, ay, a, b, dzs, e, w, z) = refs[:8], refs[8:]
-        for d, (ref, lo) in enumerate(zip(blocks, (0,) * NZ)):
-            e[d * INST : d * INST + INST] = ref[lo : lo + INST]
-        w[pl.ds(pl.multiple_of(core * TOP, 16), PART)] = near[...]
-        w[pl.ds(pl.multiple_of((1 - core) * TOP, 16), PART)] = far[...]
+        blocks, (n1, n2, f1, f2, ay, a, b, dzs, e, w, z) = refs[:NZ], refs[NZ:]
+        for d in range(NZ):
+            e[d * INST : d * INST + INST] = blocks[d][:INST]
+        for at, p1, p2 in ((core, n1, n2), (1 - core, f1, f2)):
+            w[pl.ds(pl.multiple_of(at * TOP, 16), CUT)] = p1[...]
+            w[pl.ds(pl.multiple_of(at * TOP + CUT, 16), PART - CUT)] = p2[...]
     elif r == 0:
         e, w, ay, a, b, dzs, z = refs
     else:
-        e, w, ay, a, dzs, z = refs
+        e, near, far, ay, a, b, dzs, w, z = refs
+        w[mine] = near[...]
+        w[other] = far[...]
     z[...] = dot(w[...], e[...], NT)
     top = pl.ds(TOP, CL)
     s1 = jax.nn.sigmoid(z[top])
@@ -110,56 +116,50 @@
         total = total + t
         dzs[at] = (s1 * (1.0 - s2) * t).astype(BF16)
     dzs[top] = (total * s1 * (1.0 - s1)).astype(BF16)
-    if r in (1, 3):
-        a[...] = dot(dzs[...], e[...], NN).astype(a.dtype)
-        return
-    mine = pl.ds(pl.multiple_of(core * TOP, 16), PART)
-    other = pl.ds(pl.multiple_of((1 - core) * TOP, 16), PART)
     b[...] = dot(dzs[other], e[...], NN).astype(BF16)
     a[...] = dot(dzs[mine], e[...], NN).astype(a.dtype)
-    if r == 2:
-
-        @pl.when(core == 0)
-        def _():
-            b[:CL] = jnp.zeros((CL, D), BF16)
-
-        @pl.when(core == 1)
-        def _():
-            a[:CL] = jnp.zeros((CL, D), F32)
 
 
 def rows_kernel(place, *refs):
-    dzs, ws, (near, far, own, ge) = refs[:NX], refs[NX : 2 * NX], refs[2 * NX :]
+    dzs, ws, (near, last, far, own, ge) = refs[:NX], refs[NX : 2 * NX], refs[2 * NX :]
     ge[...] = dot(dzs[0][...], ws[0][...], TN)
     for r in range(1, NX):
         ge[...] += dot(dzs[r][...], ws[r][...], TN)
     own[...] = ge[:INST]
-    near[...] = ge[INST : 5 * INST].astype(BF16)
+    near[...] = ge[INST : 4 * INST].astype(BF16)
+    last[...] = ge[4 * INST : 5 * INST].astype(BF16)
     for i, d in enumerate((7, 6, 5)):
         far[i * INST : i * INST + INST] = ge[d * INST : d * INST + INST].astype(BF16)
 
 
-def pass_kernel(place, near, far, got, out, *, d):
-    at = pl.ds((d - 1) * INST, INST)
-    out[:INST] = (near[at].astype(F32) + got[:INST].astype(F32)).astype(BF16)
-    if d == 3:
-        out[INST:] = far[at]
-    else:
-        out[INST:] = (far[at].astype(F32) + got[INST:].astype(F32)).astype(BF16)
-
-
-def merge_kernel(place, a, b, got, out, total):
-    total[...] = a[...] + b[...].astype(F32)
-    at = pl.ds(pl.multiple_of(place[1] * TOP, 16), PART)
-    total[at] = total[at] + got[...].astype(F32)
-    out[...] = total[...].astype(BF16)
-
-
-def split_kernel(place, keep, give, mine, other, own, top, p1, p2, p3, total):
+def pack_kernel(place, near, far, h1, h3):
+    for h, at in ((h1, 0), (h3, 2 * INST)):
+        h[:INST] = near[at : at + INST]
+        h[INST:] = far[at : at + INST]
+
+
+def pass_kernel(place, near, far, got3, got4, out):
+    at = pl.ds(INST, INST)
+    out[:INST] = (near[at].astype(F32) + got3[:INST].astype(F32) + got4[...].astype(F32)).astype(BF16)
+    out[INST:] = (far[at].astype(F32) + got3[INST:].astype(F32)).astype(BF16)
+
+
+def cut_kernel(place, a, b, low, high):
+    low[...] = (a[:CUT] + b[:CUT].astype(F32)).astype(BF16)
+    high[...] = (a[CUT:] + b[CUT:].astype(F32)).astype(BF16)
+
+
+def merge_kernel(place, a1, b1, a3, b3, low, high, t1, t3):
+    t1[:CUT] = (a1[:CUT] + b1[:CUT].astype(F32) + low[...].astype(F32)).astype(BF16)
+    t1[CUT:] = (a1[CUT:] + b1[CUT:].astype(F32)).astype(BF16)
+    t3[:CUT] = (a3[:CUT] + b3[:CUT].astype(F32)).astype(BF16)
+    t3[CUT:] = (a3[CUT:] + b3[CUT:].astype(F32) + high[...].astype(F32)).astype(BF16)
+
+
+def split_kernel(place, a, b, t1, t3, own, top, p1, p2, p3, total):
     core, y = place[1], place[3]
-    at = pl.ds(pl.multiple_of(core * TOP, 16), PART)
-    total[...] = (keep[...].astype(F32) + give[...].astype(F32)) + (
-        mine[at].astype(F32) + other[...].astype(F32)
+    total[...] = (a[...].astype(F32) + b[...].astype(F32)) + (
+        t1[...].astype(F32) + t3[...].astype(F32)
     )
 
     def piece(d):
@@ -189,19 +189,19 @@
     place = jnp.stack([ix, ic, iz, iy]).astype(jnp.int32)
 
     with jax.named_scope("rows"):
-        p1 = turn(jnp.concatenate([e, swap(e)], axis=0), "z", 1)
-        p2 = turn(p1, "z", 1)
-        p3 = turn(p2, "z", 1)
-        p4 = turn(p3[:INST], "z", 1)
+        p0 = jnp.concatenate([e, swap(e)], axis=0)
+        p1, p2 = turn(p0, "z", 1), turn(p0, "z", 2)
+        p3, p4 = turn(p2, "z", 1), turn(p2[:INST], "z", 2)
         q1, q2, q3 = (swap(p[INST:]) for p in (p1, p2, p3))
         blocks = (e, p1, p2, p3, p4, q3, q2, q1)
 
     with jax.named_scope("weights"):
         leaf = lw.reshape(CL, NY, NC, 4, D).transpose(2, 1, 3, 0, 4).reshape(2, TOP, D)
         w = jnp.concatenate([leaf[0], cw, leaf[1]], axis=0)
-        v1 = turn(w, "x", 1)
-        v2 = turn(lax.dynamic_slice_in_dim(v1, ic * TOP, PART, 0), "x", 1)
-        u1, u2 = swap(v1), swap(v2)
+        part = lax.dynamic_slice_in_dim(w, ic * TOP, PART, 0)
+        low, high = shift(part, "x", 1), shift(part, "x", -1)
+        low2, high2 = shift(low[:CUT], "x", 1), shift(high[CUT:], "x", -1)
+        low_o, high_o, low2_o, high2_o = (swap(p) for p in (low, high, low2, high2))
 
     with jax.named_scope("slots"):
         counts, _ = lax.optimization_barrier((counts, p1))
@@ -217,61 +217,72 @@
         side = jnp.pad(side, ((0, 0), (0, 5), (0, 128 - cap))).reshape(NZ, NX, 40, 128)
         slots = lax.all_to_all(side, "z", 0, 0, tiled=True)
     (ay,) = call(
-        slot_kernel, [((NX, WIDE, ROWS), F32)], (place, slots), [((WIDE, 512), BF16)], 2 * 10**9
+        slot_kernel, [((NX, WIDE, ROWS), F32)], (place, slots), [((WIDE, 512), BF16)]
     )
 
     wide, dzs = ((WIDE, D), BF16), ((WIDE, ROWS), BF16)
     half, half32 = ((PART, D), BF16), ((PART, D), F32)
     z = [((WIDE, ROWS), F32)]
-    work = 2 * 10**9
 
     a2, b2, dz2, rows, w2 = call(
         owner_kernel,
         [half32, half, dzs, ((ROWS, D), BF16), wide],
-        (place,) + blocks + (v2, u2, ay),
+        (place,) + blocks + (low2, high2, low2_o, high2_o, ay),
         z,
-        work,
         r=2,
     )
     with jax.named_scope("weights_x"):
-        t2 = turn((a2 + swap(b2).astype(F32)).astype(BF16), "x", -1)
-    b3, dz3 = call(owner_kernel, [wide, dzs], (place, rows, u1, ay), z, work, r=3)
+        down, up = call(
+            cut_kernel, [((CUT, D), BF16), ((PART - CUT, D), BF16)], (place, a2, swap(b2))
+        )
+    outs = [half32, half, dzs, wide]
+    a1, b1, dz1, w1 = call(owner_kernel, outs, (place, rows, low, low_o, ay), z, r=1)
+    b1 = swap(b1)
+    rows, down, up = lax.optimization_barrier((rows, down, up))
+    down, up = shift(down, "x", -1), shift(up, "x", 1)
+    a3, b3, dz3, w3 = call(owner_kernel, outs, (place, rows, high, high_o, ay), z, r=3)
+    b3 = swap(b3)
+    a0, b0, dz0 = call(owner_kernel, [half, half, dzs], (place, rows, w, ay), z, r=0)
+    b0 = swap(b0)
+    near, last, far, own = call(
+        rows_kernel,
+        [((3 * INST, D), BF16), ((INST, D), BF16), ((3 * INST, D), BF16), ((INST, D), F32)],
+        (place, dz0, dz1, dz2, dz3, w, w1, w2, w3),
+        [((ROWS, D), F32)],
+    )
+
+    with jax.named_scope("rows_back"):
+        last = turn(last, "z", -2)
+        far = swap(far)
+        pair = ((2 * INST, D), BF16)
+        h1, h3 = call(pack_kernel, [pair, pair], (place, near, far))
+        h3, h1 = turn(h3, "z", -1), turn(h1, "z", -1)
+
     with jax.named_scope("weights_x"):
-        b3 = swap(b3)
-    a1, dz1 = call(
-        owner_kernel, [((WIDE, D), F32), dzs], (place, rows, v1, ay), z, work, r=1
-    )
-    with jax.named_scope("weights_x"):
-        (t1,) = call(merge_kernel, [wide], (place, a1, b3, t2), [((WIDE, D), F32)])
-        t1 = turn(t1, "x", -1)
-    a0, b0, dz0 = call(owner_kernel, [half, half, dzs], (place, rows, w, ay), z, work, r=0)
-    near, far, own = call(
-        rows_kernel,
-        [((4 * INST, D), BF16), ((3 * INST, D), BF16), ((INST, D), F32)],
-        (place, dz0, dz1, dz2, dz3, w, v1, w2, u1),
-        [((ROWS, D), F32)],
-        work,
-    )
+        down, a0 = lax.optimization_barrier((down, a0))
+        t1, t3 = call(merge_kernel, [half, half], (place, a1, b1, a3, b3, down, up))
+        t1, t3 = shift(t1, "x", -1), shift(t3, "x", 1)
 
     with jax.named_scope("rows_back"):
-        far = swap(far)
-        run = turn(near[3 * INST :], "z", -1)
-        for d in (3, 2, 1):
-            (run,) = call(pass_kernel, [((2 * INST, D), BF16)], (place, near, far, run), d=d)
-            run = turn(run, "z", -1)
-        grad_embed = own + run[:INST].astype(F32) + swap(run[INST:]).astype(F32)
+        (h2,) = call(pass_kernel, [pair], (place, near, far, h3, last))
+        h2 = turn(h2, "z", -2)
 
     with jax.named_scope("weights_y"):
-        b0 = swap(b0)
-        other = swap(lax.dynamic_slice_in_dim(t1, (1 - ic) * TOP, PART, 0))
         send = ((80, D), BF16)
         mine, top, s1, s2, s3 = call(
             split_kernel,
             [((64, D), F32), ((CL, D), BF16), send, send, send],
-            (place, a0, b0, t1, other),
+            (place, a0, b0, t1, t3),
             [((PART, D), F32)],
         )
-        g1, g3, g2 = shift(s1, "y", 1), shift(s3, "y", 3), shift(s2, "y", 2)
+        g2, g1, g3 = shift(s2, "y", 2), shift(s1, "y", 1), shift(s3, "y", 3)
+
+    with jax.named_scope("rows_back"):
+        h2, g2 = lax.optimization_barrier((h2, g2))
+        both = h1.astype(F32) + h2.astype(F32)
+        grad_embed = (own + both[:INST]) + swap(both[INST:])
+
+    with jax.named_scope("weights_y"):
         grad_leaf, grad_cluster = call(
             finish_kernel, [((CL, 4, D), F32), ((CL, D), F32)], (place, mine, top, g1, g2, g3)
         )

time: 111 us -> 106 us (0.955); the launches traced: 109 us -> 105 us
  waiting for transfers between devices: 43.4 us -> 35.5 us
  starting transfers between devices: 36.2 us -> 40.9 us
    ppermute x12 -> x8, waiting for transfers between devices: 36.6 us -> 24.7 us  [turn(): return lax.ppermute(x, ('core', axis), pairs)]
    ppermute x15 -> x25, starting transfers between devices: 7.3 us -> 18.3 us  [shift(): return lax.ppermute(x, axis, [(i, (i + by) % n) for i in range(n)])]
    ppermute x15 -> x25, waiting for transfers between devices: 6.45 us -> 10.8 us  [shift(): return lax.ppermute(x, axis, [(i, (i + by) % n) for i in range(n)])]
    ppermute x12 -> x8, starting transfers between devices: 20.5 us -> 16.8 us  [turn(): return lax.ppermute(x, ('core', axis), pairs)]
    all_to_all x1, starting transfers between devices: 8.47 us -> 5.84 us  [shards(): slots = lax.all_to_all(side, 'z', 0, 0, tiled=True)]
  transfers between devices with their start and end apart: 28 -> 34, of which waited for: 13 -> 9; matrix products, arithmetic and copies ran while one was open for 6% -> 3% of each run, Pallas kernels for 17% -> 20%
where the time goes in v4:
time: 106 us; the launch traced here: 105 us
  starting transfers between devices  40.9 us (39%)
  waiting for transfers between devices  35.5 us (33%)
  Pallas kernels  20.7 us (20%)
  local copies, waits for them, and re-layouts  5.22 us (5%)
  other arithmetic  2.04 us (2%)
    ppermute x8, waiting for transfers between devices, turn(): return lax.ppermute(x, ('core', axis), pairs)  24.7 us
    pallas_call x12, Pallas kernels, call(): pl.pallas_call(functools.partial(kernel, **static), out_shape=tuple((jax....  20.7 us
    ppermute x25, starting transfers between devices, shift(): return lax.ppermute(x, axis, [(i, (i + by) % n) for i in range(n)])  18.3 us
    ppermute x8, starting transfers between devices, turn(): return lax.ppermute(x, ('core', axis), pairs)  16.8 us
    ppermute x25, waiting for transfers between devices, shift(): return lax.ppermute(x, axis, [(i, (i + by) % n) for i in range(n)])  10.8 us
    all_to_all x1, starting transfers between devices, shards(): slots = lax.all_to_all(side, 'z', 0, 0, tiled=True)  5.84 us
    reshape x2, local copies, waits for them, and re-layouts, shards(): lw.reshape(CL, NY, NC, 4, D).transpose(2, 1, 3, 0, 4).reshape(2, TOP, D)  2.13 us
  transfers between devices with their start and end apart: 34, of which 9 were waited for; matrix products, arithmetic and copies ran while one was open for 3% of the time, Pallas kernels for 20%

profile of v4, /device:TPU:24, one launch (start us, length us, event | category | flops | bytes accessed | tf_op | source)
XLA Modules:
  0.0 105.3 jit_solution(9001744379655067511)
XLA Ops:
  3.2 2.8 %collective-permute-start.10 = (bf16[272,768]{1,0:T(8,128)(2,1)S(1)}, bf16[272,768]{1,0:T(8,128)(2,1)S(1)}, u32[]{:S(2)}, u32[]{:S(2)}) collective-permute-start(bf16[272,768]{1,0:T(8,128)(2,1)S(1)} %constant_dynamic-slice_fusion), channel_id=1, source_target_pairs={{0,3},{1,0},{2,1},{3,2},{4,7},{5,4},{6,5},{7,6},{8,11},{9,8},{10,9... | collective-permute-start | bytes 1253384 | tf_op jit(solution)/shard_map/weights/ppermute | solution.py:45
  7.3 2.0 %collective-permute-start.1 = (bf16[128,768]{1,0:T(8,128)(2,1)S(1)}, bf16[128,768]{1,0:T(8,128)(2,1)S(1)}, u32[]{:S(2)}, u32[]{:S(2)}) collective-permute-start(bf16[128,768]{1,0:T(8,128)(2,1)S(1)} %constant_dynamic-update-slice_fusion), channel_id=1, source_target_pairs={{0,4},{4,8},{8,12},{12,16},{16,20},{20,24},{24,28},{28,0},{32,60},... | collective-permute-start | bytes 589832 | tf_op jit(solution)/shard_map/rows/ppermute | solution.py:55
  9.5 7.4 %collective-permute-done.1.refs_1_ = bf16[128,768]{1,0:T(8,128)(2,1)S(1)} collective-permute-done((bf16[128,768]{1,0:T(8,128)(2,1)S(1)}, bf16[128,768]{1,0:T(8,128)(2,1)S(1)}, u32[]{:S(2)}, u32[]{:S(2)}) %collective-permute-start.1) | collective-permute-done | bytes 196640 | tf_op jit(solution)/shard_map/rows/ppermute | solution.py:55
  18.1 5.8 %all-to-all-start = ((bf16[8,4,40,128]{3,2,1,0:T(8,128)(2,1)}), bf16[8,4,40,128]{3,2,1,0:T(8,128)(2,1)S(1)}, u32[]{:S(2)}, u32[]{:S(2)}) async-start(bf16[8,4,40,128]{3,2,1,0:T(8,128)(2,1)} %bitcast.14), calls=%async_computation | async-start | bytes 655360 | tf_op jit(solution)/shard_map/slots/all_to_all | solution.py:218
  23.9 2.9 %collective-permute-start.2 = (bf16[128,768]{1,0:T(8,128)(2,1)S(1)}, bf16[128,768]{1,0:T(8,128)(2,1)S(1)}, u32[]{:S(2)}, u32[]{:S(2)}) collective-permute-start(bf16[128,768]{1,0:T(8,128)(2,1)S(1)} %constant_dynamic-update-slice_fusion), channel_id=1, source_target_pairs={{0,8},{4,12},{8,16},{12,20},{16,24},{20,28},{24,0},{28,4},{32,56},... | collective-permute-start | bytes 589832 | tf_op jit(solution)/shard_map/rows/ppermute | solution.py:55
  26.9 9.4 %collective-permute-done.2.refs_2_ = bf16[128,768]{1,0:T(8,128)(2,1)S(1)} collective-permute-done((bf16[128,768]{1,0:T(8,128)(2,1)S(1)}, bf16[128,768]{1,0:T(8,128)(2,1)S(1)}, u32[]{:S(2)}, u32[]{:S(2)}) %collective-permute-start.2) | collective-permute-done | bytes 196640 | tf_op jit(solution)/shard_map/rows/ppermute | solution.py:55
  36.3 2.6 %collective-permute-start.3 = (bf16[128,768]{1,0:T(8,128)(2,1)S(1)}, bf16[128,768]{1,0:T(8,128)(2,1)S(1)}, u32[]{:S(2)}, u32[]{:S(2)}) collective-permute-start(bf16[128,768]{1,0:T(8,128)(2,1)S(1)} %collective-permute-done.2.refs_2_), channel_id=1, source_target_pairs={{0,4},{4,8},{8,12},{12,16},{16,20},{20,24},{24,28},{28,0},{32,60},... | collective-permute-start | bytes 589832 | tf_op jit(solution)/shard_map/rows/ppermute | solution.py:55
  38.9 3.3 %collective-permute-start.11 = (bf16[128,768]{1,0:T(8,128)(2,1)S(1)}, bf16[128,768]{1,0:T(8,128)(2,1)S(1)}, u32[]{:S(2)}, u32[]{:S(2)}) collective-permute-start(bf16[128,768]{1,0:T(8,128)(2,1)S(1)} %slice.49), channel_id=1, source_target_pairs={{0,3},{1,0},{2,1},{3,2},{4,7},{5,4},{6,5},{7,6},{8,11},{9,8},{10,9... | collective-permute-start | bytes 589832 | tf_op jit(solution)/shard_map/weights/ppermute | solution.py:45
  43.0 2.4 %collective-permute-done.11.refs_9_ = bf16[128,768]{1,0:T(8,128)(2,1)S(1)} collective-permute-done((bf16[128,768]{1,0:T(8,128)(2,1)S(1)}, bf16[128,768]{1,0:T(8,128)(2,1)S(1)}, u32[]{:S(2)}, u32[]{:S(2)}) %collective-permute-start.11) | collective-permute-done | bytes 196640 | tf_op jit(solution)/shard_map/weights/ppermute | solution.py:45
  45.4 4.1 %collective-permute-done.9.refs_8_ = bf16[144,768]{1,0:T(8,128)(2,1)S(1)} collective-permute-done((bf16[144,768]{1,0:T(8,128)(2,1)S(1)}, bf16[144,768]{1,0:T(8,128)(2,1)S(1)}, u32[]{:S(2)}, u32[]{:S(2)}) %collective-permute-start.9) | collective-permute-done | bytes 221216 | tf_op jit(solution)/shard_map/weights/ppermute | solution.py:45
  49.6 2.1 %collective-permute-start.4 = (bf16[64,768]{1,0:T(8,128)(2,1)}, bf16[64,768]{1,0:T(8,128)(2,1)}, u32[]{:S(2)}, u32[]{:S(2)}) collective-permute-start(bf16[64,768]{1,0:T(8,128)(2,1)} %get-tuple-element.88), channel_id=1, source_target_pairs={{0,8},{4,12},{8,16},{12,20},{16,24},{20,28},{24,0},{28,4},{32,56},... | collective-permute-start | bytes 294920 | tf_op jit(solution)/shard_map/rows/ppermute | solution.py:55
  54.2 3.8 %shard_map.103.refs_12_.refs_2_.refs_3_ = f32[4,528,512]{2,1,0:T(8,128)S(1)} custom-call(s32[4]{0:T(128)S(1)} %pad_add_fusion.place, bf16[8,4,40,128]{3,2,1,0:T(8,128)(2,1)S(1)} %all-to-all-done.slots), custom_call_target="tpu_custom_call" | custom-call | flops 2000000000 | bytes 1048576 | tf_op jit(solution)/shard_map/pallas_call | solution.py:32
  58.8 2.6 %shard_map.104 = (f32[272,768]{1,0:T(8,128)S(1)}, bf16[272,768]{1,0:T(8,128)(2,1)S(1)}, bf16[528,512]{1,0:T(8,128)(2,1)S(1)}, bf16[512,768]{1,0:T(8,128)(2,1)S(1)}, bf16[528,768]{1,0:T(8,128)(2,1)S(1)}) custom-call(s32[4]{0:T(128)S(1)} %pad_add_fusion.place, bf16[64,768]{1,0:T(8,128)(2,1)S(1)} %copy-done, ...), custom_call_target="tpu_custom_call" | custom-call | flops 2000000000 | bytes 1048576 | tf_op jit(solution)/shard_map/pallas_call | solution.py:32
  62.0 2.1 %shard_map.106 = (f32[272,768]{1,0:T(8,128)S(1)}, bf16[272,768]{1,0:T(8,128)(2,1)S(1)}, bf16[528,512]{1,0:T(8,128)(2,1)S(1)}, bf16[528,768]{1,0:T(8,128)(2,1)S(1)}) custom-call(s32[4]{0:T(128)S(1)} %pad_add_fusion.place, bf16[512,768]{1,0:T(8,128)(2,1)S(1)} %get-tuple-element.50.refs_0_, bf16[272,768]{1,0:T(8,128)(2,1)S(1)} %collective-permute-done.8.refs_1_, ...), custom_call_target="tpu_custom_call" | custom-call | flops 2000000000 | bytes 1048576 | tf_op jit(solution)/shard_map/pallas_call | solution.py:32
  65.0 3.2 %collective-permute-start.22 = (bf16[144,768]{1,0:T(8,128)(2,1)S(1)}, bf16[144,768]{1,0:T(8,128)(2,1)S(1)}, u32[]{:S(2)}, u32[]{:S(2)}) collective-permute-start(bf16[144,768]{1,0:T(8,128)(2,1)S(1)} %get-tuple-element.64), channel_id=1, source_target_pairs={{0,3},{1,0},{2,1},{3,2},{4,7},{5,4},{6,5},{7,6},{8,11},{9,8},{10,9... | collective-permute-start | bytes 663560 | tf_op jit(solution)/shard_map/ppermute | solution.py:45
  68.2 2.1 %shard_map.107 = (f32[272,768]{1,0:T(8,128)S(1)}, bf16[272,768]{1,0:T(8,128)(2,1)S(1)}, bf16[528,512]{1,0:T(8,128)(2,1)S(1)}, bf16[528,768]{1,0:T(8,128)(2,1)S(1)}) custom-call(s32[4]{0:T(128)S(1)} %pad_add_fusion.place, bf16[512,768]{1,0:T(8,128)(2,1)S(1)} %get-tuple-element.50.refs_0_, bf16[272,768]{1,0:T(8,128)(2,1)S(1)} %collective-permute-done.10.refs_1_, ...), custom_call_target="tpu_custom_call" | custom-call | flops 2000000000 | bytes 1048576 | tf_op jit(solution)/shard_map/pallas_call | solution.py:32
  70.4 2.1 %shard_map.105 = (bf16[272,768]{1,0:T(8,128)(2,1)S(1)}, bf16[272,768]{1,0:T(8,128)(2,1)S(1)}, bf16[528,512]{1,0:T(8,128)(2,1)S(1)}) custom-call(s32[4]{0:T(128)S(1)} %pad_add_fusion.place, bf16[512,768]{1,0:T(8,128)(2,1)S(1)} %get-tuple-element.50.refs_0_, bf16[528,768]{1,0:T(8,128)(2,1)S(1)} %pad_maximum_fusion.refs_1_.refs_4_, ...), custom_call_target="tpu_custom_call" | custom-call | flops 2000000000 | bytes 1048576 | tf_op jit(solution)/shard_map/pallas_call | solution.py:32
  72.5 3.2 %shard_map.108 = (bf16[192,768]{1,0:T(8,128)(2,1)S(1)}, bf16[64,768]{1,0:T(8,128)(2,1)S(1)}, bf16[192,768]{1,0:T(8,128)(2,1)S(1)}, f32[64,768]{1,0:T(8,128)S(1)}) custom-call(s32[4]{0:T(128)S(1)} %pad_add_fusion.place, bf16[528,512]{1,0:T(8,128)(2,1)S(1)} %get-tuple-element.51.refs_0_, bf16[528,512]{1,0:T(8,128)(2,1)S(1)} %get-tuple-element.52.refs_1_, ...), custom_call_target="tpu_custom_call" | custom-call | flops 2000000000 | bytes 1048576 | tf_op jit(solution)/shard_map/pallas_call | solution.py:32
  81.1 1.7 %collective-permute-start.20 = (bf16[64,768]{1,0:T(8,128)(2,1)S(1)}, bf16[64,768]{1,0:T(8,128)(2,1)S(1)}, u32[]{:S(2)}, u32[]{:S(2)}) collective-permute-start(bf16[64,768]{1,0:T(8,128)(2,1)S(1)} %get-tuple-element.63), channel_id=1, source_target_pairs={{0,24},{4,28},{8,0},{12,4},{16,8},{20,12},{24,16},{28,20},{32,40},... | collective-permute-start | bytes 294920 | tf_op jit(solution)/shard_map/rows_back/ppermute | solution.py:55
  82.9 4.9 %collective-permute-done.20.got4 = bf16[64,768]{1,0:T(8,128)(2,1)S(1)} collective-permute-done((bf16[64,768]{1,0:T(8,128)(2,1)S(1)}, bf16[64,768]{1,0:T(8,128)(2,1)S(1)}, u32[]{:S(2)}, u32[]{:S(2)}) %collective-permute-start.20) | collective-permute-done | bytes 98336 | tf_op jit(solution)/shard_map/rows_back/ppermute | solution.py:55
  87.8 3.4 %collective-permute-start.18 = (bf16[128,768]{1,0:T(8,128)(2,1)S(1)}, bf16[128,768]{1,0:T(8,128)(2,1)S(1)}, u32[]{:S(2)}, u32[]{:S(2)}) collective-permute-start(bf16[128,768]{1,0:T(8,128)(2,1)S(1)} %get-tuple-element.61), channel_id=1, source_target_pairs={{0,28},{4,0},{8,4},{12,8},{16,12},{20,16},{24,20},{28,24},{32,36},... | collective-permute-start | bytes 589832 | tf_op jit(solution)/shard_map/rows_back/ppermute | solution.py:55
  95.0 2.2 %collective-permute-start.31 = (bf16[80,768]{1,0:T(8,128)(2,1)S(1)}, bf16[80,768]{1,0:T(8,128)(2,1)S(1)}, u32[]{:S(2)}, u32[]{:S(2)}) collective-permute-start(bf16[80,768]{1,0:T(8,128)(2,1)S(1)} %get-tuple-element.80), channel_id=1, source_target_pairs={{0,64},{64,128},{128,192},{192,0},{1,65},{65,129},{129,193},{193,1... | collective-permute-start | bytes 368648 | tf_op jit(solution)/shard_map/weights_y/ppermute | solution.py:45
  97.2 2.9 %collective-permute-done.21 = bf16[128,768]{1,0:T(8,128)(2,1)S(1)} collective-permute-done((bf16[128,768]{1,0:T(8,128)(2,1)S(1)}, bf16[128,768]{1,0:T(8,128)(2,1)S(1)}, u32[]{:S(2)}, u32[]{:S(2)}) %collective-permute-start.21) | collective-permute-done | bytes 196640 | tf_op jit(solution)/shard_map/rows_back/ppermute | solution.py:55
  100.9 2.4 %collective-permute-done.32.g3 = bf16[80,768]{1,0:T(8,128)(2,1)S(1)} collective-permute-done((bf16[80,768]{1,0:T(8,128)(2,1)S(1)}, bf16[80,768]{1,0:T(8,128)(2,1)S(1)}, u32[]{:S(2)}, u32[]{:S(2)}) %collective-permute-start.32) | collective-permute-done | bytes 122912 | tf_op jit(solution)/shard_map/weights_y/ppermute | solution.py:45
  (100 shorter events, 22.8 us)
Async XLA Ops:
  3.2 35.7 %collective-permute-start.10 = (bf16[272,768]{1,0:T(8,128)(2,1)S(1)}, bf16[272,768]{1,0:T(8,128)(2,1)S(1)}, u32[]{:S(2)}, u32[]{:S(2)}) collective-permute-start(bf16[272,768]{1,0:T(8,128)(2,1)S(1)} %constant_dynamic-slice_fusion), channel_id=1, source_target_pairs={{0,3},{1,0},{2,1},{3,2},{4,7},{5,4},{6,5},{7,6},{8,11},{9,8},{10,9... | collective-permute-start | bytes 1253384 | tf_op jit(solution)/shard_map/weights/ppermute | solution.py:45
  6.0 36.2 %collective-permute-start.8 = (bf16[272,768]{1,0:T(8,128)(2,1)S(1)}, bf16[272,768]{1,0:T(8,128)(2,1)S(1)}, u32[]{:S(2)}, u32[]{:S(2)}) collective-permute-start(bf16[272,768]{1,0:T(8,128)(2,1)S(1)} %constant_dynamic-slice_fusion), channel_id=1, source_target_pairs={{0,1},{1,2},{2,3},{3,0},{4,5},{5,6},{6,7},{7,4},{8,9},{9,10},{10,1... | collective-permute-start | bytes 1253384 | tf_op jit(solution)/shard_map/weights/ppermute | solution.py:45
  7.3 9.6 %collective-permute-start.1 = (bf16[128,768]{1,0:T(8,128)(2,1)S(1)}, bf16[128,768]{1,0:T(8,128)(2,1)S(1)}, u32[]{:S(2)}, u32[]{:S(2)}) collective-permute-start(bf16[128,768]{1,0:T(8,128)(2,1)S(1)} %constant_dynamic-update-slice_fusion), channel_id=1, source_target_pairs={{0,4},{4,8},{8,12},{12,16},{16,20},{20,24},{24,28},{28,0},{32,60},... | collective-permute-start | bytes 589832 | tf_op jit(solution)/shard_map/rows/ppermute | solution.py:55
  18.1 36.1 %all-to-all-start = ((bf16[8,4,40,128]{3,2,1,0:T(8,128)(2,1)}), bf16[8,4,40,128]{3,2,1,0:T(8,128)(2,1)S(1)}, u32[]{:S(2)}, u32[]{:S(2)}) async-start(bf16[8,4,40,128]{3,2,1,0:T(8,128)(2,1)} %bitcast.14), calls=%async_computation | async-start | bytes 655360 | tf_op jit(solution)/shard_map/slots/all_to_all | solution.py:218
  23.9 12.4 %collective-permute-start.2 = (bf16[128,768]{1,0:T(8,128)(2,1)S(1)}, bf16[128,768]{1,0:T(8,128)(2,1)S(1)}, u32[]{:S(2)}, u32[]{:S(2)}) collective-permute-start(bf16[128,768]{1,0:T(8,128)(2,1)S(1)} %constant_dynamic-update-slice_fusion), channel_id=1, source_target_pairs={{0,8},{4,12},{8,16},{12,20},{16,24},{20,28},{24,0},{28,4},{32,56},... | collective-permute-start | bytes 589832 | tf_op jit(solution)/shard_map/rows/ppermute | solution.py:55
  36.3 16.1 %collective-permute-start.3 = (bf16[128,768]{1,0:T(8,128)(2,1)S(1)}, bf16[128,768]{1,0:T(8,128)(2,1)S(1)}, u32[]{:S(2)}, u32[]{:S(2)}) collective-permute-start(bf16[128,768]{1,0:T(8,128)(2,1)S(1)} %collective-permute-done.2.refs_2_), channel_id=1, source_target_pairs={{0,4},{4,8},{8,12},{12,16},{16,20},{20,24},{24,28},{28,0},{32,60},... | collective-permute-start | bytes 589832 | tf_op jit(solution)/shard_map/rows/ppermute | solution.py:55
  38.9 6.5 %collective-permute-start.11 = (bf16[128,768]{1,0:T(8,128)(2,1)S(1)}, bf16[128,768]{1,0:T(8,128)(2,1)S(1)}, u32[]{:S(2)}, u32[]{:S(2)}) collective-permute-start(bf16[128,768]{1,0:T(8,128)(2,1)S(1)} %slice.49), channel_id=1, source_target_pairs={{0,3},{1,0},{2,1},{3,2},{4,7},{5,4},{6,5},{7,6},{8,11},{9,8},{10,9... | collective-permute-start | bytes 589832 | tf_op jit(solution)/shard_map/weights/ppermute | solution.py:45
  42.3 7.2 %collective-permute-start.9 = (bf16[144,768]{1,0:T(8,128)(2,1)S(1)}, bf16[144,768]{1,0:T(8,128)(2,1)S(1)}, u32[]{:S(2)}, u32[]{:S(2)}) collective-permute-start(bf16[144,768]{1,0:T(8,128)(2,1)S(1)} %slice.48), channel_id=1, source_target_pairs={{0,1},{1,2},{2,3},{3,0},{4,5},{5,6},{6,7},{7,4},{8,9},{9,10},{10,1... | collective-permute-start | bytes 663560 | tf_op jit(solution)/shard_map/weights/ppermute | solution.py:45
  43.0 10.5 %collective-permute-start.6 = (bf16[64,768]{1,0:T(8,128)(2,1)S(1)}, bf16[64,768]{1,0:T(8,128)(2,1)S(1)}, u32[]{:S(2)}, u32[]{:S(2)}) collective-permute-start(bf16[64,768]{1,0:T(8,128)(2,1)S(1)} %get-tuple-element.87), channel_id=1, source_target_pairs={{0,32},{32,0},{1,33},{33,1},{2,34},{34,2},{3,35},{35,3},{4,36},{36... | collective-permute-start | bytes 294920 | tf_op jit(solution)/shard_map/rows/ppermute | solution.py:45
  45.4 13.4 %collective-permute-start.13 = (bf16[128,768]{1,0:T(8,128)(2,1)S(1)}, bf16[128,768]{1,0:T(8,128)(2,1)S(1)}, u32[]{:S(2)}, u32[]{:S(2)}) collective-permute-start(bf16[128,768]{1,0:T(8,128)(2,1)S(1)} %collective-permute-done.11.refs_9_), channel_id=1, source_target_pairs={{0,32},{32,0},{1,33},{33,1},{2,34},{34,2},{3,35},{35,3},{4,36},{36... | collective-permute-start | bytes 589832 | tf_op jit(solution)/shard_map/weights/ppermute | solution.py:45
  49.5 9.3 %collective-permute-start.12 = (bf16[144,768]{1,0:T(8,128)(2,1)S(1)}, bf16[144,768]{1,0:T(8,128)(2,1)S(1)}, u32[]{:S(2)}, u32[]{:S(2)}) collective-permute-start(bf16[144,768]{1,0:T(8,128)(2,1)S(1)} %collective-permute-done.9.refs_8_), channel_id=1, source_target_pairs={{0,32},{32,0},{1,33},{33,1},{2,34},{34,2},{3,35},{35,3},{4,36},{36... | collective-permute-start | bytes 663560 | tf_op jit(solution)/shard_map/weights/ppermute | solution.py:45
  49.6 8.5 %collective-permute-start.4 = (bf16[64,768]{1,0:T(8,128)(2,1)}, bf16[64,768]{1,0:T(8,128)(2,1)}, u32[]{:S(2)}, u32[]{:S(2)}) collective-permute-start(bf16[64,768]{1,0:T(8,128)(2,1)} %get-tuple-element.88), channel_id=1, source_target_pairs={{0,8},{4,12},{8,16},{12,20},{16,24},{20,28},{24,0},{28,4},{32,56},... | collective-permute-start | bytes 294920 | tf_op jit(solution)/shard_map/rows/ppermute | solution.py:55
  61.5 6.7 %collective-permute-start.16 = (bf16[272,768]{1,0:T(8,128)(2,1)S(1)}, bf16[272,768]{1,0:T(8,128)(2,1)S(1)}, u32[]{:S(2)}, u32[]{:S(2)}) collective-permute-start(bf16[272,768]{1,0:T(8,128)(2,1)S(1)} %collective-permute-done.10.refs_1_), channel_id=1, source_target_pairs={{0,32},{32,0},{1,33},{33,1},{2,34},{34,2},{3,35},{35,3},{4,36},{36... | collective-permute-start | bytes 1253384 | tf_op jit(solution)/shard_map/weights/ppermute | solution.py:45
  64.1 12.3 %collective-permute-start.24 = (bf16[272,768]{1,0:T(8,128)(2,1)S(1)}, bf16[272,768]{1,0:T(8,128)(2,1)S(1)}, u32[]{:S(2)}, u32[]{:S(2)}) collective-permute-start(bf16[272,768]{1,0:T(8,128)(2,1)S(1)} %get-tuple-element.69), channel_id=1, source_target_pairs={{0,32},{32,0},{1,33},{33,1},{2,34},{34,2},{3,35},{35,3},{4,36},{36... | collective-permute-start | bytes 1253384 | tf_op jit(solution)/shard_map/ppermute | solution.py:45
  64.9 11.5 %collective-permute-start.26 = (bf16[128,768]{1,0:T(8,128)(2,1)S(1)}, bf16[128,768]{1,0:T(8,128)(2,1)S(1)}, u32[]{:S(2)}, u32[]{:S(2)}) collective-permute-start(bf16[128,768]{1,0:T(8,128)(2,1)S(1)} %get-tuple-element.73), channel_id=1, source_target_pairs={{0,1},{1,2},{2,3},{3,0},{4,5},{5,6},{6,7},{7,4},{8,9},{9,10},{10,1... | collective-permute-start | bytes 589832 | tf_op jit(solution)/shard_map/ppermute | solution.py:45
  65.0 11.3 %collective-permute-start.22 = (bf16[144,768]{1,0:T(8,128)(2,1)S(1)}, bf16[144,768]{1,0:T(8,128)(2,1)S(1)}, u32[]{:S(2)}, u32[]{:S(2)}) collective-permute-start(bf16[144,768]{1,0:T(8,128)(2,1)S(1)} %get-tuple-element.64), channel_id=1, source_target_pairs={{0,3},{1,0},{2,1},{3,2},{4,7},{5,4},{6,5},{7,6},{8,11},{9,8},{10,9... | collective-permute-start | bytes 663560 | tf_op jit(solution)/shard_map/ppermute | solution.py:45
  76.3 16.4 %collective-permute-start.23 = (bf16[272,768]{1,0:T(8,128)(2,1)S(1)}, bf16[272,768]{1,0:T(8,128)(2,1)S(1)}, u32[]{:S(2)}, u32[]{:S(2)}) collective-permute-start(bf16[272,768]{1,0:T(8,128)(2,1)S(1)} %get-tuple-element.67), channel_id=1, source_target_pairs={{0,32},{32,0},{1,33},{33,1},{2,34},{34,2},{3,35},{35,3},{4,36},{36... | collective-permute-start | bytes 1253384 | tf_op jit(solution)/shard_map/ppermute | solution.py:45
  77.2 15.5 %collective-permute-start.27 = (bf16[272,768]{1,0:T(8,128)(2,1)S(1)}, bf16[272,768]{1,0:T(8,128)(2,1)S(1)}, u32[]{:S(2)}, u32[]{:S(2)}) collective-permute-start(bf16[272,768]{1,0:T(8,128)(2,1)S(1)} %get-tuple-element.74), channel_id=1, source_target_pairs={{0,3},{1,0},{2,1},{3,2},{4,7},{5,4},{6,5},{7,6},{8,11},{9,8},{10,9... | collective-permute-start | bytes 1253384 | tf_op jit(solution)/shard_map/weights_x/ppermute | solution.py:45
  78.0 14.7 %collective-permute-start.28 = (bf16[272,768]{1,0:T(8,128)(2,1)S(1)}, bf16[272,768]{1,0:T(8,128)(2,1)S(1)}, u32[]{:S(2)}, u32[]{:S(2)}) collective-permute-start(bf16[272,768]{1,0:T(8,128)(2,1)S(1)} %get-tuple-element.75), channel_id=1, source_target_pairs={{0,1},{1,2},{2,3},{3,0},{4,5},{5,6},{6,7},{7,4},{8,9},{9,10},{10,1... | collective-permute-start | bytes 1253384 | tf_op jit(solution)/shard_map/weights_x/ppermute | solution.py:45
  80.1 11.0 %collective-permute-start.19 = (bf16[128,768]{1,0:T(8,128)(2,1)S(1)}, bf16[128,768]{1,0:T(8,128)(2,1)S(1)}, u32[]{:S(2)}, u32[]{:S(2)}) collective-permute-start(bf16[128,768]{1,0:T(8,128)(2,1)S(1)} %get-tuple-element.62), channel_id=1, source_target_pairs={{0,28},{4,0},{8,4},{12,8},{16,12},{20,16},{24,20},{28,24},{32,36},... | collective-permute-start | bytes 589832 | tf_op jit(solution)/shard_map/rows_back/ppermute | solution.py:55
  81.1 6.6 %collective-permute-start.20 = (bf16[64,768]{1,0:T(8,128)(2,1)S(1)}, bf16[64,768]{1,0:T(8,128)(2,1)S(1)}, u32[]{:S(2)}, u32[]{:S(2)}) collective-permute-start(bf16[64,768]{1,0:T(8,128)(2,1)S(1)} %get-tuple-element.63), channel_id=1, source_target_pairs={{0,24},{4,28},{8,0},{12,4},{16,8},{20,12},{24,16},{28,20},{32,40},... | collective-permute-start | bytes 294920 | tf_op jit(solution)/shard_map/rows_back/ppermute | solution.py:55
  87.8 13.0 %collective-permute-start.18 = (bf16[128,768]{1,0:T(8,128)(2,1)S(1)}, bf16[128,768]{1,0:T(8,128)(2,1)S(1)}, u32[]{:S(2)}, u32[]{:S(2)}) collective-permute-start(bf16[128,768]{1,0:T(8,128)(2,1)S(1)} %get-tuple-element.61), channel_id=1, source_target_pairs={{0,28},{4,0},{8,4},{12,8},{16,12},{20,16},{24,20},{28,24},{32,36},... | collective-permute-start | bytes 589832 | tf_op jit(solution)/shard_map/rows_back/ppermute | solution.py:55
  91.7 8.3 %collective-permute-start.21 = (bf16[128,768]{1,0:T(8,128)(2,1)S(1)}, bf16[128,768]{1,0:T(8,128)(2,1)S(1)}, u32[]{:S(2)}, u32[]{:S(2)}) collective-permute-start(bf16[128,768]{1,0:T(8,128)(2,1)S(1)} %rows_back.3), channel_id=1, source_target_pairs={{0,24},{4,28},{8,0},{12,4},{16,8},{20,12},{24,16},{28,20},{32,40},... | collective-permute-start | bytes 589832 | tf_op jit(solution)/shard_map/rows_back/ppermute | solution.py:55
  93.7 7.0 %collective-permute-start.29 = (bf16[80,768]{1,0:T(8,128)(2,1)S(1)}, bf16[80,768]{1,0:T(8,128)(2,1)S(1)}, u32[]{:S(2)}, u32[]{:S(2)}) collective-permute-start(bf16[80,768]{1,0:T(8,128)(2,1)S(1)} %get-tuple-element.76), channel_id=1, source_target_pairs={{0,128},{64,192},{128,0},{192,64},{1,129},{65,193},{129,1},{193,65... | collective-permute-start | bytes 368648 | tf_op jit(solution)/shard_map/weights_y/ppermute | solution.py:45
  (19 other events, 97.9 us)

commit v5 on v4

--- a/solution.py
+++ b/solution.py
@@ -17,6 +17,9 @@
 TOP = 256
 PART = 272
 CUT = 144
+ORDER = (0, 1, 7, 2, 6, 3, 4, 5)
+ROW_AT = (0, 0, 0, 32, 0, 0, 32, 32)
+SLOT_AT = (0, 64, 64, 256, 64, 64, 0, 0)
 NT = (((1,), (1,)), ((), ()))
 NN = (((1,), (0,)), ((), ()))
 TN = (((0,), (0,)), ((), ()))
@@ -55,34 +58,58 @@
     return lax.ppermute(x, ("core", axis), pairs)
 
 
-def slot_kernel(place, slots, ay, wide):
-    x, z, sign = place[0], place[2], 1 - 2 * place[1]
+def load_kernel(place, e, eo, want, want_o, side, side_o, m1, m2, s0):
+    z, sign = place[2], 1 - 2 * place[1]
+
+    def put(ref, lo, d, wants, sides):
+        to = lax.rem(z + sign * d + NZ, NZ)
+        for x in range(NX):
+            ref[lo : lo + 32, x * 128 : x * 128 + 128] = wants[to, x]
+        ref[lo : lo + 32, 512:640] = sides[to]
+        ref[lo : lo + 32, 640:768] = jnp.zeros((32, 128), BF16)
+
+    put(s0, 0, 0, want, side)
+    m1[0:64], m1[96:160] = e[...], eo[...]
+    put(m1, 64, 1, want, side)
+    put(m1, 160, 1, want_o, side_o)
+    m2[32:96], m2[160:224] = e[...], eo[...]
+    put(m2, 0, 4, want, side)
+    put(m2, 96, 3, want, side)
+    put(m2, 128, 3, want_o, side_o)
+    put(m2, 224, 2, want_o, side_o)
+    put(m2, 256, 2, want, side)
+
+
+def kid_row(k):
+    core, y = k // 4 % NC, k // 8
+    return core * (TOP + CL) + (y * 4 + k % 4) * CL
+
+
+def slot_kernel(place, b0, b1, b2, b3, ay, wide, sides, *, offsets):
+    x = place[0]
     lane_row = lax.broadcasted_iota(jnp.int32, (256, 128), 0)
     cluster_row = lax.broadcasted_iota(jnp.int32, (CL, 128), 0)
-
-    def step(i, _):
-        r, g = i // 2, lax.rem(i, 2)
+    blocks = (b0, b1, b2, b3)
+    for q, (b, lo) in enumerate(zip(blocks, offsets)):
+        sides[q] = b[lo : lo + 32, 512:640].astype(F32)
+
+    def step(r, _):
         owner = lax.rem(x - r + NX, NX)
         left = []
-        for q in range(4):
-            source = lax.rem(z - sign * (g * 4 + q) + NZ, NZ)
-            side = slots[source, owner].astype(F32)
-            alpha = side[KIDS : KIDS + 1]
-            inst = side[KIDS + 1 : KIDS + 2].astype(jnp.int32)
-            clus = side[KIDS + 2 : KIDS + 3].astype(jnp.int32)
+        for q, (b, lo) in enumerate(zip(blocks, offsets)):
+            want = b[lo : lo + 32, pl.ds(pl.multiple_of(owner * 128, 128), 128)].astype(F32)
+            side = sides[q, pl.ds(pl.multiple_of(owner * 8, 8), 8)]
+            alpha, inst, clus = side[0:1], side[1:2].astype(jnp.int32), side[2:3].astype(jnp.int32)
             left.append(jnp.where(lane_row == inst + q * INST, alpha, 0.0).astype(BF16))
             member = cluster_row == clus
             for k in range(KIDS + 1):
-                at = TOP if k == KIDS else k * CL + (CL if k * CL >= TOP else 0)
-                wide[at : at + CL, q * 128 : q * 128 + 128] = jnp.where(
-                    member, side[k : k + 1], 0.0
-                ).astype(BF16)
-        ay[r, :, pl.ds(pl.multiple_of(g * 256, 256), 256)] = dot(
-            wide[...], jnp.concatenate(left, axis=1), NT
-        )
+                at = TOP if k == KIDS else kid_row(k)
+                row = alpha if k == KIDS else want[k : k + 1]
+                wide[at : at + CL, q * 128 : q * 128 + 128] = jnp.where(member, row, 0.0).astype(BF16)
+        ay[r] = dot(wide[...], jnp.concatenate(left, axis=1), NT)
         return 0
 
-    lax.fori_loop(0, 2 * NX, step, 0)
+    lax.fori_loop(0, NX, step, 0)
 
 
 def owner_kernel(place, *refs, r):
@@ -90,32 +117,34 @@
     mine = pl.ds(pl.multiple_of(core * TOP, 16), PART)
     other = pl.ds(pl.multiple_of((1 - core) * TOP, 16), PART)
     if r == 2:
-        blocks, (n1, n2, f1, f2, ay, a, b, dzs, e, w, z) = refs[:NZ], refs[NZ:]
+        blocks, (n1, n2, f1, f2, ay1, ay2, a, b, dzs, e, w, z) = refs[:NZ], refs[NZ:]
         for d in range(NZ):
-            e[d * INST : d * INST + INST] = blocks[d][:INST]
+            lo = ROW_AT[d]
+            e[d * INST : d * INST + INST] = blocks[d][lo : lo + INST]
         for at, p1, p2 in ((core, n1, n2), (1 - core, f1, f2)):
             w[pl.ds(pl.multiple_of(at * TOP, 16), CUT)] = p1[...]
             w[pl.ds(pl.multiple_of(at * TOP + CUT, 16), PART - CUT)] = p2[...]
     elif r == 0:
-        e, w, ay, a, b, dzs, z = refs
+        e, w, ay1, ay2, a, b, dzs, z = refs
     else:
-        e, near, far, ay, a, b, dzs, w, z = refs
+        e, near, far, ay1, ay2, a, b, dzs, w, z = refs
         w[mine] = near[...]
         w[other] = far[...]
     z[...] = dot(w[...], e[...], NT)
     top = pl.ds(TOP, CL)
-    s1 = jax.nn.sigmoid(z[top])
-    s1a = s1 * ay[r, top]
-    total = jnp.zeros((CL, ROWS), F32)
-    for k in range(KIDS + 1):
-        if k * CL == TOP:
-            continue
-        at = pl.ds(k * CL, CL)
-        s2 = jax.nn.sigmoid(z[at])
-        t = s2 * (s1a * s2 - ay[r, at])
-        total = total + t
-        dzs[at] = (s1 * (1.0 - s2) * t).astype(BF16)
-    dzs[top] = (total * s1 * (1.0 - s1)).astype(BF16)
+    for ay, lanes in ((ay1, pl.ds(0, 256)), (ay2, pl.ds(256, 256))):
+        s1 = jax.nn.sigmoid(z[top, lanes])
+        s1a = s1 * ay[r, top]
+        total = jnp.zeros((CL, 256), F32)
+        for k in range(KIDS + 1):
+            if k * CL == TOP:
+                continue
+            at = pl.ds(k * CL, CL)
+            s2 = jax.nn.sigmoid(z[at, lanes])
+            t = s2 * (s1a * s2 - ay[r, at])
+            total = total + t
+            dzs[at, lanes] = (s1 * (1.0 - s2) * t).astype(BF16)
+        dzs[top, lanes] = (total * s1 * (1.0 - s1)).astype(BF16)
     b[...] = dot(dzs[other], e[...], NN).astype(BF16)
     a[...] = dot(dzs[mine], e[...], NN).astype(a.dtype)
 
@@ -125,11 +154,14 @@
     ge[...] = dot(dzs[0][...], ws[0][...], TN)
     for r in range(1, NX):
         ge[...] += dot(dzs[r][...], ws[r][...], TN)
-    own[...] = ge[:INST]
-    near[...] = ge[INST : 4 * INST].astype(BF16)
-    last[...] = ge[4 * INST : 5 * INST].astype(BF16)
-    for i, d in enumerate((7, 6, 5)):
-        far[i * INST : i * INST + INST] = ge[d * INST : d * INST + INST].astype(BF16)
+    def block(d):
+        return ge[ORDER.index(d) * INST : ORDER.index(d) * INST + INST]
+
+    own[...] = block(0)
+    last[...] = block(4).astype(BF16)
+    for i, d in enumerate((1, 2, 3)):
+        near[i * INST : i * INST + INST] = block(d).astype(BF16)
+        far[i * INST : i * INST + INST] = block(NZ - d).astype(BF16)
 
 
 def pack_kernel(place, near, far, h1, h3):
@@ -188,37 +220,47 @@
     iy, ic, iz, ix = (lax.axis_index(n) for n in ("y", "core", "z", "x"))
     place = jnp.stack([ix, ic, iz, iy]).astype(jnp.int32)
 
-    with jax.named_scope("rows"):
-        p0 = jnp.concatenate([e, swap(e)], axis=0)
-        p1, p2 = turn(p0, "z", 1), turn(p0, "z", 2)
-        p3, p4 = turn(p2, "z", 1), turn(p2[:INST], "z", 2)
-        q1, q2, q3 = (swap(p[INST:]) for p in (p1, p2, p3))
-        blocks = (e, p1, p2, p3, p4, q3, q2, q1)
-
     with jax.named_scope("weights"):
         leaf = lw.reshape(CL, NY, NC, 4, D).transpose(2, 1, 3, 0, 4).reshape(2, TOP, D)
         w = jnp.concatenate([leaf[0], cw, leaf[1]], axis=0)
         part = lax.dynamic_slice_in_dim(w, ic * TOP, PART, 0)
         low, high = shift(part, "x", 1), shift(part, "x", -1)
         low2, high2 = shift(low[:CUT], "x", 1), shift(high[CUT:], "x", -1)
-        low_o, high_o, low2_o, high2_o = (swap(p) for p in (low, high, low2, high2))
 
     with jax.named_scope("slots"):
-        counts, _ = lax.optimization_barrier((counts, p1))
         cap = prefix.shape[-1]
         owners = NZ * NX
         inst, clus = inst.reshape(owners, 1, cap), clus.reshape(owners, 1, cap)
         valid = jnp.arange(cap, dtype=jnp.int32)[None, None, :] < counts.reshape(owners, 1, 1)
         nothing = jnp.zeros((), BF16)
         alpha = jnp.where(valid, prefix.reshape(owners, 1, cap), nothing)
-        want = targets.reshape(owners, cap, NY, NC, 4).transpose(0, 3, 2, 4, 1)
-        want = jnp.where(valid, want.reshape(owners, KIDS, cap), nothing)
-        side = jnp.concatenate([want, alpha, inst.astype(BF16), clus.astype(BF16)], axis=1)
-        side = jnp.pad(side, ((0, 0), (0, 5), (0, 128 - cap))).reshape(NZ, NX, 40, 128)
-        slots = lax.all_to_all(side, "z", 0, 0, tiled=True)
-    (ay,) = call(
-        slot_kernel, [((NX, WIDE, ROWS), F32)], (place, slots), [((WIDE, 512), BF16)]
-    )
+        want = jnp.where(valid, jnp.swapaxes(targets.reshape(owners, cap, KIDS), 1, 2), nothing)
+        want = jnp.pad(want, ((0, 0), (0, 0), (0, 128 - cap))).reshape(NZ, NX, KIDS, 128)
+        side = jnp.concatenate([alpha, inst.astype(BF16), clus.astype(BF16)], axis=1)
+        side = jnp.pad(side, ((0, 0), (0, 5), (0, 128 - cap))).reshape(NZ, NX * 8, 128)
+
+    with jax.named_scope("rows"):
+        m1, m2, s0 = call(
+            load_kernel,
+            [((192, D), BF16), ((288, D), BF16), ((32, D), BF16)],
+            (place, e, swap(e), want, swap(want), side, swap(side)),
+        )
+        m2, m1 = turn(m2, "z", 2), turn(m1, "z", 1)
+        m3, m4 = turn(m2[32:224], "z", 1), turn(m2[:96], "z", 2)
+        q2, q1, q3 = swap(m2[160:256]), swap(m1[96:]), swap(m3[96:])
+        low2, high2, m4 = lax.optimization_barrier((low2, high2, m4))
+    with jax.named_scope("weights"):
+        low_o, high_o, low2_o, high2_o = (swap(p) for p in (low, high, low2, high2))
+    halves = []
+    for blocks, at in (((s0, m1, q1, m2), SLOT_AT[:4]), ((q2, m3, m4, q3), SLOT_AT[4:])):
+        halves += call(
+            slot_kernel,
+            [((NX, WIDE, 256), F32)],
+            (place,) + blocks,
+            [((WIDE, 512), BF16), ((4, 32, 128), F32)],
+            offsets=at,
+        )
+    blocks, ay = (e, m1, q1, m2, q2, m3, m4, q3), tuple(halves)
 
     wide, dzs = ((WIDE, D), BF16), ((WIDE, ROWS), BF16)
     half, half32 = ((PART, D), BF16), ((PART, D), F32)
@@ -227,7 +269,7 @@
     a2, b2, dz2, rows, w2 = call(
         owner_kernel,
         [half32, half, dzs, ((ROWS, D), BF16), wide],
-        (place,) + blocks + (low2, high2, low2_o, high2_o, ay),
+        (place,) + blocks + (low2, high2, low2_o, high2_o) + ay,
         z,
         r=2,
     )
@@ -236,13 +278,13 @@
             cut_kernel, [((CUT, D), BF16), ((PART - CUT, D), BF16)], (place, a2, swap(b2))
         )
     outs = [half32, half, dzs, wide]
-    a1, b1, dz1, w1 = call(owner_kernel, outs, (place, rows, low, low_o, ay), z, r=1)
+    a1, b1, dz1, w1 = call(owner_kernel, outs, (place, rows, low, low_o) + ay, z, r=1)
     b1 = swap(b1)
     rows, down, up = lax.optimization_barrier((rows, down, up))
     down, up = shift(down, "x", -1), shift(up, "x", 1)
-    a3, b3, dz3, w3 = call(owner_kernel, outs, (place, rows, high, high_o, ay), z, r=3)
+    a3, b3, dz3, w3 = call(owner_kernel, outs, (place, rows, high, high_o) + ay, z, r=3)
     b3 = swap(b3)
-    a0, b0, dz0 = call(owner_kernel, [half, half, dzs], (place, rows, w, ay), z, r=0)
+    a0, b0, dz0 = call(owner_kernel, [half, half, dzs], (place, rows, w) + ay, z, r=0)
     b0 = swap(b0)
     near, last, far, own = call(
         rows_kernel,

time: 106 us -> 90.2 us (0.85)
  waiting for transfers between devices: 35.5 us -> 22.8 us
  local copies, waits for them, and re-layouts: 5.22 us -> 1.22 us
  other arithmetic: 2.04 us -> 4.2 us
  starting transfers between devices: 40.9 us -> 39 us
    ppermute x8, waiting for transfers between devices: 24.7 us -> 8.7 us  [turn(): return lax.ppermute(x, ('core', axis), pairs)]
    all_to_all x1 -> x0, starting transfers between devices: 5.84 us -> none  [shards(): slots = lax.all_to_all(side, 'z', 0, 0, tiled=True)]
    ppermute x25 -> x27, starting transfers between devices: 18.3 us -> 21.8 us  [shift(): return lax.ppermute(x, axis, [(i, (i + by) % n) for i in range(n)])]
    ppermute x25 -> x27, waiting for transfers between devices: 10.8 us -> 14.1 us  [shift(): return lax.ppermute(x, axis, [(i, (i + by) % n) for i in range(n)])]
    slice x3 -> x4, local copies, waits for them, and re-layouts: 1.95 us -> 0.06 us  [the longest x2 0.04 us: shards(): m3, m4 = (turn(m2[32:224], 'z', 1), turn(m2[:96], 'z', 2))]
    reshape x2, local copies, waits for them, and re-layouts: 2.13 us -> 0.62 us  [shards(): lw.reshape(CL, NY, NC, 4, D).transpose(2, 1, 3, 0, 4).reshape(2, TOP, D)]
    pallas_call x12 -> x14, Pallas kernels: 20.7 us -> 21.2 us  [call(): pl.pallas_call(functools.partial(kernel, **static), out_shape=tuple((jax....]
  transfers between devices with their start and end apart: 34 -> 35, of which waited for: 9 -> 9; matrix products, arithmetic and copies ran while one was open for 3% -> 3% of each run, Pallas kernels for 20% -> 23%
where the time goes in v5:
time: 90.2 us; the launch traced here: 89.5 us
  starting transfers between devices  39 us (43%)
  waiting for transfers between devices  22.8 us (25%)
  Pallas kernels  21.2 us (24%)
  other arithmetic  4.2 us (5%)
  local copies, waits for them, and re-layouts  1.22 us (1%)
  between operations  0.98 us (1%)
    ppermute x27, starting transfers between devices, shift(): return lax.ppermute(x, axis, [(i, (i + by) % n) for i in range(n)])  21.8 us
    pallas_call x14, Pallas kernels, call(): pl.pallas_call(functools.partial(kernel, **static), out_shape=tuple((jax....  21.2 us
    ppermute x8, starting transfers between devices, turn(): return lax.ppermute(x, ('core', axis), pairs)  17.2 us
    ppermute x27, waiting for transfers between devices, shift(): return lax.ppermute(x, axis, [(i, (i + by) % n) for i in range(n)])  14.1 us
    ppermute x8, waiting for transfers between devices, turn(): return lax.ppermute(x, ('core', axis), pairs)  8.7 us
  transfers between devices with their start and end apart: 35, of which 9 were waited for; matrix products, arithmetic and copies ran while one was open for 3% of the time, Pallas kernels for 23%

profile of v5, /device:TPU:24, one launch (start us, length us, event | category | flops | bytes accessed | tf_op | source)
XLA Modules:
  0.0 89.5 jit_solution(3058309083823401790)
XLA Ops:
  7.0 3.3 %collective-permute-start.5 = (bf16[288,768]{1,0:T(8,128)(2,1)S(1)}, bf16[288,768]{1,0:T(8,128)(2,1)S(1)}, u32[]{:S(2)}, u32[]{:S(2)}) collective-permute-start(bf16[288,768]{1,0:T(8,128)(2,1)S(1)} %get-tuple-element.50), channel_id=1, source_target_pairs={{0,8},{4,12},{8,16},{12,20},{16,24},{20,28},{24,0},{28,4},{32,56},... | collective-permute-start | bytes 1327112 | tf_op jit(solution)/shard_map/rows/ppermute | solution.py:58
  10.4 2.8 %collective-permute-start.10 = (bf16[272,768]{1,0:T(8,128)(2,1)S(1)}, bf16[272,768]{1,0:T(8,128)(2,1)S(1)}, u32[]{:S(2)}, u32[]{:S(2)}) collective-permute-start(bf16[272,768]{1,0:T(8,128)(2,1)S(1)} %constant_dynamic-slice_fusion), channel_id=1, source_target_pairs={{0,3},{1,0},{2,1},{3,2},{4,7},{5,4},{6,5},{7,6},{8,11},{9,8},{10,9... | collective-permute-start | bytes 1253384 | tf_op jit(solution)/shard_map/weights/ppermute | solution.py:48
  13.3 1.9 %collective-permute-start.3 = (bf16[192,768]{1,0:T(8,128)(2,1)S(1)}, bf16[192,768]{1,0:T(8,128)(2,1)S(1)}, u32[]{:S(2)}, u32[]{:S(2)}) collective-permute-start(bf16[192,768]{1,0:T(8,128)(2,1)S(1)} %get-tuple-element.49), channel_id=1, source_target_pairs={{0,4},{4,8},{8,12},{12,16},{16,20},{20,24},{24,28},{28,0},{32,60},... | collective-permute-start | bytes 884744 | tf_op jit(solution)/shard_map/rows/ppermute | solution.py:58
  15.2 5.9 %collective-permute-done.10.refs_1_ = bf16[272,768]{1,0:T(8,128)(2,1)S(1)} collective-permute-done((bf16[272,768]{1,0:T(8,128)(2,1)S(1)}, bf16[272,768]{1,0:T(8,128)(2,1)S(1)}, u32[]{:S(2)}, u32[]{:S(2)}) %collective-permute-start.10) | collective-permute-done | bytes 417824 | tf_op jit(solution)/shard_map/weights/ppermute | solution.py:48
  21.0 3.8 %collective-permute-start.11 = (bf16[128,768]{1,0:T(8,128)(2,1)S(1)}, bf16[128,768]{1,0:T(8,128)(2,1)S(1)}, u32[]{:S(2)}, u32[]{:S(2)}) collective-permute-start(bf16[128,768]{1,0:T(8,128)(2,1)S(1)} %slice.52), channel_id=1, source_target_pairs={{0,3},{1,0},{2,1},{3,2},{4,7},{5,4},{6,5},{7,6},{8,11},{9,8},{10,9... | collective-permute-start | bytes 589832 | tf_op jit(solution)/shard_map/weights/ppermute | solution.py:48
  25.2 3.0 %collective-permute-start.7 = (bf16[192,768]{1,0:T(8,128)(2,1)S(1)}, bf16[192,768]{1,0:T(8,128)(2,1)S(1)}, u32[]{:S(2)}, u32[]{:S(2)}) collective-permute-start(bf16[192,768]{1,0:T(8,128)(2,1)S(1)} %slice.48), channel_id=1, source_target_pairs={{0,4},{4,8},{8,12},{12,16},{16,20},{20,24},{24,28},{28,0},{32,60},... | collective-permute-start | bytes 884744 | tf_op jit(solution)/shard_map/rows/ppermute | solution.py:58
  30.2 3.2 %collective-permute-done.9.refs_8_ = bf16[144,768]{1,0:T(8,128)(2,1)S(1)} collective-permute-done((bf16[144,768]{1,0:T(8,128)(2,1)S(1)}, bf16[144,768]{1,0:T(8,128)(2,1)S(1)}, u32[]{:S(2)}, u32[]{:S(2)}) %collective-permute-start.9) | collective-permute-done | bytes 221216 | tf_op jit(solution)/shard_map/weights/ppermute | solution.py:48
  34.4 3.5 %collective-permute-done.12.b2.refs_6_ = bf16[96,768]{1,0:T(8,128)(2,1)S(1)} collective-permute-done((bf16[96,768]{1,0:T(8,128)(2,1)S(1)}, bf16[96,768]{1,0:T(8,128)(2,1)S(1)}, u32[]{:S(2)}, u32[]{:S(2)}) %collective-permute-start.12) | collective-permute-done | bytes 147488 | tf_op jit(solution)/shard_map/rows/ppermute | solution.py:58
  38.7 2.1 %shard_map.103.refs_12_.refs_2_.refs_3_ = f32[4,528,256]{2,1,0:T(8,128)S(1)} custom-call(s32[4]{0:T(128)S(1)} %pad_add_fusion.place, bf16[32,768]{1,0:T(8,128)(2,1)S(1)} %get-tuple-element.54.b0, bf16[192,768]{1,0:T(8,128)(2,1)S(1)} %collective-permute-done.3.b1.refs_1_, bf16[96,768]{1,0:T(8,128)(2,1)S(1)} %collective-permute-done.4.b2.refs_2_, ...), custom_call_target="tpu_custom_call" | custom-call | flops 2000000000 | bytes 1048576 | tf_op jit(solution)/shard_map/pallas_call | solution.py:35
  40.9 2.1 %shard_map.104.refs_13_.refs_3_.refs_4_ = f32[4,528,256]{2,1,0:T(8,128)S(1)} custom-call(s32[4]{0:T(128)S(1)} %pad_add_fusion.place, bf16[96,768]{1,0:T(8,128)(2,1)S(1)} %collective-permute-done.6.b0.refs_4_, bf16[192,768]{1,0:T(8,128)(2,1)S(1)} %collective-permute-done.7.b1.refs_5_, bf16[96,768]{1,0:T(8,128)(2,1)S(1)} %collective-permute-done.12.b2.refs_6_, ...), custom_call_target="tpu_custom_call" | custom-call | flops 2000000000 | bytes 1048576 | tf_op jit(solution)/shard_map/pallas_call | solution.py:35
  43.0 2.1 %shard_map.105 = (f32[272,768]{1,0:T(8,128)S(1)}, bf16[272,768]{1,0:T(8,128)(2,1)S(1)}, bf16[528,512]{1,0:T(8,128)(2,1)S(1)}, bf16[512,768]{1,0:T(8,128)(2,1)S(1)}, bf16[528,768]{1,0:T(8,128)(2,1)S(1)}) custom-call(s32[4]{0:T(128)S(1)} %pad_add_fusion.place, bf16[64,768]{1,0:T(8,128)(2,1)S(1)} %copy-done, ...), custom_call_target="tpu_custom_call" | custom-call | flops 2000000000 | bytes 1048576 | tf_op jit(solution)/shard_map/pallas_call | solution.py:35
  45.8 2.1 %shard_map.107 = (f32[272,768]{1,0:T(8,128)S(1)}, bf16[272,768]{1,0:T(8,128)(2,1)S(1)}, bf16[528,512]{1,0:T(8,128)(2,1)S(1)}, bf16[528,768]{1,0:T(8,128)(2,1)S(1)}) custom-call(s32[4]{0:T(128)S(1)} %pad_add_fusion.place, bf16[512,768]{1,0:T(8,128)(2,1)S(1)} %get-tuple-element.60.refs_0_, bf16[272,768]{1,0:T(8,128)(2,1)S(1)} %collective-permute-done.8.refs_1_, ...), custom_call_target="tpu_custom_call" | custom-call | flops 2000000000 | bytes 1048576 | tf_op jit(solution)/shard_map/pallas_call | solution.py:35
  49.1 3.3 %collective-permute-start.24 = (bf16[144,768]{1,0:T(8,128)(2,1)S(1)}, bf16[144,768]{1,0:T(8,128)(2,1)S(1)}, u32[]{:S(2)}, u32[]{:S(2)}) collective-permute-start(bf16[144,768]{1,0:T(8,128)(2,1)S(1)} %get-tuple-element.74), channel_id=1, source_target_pairs={{0,3},{1,0},{2,1},{3,2},{4,7},{5,4},{6,5},{7,6},{8,11},{9,8},{10,9... | collective-permute-start | bytes 663560 | tf_op jit(solution)/shard_map/ppermute | solution.py:48
  52.4 2.1 %shard_map.108 = (f32[272,768]{1,0:T(8,128)S(1)}, bf16[272,768]{1,0:T(8,128)(2,1)S(1)}, bf16[528,512]{1,0:T(8,128)(2,1)S(1)}, bf16[528,768]{1,0:T(8,128)(2,1)S(1)}) custom-call(s32[4]{0:T(128)S(1)} %pad_add_fusion.place, bf16[512,768]{1,0:T(8,128)(2,1)S(1)} %get-tuple-element.60.refs_0_, bf16[272,768]{1,0:T(8,128)(2,1)S(1)} %collective-permute-done.10.refs_1_, ...), custom_call_target="tpu_custom_call" | custom-call | flops 2000000000 | bytes 1048576 | tf_op jit(solution)/shard_map/pallas_call | solution.py:35
  54.6 2.1 %shard_map.106 = (bf16[272,768]{1,0:T(8,128)(2,1)S(1)}, bf16[272,768]{1,0:T(8,128)(2,1)S(1)}, bf16[528,512]{1,0:T(8,128)(2,1)S(1)}) custom-call(s32[4]{0:T(128)S(1)} %pad_add_fusion.place, bf16[512,768]{1,0:T(8,128)(2,1)S(1)} %get-tuple-element.60.refs_0_, bf16[528,768]{1,0:T(8,128)(2,1)S(1)} %pad_maximum_fusion.refs_1_.refs_4_, ...), custom_call_target="tpu_custom_call" | custom-call | flops 2000000000 | bytes 1048576 | tf_op jit(solution)/shard_map/pallas_call | solution.py:35
  56.7 3.2 %shard_map.109 = (bf16[192,768]{1,0:T(8,128)(2,1)S(1)}, bf16[64,768]{1,0:T(8,128)(2,1)S(1)}, bf16[192,768]{1,0:T(8,128)(2,1)S(1)}, f32[64,768]{1,0:T(8,128)S(1)}) custom-call(s32[4]{0:T(128)S(1)} %pad_add_fusion.place, bf16[528,512]{1,0:T(8,128)(2,1)S(1)} %get-tuple-element.61.refs_0_, bf16[528,512]{1,0:T(8,128)(2,1)S(1)} %get-tuple-element.62.refs_1_, ...), custom_call_target="tpu_custom_call" | custom-call | flops 2000000000 | bytes 1048576 | tf_op jit(solution)/shard_map/pallas_call | solution.py:35
  61.6 2.0 %collective-permute-start.29 = (bf16[272,768]{1,0:T(8,128)(2,1)S(1)}, bf16[272,768]{1,0:T(8,128)(2,1)S(1)}, u32[]{:S(2)}, u32[]{:S(2)}) collective-permute-start(bf16[272,768]{1,0:T(8,128)(2,1)S(1)} %get-tuple-element.84), channel_id=1, source_target_pairs={{0,3},{1,0},{2,1},{3,2},{4,7},{5,4},{6,5},{7,6},{8,11},{9,8},{10,9... | collective-permute-start | bytes 1253384 | tf_op jit(solution)/shard_map/weights_x/ppermute | solution.py:48
  64.3 2.0 %collective-permute-start.21 = (bf16[128,768]{1,0:T(8,128)(2,1)S(1)}, bf16[128,768]{1,0:T(8,128)(2,1)S(1)}, u32[]{:S(2)}, u32[]{:S(2)}) collective-permute-start(bf16[128,768]{1,0:T(8,128)(2,1)S(1)} %get-tuple-element.72), channel_id=1, source_target_pairs={{0,28},{4,0},{8,4},{12,8},{16,12},{20,16},{24,20},{28,24},{32,36},... | collective-permute-start | bytes 589832 | tf_op jit(solution)/shard_map/rows_back/ppermute | solution.py:58
  66.3 2.5 %collective-permute-start.22 = (bf16[64,768]{1,0:T(8,128)(2,1)S(1)}, bf16[64,768]{1,0:T(8,128)(2,1)S(1)}, u32[]{:S(2)}, u32[]{:S(2)}) collective-permute-start(bf16[64,768]{1,0:T(8,128)(2,1)S(1)} %get-tuple-element.73), channel_id=1, source_target_pairs={{0,24},{4,28},{8,0},{12,4},{16,8},{20,12},{24,16},{28,20},{32,40},... | collective-permute-start | bytes 294920 | tf_op jit(solution)/shard_map/rows_back/ppermute | solution.py:58
  68.8 3.7 %collective-permute-done.22.got4 = bf16[64,768]{1,0:T(8,128)(2,1)S(1)} collective-permute-done((bf16[64,768]{1,0:T(8,128)(2,1)S(1)}, bf16[64,768]{1,0:T(8,128)(2,1)S(1)}, u32[]{:S(2)}, u32[]{:S(2)}) %collective-permute-start.22) | collective-permute-done | bytes 98336 | tf_op jit(solution)/shard_map/rows_back/ppermute | solution.py:58
  74.5 2.4 %collective-permute-start.23 = (bf16[128,768]{1,0:T(8,128)(2,1)S(1)}, bf16[128,768]{1,0:T(8,128)(2,1)S(1)}, u32[]{:S(2)}, u32[]{:S(2)}) collective-permute-start(bf16[128,768]{1,0:T(8,128)(2,1)S(1)} %rows_back.3), channel_id=1, source_target_pairs={{0,24},{4,28},{8,0},{12,4},{16,8},{20,12},{24,16},{28,20},{32,40},... | collective-permute-start | bytes 589832 | tf_op jit(solution)/shard_map/rows_back/ppermute | solution.py:58
  79.2 2.2 %collective-permute-start.33 = (bf16[80,768]{1,0:T(8,128)(2,1)S(1)}, bf16[80,768]{1,0:T(8,128)(2,1)S(1)}, u32[]{:S(2)}, u32[]{:S(2)}) collective-permute-start(bf16[80,768]{1,0:T(8,128)(2,1)S(1)} %get-tuple-element.90), channel_id=1, source_target_pairs={{0,64},{64,128},{128,192},{192,0},{1,65},{65,129},{129,193},{193,1... | collective-permute-start | bytes 368648 | tf_op jit(solution)/shard_map/weights_y/ppermute | solution.py:48
  82.8 1.8 %collective-permute-done.31.g2 = bf16[80,768]{1,0:T(8,128)(2,1)S(1)} collective-permute-done((bf16[80,768]{1,0:T(8,128)(2,1)S(1)}, bf16[80,768]{1,0:T(8,128)(2,1)S(1)}, u32[]{:S(2)}, u32[]{:S(2)}) %collective-permute-start.31) | collective-permute-done | bytes 122912 | tf_op jit(solution)/shard_map/weights_y/ppermute | solution.py:48
  84.8 2.6 %collective-permute-done.34.g3 = bf16[80,768]{1,0:T(8,128)(2,1)S(1)} collective-permute-done((bf16[80,768]{1,0:T(8,128)(2,1)S(1)}, bf16[80,768]{1,0:T(8,128)(2,1)S(1)}, u32[]{:S(2)}, u32[]{:S(2)}) %collective-permute-start.34) | collective-permute-done | bytes 122912 | tf_op jit(solution)/shard_map/weights_y/ppermute | solution.py:48
  (89 shorter events, 22.8 us)
Async XLA Ops:
  7.0 18.1 %collective-permute-start.5 = (bf16[288,768]{1,0:T(8,128)(2,1)S(1)}, bf16[288,768]{1,0:T(8,128)(2,1)S(1)}, u32[]{:S(2)}, u32[]{:S(2)}) collective-permute-start(bf16[288,768]{1,0:T(8,128)(2,1)S(1)} %get-tuple-element.50), channel_id=1, source_target_pairs={{0,8},{4,12},{8,16},{12,20},{16,24},{20,28},{24,0},{28,4},{32,56},... | collective-permute-start | bytes 1327112 | tf_op jit(solution)/shard_map/rows/ppermute | solution.py:58
  10.4 10.6 %collective-permute-start.10 = (bf16[272,768]{1,0:T(8,128)(2,1)S(1)}, bf16[272,768]{1,0:T(8,128)(2,1)S(1)}, u32[]{:S(2)}, u32[]{:S(2)}) collective-permute-start(bf16[272,768]{1,0:T(8,128)(2,1)S(1)} %constant_dynamic-slice_fusion), channel_id=1, source_target_pairs={{0,3},{1,0},{2,1},{3,2},{4,7},{5,4},{6,5},{7,6},{8,11},{9,8},{10,9... | collective-permute-start | bytes 1253384 | tf_op jit(solution)/shard_map/weights/ppermute | solution.py:48
  13.3 11.7 %collective-permute-start.8 = (bf16[272,768]{1,0:T(8,128)(2,1)S(1)}, bf16[272,768]{1,0:T(8,128)(2,1)S(1)}, u32[]{:S(2)}, u32[]{:S(2)}) collective-permute-start(bf16[272,768]{1,0:T(8,128)(2,1)S(1)} %constant_dynamic-slice_fusion), channel_id=1, source_target_pairs={{0,1},{1,2},{2,3},{3,0},{4,5},{5,6},{6,7},{7,4},{8,9},{9,10},{10,1... | collective-permute-start | bytes 1253384 | tf_op jit(solution)/shard_map/weights/ppermute | solution.py:48
  13.3 15.6 %collective-permute-start.3 = (bf16[192,768]{1,0:T(8,128)(2,1)S(1)}, bf16[192,768]{1,0:T(8,128)(2,1)S(1)}, u32[]{:S(2)}, u32[]{:S(2)}) collective-permute-start(bf16[192,768]{1,0:T(8,128)(2,1)S(1)} %get-tuple-element.49), channel_id=1, source_target_pairs={{0,4},{4,8},{8,12},{12,16},{16,20},{20,24},{24,28},{28,0},{32,60},... | collective-permute-start | bytes 884744 | tf_op jit(solution)/shard_map/rows/ppermute | solution.py:58
  21.0 9.0 %collective-permute-start.11 = (bf16[128,768]{1,0:T(8,128)(2,1)S(1)}, bf16[128,768]{1,0:T(8,128)(2,1)S(1)}, u32[]{:S(2)}, u32[]{:S(2)}) collective-permute-start(bf16[128,768]{1,0:T(8,128)(2,1)S(1)} %slice.52), channel_id=1, source_target_pairs={{0,3},{1,0},{2,1},{3,2},{4,7},{5,4},{6,5},{7,6},{8,11},{9,8},{10,9... | collective-permute-start | bytes 589832 | tf_op jit(solution)/shard_map/weights/ppermute | solution.py:48
  25.0 8.4 %collective-permute-start.9 = (bf16[144,768]{1,0:T(8,128)(2,1)S(1)}, bf16[144,768]{1,0:T(8,128)(2,1)S(1)}, u32[]{:S(2)}, u32[]{:S(2)}) collective-permute-start(bf16[144,768]{1,0:T(8,128)(2,1)S(1)} %slice.51), channel_id=1, source_target_pairs={{0,1},{1,2},{2,3},{3,0},{4,5},{5,6},{6,7},{7,4},{8,9},{9,10},{10,1... | collective-permute-start | bytes 663560 | tf_op jit(solution)/shard_map/weights/ppermute | solution.py:48
  25.2 12.7 %collective-permute-start.7 = (bf16[192,768]{1,0:T(8,128)(2,1)S(1)}, bf16[192,768]{1,0:T(8,128)(2,1)S(1)}, u32[]{:S(2)}, u32[]{:S(2)}) collective-permute-start(bf16[192,768]{1,0:T(8,128)(2,1)S(1)} %slice.48), channel_id=1, source_target_pairs={{0,4},{4,8},{8,12},{12,16},{16,20},{20,24},{24,28},{28,0},{32,60},... | collective-permute-start | bytes 884744 | tf_op jit(solution)/shard_map/rows/ppermute | solution.py:58
  28.1 9.8 %collective-permute-start.12 = (bf16[96,768]{1,0:T(8,128)(2,1)S(1)}, bf16[96,768]{1,0:T(8,128)(2,1)S(1)}, u32[]{:S(2)}, u32[]{:S(2)}) collective-permute-start(bf16[96,768]{1,0:T(8,128)(2,1)S(1)} %get-tuple-element.97), channel_id=1, source_target_pairs={{0,8},{4,12},{8,16},{12,20},{16,24},{20,28},{24,0},{28,4},{32,56},... | collective-permute-start | bytes 442376 | tf_op jit(solution)/shard_map/rows/ppermute | solution.py:58
  28.9 9.5 %collective-permute-start.4 = (bf16[96,768]{1,0:T(8,128)(2,1)S(1)}, bf16[96,768]{1,0:T(8,128)(2,1)S(1)}, u32[]{:S(2)}, u32[]{:S(2)}) collective-permute-start(bf16[96,768]{1,0:T(8,128)(2,1)S(1)} %slice.46), channel_id=1, source_target_pairs={{0,32},{32,0},{1,33},{33,1},{2,34},{34,2},{3,35},{35,3},{4,36},{36... | collective-permute-start | bytes 442376 | tf_op jit(solution)/shard_map/rows/ppermute | solution.py:48
  30.0 15.8 %collective-permute-start.17 = (bf16[272,768]{1,0:T(8,128)(2,1)S(1)}, bf16[272,768]{1,0:T(8,128)(2,1)S(1)}, u32[]{:S(2)}, u32[]{:S(2)}) collective-permute-start(bf16[272,768]{1,0:T(8,128)(2,1)S(1)} %collective-permute-done.8.refs_1_), channel_id=1, source_target_pairs={{0,32},{32,0},{1,33},{33,1},{2,34},{34,2},{3,35},{35,3},{4,36},{36... | collective-permute-start | bytes 1253384 | tf_op jit(solution)/shard_map/weights/ppermute | solution.py:48
  33.5 7.4 %collective-permute-start.6 = (bf16[96,768]{1,0:T(8,128)(2,1)S(1)}, bf16[96,768]{1,0:T(8,128)(2,1)S(1)}, u32[]{:S(2)}, u32[]{:S(2)}) collective-permute-start(bf16[96,768]{1,0:T(8,128)(2,1)S(1)} %get-tuple-element.98), channel_id=1, source_target_pairs={{0,32},{32,0},{1,33},{33,1},{2,34},{34,2},{3,35},{35,3},{4,36},{36... | collective-permute-start | bytes 442376 | tf_op jit(solution)/shard_map/rows/ppermute | solution.py:48
  45.7 6.7 %collective-permute-start.18 = (bf16[272,768]{1,0:T(8,128)(2,1)S(1)}, bf16[272,768]{1,0:T(8,128)(2,1)S(1)}, u32[]{:S(2)}, u32[]{:S(2)}) collective-permute-start(bf16[272,768]{1,0:T(8,128)(2,1)S(1)} %collective-permute-done.10.refs_1_), channel_id=1, source_target_pairs={{0,32},{32,0},{1,33},{33,1},{2,34},{34,2},{3,35},{35,3},{4,36},{36... | collective-permute-start | bytes 1253384 | tf_op jit(solution)/shard_map/weights/ppermute | solution.py:48
  47.9 12.9 %collective-permute-start.26 = (bf16[272,768]{1,0:T(8,128)(2,1)S(1)}, bf16[272,768]{1,0:T(8,128)(2,1)S(1)}, u32[]{:S(2)}, u32[]{:S(2)}) collective-permute-start(bf16[272,768]{1,0:T(8,128)(2,1)S(1)} %get-tuple-element.79), channel_id=1, source_target_pairs={{0,32},{32,0},{1,33},{33,1},{2,34},{34,2},{3,35},{35,3},{4,36},{36... | collective-permute-start | bytes 1253384 | tf_op jit(solution)/shard_map/ppermute | solution.py:48
  49.0 11.8 %collective-permute-start.28 = (bf16[128,768]{1,0:T(8,128)(2,1)S(1)}, bf16[128,768]{1,0:T(8,128)(2,1)S(1)}, u32[]{:S(2)}, u32[]{:S(2)}) collective-permute-start(bf16[128,768]{1,0:T(8,128)(2,1)S(1)} %get-tuple-element.83), channel_id=1, source_target_pairs={{0,1},{1,2},{2,3},{3,0},{4,5},{5,6},{6,7},{7,4},{8,9},{9,10},{10,1... | collective-permute-start | bytes 589832 | tf_op jit(solution)/shard_map/ppermute | solution.py:48
  49.1 11.3 %collective-permute-start.24 = (bf16[144,768]{1,0:T(8,128)(2,1)S(1)}, bf16[144,768]{1,0:T(8,128)(2,1)S(1)}, u32[]{:S(2)}, u32[]{:S(2)}) collective-permute-start(bf16[144,768]{1,0:T(8,128)(2,1)S(1)} %get-tuple-element.74), channel_id=1, source_target_pairs={{0,3},{1,0},{2,1},{3,2},{4,7},{5,4},{6,5},{7,6},{8,11},{9,8},{10,9... | collective-permute-start | bytes 663560 | tf_op jit(solution)/shard_map/ppermute | solution.py:48
  54.5 6.3 %collective-permute-start.27 = (bf16[272,768]{1,0:T(8,128)(2,1)S(1)}, bf16[272,768]{1,0:T(8,128)(2,1)S(1)}, u32[]{:S(2)}, u32[]{:S(2)}) collective-permute-start(bf16[272,768]{1,0:T(8,128)(2,1)S(1)} %get-tuple-element.81), channel_id=1, source_target_pairs={{0,32},{32,0},{1,33},{33,1},{2,34},{34,2},{3,35},{35,3},{4,36},{36... | collective-permute-start | bytes 1253384 | tf_op jit(solution)/shard_map/ppermute | solution.py:48
  60.4 16.4 %collective-permute-start.25 = (bf16[272,768]{1,0:T(8,128)(2,1)S(1)}, bf16[272,768]{1,0:T(8,128)(2,1)S(1)}, u32[]{:S(2)}, u32[]{:S(2)}) collective-permute-start(bf16[272,768]{1,0:T(8,128)(2,1)S(1)} %get-tuple-element.77), channel_id=1, source_target_pairs={{0,32},{32,0},{1,33},{33,1},{2,34},{34,2},{3,35},{35,3},{4,36},{36... | collective-permute-start | bytes 1253384 | tf_op jit(solution)/shard_map/ppermute | solution.py:48
  61.6 15.3 %collective-permute-start.29 = (bf16[272,768]{1,0:T(8,128)(2,1)S(1)}, bf16[272,768]{1,0:T(8,128)(2,1)S(1)}, u32[]{:S(2)}, u32[]{:S(2)}) collective-permute-start(bf16[272,768]{1,0:T(8,128)(2,1)S(1)} %get-tuple-element.84), channel_id=1, source_target_pairs={{0,3},{1,0},{2,1},{3,2},{4,7},{5,4},{6,5},{7,6},{8,11},{9,8},{10,9... | collective-permute-start | bytes 1253384 | tf_op jit(solution)/shard_map/weights_x/ppermute | solution.py:48
  63.6 13.3 %collective-permute-start.30 = (bf16[272,768]{1,0:T(8,128)(2,1)S(1)}, bf16[272,768]{1,0:T(8,128)(2,1)S(1)}, u32[]{:S(2)}, u32[]{:S(2)}) collective-permute-start(bf16[272,768]{1,0:T(8,128)(2,1)S(1)} %get-tuple-element.85), channel_id=1, source_target_pairs={{0,1},{1,2},{2,3},{3,0},{4,5},{5,6},{6,7},{7,4},{8,9},{9,10},{10,1... | collective-permute-start | bytes 1253384 | tf_op jit(solution)/shard_map/weights_x/ppermute | solution.py:48
  64.3 9.6 %collective-permute-start.21 = (bf16[128,768]{1,0:T(8,128)(2,1)S(1)}, bf16[128,768]{1,0:T(8,128)(2,1)S(1)}, u32[]{:S(2)}, u32[]{:S(2)}) collective-permute-start(bf16[128,768]{1,0:T(8,128)(2,1)S(1)} %get-tuple-element.72), channel_id=1, source_target_pairs={{0,28},{4,0},{8,4},{12,8},{16,12},{20,16},{24,20},{28,24},{32,36},... | collective-permute-start | bytes 589832 | tf_op jit(solution)/shard_map/rows_back/ppermute | solution.py:58
  66.3 6.3 %collective-permute-start.22 = (bf16[64,768]{1,0:T(8,128)(2,1)S(1)}, bf16[64,768]{1,0:T(8,128)(2,1)S(1)}, u32[]{:S(2)}, u32[]{:S(2)}) collective-permute-start(bf16[64,768]{1,0:T(8,128)(2,1)S(1)} %get-tuple-element.73), channel_id=1, source_target_pairs={{0,24},{4,28},{8,0},{12,4},{16,8},{20,12},{24,16},{28,20},{32,40},... | collective-permute-start | bytes 294920 | tf_op jit(solution)/shard_map/rows_back/ppermute | solution.py:58
  72.6 12.1 %collective-permute-start.20 = (bf16[128,768]{1,0:T(8,128)(2,1)S(1)}, bf16[128,768]{1,0:T(8,128)(2,1)S(1)}, u32[]{:S(2)}, u32[]{:S(2)}) collective-permute-start(bf16[128,768]{1,0:T(8,128)(2,1)S(1)} %get-tuple-element.71), channel_id=1, source_target_pairs={{0,28},{4,0},{8,4},{12,8},{16,12},{20,16},{24,20},{28,24},{32,36},... | collective-permute-start | bytes 589832 | tf_op jit(solution)/shard_map/rows_back/ppermute | solution.py:58
  74.5 8.4 %collective-permute-start.23 = (bf16[128,768]{1,0:T(8,128)(2,1)S(1)}, bf16[128,768]{1,0:T(8,128)(2,1)S(1)}, u32[]{:S(2)}, u32[]{:S(2)}) collective-permute-start(bf16[128,768]{1,0:T(8,128)(2,1)S(1)} %rows_back.3), channel_id=1, source_target_pairs={{0,24},{4,28},{8,0},{12,4},{16,8},{20,12},{24,16},{28,20},{32,40},... | collective-permute-start | bytes 589832 | tf_op jit(solution)/shard_map/rows_back/ppermute | solution.py:58
  77.8 6.8 %collective-permute-start.31 = (bf16[80,768]{1,0:T(8,128)(2,1)S(1)}, bf16[80,768]{1,0:T(8,128)(2,1)S(1)}, u32[]{:S(2)}, u32[]{:S(2)}) collective-permute-start(bf16[80,768]{1,0:T(8,128)(2,1)S(1)} %get-tuple-element.86), channel_id=1, source_target_pairs={{0,128},{64,192},{128,0},{192,64},{1,129},{65,193},{129,1},{193,65... | collective-permute-start | bytes 368648 | tf_op jit(solution)/shard_map/weights_y/ppermute | solution.py:48
  (14 other events, 50.2 us)

commit v6 on v5

--- a/solution.py
+++ b/solution.py
@@ -17,9 +17,9 @@
 TOP = 256
 PART = 272
 CUT = 144
-ORDER = (0, 1, 7, 2, 6, 3, 4, 5)
-ROW_AT = (0, 0, 0, 32, 0, 0, 32, 32)
-SLOT_AT = (0, 64, 64, 256, 64, 64, 0, 0)
+ORDER = (0, 1, 7, 4, 2, 6, 3, 5)
+ROW_AT = (0, 0, 0, 32, 32, 0, 0, 32)
+SLOT_AT = (0, 64, 64, 0, 256, 64, 64, 0)
 NT = (((1,), (1,)), ((), ()))
 NN = (((1,), (0,)), ((), ()))
 TN = (((0,), (0,)), ((), ()))
@@ -58,15 +58,27 @@
     return lax.ppermute(x, ("core", axis), pairs)
 
 
+def side_kernel(counts, inst, clus, prefix, side, rows):
+    rows[...] = jnp.zeros(rows.shape, F32)
+    lane = lax.broadcasted_iota(jnp.int32, (1, inst.shape[1]), 1)
+    for o in range(NZ * NX):
+        alpha = jnp.where(lane < counts[o], prefix[o : o + 1].astype(F32), 0.0)
+        rows[o * 8 : o * 8 + 1, : inst.shape[1]] = alpha
+        rows[o * 8 + 1 : o * 8 + 2, : inst.shape[1]] = inst[o : o + 1].astype(F32)
+        rows[o * 8 + 2 : o * 8 + 3, : inst.shape[1]] = clus[o : o + 1].astype(F32)
+    for z in range(NZ):
+        side[z] = rows[z * 32 : z * 32 + 32].astype(BF16)
+
+
 def load_kernel(place, e, eo, want, want_o, side, side_o, m1, m2, s0):
     z, sign = place[2], 1 - 2 * place[1]
 
     def put(ref, lo, d, wants, sides):
         to = lax.rem(z + sign * d + NZ, NZ)
+        ref[lo : lo + 32] = jnp.zeros((32, D), BF16)
         for x in range(NX):
-            ref[lo : lo + 32, x * 128 : x * 128 + 128] = wants[to, x]
+            ref[lo : lo + 32, x * 128 : x * 128 + wants.shape[2]] = wants[to * NX + x]
         ref[lo : lo + 32, 512:640] = sides[to]
-        ref[lo : lo + 32, 640:768] = jnp.zeros((32, 128), BF16)
 
     put(s0, 0, 0, want, side)
     m1[0:64], m1[96:160] = e[...], eo[...]
@@ -151,9 +163,7 @@
 
 def rows_kernel(place, *refs):
     dzs, ws, (near, last, far, own, ge) = refs[:NX], refs[NX : 2 * NX], refs[2 * NX :]
-    ge[...] = dot(dzs[0][...], ws[0][...], TN)
-    for r in range(1, NX):
-        ge[...] += dot(dzs[r][...], ws[r][...], TN)
+    ge[...] = sum(dot(dzs[r][...], ws[r][...], TN) for r in range(NX))
     def block(d):
         return ge[ORDER.index(d) * INST : ORDER.index(d) * INST + INST]
 
@@ -164,16 +174,11 @@
         far[i * INST : i * INST + INST] = block(NZ - d).astype(BF16)
 
 
-def pack_kernel(place, near, far, h1, h3):
-    for h, at in ((h1, 0), (h3, 2 * INST)):
+def pack_kernel(place, near, last, far, h1, h2, h3):
+    for h, at in ((h1, 0), (h2, INST), (h3, 2 * INST)):
         h[:INST] = near[at : at + INST]
-        h[INST:] = far[at : at + INST]
-
-
-def pass_kernel(place, near, far, got3, got4, out):
-    at = pl.ds(INST, INST)
-    out[:INST] = (near[at].astype(F32) + got3[:INST].astype(F32) + got4[...].astype(F32)).astype(BF16)
-    out[INST:] = (far[at].astype(F32) + got3[INST:].astype(F32)).astype(BF16)
+        h[INST : 2 * INST] = far[at : at + INST]
+    h3[2 * INST :] = last[...]
 
 
 def cut_kernel(place, a, b, low, high):
@@ -225,19 +230,18 @@
         w = jnp.concatenate([leaf[0], cw, leaf[1]], axis=0)
         part = lax.dynamic_slice_in_dim(w, ic * TOP, PART, 0)
         low, high = shift(part, "x", 1), shift(part, "x", -1)
-        low2, high2 = shift(low[:CUT], "x", 1), shift(high[CUT:], "x", -1)
 
     with jax.named_scope("slots"):
         cap = prefix.shape[-1]
         owners = NZ * NX
-        inst, clus = inst.reshape(owners, 1, cap), clus.reshape(owners, 1, cap)
-        valid = jnp.arange(cap, dtype=jnp.int32)[None, None, :] < counts.reshape(owners, 1, 1)
-        nothing = jnp.zeros((), BF16)
-        alpha = jnp.where(valid, prefix.reshape(owners, 1, cap), nothing)
-        want = jnp.where(valid, jnp.swapaxes(targets.reshape(owners, cap, KIDS), 1, 2), nothing)
-        want = jnp.pad(want, ((0, 0), (0, 0), (0, 128 - cap))).reshape(NZ, NX, KIDS, 128)
-        side = jnp.concatenate([alpha, inst.astype(BF16), clus.astype(BF16)], axis=1)
-        side = jnp.pad(side, ((0, 0), (0, 5), (0, 128 - cap))).reshape(NZ, NX * 8, 128)
+        want = jnp.swapaxes(targets.reshape(owners, cap, KIDS), 1, 2)
+        (side,) = call(
+            side_kernel,
+            [((NZ, NX * 8, 128), BF16)],
+            (counts.reshape(owners),)
+            + tuple(v.reshape(owners, cap) for v in (inst, clus, prefix)),
+            [((owners * 8, 128), F32)],
+        )
 
     with jax.named_scope("rows"):
         m1, m2, s0 = call(
@@ -248,19 +252,24 @@
         m2, m1 = turn(m2, "z", 2), turn(m1, "z", 1)
         m3, m4 = turn(m2[32:224], "z", 1), turn(m2[:96], "z", 2)
         q2, q1, q3 = swap(m2[160:256]), swap(m1[96:]), swap(m3[96:])
-        low2, high2, m4 = lax.optimization_barrier((low2, high2, m4))
-    with jax.named_scope("weights"):
-        low_o, high_o, low2_o, high2_o = (swap(p) for p in (low, high, low2, high2))
-    halves = []
-    for blocks, at in (((s0, m1, q1, m2), SLOT_AT[:4]), ((q2, m3, m4, q3), SLOT_AT[4:])):
-        halves += call(
+
+    def sum_slots(blocks, at):
+        return call(
             slot_kernel,
             [((NX, WIDE, 256), F32)],
             (place,) + blocks,
             [((WIDE, 512), BF16), ((4, 32, 128), F32)],
             offsets=at,
-        )
-    blocks, ay = (e, m1, q1, m2, q2, m3, m4, q3), tuple(halves)
+        )[0]
+
+    ay1 = sum_slots((s0, m1, q1, m4), SLOT_AT[:4])
+    with jax.named_scope("weights"):
+        near_low, near_high, _ = lax.optimization_barrier((low, high, m2))
+        low2, high2 = shift(near_low[:CUT], "x", 1), shift(near_high[CUT:], "x", -1)
+        low2, high2, ay1 = lax.optimization_barrier((low2, high2, ay1))
+        low_o, high_o, low2_o, high2_o = (swap(p) for p in (low, high, low2, high2))
+    ay2 = sum_slots((m2, q2, m3, q3), SLOT_AT[4:])
+    blocks, ay = (e, m1, q1, m4, m2, q2, m3, q3), (ay1, ay2)
 
     wide, dzs = ((WIDE, D), BF16), ((WIDE, ROWS), BF16)
     half, half32 = ((PART, D), BF16), ((PART, D), F32)
@@ -294,20 +303,20 @@
     )
 
     with jax.named_scope("rows_back"):
-        last = turn(last, "z", -2)
         far = swap(far)
-        pair = ((2 * INST, D), BF16)
-        h1, h3 = call(pack_kernel, [pair, pair], (place, near, far))
-        h3, h1 = turn(h3, "z", -1), turn(h1, "z", -1)
 
     with jax.named_scope("weights_x"):
         down, a0 = lax.optimization_barrier((down, a0))
         t1, t3 = call(merge_kernel, [half, half], (place, a1, b1, a3, b3, down, up))
+        near, _ = lax.optimization_barrier((near, t1))
         t1, t3 = shift(t1, "x", -1), shift(t3, "x", 1)
 
     with jax.named_scope("rows_back"):
-        (h2,) = call(pass_kernel, [pair], (place, near, far, h3, last))
-        h2 = turn(h2, "z", -2)
+        pair = ((2 * INST, D), BF16)
+        h1, h2, h3 = call(
+            pack_kernel, [pair, pair, ((3 * INST, D), BF16)], (place, near, last, far)
+        )
+        h3, h2, h1 = turn(h3, "z", -3), turn(h2, "z", -2), turn(h1, "z", -1)
 
     with jax.named_scope("weights_y"):
         send = ((80, D), BF16)
@@ -321,8 +330,9 @@
 
     with jax.named_scope("rows_back"):
         h2, g2 = lax.optimization_barrier((h2, g2))
-        both = h1.astype(F32) + h2.astype(F32)
-        grad_embed = (own + both[:INST]) + swap(both[INST:])
+        last = turn(h3[2 * INST :], "z", -1)
+        both = h1.astype(F32) + h2.astype(F32) + h3[: 2 * INST].astype(F32)
+        grad_embed = (own + both[:INST] + last.astype(F32)) + swap(both[INST:])
 
     with jax.named_scope("weights_y"):
         grad_leaf, grad_cluster = call(

time: 90.2 us -> 95.3 us (1.057)
  the two profiles are of different devices: /device:TPU:24 before, /device:TPU:1 now
where the time goes in v6:
time: 95.3 us; the launch traced here: 95 us
  starting transfers between devices  44.5 us (47%)
  waiting for transfers between devices  23.6 us (25%)
  Pallas kernels  21.3 us (22%)
  local copies, waits for them, and re-layouts  3.79 us (4%)
    ppermute x27, starting transfers between devices, shift(): return lax.ppermute(x, axis, [(i, (i + by) % n) for i in range(n)])  30 us
    pallas_call x14, Pallas kernels, call(): pl.pallas_call(functools.partial(kernel, **static), out_shape=tuple((jax....  21.3 us
    ppermute x8, waiting for transfers between devices, turn(): return lax.ppermute(x, ('core', axis), pairs)  20.3 us
    ppermute x8, starting transfers between devices, turn(): return lax.ppermute(x, ('core', axis), pairs)  14.5 us
    ppermute x27, waiting for transfers between devices, shift(): return lax.ppermute(x, axis, [(i, (i + by) % n) for i in range(n)])  3.27 us
    unnamed x16, local copies, waits for them, and re-layouts  2.98 us
  transfers between devices with their start and end apart: 35, of which 6 were waited for; matrix products, arithmetic and copies ran while one was open for 1% of the time, Pallas kernels for 22%

profile of v6, /device:TPU:1, one launch (start us, length us, event | category | flops | bytes accessed | tf_op | source)
XLA Modules:
  0.0 95.0 jit_solution(8310550456007618411)
XLA Ops:
  0.6 3.3 %collective-permute-start.1 = (bf16[32,32,96]{2,1,0:T(8,128)(2,1)}, bf16[32,32,96]{2,1,0:T(8,128)(2,1)S(1)}, u32[]{:S(2)}, u32[]{:S(2)}) collective-permute-start(bf16[32,32,96]{2,1,0:T(8,128)(2,1)} %bitcast.16), channel_id=1, source_target_pairs={{0,32},{32,0},{1,33},{33,1},{2,34},{34,2},{3,35},{35,3},{4,36},{36... | collective-permute-start | bytes 589832 | tf_op jit(solution)/shard_map/rows/ppermute | solution.py:48
  9.6 4.4 %collective-permute-start.5 = (bf16[288,768]{1,0:T(8,128)(2,1)S(1)}, bf16[288,768]{1,0:T(8,128)(2,1)S(1)}, u32[]{:S(2)}, u32[]{:S(2)}) collective-permute-start(bf16[288,768]{1,0:T(8,128)(2,1)S(1)} %get-tuple-element.54), channel_id=1, source_target_pairs={{0,8},{4,12},{8,16},{12,20},{16,24},{20,28},{24,0},{28,4},{32,56},... | collective-permute-start | bytes 1327112 | tf_op jit(solution)/shard_map/rows/ppermute | solution.py:58
  14.9 2.6 %collective-permute-start.11 = (bf16[272,768]{1,0:T(8,128)(2,1)S(1)}, bf16[272,768]{1,0:T(8,128)(2,1)S(1)}, u32[]{:S(2)}, u32[]{:S(2)}) collective-permute-start(bf16[272,768]{1,0:T(8,128)(2,1)S(1)} %constant_dynamic-slice_fusion), channel_id=1, source_target_pairs={{0,3},{1,0},{2,1},{3,2},{4,7},{5,4},{6,5},{7,6},{8,11},{9,8},{10,9... | collective-permute-start | bytes 1253384 | tf_op jit(solution)/shard_map/weights/ppermute | solution.py:48
  17.5 10.8 %collective-permute-done.3.b1.refs_1_ = bf16[192,768]{1,0:T(8,128)(2,1)S(1)} collective-permute-done((bf16[192,768]{1,0:T(8,128)(2,1)S(1)}, bf16[192,768]{1,0:T(8,128)(2,1)S(1)}, u32[]{:S(2)}, u32[]{:S(2)}) %collective-permute-start.3) | collective-permute-done | bytes 294944 | tf_op jit(solution)/shard_map/rows/ppermute | solution.py:58
  28.5 2.3 %collective-permute-start.8 = (bf16[192,768]{1,0:T(8,128)(2,1)S(1)}, bf16[192,768]{1,0:T(8,128)(2,1)S(1)}, u32[]{:S(2)}, u32[]{:S(2)}) collective-permute-start(bf16[192,768]{1,0:T(8,128)(2,1)S(1)} %slice.57), channel_id=1, source_target_pairs={{0,4},{4,8},{8,12},{12,16},{16,20},{20,24},{24,28},{28,0},{32,60},... | collective-permute-start | bytes 884744 | tf_op jit(solution)/shard_map/rows/ppermute | solution.py:58
  33.4 1.5 %collective-permute-start.13 = (bf16[128,768]{1,0:T(8,128)(2,1)S(1)}, bf16[128,768]{1,0:T(8,128)(2,1)S(1)}, u32[]{:S(2)}, u32[]{:S(2)}) collective-permute-start(bf16[128,768]{1,0:T(8,128)(2,1)S(1)} %slice.49), channel_id=1, source_target_pairs={{0,3},{1,0},{2,1},{3,2},{4,7},{5,4},{6,5},{7,6},{8,11},{9,8},{10,9... | collective-permute-start | bytes 589832 | tf_op jit(solution)/shard_map/weights/ppermute | solution.py:48
  34.9 2.0 %collective-permute-start.7 = (bf16[96,768]{1,0:T(8,128)(2,1)S(1)}, bf16[96,768]{1,0:T(8,128)(2,1)S(1)}, u32[]{:S(2)}, u32[]{:S(2)}) collective-permute-start(bf16[96,768]{1,0:T(8,128)(2,1)S(1)} %get-tuple-element.105), channel_id=1, source_target_pairs={{0,32},{32,0},{1,33},{33,1},{2,34},{34,2},{3,35},{35,3},{4,36},{36... | collective-permute-start | bytes 442376 | tf_op jit(solution)/shard_map/rows/ppermute | solution.py:48
  37.7 2.1 %shard_map.103.refs_12_.refs_2_.refs_3_ = f32[4,528,256]{2,1,0:T(8,128)S(1)} custom-call(s32[4]{0:T(128)S(1)} %pad_add_fusion.place, bf16[32,768]{1,0:T(8,128)(2,1)S(1)} %get-tuple-element.57.b0, bf16[192,768]{1,0:T(8,128)(2,1)S(1)} %collective-permute-done.3.b1.refs_1_, bf16[96,768]{1,0:T(8,128)(2,1)S(1)} %collective-permute-done.4.b2.refs_2_, ...), custom_call_target="tpu_custom_call" | custom-call | flops 2000000000 | bytes 1048576 | tf_op jit(solution)/shard_map/pallas_call | solution.py:35
  39.9 2.4 %collective-permute-start.14 = (bf16[144,768]{1,0:T(8,128)(2,1)S(1)}, bf16[144,768]{1,0:T(8,128)(2,1)S(1)}, u32[]{:S(2)}, u32[]{:S(2)}) collective-permute-start(bf16[144,768]{1,0:T(8,128)(2,1)S(1)} %collective-permute-done.12.refs_8_), channel_id=1, source_target_pairs={{0,32},{32,0},{1,33},{33,1},{2,34},{34,2},{3,35},{35,3},{4,36},{36... | collective-permute-start | bytes 663560 | tf_op jit(solution)/shard_map/weights/ppermute | solution.py:48
  42.8 2.1 %shard_map.104.refs_13_.refs_3_.refs_4_ = f32[4,528,256]{2,1,0:T(8,128)S(1)} custom-call(s32[4]{0:T(128)S(1)} %pad_add_fusion.place, bf16[288,768]{1,0:T(8,128)(2,1)S(1)} %collective-permute-done.5.b0.refs_4_, bf16[96,768]{1,0:T(8,128)(2,1)S(1)} %collective-permute-done.7.b1.refs_5_, bf16[192,768]{1,0:T(8,128)(2,1)S(1)} %collective-permute-done.8.b2.refs_6_, ...), custom_call_target="tpu_custom_call" | custom-call | flops 2000000000 | bytes 1048576 | tf_op jit(solution)/shard_map/pallas_call | solution.py:35
  44.9 2.1 %shard_map.105 = (f32[272,768]{1,0:T(8,128)S(1)}, bf16[272,768]{1,0:T(8,128)(2,1)S(1)}, bf16[528,512]{1,0:T(8,128)(2,1)S(1)}, bf16[512,768]{1,0:T(8,128)(2,1)S(1)}, bf16[528,768]{1,0:T(8,128)(2,1)S(1)}) custom-call(s32[4]{0:T(128)S(1)} %pad_add_fusion.place, bf16[64,768]{1,0:T(8,128)(2,1)S(1)} %copy-done.1, ...), custom_call_target="tpu_custom_call" | custom-call | flops 2000000000 | bytes 1048576 | tf_op jit(solution)/shard_map/pallas_call | solution.py:35
  47.6 2.1 %shard_map.107 = (f32[272,768]{1,0:T(8,128)S(1)}, bf16[272,768]{1,0:T(8,128)(2,1)S(1)}, bf16[528,512]{1,0:T(8,128)(2,1)S(1)}, bf16[528,768]{1,0:T(8,128)(2,1)S(1)}) custom-call(s32[4]{0:T(128)S(1)} %pad_add_fusion.place, bf16[512,768]{1,0:T(8,128)(2,1)S(1)} %get-tuple-element.66.refs_0_, bf16[272,768]{1,0:T(8,128)(2,1)S(1)} %collective-permute-done.10.refs_1_, ...), custom_call_target="tpu_custom_call" | custom-call | flops 2000000000 | bytes 1048576 | tf_op jit(solution)/shard_map/pallas_call | solution.py:35
  50.6 2.1 %shard_map.108 = (f32[272,768]{1,0:T(8,128)S(1)}, bf16[272,768]{1,0:T(8,128)(2,1)S(1)}, bf16[528,512]{1,0:T(8,128)(2,1)S(1)}, bf16[528,768]{1,0:T(8,128)(2,1)S(1)}) custom-call(s32[4]{0:T(128)S(1)} %pad_add_fusion.place, bf16[512,768]{1,0:T(8,128)(2,1)S(1)} %get-tuple-element.66.refs_0_, bf16[272,768]{1,0:T(8,128)(2,1)S(1)} %collective-permute-done.11.refs_1_, ...), custom_call_target="tpu_custom_call" | custom-call | flops 2000000000 | bytes 1048576 | tf_op jit(solution)/shard_map/pallas_call | solution.py:35
  54.1 1.8 %collective-permute-start.21 = (bf16[144,768]{1,0:T(8,128)(2,1)S(1)}, bf16[144,768]{1,0:T(8,128)(2,1)S(1)}, u32[]{:S(2)}, u32[]{:S(2)}) collective-permute-start(bf16[144,768]{1,0:T(8,128)(2,1)S(1)} %get-tuple-element.80), channel_id=1, source_target_pairs={{0,3},{1,0},{2,1},{3,2},{4,7},{5,4},{6,5},{7,6},{8,11},{9,8},{10,9... | collective-permute-start | bytes 663560 | tf_op jit(solution)/shard_map/ppermute | solution.py:48
  55.9 2.1 %shard_map.106 = (bf16[272,768]{1,0:T(8,128)(2,1)S(1)}, bf16[272,768]{1,0:T(8,128)(2,1)S(1)}, bf16[528,512]{1,0:T(8,128)(2,1)S(1)}) custom-call(s32[4]{0:T(128)S(1)} %pad_add_fusion.place, bf16[512,768]{1,0:T(8,128)(2,1)S(1)} %get-tuple-element.66.refs_0_, bf16[528,768]{1,0:T(8,128)(2,1)S(1)} %pad_maximum_fusion.refs_1_.refs_4_, ...), custom_call_target="tpu_custom_call" | custom-call | flops 2000000000 | bytes 1048576 | tf_op jit(solution)/shard_map/pallas_call | solution.py:35
  58.7 3.2 %shard_map.109 = (bf16[192,768]{1,0:T(8,128)(2,1)S(1)}, bf16[64,768]{1,0:T(8,128)(2,1)S(1)}, bf16[192,768]{1,0:T(8,128)(2,1)S(1)}, f32[64,768]{1,0:T(8,128)S(1)}) custom-call(s32[4]{0:T(128)S(1)} %pad_add_fusion.place, bf16[528,512]{1,0:T(8,128)(2,1)S(1)} %get-tuple-element.67.refs_0_, bf16[528,512]{1,0:T(8,128)(2,1)S(1)} %get-tuple-element.68.refs_1_, ...), custom_call_target="tpu_custom_call" | custom-call | flops 2000000000 | bytes 1048576 | tf_op jit(solution)/shard_map/pallas_call | solution.py:35
  64.0 1.9 %collective-permute-start.27 = (bf16[272,768]{1,0:T(8,128)(2,1)S(1)}, bf16[272,768]{1,0:T(8,128)(2,1)S(1)}, u32[]{:S(2)}, u32[]{:S(2)}) collective-permute-start(bf16[272,768]{1,0:T(8,128)(2,1)S(1)} %get-tuple-element.84), channel_id=1, source_target_pairs={{0,3},{1,0},{2,1},{3,2},{4,7},{5,4},{6,5},{7,6},{8,11},{9,8},{10,9... | collective-permute-start | bytes 1253384 | tf_op jit(solution)/shard_map/weights_x/ppermute | solution.py:48
  69.1 3.1 %collective-permute-start.30 = (bf16[192,768]{1,0:T(8,128)(2,1)S(1)}, bf16[192,768]{1,0:T(8,128)(2,1)S(1)}, u32[]{:S(2)}, u32[]{:S(2)}) collective-permute-start(bf16[192,768]{1,0:T(8,128)(2,1)S(1)} %get-tuple-element.95), channel_id=1, source_target_pairs={{0,20},{4,24},{8,28},{12,0},{16,4},{20,8},{24,12},{28,16},{32,44},... | collective-permute-start | bytes 884744 | tf_op jit(solution)/shard_map/rows_back/ppermute | solution.py:58
  72.2 2.9 %collective-permute-done.28.t3 = bf16[272,768]{1,0:T(8,128)(2,1)S(1)} collective-permute-done((bf16[272,768]{1,0:T(8,128)(2,1)S(1)}, bf16[272,768]{1,0:T(8,128)(2,1)S(1)}, u32[]{:S(2)}, u32[]{:S(2)}) %collective-permute-start.28) | collective-permute-done | bytes 417824 | tf_op jit(solution)/shard_map/weights_x/ppermute | solution.py:48
  76.0 3.0 %collective-permute-start.29 = (bf16[80,768]{1,0:T(8,128)(2,1)S(1)}, bf16[80,768]{1,0:T(8,128)(2,1)S(1)}, u32[]{:S(2)}, u32[]{:S(2)}) collective-permute-start(bf16[80,768]{1,0:T(8,128)(2,1)S(1)} %get-tuple-element.93), channel_id=1, source_target_pairs={{0,128},{64,192},{128,0},{192,64},{1,129},{65,193},{129,1},{193,65... | collective-permute-start | bytes 368648 | tf_op jit(solution)/shard_map/weights_y/ppermute | solution.py:48
  79.4 2.3 %collective-permute-start.34 = (bf16[80,768]{1,0:T(8,128)(2,1)S(1)}, bf16[80,768]{1,0:T(8,128)(2,1)S(1)}, u32[]{:S(2)}, u32[]{:S(2)}) collective-permute-start(bf16[80,768]{1,0:T(8,128)(2,1)S(1)} %get-tuple-element.100), channel_id=1, source_target_pairs={{0,192},{64,0},{128,64},{192,128},{1,193},{65,1},{129,65},{193,129... | collective-permute-start | bytes 368648 | tf_op jit(solution)/shard_map/weights_y/ppermute | solution.py:48
  81.7 5.6 %collective-permute-done.30 = bf16[192,768]{1,0:T(8,128)(2,1)S(1)} collective-permute-done((bf16[192,768]{1,0:T(8,128)(2,1)S(1)}, bf16[192,768]{1,0:T(8,128)(2,1)S(1)}, u32[]{:S(2)}, u32[]{:S(2)}) %collective-permute-start.30) | collective-permute-done | bytes 294944 | tf_op jit(solution)/shard_map/rows_back/ppermute | solution.py:58
  87.4 2.1 %collective-permute-start.32 = (f32[64,768]{1,0:T(8,128)S(1)}, f32[64,768]{1,0:T(8,128)S(1)}, u32[]{:S(2)}, u32[]{:S(2)}) collective-permute-start(f32[64,768]{1,0:T(8,128)S(1)} %slice.64), channel_id=1, source_target_pairs={{0,32},{32,0},{1,33},{33,1},{2,34},{34,2},{3,35},{35,3},{4,36},{36... | collective-permute-start | bytes 589832 | tf_op jit(solution)/shard_map/rows_back/ppermute | solution.py:48
  90.9 3.3 %collective-permute-done.31 = bf16[64,768]{1,0:T(8,128)(2,1)S(1)} collective-permute-done((bf16[64,768]{1,0:T(8,128)(2,1)S(1)}, bf16[64,768]{1,0:T(8,128)(2,1)S(1)}, u32[]{:S(2)}, u32[]{:S(2)}) %collective-permute-start.31) | collective-permute-done | bytes 98336 | tf_op jit(solution)/shard_map/rows_back/ppermute | solution.py:58
  (92 shorter events, 23.1 us)
Async XLA Ops:
  0.6 8.3 %collective-permute-start.1 = (bf16[32,32,96]{2,1,0:T(8,128)(2,1)}, bf16[32,32,96]{2,1,0:T(8,128)(2,1)S(1)}, u32[]{:S(2)}, u32[]{:S(2)}) collective-permute-start(bf16[32,32,96]{2,1,0:T(8,128)(2,1)} %bitcast.16), channel_id=1, source_target_pairs={{0,32},{32,0},{1,33},{33,1},{2,34},{34,2},{3,35},{35,3},{4,36},{36... | collective-permute-start | bytes 589832 | tf_op jit(solution)/shard_map/rows/ppermute | solution.py:48
  9.6 18.8 %collective-permute-start.5 = (bf16[288,768]{1,0:T(8,128)(2,1)S(1)}, bf16[288,768]{1,0:T(8,128)(2,1)S(1)}, u32[]{:S(2)}, u32[]{:S(2)}) collective-permute-start(bf16[288,768]{1,0:T(8,128)(2,1)S(1)} %get-tuple-element.54), channel_id=1, source_target_pairs={{0,8},{4,12},{8,16},{12,20},{16,24},{20,28},{24,0},{28,4},{32,56},... | collective-permute-start | bytes 1327112 | tf_op jit(solution)/shard_map/rows/ppermute | solution.py:58
  14.0 14.3 %collective-permute-start.3 = (bf16[192,768]{1,0:T(8,128)(2,1)S(1)}, bf16[192,768]{1,0:T(8,128)(2,1)S(1)}, u32[]{:S(2)}, u32[]{:S(2)}) collective-permute-start(bf16[192,768]{1,0:T(8,128)(2,1)S(1)} %get-tuple-element.53), channel_id=1, source_target_pairs={{0,4},{4,8},{8,12},{12,16},{16,20},{20,24},{24,28},{28,0},{32,60},... | collective-permute-start | bytes 884744 | tf_op jit(solution)/shard_map/rows/ppermute | solution.py:58
  14.9 17.1 %collective-permute-start.11 = (bf16[272,768]{1,0:T(8,128)(2,1)S(1)}, bf16[272,768]{1,0:T(8,128)(2,1)S(1)}, u32[]{:S(2)}, u32[]{:S(2)}) collective-permute-start(bf16[272,768]{1,0:T(8,128)(2,1)S(1)} %constant_dynamic-slice_fusion), channel_id=1, source_target_pairs={{0,3},{1,0},{2,1},{3,2},{4,7},{5,4},{6,5},{7,6},{8,11},{9,8},{10,9... | collective-permute-start | bytes 1253384 | tf_op jit(solution)/shard_map/weights/ppermute | solution.py:48
  17.5 14.5 %collective-permute-start.10 = (bf16[272,768]{1,0:T(8,128)(2,1)S(1)}, bf16[272,768]{1,0:T(8,128)(2,1)S(1)}, u32[]{:S(2)}, u32[]{:S(2)}) collective-permute-start(bf16[272,768]{1,0:T(8,128)(2,1)S(1)} %constant_dynamic-slice_fusion), channel_id=1, source_target_pairs={{0,1},{1,2},{2,3},{3,0},{4,5},{5,6},{6,7},{7,4},{8,9},{9,10},{10,1... | collective-permute-start | bytes 1253384 | tf_op jit(solution)/shard_map/weights/ppermute | solution.py:48
  28.3 8.7 %collective-permute-start.4 = (bf16[96,768]{1,0:T(8,128)(2,1)S(1)}, bf16[96,768]{1,0:T(8,128)(2,1)S(1)}, u32[]{:S(2)}, u32[]{:S(2)}) collective-permute-start(bf16[96,768]{1,0:T(8,128)(2,1)S(1)} %slice.54), channel_id=1, source_target_pairs={{0,32},{32,0},{1,33},{33,1},{2,34},{34,2},{3,35},{35,3},{4,36},{36... | collective-permute-start | bytes 442376 | tf_op jit(solution)/shard_map/rows/ppermute | solution.py:48
  28.5 6.4 %collective-permute-start.8 = (bf16[192,768]{1,0:T(8,128)(2,1)S(1)}, bf16[192,768]{1,0:T(8,128)(2,1)S(1)}, u32[]{:S(2)}, u32[]{:S(2)}) collective-permute-start(bf16[192,768]{1,0:T(8,128)(2,1)S(1)} %slice.57), channel_id=1, source_target_pairs={{0,4},{4,8},{8,12},{12,16},{16,20},{20,24},{24,28},{28,0},{32,60},... | collective-permute-start | bytes 884744 | tf_op jit(solution)/shard_map/rows/ppermute | solution.py:58
  30.8 6.9 %collective-permute-start.6 = (bf16[96,768]{1,0:T(8,128)(2,1)S(1)}, bf16[96,768]{1,0:T(8,128)(2,1)S(1)}, u32[]{:S(2)}, u32[]{:S(2)}) collective-permute-start(bf16[96,768]{1,0:T(8,128)(2,1)S(1)} %get-tuple-element.106), channel_id=1, source_target_pairs={{0,8},{4,12},{8,16},{12,20},{16,24},{20,28},{24,0},{28,4},{32,56},... | collective-permute-start | bytes 442376 | tf_op jit(solution)/shard_map/rows/ppermute | solution.py:58
  32.1 7.8 %collective-permute-start.12 = (bf16[144,768]{1,0:T(8,128)(2,1)S(1)}, bf16[144,768]{1,0:T(8,128)(2,1)S(1)}, u32[]{:S(2)}, u32[]{:S(2)}) collective-permute-start(bf16[144,768]{1,0:T(8,128)(2,1)S(1)} %slice.48), channel_id=1, source_target_pairs={{0,1},{1,2},{2,3},{3,0},{4,5},{5,6},{6,7},{7,4},{8,9},{9,10},{10,1... | collective-permute-start | bytes 663560 | tf_op jit(solution)/shard_map/weights/ppermute | solution.py:48
  33.4 6.4 %collective-permute-start.13 = (bf16[128,768]{1,0:T(8,128)(2,1)S(1)}, bf16[128,768]{1,0:T(8,128)(2,1)S(1)}, u32[]{:S(2)}, u32[]{:S(2)}) collective-permute-start(bf16[128,768]{1,0:T(8,128)(2,1)S(1)} %slice.49), channel_id=1, source_target_pairs={{0,3},{1,0},{2,1},{3,2},{4,7},{5,4},{6,5},{7,6},{8,11},{9,8},{10,9... | collective-permute-start | bytes 589832 | tf_op jit(solution)/shard_map/weights/ppermute | solution.py:48
  34.9 7.9 %collective-permute-start.7 = (bf16[96,768]{1,0:T(8,128)(2,1)S(1)}, bf16[96,768]{1,0:T(8,128)(2,1)S(1)}, u32[]{:S(2)}, u32[]{:S(2)}) collective-permute-start(bf16[96,768]{1,0:T(8,128)(2,1)S(1)} %get-tuple-element.105), channel_id=1, source_target_pairs={{0,32},{32,0},{1,33},{33,1},{2,34},{34,2},{3,35},{35,3},{4,36},{36... | collective-permute-start | bytes 442376 | tf_op jit(solution)/shard_map/rows/ppermute | solution.py:48
  49.7 12.5 %collective-permute-start.19 = (bf16[272,768]{1,0:T(8,128)(2,1)S(1)}, bf16[272,768]{1,0:T(8,128)(2,1)S(1)}, u32[]{:S(2)}, u32[]{:S(2)}) collective-permute-start(bf16[272,768]{1,0:T(8,128)(2,1)S(1)} %get-tuple-element.77), channel_id=1, source_target_pairs={{0,32},{32,0},{1,33},{33,1},{2,34},{34,2},{3,35},{35,3},{4,36},{36... | collective-permute-start | bytes 1253384 | tf_op jit(solution)/shard_map/ppermute | solution.py:48
  52.7 9.6 %collective-permute-start.20 = (bf16[272,768]{1,0:T(8,128)(2,1)S(1)}, bf16[272,768]{1,0:T(8,128)(2,1)S(1)}, u32[]{:S(2)}, u32[]{:S(2)}) collective-permute-start(bf16[272,768]{1,0:T(8,128)(2,1)S(1)} %get-tuple-element.79), channel_id=1, source_target_pairs={{0,32},{32,0},{1,33},{33,1},{2,34},{34,2},{3,35},{35,3},{4,36},{36... | collective-permute-start | bytes 1253384 | tf_op jit(solution)/shard_map/ppermute | solution.py:48
  53.2 9.1 %collective-permute-start.22 = (bf16[128,768]{1,0:T(8,128)(2,1)S(1)}, bf16[128,768]{1,0:T(8,128)(2,1)S(1)}, u32[]{:S(2)}, u32[]{:S(2)}) collective-permute-start(bf16[128,768]{1,0:T(8,128)(2,1)S(1)} %get-tuple-element.83), channel_id=1, source_target_pairs={{0,1},{1,2},{2,3},{3,0},{4,5},{5,6},{6,7},{7,4},{8,9},{9,10},{10,1... | collective-permute-start | bytes 589832 | tf_op jit(solution)/shard_map/ppermute | solution.py:48
  54.1 7.8 %collective-permute-start.21 = (bf16[144,768]{1,0:T(8,128)(2,1)S(1)}, bf16[144,768]{1,0:T(8,128)(2,1)S(1)}, u32[]{:S(2)}, u32[]{:S(2)}) collective-permute-start(bf16[144,768]{1,0:T(8,128)(2,1)S(1)} %get-tuple-element.80), channel_id=1, source_target_pairs={{0,3},{1,0},{2,1},{3,2},{4,7},{5,4},{6,5},{7,6},{8,11},{9,8},{10,9... | collective-permute-start | bytes 663560 | tf_op jit(solution)/shard_map/ppermute | solution.py:48
  58.0 11.1 %collective-permute-start.26 = (bf16[272,768]{1,0:T(8,128)(2,1)S(1)}, bf16[272,768]{1,0:T(8,128)(2,1)S(1)}, u32[]{:S(2)}, u32[]{:S(2)}) collective-permute-start(bf16[272,768]{1,0:T(8,128)(2,1)S(1)} %get-tuple-element.91), channel_id=1, source_target_pairs={{0,32},{32,0},{1,33},{33,1},{2,34},{34,2},{3,35},{35,3},{4,36},{36... | collective-permute-start | bytes 1253384 | tf_op jit(solution)/shard_map/ppermute | solution.py:48
  63.0 12.1 %collective-permute-start.28 = (bf16[272,768]{1,0:T(8,128)(2,1)S(1)}, bf16[272,768]{1,0:T(8,128)(2,1)S(1)}, u32[]{:S(2)}, u32[]{:S(2)}) collective-permute-start(bf16[272,768]{1,0:T(8,128)(2,1)S(1)} %get-tuple-element.92), channel_id=1, source_target_pairs={{0,1},{1,2},{2,3},{3,0},{4,5},{5,6},{6,7},{7,4},{8,9},{9,10},{10,1... | collective-permute-start | bytes 1253384 | tf_op jit(solution)/shard_map/weights_x/ppermute | solution.py:48
  64.0 11.1 %collective-permute-start.27 = (bf16[272,768]{1,0:T(8,128)(2,1)S(1)}, bf16[272,768]{1,0:T(8,128)(2,1)S(1)}, u32[]{:S(2)}, u32[]{:S(2)}) collective-permute-start(bf16[272,768]{1,0:T(8,128)(2,1)S(1)} %get-tuple-element.84), channel_id=1, source_target_pairs={{0,3},{1,0},{2,1},{3,2},{4,7},{5,4},{6,5},{7,6},{8,11},{9,8},{10,9... | collective-permute-start | bytes 1253384 | tf_op jit(solution)/shard_map/weights_x/ppermute | solution.py:48
  66.5 15.3 %collective-permute-start.24 = (bf16[128,768]{1,0:T(8,128)(2,1)S(1)}, bf16[128,768]{1,0:T(8,128)(2,1)S(1)}, u32[]{:S(2)}, u32[]{:S(2)}) collective-permute-start(bf16[128,768]{1,0:T(8,128)(2,1)S(1)} %get-tuple-element.88), channel_id=1, source_target_pairs={{0,28},{4,0},{8,4},{12,8},{16,12},{20,16},{24,20},{28,24},{32,36},... | collective-permute-start | bytes 589832 | tf_op jit(solution)/shard_map/rows_back/ppermute | solution.py:58
  67.8 11.6 %collective-permute-start.25 = (bf16[128,768]{1,0:T(8,128)(2,1)S(1)}, bf16[128,768]{1,0:T(8,128)(2,1)S(1)}, u32[]{:S(2)}, u32[]{:S(2)}) collective-permute-start(bf16[128,768]{1,0:T(8,128)(2,1)S(1)} %get-tuple-element.89), channel_id=1, source_target_pairs={{0,24},{4,28},{8,0},{12,4},{16,8},{20,12},{24,16},{28,20},{32,40},... | collective-permute-start | bytes 589832 | tf_op jit(solution)/shard_map/rows_back/ppermute | solution.py:58
  69.1 18.2 %collective-permute-start.30 = (bf16[192,768]{1,0:T(8,128)(2,1)S(1)}, bf16[192,768]{1,0:T(8,128)(2,1)S(1)}, u32[]{:S(2)}, u32[]{:S(2)}) collective-permute-start(bf16[192,768]{1,0:T(8,128)(2,1)S(1)} %get-tuple-element.95), channel_id=1, source_target_pairs={{0,20},{4,24},{8,28},{12,0},{16,4},{20,8},{24,12},{28,16},{32,44},... | collective-permute-start | bytes 884744 | tf_op jit(solution)/shard_map/rows_back/ppermute | solution.py:58
  79.0 10.6 %collective-permute-start.33 = (bf16[80,768]{1,0:T(8,128)(2,1)S(1)}, bf16[80,768]{1,0:T(8,128)(2,1)S(1)}, u32[]{:S(2)}, u32[]{:S(2)}) collective-permute-start(bf16[80,768]{1,0:T(8,128)(2,1)S(1)} %get-tuple-element.98), channel_id=1, source_target_pairs={{0,64},{64,128},{128,192},{192,0},{1,65},{65,129},{129,193},{193,1... | collective-permute-start | bytes 368648 | tf_op jit(solution)/shard_map/weights_y/ppermute | solution.py:48
  79.4 10.2 %collective-permute-start.34 = (bf16[80,768]{1,0:T(8,128)(2,1)S(1)}, bf16[80,768]{1,0:T(8,128)(2,1)S(1)}, u32[]{:S(2)}, u32[]{:S(2)}) collective-permute-start(bf16[80,768]{1,0:T(8,128)(2,1)S(1)} %get-tuple-element.100), channel_id=1, source_target_pairs={{0,192},{64,0},{128,64},{192,128},{1,193},{65,1},{129,65},{193,129... | collective-permute-start | bytes 368648 | tf_op jit(solution)/shard_map/weights_y/ppermute | solution.py:48
  87.4 6.9 %collective-permute-start.32 = (f32[64,768]{1,0:T(8,128)S(1)}, f32[64,768]{1,0:T(8,128)S(1)}, u32[]{:S(2)}, u32[]{:S(2)}) collective-permute-start(f32[64,768]{1,0:T(8,128)S(1)} %slice.64), channel_id=1, source_target_pairs={{0,32},{32,0},{1,33},{33,1},{2,34},{34,2},{3,35},{35,3},{4,36},{36... | collective-permute-start | bytes 589832 | tf_op jit(solution)/shard_map/rows_back/ppermute | solution.py:48
  (19 other events, 54.7 us)

commit v7 on v5

--- a/solution.py
+++ b/solution.py
@@ -17,9 +17,21 @@
 TOP = 256
 PART = 272
 CUT = 144
-ORDER = (0, 1, 7, 2, 6, 3, 4, 5)
-ROW_AT = (0, 0, 0, 32, 0, 0, 32, 32)
-SLOT_AT = (0, 64, 64, 256, 64, 64, 0, 0)
+ORDER = (0, 1, 7, 2, 6, 3, 5, 4)
+ROW_AT = (
+    ((0, 0, 64),),
+    ((1, 0, 64),),
+    ((2, 0, 64),),
+    ((3, 16, 64),),
+    ((4, 48, 32), (4, 16, 32)),
+    ((5, 0, 64),),
+    ((6, 32, 32), (6, 0, 32)),
+    ((7, 16, 32), (8, 16, 32)),
+)
+SLOT_AT = (
+    (((0, 0, 32),), ((1, 64, 32),), ((2, 64, 32),), ((3, 112, 32),)),
+    (((0, 112, 32),), ((1, 64, 32),), ((2, 64, 32),), ((3, 0, 16), (4, 0, 16))),
+)
 NT = (((1,), (1,)), ((), ()))
 NN = (((1,), (0,)), ((), ()))
 TN = (((0,), (0,)), ((), ()))
@@ -31,13 +43,15 @@
     return lax.dot_general(a, b, dims, preferred_element_type=F32)
 
 
-def call(kernel, out, args, scratch=(), **static):
+def call(kernel, out, args, scratch=(), own=0, **static):
+    specs = [SMEM] + [VMEM] * (len(args) - 1 - own)
+    specs += [pl.BlockSpec(memory_space=pltpu.HBM)] * own
     return pl.pallas_call(
         functools.partial(kernel, **static),
         out_shape=tuple(jax.ShapeDtypeStruct(s, t) for s, t in out),
-        in_specs=[SMEM] + [VMEM] * (len(args) - 1),
+        in_specs=specs,
         out_specs=(VMEM,) * len(out),
-        scratch_shapes=[pltpu.VMEM(s, t) for s, t in scratch],
+        scratch_shapes=[s if t is None else pltpu.VMEM(s, t) for s, t in scratch],
         compiler_params=pltpu.CompilerParams(vmem_limit_bytes=16 * 1024 * 1024),
         cost_estimate=pl.CostEstimate(flops=2 * 10**9, bytes_accessed=1 << 20, transcendentals=0),
     )(*args)
@@ -58,26 +72,62 @@
     return lax.ppermute(x, ("core", axis), pairs)
 
 
-def load_kernel(place, e, eo, want, want_o, side, side_o, m1, m2, s0):
-    z, sign = place[2], 1 - 2 * place[1]
-
-    def put(ref, lo, d, wants, sides):
-        to = lax.rem(z + sign * d + NZ, NZ)
+def prepare_kernel(place, lw, cw, w, part, raw, top, kids, sems):
+    copies = [
+        pltpu.make_async_copy(lw, raw, sems.at[0]),
+        pltpu.make_async_copy(cw, top, sems.at[1]),
+    ]
+    for c in copies:
+        c.start()
+    for c in copies:
+        c.wait()
+    for c in range(CL):
+        for j in range(D // 128):
+            kids[j, pl.ds(c, KIDS, stride=CL)] = raw[c, :, j * 128 : j * 128 + 128].astype(F32)
+    for y in range(NY):
+        for core in range(NC):
+            to, at = core * PART + y * 64, (y * NC + core) * 64
+            for j in range(D // 128):
+                w[to : to + 64, j * 128 : j * 128 + 128] = kids[j, at : at + 64].astype(BF16)
+    w[TOP : TOP + CL] = top[...]
+    part[...] = w[pl.ds(pl.multiple_of(place[1] * TOP, 16), PART)]
+
+
+def load_kernel(place, counts, inst, clus, prefix, e, want, *refs):
+    (up1, dn1, up2, dn2, s0), (n, i, c, a, ev, wv, rows, side, sems) = refs[:5], refs[5:]
+    pairs = ((counts, n), (inst, i), (clus, c), (prefix, a), (e, ev), (want, wv))
+    copies = [pltpu.make_async_copy(x, v, sems.at[k]) for k, (x, v) in enumerate(pairs)]
+    for copy in copies:
+        copy.start()
+    for copy in copies:
+        copy.wait()
+    cap = inst.shape[1]
+    rows[...] = jnp.zeros(rows.shape, F32)
+    lane = lax.broadcasted_iota(jnp.int32, (1, cap), 1)
+    for o in range(NZ * NX):
+        alpha = jnp.where(lane < n[o], a[o : o + 1].astype(F32), 0.0)
+        rows[o * 8 : o * 8 + 1, :cap] = alpha
+        rows[o * 8 + 1 : o * 8 + 2, :cap] = i[o : o + 1].astype(F32)
+        rows[o * 8 + 2 : o * 8 + 3, :cap] = c[o : o + 1].astype(F32)
+    for z in range(NZ):
+        side[z] = rows[z * 32 : z * 32 + 32].astype(BF16)
+
+    def put(ref, lo, d, first=0, count=32):
+        to = lax.rem(place[2] + d + NZ, NZ)
+        ref[lo : lo + count] = jnp.zeros((count, D), BF16)
         for x in range(NX):
-            ref[lo : lo + 32, x * 128 : x * 128 + 128] = wants[to, x]
-        ref[lo : lo + 32, 512:640] = sides[to]
-        ref[lo : lo + 32, 640:768] = jnp.zeros((32, 128), BF16)
-
-    put(s0, 0, 0, want, side)
-    m1[0:64], m1[96:160] = e[...], eo[...]
-    put(m1, 64, 1, want, side)
-    put(m1, 160, 1, want_o, side_o)
-    m2[32:96], m2[160:224] = e[...], eo[...]
-    put(m2, 0, 4, want, side)
-    put(m2, 96, 3, want, side)
-    put(m2, 128, 3, want_o, side_o)
-    put(m2, 224, 2, want_o, side_o)
-    put(m2, 256, 2, want, side)
+            ref[lo : lo + count, x * 128 : x * 128 + cap] = wv[to * NX + x, first : first + count]
+        ref[lo : lo + count, 512:640] = side[to, first : first + count]
+
+    put(s0, 0, 0)
+    for ref1, ref2, by, half in ((up1, up2, 1, 0), (dn1, dn2, -1, 1)):
+        ref1[0:64] = ev[...]
+        put(ref1, 64, by)
+        put(ref2, 0, 4, 16 * half, 16)
+        ref2[16:48] = ev[half * 32 : half * 32 + 32]
+        ref2[48:80] = ev[32 - half * 32 : 64 - half * 32]
+        put(ref2, 80, 3 * by)
+        put(ref2, 112, 2 * by)
 
 
 def kid_row(k):
@@ -85,19 +135,23 @@
     return core * (TOP + CL) + (y * 4 + k % 4) * CL
 
 
-def slot_kernel(place, b0, b1, b2, b3, ay, wide, sides, *, offsets):
+def slot_kernel(place, *refs, spots):
+    blocks, (ay, wide, wants, sides) = refs[:-4], refs[-4:]
     x = place[0]
     lane_row = lax.broadcasted_iota(jnp.int32, (256, 128), 0)
     cluster_row = lax.broadcasted_iota(jnp.int32, (CL, 128), 0)
-    blocks = (b0, b1, b2, b3)
-    for q, (b, lo) in enumerate(zip(blocks, offsets)):
-        sides[q] = b[lo : lo + 32, 512:640].astype(F32)
+    for q in range(4):
+        to = 0
+        for ref, lo, n in spots[q]:
+            sides[q, to : to + n] = blocks[ref][lo : lo + n, 512:640].astype(F32)
+            wants[q, to : to + n] = blocks[ref][lo : lo + n, :512].astype(F32)
+            to += n
 
     def step(r, _):
         owner = lax.rem(x - r + NX, NX)
         left = []
-        for q, (b, lo) in enumerate(zip(blocks, offsets)):
-            want = b[lo : lo + 32, pl.ds(pl.multiple_of(owner * 128, 128), 128)].astype(F32)
+        for q in range(4):
+            want = wants[q, :, pl.ds(pl.multiple_of(owner * 128, 128), 128)]
             side = sides[q, pl.ds(pl.multiple_of(owner * 8, 8), 8)]
             alpha, inst, clus = side[0:1], side[1:2].astype(jnp.int32), side[2:3].astype(jnp.int32)
             left.append(jnp.where(lane_row == inst + q * INST, alpha, 0.0).astype(BF16))
@@ -117,10 +171,12 @@
     mine = pl.ds(pl.multiple_of(core * TOP, 16), PART)
     other = pl.ds(pl.multiple_of((1 - core) * TOP, 16), PART)
     if r == 2:
-        blocks, (n1, n2, f1, f2, ay1, ay2, a, b, dzs, e, w, z) = refs[:NZ], refs[NZ:]
+        blocks, (n1, n2, f1, f2, ay1, ay2, a, b, dzs, e, w, z) = refs[:9], refs[9:]
         for d in range(NZ):
-            lo = ROW_AT[d]
-            e[d * INST : d * INST + INST] = blocks[d][lo : lo + INST]
+            to = d * INST
+            for ref, lo, n in ROW_AT[d]:
+                e[to : to + n] = blocks[ref][lo : lo + n]
+                to += n
         for at, p1, p2 in ((core, n1, n2), (1 - core, f1, f2)):
             w[pl.ds(pl.multiple_of(at * TOP, 16), CUT)] = p1[...]
             w[pl.ds(pl.multiple_of(at * TOP + CUT, 16), PART - CUT)] = p2[...]
@@ -151,11 +207,11 @@
 
 def rows_kernel(place, *refs):
     dzs, ws, (near, last, far, own, ge) = refs[:NX], refs[NX : 2 * NX], refs[2 * NX :]
-    ge[...] = dot(dzs[0][...], ws[0][...], TN)
-    for r in range(1, NX):
-        ge[...] += dot(dzs[r][...], ws[r][...], TN)
+    ge[...] = sum(dot(dzs[r][...], ws[r][...], TN) for r in range(NX))
+
     def block(d):
-        return ge[ORDER.index(d) * INST : ORDER.index(d) * INST + INST]
+        at = jnp.where(place[1] == 0, ORDER.index(d), ORDER.index(-d % NZ))
+        return ge[pl.ds(pl.multiple_of(at * INST, INST), INST)]
 
     own[...] = block(0)
     last[...] = block(4).astype(BF16)
@@ -221,46 +277,63 @@
     place = jnp.stack([ix, ic, iz, iy]).astype(jnp.int32)
 
     with jax.named_scope("weights"):
-        leaf = lw.reshape(CL, NY, NC, 4, D).transpose(2, 1, 3, 0, 4).reshape(2, TOP, D)
-        w = jnp.concatenate([leaf[0], cw, leaf[1]], axis=0)
-        part = lax.dynamic_slice_in_dim(w, ic * TOP, PART, 0)
+        w, part = call(
+            prepare_kernel,
+            [((WIDE, D), BF16), ((PART, D), BF16)],
+            (place, lw, cw),
+            [
+                ((CL, KIDS, D), BF16),
+                ((CL, D), BF16),
+                ((D // 128, KIDS * CL, 128), F32),
+                (pltpu.SemaphoreType.DMA((2,)), None),
+            ],
+            own=2,
+        )
         low, high = shift(part, "x", 1), shift(part, "x", -1)
-        low2, high2 = shift(low[:CUT], "x", 1), shift(high[CUT:], "x", -1)
-
-    with jax.named_scope("slots"):
+
+    with jax.named_scope("rows"):
         cap = prefix.shape[-1]
         owners = NZ * NX
-        inst, clus = inst.reshape(owners, 1, cap), clus.reshape(owners, 1, cap)
-        valid = jnp.arange(cap, dtype=jnp.int32)[None, None, :] < counts.reshape(owners, 1, 1)
-        nothing = jnp.zeros((), BF16)
-        alpha = jnp.where(valid, prefix.reshape(owners, 1, cap), nothing)
-        want = jnp.where(valid, jnp.swapaxes(targets.reshape(owners, cap, KIDS), 1, 2), nothing)
-        want = jnp.pad(want, ((0, 0), (0, 0), (0, 128 - cap))).reshape(NZ, NX, KIDS, 128)
-        side = jnp.concatenate([alpha, inst.astype(BF16), clus.astype(BF16)], axis=1)
-        side = jnp.pad(side, ((0, 0), (0, 5), (0, 128 - cap))).reshape(NZ, NX * 8, 128)
-
-    with jax.named_scope("rows"):
-        m1, m2, s0 = call(
+        want = jnp.swapaxes(targets.reshape(owners, cap, KIDS), 1, 2)
+        flat = tuple(v.reshape(owners, cap) for v in (inst, clus, prefix))
+        up1, dn1, up2, dn2, s0 = call(
             load_kernel,
-            [((192, D), BF16), ((288, D), BF16), ((32, D), BF16)],
-            (place, e, swap(e), want, swap(want), side, swap(side)),
+            [((n, D), BF16) for n in (96, 96, 144, 144, 32)],
+            (place, counts.reshape(owners)) + flat + (e, want),
+            [
+                (pltpu.SMEM((owners,), jnp.int32), None),
+                ((owners, cap), jnp.int32),
+                ((owners, cap), jnp.int32),
+                ((owners, cap), BF16),
+                ((INST, D), BF16),
+                ((owners, KIDS, cap), BF16),
+                ((owners * 8, 128), F32),
+                ((NZ, 32, 128), BF16),
+                (pltpu.SemaphoreType.DMA((6,)), None),
+            ],
+            own=6,
         )
-        m2, m1 = turn(m2, "z", 2), turn(m1, "z", 1)
-        m3, m4 = turn(m2[32:224], "z", 1), turn(m2[:96], "z", 2)
-        q2, q1, q3 = swap(m2[160:256]), swap(m1[96:]), swap(m3[96:])
-        low2, high2, m4 = lax.optimization_barrier((low2, high2, m4))
-    with jax.named_scope("weights"):
-        low_o, high_o, low2_o, high2_o = (swap(p) for p in (low, high, low2, high2))
-    halves = []
-    for blocks, at in (((s0, m1, q1, m2), SLOT_AT[:4]), ((q2, m3, m4, q3), SLOT_AT[4:])):
-        halves += call(
+        up2, dn2 = shift(up2, "z", 2), shift(dn2, "z", -2)
+        up1, dn1 = shift(up1, "z", 1), shift(dn1, "z", -1)
+        up3, dn3 = shift(up2[16:112], "z", 1), shift(dn2[16:112], "z", -1)
+        up4, dn4 = shift(up2[:48], "z", 2), shift(dn2[:48], "z", -2)
+
+    def sum_slots(blocks, spots):
+        return call(
             slot_kernel,
             [((NX, WIDE, 256), F32)],
             (place,) + blocks,
-            [((WIDE, 512), BF16), ((4, 32, 128), F32)],
-            offsets=at,
-        )
-    blocks, ay = (e, m1, q1, m2, q2, m3, m4, q3), tuple(halves)
+            [((WIDE, 512), BF16), ((4, 32, 512), F32), ((4, 32, 128), F32)],
+            spots=spots,
+        )[0]
+
+    ay1 = sum_slots((s0, up1, dn1, up2), SLOT_AT[0])
+    with jax.named_scope("weights"):
+        low2, high2 = shift(low[:CUT], "x", 1), shift(high[CUT:], "x", -1)
+        low2, high2, up4, dn4, ay1 = lax.optimization_barrier((low2, high2, up4, dn4, ay1))
+        low_o, high_o, low2_o, high2_o = (swap(p) for p in (low, high, low2, high2))
+    ay2 = sum_slots((dn2, up3, dn3, up4, dn4), SLOT_AT[1])
+    blocks, ay = (e, up1, dn1, up2, dn2, up3, dn3, up4, dn4), (ay1, ay2)
 
     wide, dzs = ((WIDE, D), BF16), ((WIDE, ROWS), BF16)
     half, half32 = ((PART, D), BF16), ((PART, D), F32)

time: 90.2 us -> 89.9 us (level)
  other arithmetic: 4.2 us -> 0.84 us
  Pallas kernels: 21.2 us -> 23.7 us
  starting transfers between devices: 39 us -> 40.9 us
  waiting for transfers between devices: 22.8 us -> 21.3 us
    ppermute x27 -> x29, starting transfers between devices: 21.8 us -> 32.6 us  [shift(): return lax.ppermute(x, axis, [(i, (i + by) % n) for i in range(n)])]
    ppermute x8 -> x4, starting transfers between devices: 17.2 us -> 8.3 us  [turn(): return lax.ppermute(x, ('core', axis), pairs)]
    pallas_call x14 -> x15, Pallas kernels: 21.2 us -> 23.7 us  [call(): pl.pallas_call(functools.partial(kernel, **static), out_shape=tuple((jax....]
    select_n x2 -> x0, other arithmetic: 1.83 us -> none  [the longest x1 0.98 us: shards(): jnp.where(valid, jnp.swapaxes(targets.reshape(owners, cap, KIDS), 1, 2),...]
    ppermute x8 -> x4, waiting for transfers between devices: 8.7 us -> 6.97 us  [turn(): return lax.ppermute(x, ('core', axis), pairs)]
    unnamed x7 -> x16, local copies, waits for them, and re-layouts: 0.32 us -> 1.9 us
    ppermute x27 -> x29, waiting for transfers between devices: 14.1 us -> 14.3 us  [shift(): return lax.ppermute(x, axis, [(i, (i + by) % n) for i in range(n)])]
  transfers between devices with their start and end apart: 35 -> 33, of which waited for: 9 -> 7; matrix products, arithmetic and copies ran while one was open for 3% -> 0% of each run, Pallas kernels for 23% -> 25%
where the time goes in v7:
time: 89.9 us; the launch traced here: 89.6 us
  starting transfers between devices  40.9 us (45%)
  Pallas kernels  23.7 us (26%)
  waiting for transfers between devices  21.3 us (24%)
  local copies, waits for them, and re-layouts  1.98 us (2%)
  between operations  0.95 us (1%)
    ppermute x29, starting transfers between devices, shift(): return lax.ppermute(x, axis, [(i, (i + by) % n) for i in range(n)])  32.6 us
    pallas_call x15, Pallas kernels, call(): pl.pallas_call(functools.partial(kernel, **static), out_shape=tuple((jax....  23.7 us
    ppermute x29, waiting for transfers between devices, shift(): return lax.ppermute(x, axis, [(i, (i + by) % n) for i in range(n)])  14.3 us
    ppermute x4, starting transfers between devices, turn(): return lax.ppermute(x, ('core', axis), pairs)  8.3 us
    ppermute x4, waiting for transfers between devices, turn(): return lax.ppermute(x, ('core', axis), pairs)  6.97 us
    unnamed x16, local copies, waits for them, and re-layouts  1.9 us
  transfers between devices with their start and end apart: 33, of which 7 were waited for; matrix products, arithmetic and copies ran while one was open for 0% of the time, Pallas kernels for 25%

profile of v7, /device:TPU:24, one launch (start us, length us, event | category | flops | bytes accessed | tf_op | source)
XLA Modules:
  0.0 89.6 jit_solution(5710866110484619131)
XLA Ops:
  2.6 1.6 %weights.1 = (bf16[528,768]{1,0:T(8,128)(2,1)S(1)}, bf16[272,768]{1,0:T(8,128)(2,1)S(1)}) custom-call(s32[4]{0:T(128)S(1)} %pad_add_fusion.place, bf16[16,32,768]{2,1,0:T(8,128)(2,1)S(1)} %copy-done, bf16[16,768]{1,0:T(8,128)(2,1)S(1)} %copy-done.3), custom_call_target="tpu_custom_call" | custom-call | flops 2000000000 | bytes 1048576 | tf_op jit(solution)/shard_map/weights/pallas_call | solution.py:49
  4.2 2.8 %collective-permute-start.8 = (bf16[272,768]{1,0:T(8,128)(2,1)S(1)}, bf16[272,768]{1,0:T(8,128)(2,1)S(1)}, u32[]{:S(2)}, u32[]{:S(2)}) collective-permute-start(bf16[272,768]{1,0:T(8,128)(2,1)S(1)} %get-tuple-element.59), channel_id=1, source_target_pairs={{0,3},{1,0},{2,1},{3,2},{4,7},{5,4},{6,5},{7,6},{8,11},{9,8},{10,9... | collective-permute-start | bytes 1253384 | tf_op jit(solution)/shard_map/weights/ppermute | solution.py:62
  8.4 3.3 %collective-permute-start.2 = (bf16[144,768]{1,0:T(8,128)(2,1)S(1)}, bf16[144,768]{1,0:T(8,128)(2,1)S(1)}, u32[]{:S(2)}, u32[]{:S(2)}) collective-permute-start(bf16[144,768]{1,0:T(8,128)(2,1)S(1)} %get-tuple-element.57), channel_id=1, source_target_pairs={{0,8},{4,12},{8,16},{12,20},{16,24},{20,28},{24,0},{28,4},{1,9},{5... | collective-permute-start | bytes 663560 | tf_op jit(solution)/shard_map/rows/ppermute | solution.py:62
  11.8 3.1 %collective-permute-start.3 = (bf16[144,768]{1,0:T(8,128)(2,1)S(1)}, bf16[144,768]{1,0:T(8,128)(2,1)S(1)}, u32[]{:S(2)}, u32[]{:S(2)}) collective-permute-start(bf16[144,768]{1,0:T(8,128)(2,1)S(1)} %get-tuple-element.58), channel_id=1, source_target_pairs={{0,24},{4,28},{8,0},{12,4},{16,8},{20,12},{24,16},{28,20},{1,25},{... | collective-permute-start | bytes 663560 | tf_op jit(solution)/shard_map/rows/ppermute | solution.py:62
  15.9 9.7 %collective-permute-done.2.refs_3_ = bf16[144,768]{1,0:T(8,128)(2,1)S(1)} collective-permute-done((bf16[144,768]{1,0:T(8,128)(2,1)S(1)}, bf16[144,768]{1,0:T(8,128)(2,1)S(1)}, u32[]{:S(2)}, u32[]{:S(2)}) %collective-permute-start.2) | collective-permute-done | bytes 221216 | tf_op jit(solution)/shard_map/rows/ppermute | solution.py:62
  27.9 3.0 %collective-permute-start.9 = (bf16[128,768]{1,0:T(8,128)(2,1)S(1)}, bf16[128,768]{1,0:T(8,128)(2,1)S(1)}, u32[]{:S(2)}, u32[]{:S(2)}) collective-permute-start(bf16[128,768]{1,0:T(8,128)(2,1)S(1)} %slice.35), channel_id=1, source_target_pairs={{0,3},{1,0},{2,1},{3,2},{4,7},{5,4},{6,5},{7,6},{8,11},{9,8},{10,9... | collective-permute-start | bytes 589832 | tf_op jit(solution)/shard_map/weights/ppermute | solution.py:62
  31.9 3.8 %collective-permute-start.11 = (bf16[48,768]{1,0:T(8,128)(2,1)S(1)}, bf16[48,768]{1,0:T(8,128)(2,1)S(1)}, u32[]{:S(2)}, u32[]{:S(2)}) collective-permute-start(bf16[48,768]{1,0:T(8,128)(2,1)S(1)} %slice.37), channel_id=1, source_target_pairs={{0,24},{4,28},{8,0},{12,4},{16,8},{20,12},{24,16},{28,20},{1,25},{... | collective-permute-start | bytes 221192 | tf_op jit(solution)/shard_map/rows/ppermute | solution.py:62
  36.6 2.1 %shard_map.103.refs_13_.refs_2_.refs_3_ = f32[4,528,256]{2,1,0:T(8,128)S(1)} custom-call(s32[4]{0:T(128)S(1)} %pad_add_fusion.place, bf16[32,768]{1,0:T(8,128)(2,1)S(1)} %get-tuple-element.60.refs_0_, bf16[96,768]{1,0:T(8,128)(2,1)S(1)} %collective-permute-done.refs_1_, bf16[96,768]{1,0:T(8,128)(2,1)S(1)} %collective-permute-done.1.refs_2_, ...), custom_call_target="tpu_custom_call" | custom-call | flops 2000000000 | bytes 1048576 | tf_op jit(solution)/shard_map/pallas_call | solution.py:49
  39.5 1.3 %collective-permute-done.5.refs_2_.refs_6_ = bf16[96,768]{1,0:T(8,128)(2,1)S(1)} collective-permute-done((bf16[96,768]{1,0:T(8,128)(2,1)S(1)}, bf16[96,768]{1,0:T(8,128)(2,1)S(1)}, u32[]{:S(2)}, u32[]{:S(2)}) %collective-permute-start.5) | collective-permute-done | bytes 147488 | tf_op jit(solution)/shard_map/rows/ppermute | solution.py:62
  40.9 2.1 %shard_map.104.refs_14_.refs_3_.refs_4_ = f32[4,528,256]{2,1,0:T(8,128)S(1)} custom-call(s32[4]{0:T(128)S(1)} %pad_add_fusion.place, bf16[144,768]{1,0:T(8,128)(2,1)S(1)} %collective-permute-done.3.refs_0_.refs_4_, bf16[96,768]{1,0:T(8,128)(2,1)S(1)} %collective-permute-done.4.refs_1_.refs_5_, bf16[96,768]{1,0:T(8,128)(2,1)S(1)} %collective-permute-done.5.refs_2_.refs_6_, ...), custom_call_target="tpu_custom_call" | custom-call | flops 2000000000 | bytes 1048576 | tf_op jit(solution)/shard_map/pallas_call | solution.py:49
  42.9 2.1 %shard_map.105 = (f32[272,768]{1,0:T(8,128)S(1)}, bf16[272,768]{1,0:T(8,128)(2,1)S(1)}, bf16[528,512]{1,0:T(8,128)(2,1)S(1)}, bf16[512,768]{1,0:T(8,128)(2,1)S(1)}, bf16[528,768]{1,0:T(8,128)(2,1)S(1)}) custom-call(s32[4]{0:T(128)S(1)} %pad_add_fusion.place, bf16[64,768]{1,0:T(8,128)(2,1)S(1)} %copy-done.2, ...), custom_call_target="tpu_custom_call" | custom-call | flops 2000000000 | bytes 1048576 | tf_op jit(solution)/shard_map/pallas_call | solution.py:49
  45.7 2.1 %shard_map.107 = (f32[272,768]{1,0:T(8,128)S(1)}, bf16[272,768]{1,0:T(8,128)(2,1)S(1)}, bf16[528,512]{1,0:T(8,128)(2,1)S(1)}, bf16[528,768]{1,0:T(8,128)(2,1)S(1)}) custom-call(s32[4]{0:T(128)S(1)} %pad_add_fusion.place, bf16[512,768]{1,0:T(8,128)(2,1)S(1)} %get-tuple-element.71.refs_0_, bf16[272,768]{1,0:T(8,128)(2,1)S(1)} %collective-permute-done.6.refs_1_, ...), custom_call_target="tpu_custom_call" | custom-call | flops 2000000000 | bytes 1048576 | tf_op jit(solution)/shard_map/pallas_call | solution.py:49
  48.7 3.2 %collective-permute-start.22 = (bf16[144,768]{1,0:T(8,128)(2,1)S(1)}, bf16[144,768]{1,0:T(8,128)(2,1)S(1)}, u32[]{:S(2)}, u32[]{:S(2)}) collective-permute-start(bf16[144,768]{1,0:T(8,128)(2,1)S(1)} %get-tuple-element.86), channel_id=1, source_target_pairs={{0,3},{1,0},{2,1},{3,2},{4,7},{5,4},{6,5},{7,6},{8,11},{9,8},{10,9... | collective-permute-start | bytes 663560 | tf_op jit(solution)/shard_map/ppermute | solution.py:62
  51.9 2.1 %shard_map.108 = (f32[272,768]{1,0:T(8,128)S(1)}, bf16[272,768]{1,0:T(8,128)(2,1)S(1)}, bf16[528,512]{1,0:T(8,128)(2,1)S(1)}, bf16[528,768]{1,0:T(8,128)(2,1)S(1)}) custom-call(s32[4]{0:T(128)S(1)} %pad_add_fusion.place, bf16[512,768]{1,0:T(8,128)(2,1)S(1)} %get-tuple-element.71.refs_0_, bf16[272,768]{1,0:T(8,128)(2,1)S(1)} %collective-permute-done.8.refs_1_, ...), custom_call_target="tpu_custom_call" | custom-call | flops 2000000000 | bytes 1048576 | tf_op jit(solution)/shard_map/pallas_call | solution.py:49
  54.1 2.1 %shard_map.106 = (bf16[272,768]{1,0:T(8,128)(2,1)S(1)}, bf16[272,768]{1,0:T(8,128)(2,1)S(1)}, bf16[528,512]{1,0:T(8,128)(2,1)S(1)}) custom-call(s32[4]{0:T(128)S(1)} %pad_add_fusion.place, bf16[512,768]{1,0:T(8,128)(2,1)S(1)} %get-tuple-element.71.refs_0_, bf16[528,768]{1,0:T(8,128)(2,1)S(1)} %get-tuple-element.72.refs_1_.refs_4_, ...), custom_call_target="tpu_custom_call" | custom-call | flops 2000000000 | bytes 1048576 | tf_op jit(solution)/shard_map/pallas_call | solution.py:49
  56.2 3.4 %shard_map.109 = (bf16[192,768]{1,0:T(8,128)(2,1)S(1)}, bf16[64,768]{1,0:T(8,128)(2,1)S(1)}, bf16[192,768]{1,0:T(8,128)(2,1)S(1)}, f32[64,768]{1,0:T(8,128)S(1)}) custom-call(s32[4]{0:T(128)S(1)} %pad_add_fusion.place, bf16[528,512]{1,0:T(8,128)(2,1)S(1)} %get-tuple-element.73.refs_0_, bf16[528,512]{1,0:T(8,128)(2,1)S(1)} %get-tuple-element.74.refs_1_, ...), custom_call_target="tpu_custom_call" | custom-call | flops 2000000000 | bytes 1048576 | tf_op jit(solution)/shard_map/pallas_call | solution.py:49
  64.0 2.4 %collective-permute-start.19 = (bf16[128,768]{1,0:T(8,128)(2,1)S(1)}, bf16[128,768]{1,0:T(8,128)(2,1)S(1)}, u32[]{:S(2)}, u32[]{:S(2)}) collective-permute-start(bf16[128,768]{1,0:T(8,128)(2,1)S(1)} %get-tuple-element.84), channel_id=1, source_target_pairs={{0,28},{4,0},{8,4},{12,8},{16,12},{20,16},{24,20},{28,24},{32,36},... | collective-permute-start | bytes 589832 | tf_op jit(solution)/shard_map/rows_back/ppermute | solution.py:72
  66.4 2.1 %collective-permute-start.20 = (bf16[64,768]{1,0:T(8,128)(2,1)S(1)}, bf16[64,768]{1,0:T(8,128)(2,1)S(1)}, u32[]{:S(2)}, u32[]{:S(2)}) collective-permute-start(bf16[64,768]{1,0:T(8,128)(2,1)S(1)} %get-tuple-element.85), channel_id=1, source_target_pairs={{0,24},{4,28},{8,0},{12,4},{16,8},{20,12},{24,16},{28,20},{32,40},... | collective-permute-start | bytes 294920 | tf_op jit(solution)/shard_map/rows_back/ppermute | solution.py:72
  68.6 4.1 %collective-permute-done.20.got4 = bf16[64,768]{1,0:T(8,128)(2,1)S(1)} collective-permute-done((bf16[64,768]{1,0:T(8,128)(2,1)S(1)}, bf16[64,768]{1,0:T(8,128)(2,1)S(1)}, u32[]{:S(2)}, u32[]{:S(2)}) %collective-permute-start.20) | collective-permute-done | bytes 98336 | tf_op jit(solution)/shard_map/rows_back/ppermute | solution.py:72
  72.6 1.5 %collective-permute-start.18 = (bf16[128,768]{1,0:T(8,128)(2,1)S(1)}, bf16[128,768]{1,0:T(8,128)(2,1)S(1)}, u32[]{:S(2)}, u32[]{:S(2)}) collective-permute-start(bf16[128,768]{1,0:T(8,128)(2,1)S(1)} %get-tuple-element.83), channel_id=1, source_target_pairs={{0,28},{4,0},{8,4},{12,8},{16,12},{20,16},{24,20},{28,24},{32,36},... | collective-permute-start | bytes 589832 | tf_op jit(solution)/shard_map/rows_back/ppermute | solution.py:72
  74.8 2.2 %collective-permute-start.21 = (bf16[128,768]{1,0:T(8,128)(2,1)S(1)}, bf16[128,768]{1,0:T(8,128)(2,1)S(1)}, u32[]{:S(2)}, u32[]{:S(2)}) collective-permute-start(bf16[128,768]{1,0:T(8,128)(2,1)S(1)} %rows_back.3), channel_id=1, source_target_pairs={{0,24},{4,28},{8,0},{12,4},{16,8},{20,12},{24,16},{28,20},{32,40},... | collective-permute-start | bytes 589832 | tf_op jit(solution)/shard_map/rows_back/ppermute | solution.py:72
  79.3 2.2 %collective-permute-start.31 = (bf16[80,768]{1,0:T(8,128)(2,1)S(1)}, bf16[80,768]{1,0:T(8,128)(2,1)S(1)}, u32[]{:S(2)}, u32[]{:S(2)}) collective-permute-start(bf16[80,768]{1,0:T(8,128)(2,1)S(1)} %get-tuple-element.102), channel_id=1, source_target_pairs={{0,64},{64,128},{128,192},{192,0},{1,65},{65,129},{129,193},{193,1... | collective-permute-start | bytes 368648 | tf_op jit(solution)/shard_map/weights_y/ppermute | solution.py:62
  81.5 2.9 %collective-permute-done.21 = bf16[128,768]{1,0:T(8,128)(2,1)S(1)} collective-permute-done((bf16[128,768]{1,0:T(8,128)(2,1)S(1)}, bf16[128,768]{1,0:T(8,128)(2,1)S(1)}, u32[]{:S(2)}, u32[]{:S(2)}) %collective-permute-start.21) | collective-permute-done | bytes 196640 | tf_op jit(solution)/shard_map/rows_back/ppermute | solution.py:72
  85.6 2.0 %collective-permute-done.32.g3 = bf16[80,768]{1,0:T(8,128)(2,1)S(1)} collective-permute-done((bf16[80,768]{1,0:T(8,128)(2,1)S(1)}, bf16[80,768]{1,0:T(8,128)(2,1)S(1)}, u32[]{:S(2)}, u32[]{:S(2)}) %collective-permute-start.32) | collective-permute-done | bytes 122912 | tf_op jit(solution)/shard_map/weights_y/ppermute | solution.py:62
  (83 shorter events, 21.3 us)
Async XLA Ops:
  4.2 23.3 %collective-permute-start.8 = (bf16[272,768]{1,0:T(8,128)(2,1)S(1)}, bf16[272,768]{1,0:T(8,128)(2,1)S(1)}, u32[]{:S(2)}, u32[]{:S(2)}) collective-permute-start(bf16[272,768]{1,0:T(8,128)(2,1)S(1)} %get-tuple-element.59), channel_id=1, source_target_pairs={{0,3},{1,0},{2,1},{3,2},{4,7},{5,4},{6,5},{7,6},{8,11},{9,8},{10,9... | collective-permute-start | bytes 1253384 | tf_op jit(solution)/shard_map/weights/ppermute | solution.py:62
  7.1 19.7 %collective-permute-start.6 = (bf16[272,768]{1,0:T(8,128)(2,1)S(1)}, bf16[272,768]{1,0:T(8,128)(2,1)S(1)}, u32[]{:S(2)}, u32[]{:S(2)}) collective-permute-start(bf16[272,768]{1,0:T(8,128)(2,1)S(1)} %get-tuple-element.59), channel_id=1, source_target_pairs={{0,1},{1,2},{2,3},{3,0},{4,5},{5,6},{6,7},{7,4},{8,9},{9,10},{10,1... | collective-permute-start | bytes 1253384 | tf_op jit(solution)/shard_map/weights/ppermute | solution.py:62
  8.4 17.2 %collective-permute-start.2 = (bf16[144,768]{1,0:T(8,128)(2,1)S(1)}, bf16[144,768]{1,0:T(8,128)(2,1)S(1)}, u32[]{:S(2)}, u32[]{:S(2)}) collective-permute-start(bf16[144,768]{1,0:T(8,128)(2,1)S(1)} %get-tuple-element.57), channel_id=1, source_target_pairs={{0,8},{4,12},{8,16},{12,20},{16,24},{20,28},{24,0},{28,4},{1,9},{5... | collective-permute-start | bytes 663560 | tf_op jit(solution)/shard_map/rows/ppermute | solution.py:62
  11.8 16.2 %collective-permute-start.3 = (bf16[144,768]{1,0:T(8,128)(2,1)S(1)}, bf16[144,768]{1,0:T(8,128)(2,1)S(1)}, u32[]{:S(2)}, u32[]{:S(2)}) collective-permute-start(bf16[144,768]{1,0:T(8,128)(2,1)S(1)} %get-tuple-element.58), channel_id=1, source_target_pairs={{0,24},{4,28},{8,0},{12,4},{16,8},{20,12},{24,16},{28,20},{1,25},{... | collective-permute-start | bytes 663560 | tf_op jit(solution)/shard_map/rows/ppermute | solution.py:62
  14.9 16.1 %collective-permute-start = (bf16[96,768]{1,0:T(8,128)(2,1)S(1)}, bf16[96,768]{1,0:T(8,128)(2,1)S(1)}, u32[]{:S(2)}, u32[]{:S(2)}) collective-permute-start(bf16[96,768]{1,0:T(8,128)(2,1)S(1)} %get-tuple-element.55), channel_id=1, source_target_pairs={{0,4},{4,8},{8,12},{12,16},{16,20},{20,24},{24,28},{28,0},{1,5},{5... | collective-permute-start | bytes 442376 | tf_op jit(solution)/shard_map/rows/ppermute | solution.py:62
  25.6 6.3 %collective-permute-start.1 = (bf16[96,768]{1,0:T(8,128)(2,1)S(1)}, bf16[96,768]{1,0:T(8,128)(2,1)S(1)}, u32[]{:S(2)}, u32[]{:S(2)}) collective-permute-start(bf16[96,768]{1,0:T(8,128)(2,1)S(1)} %get-tuple-element.56), channel_id=1, source_target_pairs={{0,28},{4,0},{8,4},{12,8},{16,12},{20,16},{24,20},{28,24},{1,29},{... | collective-permute-start | bytes 442376 | tf_op jit(solution)/shard_map/rows/ppermute | solution.py:62
  26.8 8.9 %collective-permute-start.10 = (bf16[48,768]{1,0:T(8,128)(2,1)S(1)}, bf16[48,768]{1,0:T(8,128)(2,1)S(1)}, u32[]{:S(2)}, u32[]{:S(2)}) collective-permute-start(bf16[48,768]{1,0:T(8,128)(2,1)S(1)} %slice.36), channel_id=1, source_target_pairs={{0,8},{4,12},{8,16},{12,20},{16,24},{20,28},{24,0},{28,4},{1,9},{5... | collective-permute-start | bytes 221192 | tf_op jit(solution)/shard_map/rows/ppermute | solution.py:62
  27.6 11.4 %collective-permute-start.7 = (bf16[144,768]{1,0:T(8,128)(2,1)S(1)}, bf16[144,768]{1,0:T(8,128)(2,1)S(1)}, u32[]{:S(2)}, u32[]{:S(2)}) collective-permute-start(bf16[144,768]{1,0:T(8,128)(2,1)S(1)} %slice.34), channel_id=1, source_target_pairs={{0,1},{1,2},{2,3},{3,0},{4,5},{5,6},{6,7},{7,4},{8,9},{9,10},{10,1... | collective-permute-start | bytes 663560 | tf_op jit(solution)/shard_map/weights/ppermute | solution.py:62
  27.9 11.0 %collective-permute-start.9 = (bf16[128,768]{1,0:T(8,128)(2,1)S(1)}, bf16[128,768]{1,0:T(8,128)(2,1)S(1)}, u32[]{:S(2)}, u32[]{:S(2)}) collective-permute-start(bf16[128,768]{1,0:T(8,128)(2,1)S(1)} %slice.35), channel_id=1, source_target_pairs={{0,3},{1,0},{2,1},{3,2},{4,7},{5,4},{6,5},{7,6},{8,11},{9,8},{10,9... | collective-permute-start | bytes 589832 | tf_op jit(solution)/shard_map/weights/ppermute | solution.py:62
  31.0 8.5 %collective-permute-start.4 = (bf16[96,768]{1,0:T(8,128)(2,1)S(1)}, bf16[96,768]{1,0:T(8,128)(2,1)S(1)}, u32[]{:S(2)}, u32[]{:S(2)}) collective-permute-start(bf16[96,768]{1,0:T(8,128)(2,1)S(1)} %slice.32), channel_id=1, source_target_pairs={{0,4},{4,8},{8,12},{12,16},{16,20},{20,24},{24,28},{28,0},{1,5},{5... | collective-permute-start | bytes 442376 | tf_op jit(solution)/shard_map/rows/ppermute | solution.py:62
  31.9 7.0 %collective-permute-start.11 = (bf16[48,768]{1,0:T(8,128)(2,1)S(1)}, bf16[48,768]{1,0:T(8,128)(2,1)S(1)}, u32[]{:S(2)}, u32[]{:S(2)}) collective-permute-start(bf16[48,768]{1,0:T(8,128)(2,1)S(1)} %slice.37), channel_id=1, source_target_pairs={{0,24},{4,28},{8,0},{12,4},{16,8},{20,12},{24,16},{28,20},{1,25},{... | collective-permute-start | bytes 221192 | tf_op jit(solution)/shard_map/rows/ppermute | solution.py:62
  45.2 6.7 %collective-permute-start.16 = (bf16[272,768]{1,0:T(8,128)(2,1)S(1)}, bf16[272,768]{1,0:T(8,128)(2,1)S(1)}, u32[]{:S(2)}, u32[]{:S(2)}) collective-permute-start(bf16[272,768]{1,0:T(8,128)(2,1)S(1)} %collective-permute-done.8.refs_1_), channel_id=1, source_target_pairs={{0,32},{32,0},{1,33},{33,1},{2,34},{34,2},{3,35},{35,3},{4,36},{36... | collective-permute-start | bytes 1253384 | tf_op jit(solution)/shard_map/weights/ppermute | solution.py:62
  47.8 12.8 %collective-permute-start.24 = (bf16[272,768]{1,0:T(8,128)(2,1)S(1)}, bf16[272,768]{1,0:T(8,128)(2,1)S(1)}, u32[]{:S(2)}, u32[]{:S(2)}) collective-permute-start(bf16[272,768]{1,0:T(8,128)(2,1)S(1)} %get-tuple-element.91), channel_id=1, source_target_pairs={{0,32},{32,0},{1,33},{33,1},{2,34},{34,2},{3,35},{35,3},{4,36},{36... | collective-permute-start | bytes 1253384 | tf_op jit(solution)/shard_map/ppermute | solution.py:62
  48.6 11.9 %collective-permute-start.26 = (bf16[128,768]{1,0:T(8,128)(2,1)S(1)}, bf16[128,768]{1,0:T(8,128)(2,1)S(1)}, u32[]{:S(2)}, u32[]{:S(2)}) collective-permute-start(bf16[128,768]{1,0:T(8,128)(2,1)S(1)} %get-tuple-element.95), channel_id=1, source_target_pairs={{0,1},{1,2},{2,3},{3,0},{4,5},{5,6},{6,7},{7,4},{8,9},{9,10},{10,1... | collective-permute-start | bytes 589832 | tf_op jit(solution)/shard_map/ppermute | solution.py:62
  48.7 11.5 %collective-permute-start.22 = (bf16[144,768]{1,0:T(8,128)(2,1)S(1)}, bf16[144,768]{1,0:T(8,128)(2,1)S(1)}, u32[]{:S(2)}, u32[]{:S(2)}) collective-permute-start(bf16[144,768]{1,0:T(8,128)(2,1)S(1)} %get-tuple-element.86), channel_id=1, source_target_pairs={{0,3},{1,0},{2,1},{3,2},{4,7},{5,4},{6,5},{7,6},{8,11},{9,8},{10,9... | collective-permute-start | bytes 663560 | tf_op jit(solution)/shard_map/ppermute | solution.py:62
  54.0 6.5 %collective-permute-start.25 = (bf16[272,768]{1,0:T(8,128)(2,1)S(1)}, bf16[272,768]{1,0:T(8,128)(2,1)S(1)}, u32[]{:S(2)}, u32[]{:S(2)}) collective-permute-start(bf16[272,768]{1,0:T(8,128)(2,1)S(1)} %get-tuple-element.93), channel_id=1, source_target_pairs={{0,32},{32,0},{1,33},{33,1},{2,34},{34,2},{3,35},{35,3},{4,36},{36... | collective-permute-start | bytes 1253384 | tf_op jit(solution)/shard_map/ppermute | solution.py:62
  60.2 16.8 %collective-permute-start.23 = (bf16[272,768]{1,0:T(8,128)(2,1)S(1)}, bf16[272,768]{1,0:T(8,128)(2,1)S(1)}, u32[]{:S(2)}, u32[]{:S(2)}) collective-permute-start(bf16[272,768]{1,0:T(8,128)(2,1)S(1)} %get-tuple-element.89), channel_id=1, source_target_pairs={{0,32},{32,0},{1,33},{33,1},{2,34},{34,2},{3,35},{35,3},{4,36},{36... | collective-permute-start | bytes 1253384 | tf_op jit(solution)/shard_map/ppermute | solution.py:62
  61.3 15.7 %collective-permute-start.27 = (bf16[272,768]{1,0:T(8,128)(2,1)S(1)}, bf16[272,768]{1,0:T(8,128)(2,1)S(1)}, u32[]{:S(2)}, u32[]{:S(2)}) collective-permute-start(bf16[272,768]{1,0:T(8,128)(2,1)S(1)} %get-tuple-element.96), channel_id=1, source_target_pairs={{0,3},{1,0},{2,1},{3,2},{4,7},{5,4},{6,5},{7,6},{8,11},{9,8},{10,9... | collective-permute-start | bytes 1253384 | tf_op jit(solution)/shard_map/weights_x/ppermute | solution.py:62
  62.2 14.8 %collective-permute-start.28 = (bf16[272,768]{1,0:T(8,128)(2,1)S(1)}, bf16[272,768]{1,0:T(8,128)(2,1)S(1)}, u32[]{:S(2)}, u32[]{:S(2)}) collective-permute-start(bf16[272,768]{1,0:T(8,128)(2,1)S(1)} %get-tuple-element.97), channel_id=1, source_target_pairs={{0,1},{1,2},{2,3},{3,0},{4,5},{5,6},{6,7},{7,4},{8,9},{9,10},{10,1... | collective-permute-start | bytes 1253384 | tf_op jit(solution)/shard_map/weights_x/ppermute | solution.py:62
  64.0 10.2 %collective-permute-start.19 = (bf16[128,768]{1,0:T(8,128)(2,1)S(1)}, bf16[128,768]{1,0:T(8,128)(2,1)S(1)}, u32[]{:S(2)}, u32[]{:S(2)}) collective-permute-start(bf16[128,768]{1,0:T(8,128)(2,1)S(1)} %get-tuple-element.84), channel_id=1, source_target_pairs={{0,28},{4,0},{8,4},{12,8},{16,12},{20,16},{24,20},{28,24},{32,36},... | collective-permute-start | bytes 589832 | tf_op jit(solution)/shard_map/rows_back/ppermute | solution.py:72
  72.6 12.8 %collective-permute-start.18 = (bf16[128,768]{1,0:T(8,128)(2,1)S(1)}, bf16[128,768]{1,0:T(8,128)(2,1)S(1)}, u32[]{:S(2)}, u32[]{:S(2)}) collective-permute-start(bf16[128,768]{1,0:T(8,128)(2,1)S(1)} %get-tuple-element.83), channel_id=1, source_target_pairs={{0,28},{4,0},{8,4},{12,8},{16,12},{20,16},{24,20},{28,24},{32,36},... | collective-permute-start | bytes 589832 | tf_op jit(solution)/shard_map/rows_back/ppermute | solution.py:72
  74.8 9.6 %collective-permute-start.21 = (bf16[128,768]{1,0:T(8,128)(2,1)S(1)}, bf16[128,768]{1,0:T(8,128)(2,1)S(1)}, u32[]{:S(2)}, u32[]{:S(2)}) collective-permute-start(bf16[128,768]{1,0:T(8,128)(2,1)S(1)} %rows_back.3), channel_id=1, source_target_pairs={{0,24},{4,28},{8,0},{12,4},{16,8},{20,12},{24,16},{28,20},{32,40},... | collective-permute-start | bytes 589832 | tf_op jit(solution)/shard_map/rows_back/ppermute | solution.py:72
  78.0 7.5 %collective-permute-start.29 = (bf16[80,768]{1,0:T(8,128)(2,1)S(1)}, bf16[80,768]{1,0:T(8,128)(2,1)S(1)}, u32[]{:S(2)}, u32[]{:S(2)}) collective-permute-start(bf16[80,768]{1,0:T(8,128)(2,1)S(1)} %get-tuple-element.98), channel_id=1, source_target_pairs={{0,128},{64,192},{128,0},{192,64},{1,129},{65,193},{129,1},{193,65... | collective-permute-start | bytes 368648 | tf_op jit(solution)/shard_map/weights_y/ppermute | solution.py:62
  79.3 6.3 %collective-permute-start.31 = (bf16[80,768]{1,0:T(8,128)(2,1)S(1)}, bf16[80,768]{1,0:T(8,128)(2,1)S(1)}, u32[]{:S(2)}, u32[]{:S(2)}) collective-permute-start(bf16[80,768]{1,0:T(8,128)(2,1)S(1)} %get-tuple-element.102), channel_id=1, source_target_pairs={{0,64},{64,128},{128,192},{192,0},{1,65},{65,129},{129,193},{193,1... | collective-permute-start | bytes 368648 | tf_op jit(solution)/shard_map/weights_y/ppermute | solution.py:62
  (17 other events, 70.5 us)

commit v8 on v7

--- a/solution.py
+++ b/solution.py
@@ -290,6 +290,7 @@
             own=2,
         )
         low, high = shift(part, "x", 1), shift(part, "x", -1)
+        low2, high2 = shift(low[:CUT], "x", 1), shift(high[CUT:], "x", -1)
 
     with jax.named_scope("rows"):
         cap = prefix.shape[-1]
@@ -315,6 +316,7 @@
         )
         up2, dn2 = shift(up2, "z", 2), shift(dn2, "z", -2)
         up1, dn1 = shift(up1, "z", 1), shift(dn1, "z", -1)
+        low2, high2, up2, dn2 = lax.optimization_barrier((low2, high2, up2, dn2))
         up3, dn3 = shift(up2[16:112], "z", 1), shift(dn2[16:112], "z", -1)
         up4, dn4 = shift(up2[:48], "z", 2), shift(dn2[:48], "z", -2)
 
@@ -329,7 +331,6 @@
 
     ay1 = sum_slots((s0, up1, dn1, up2), SLOT_AT[0])
     with jax.named_scope("weights"):
-        low2, high2 = shift(low[:CUT], "x", 1), shift(high[CUT:], "x", -1)
         low2, high2, up4, dn4, ay1 = lax.optimization_barrier((low2, high2, up4, dn4, ay1))
         low_o, high_o, low2_o, high2_o = (swap(p) for p in (low, high, low2, high2))
     ay2 = sum_slots((dn2, up3, dn3, up4, dn4), SLOT_AT[1])

time: 89.9 us -> 88.5 us (0.984)
  waiting for transfers between devices: 21.3 us -> 17.4 us
  starting transfers between devices: 40.9 us -> 43.5 us
    ppermute x29, starting transfers between devices: 32.6 us -> 38.7 us  [shift(): return lax.ppermute(x, axis, [(i, (i + by) % n) for i in range(n)])]
    ppermute x29, waiting for transfers between devices: 14.3 us -> 9.52 us  [shift(): return lax.ppermute(x, axis, [(i, (i + by) % n) for i in range(n)])]
    ppermute x4, starting transfers between devices: 8.3 us -> 4.78 us  [turn(): return lax.ppermute(x, ('core', axis), pairs)]
    ppermute x4, waiting for transfers between devices: 6.97 us -> 7.88 us  [turn(): return lax.ppermute(x, ('core', axis), pairs)]
  transfers between devices with their start and end apart: 33 -> 33, of which waited for: 7 -> 8; matrix products, arithmetic and copies ran while one was open for 0% -> 0% of each run, Pallas kernels for 25% -> 25%
where the time goes in v8:
time: 88.5 us; the launch traced here: 88.3 us
  starting transfers between devices  43.5 us (49%)
  Pallas kernels  23.6 us (27%)
  waiting for transfers between devices  17.4 us (20%)
  local copies, waits for them, and re-layouts  1.98 us (2%)
  between operations  0.95 us (1%)
    ppermute x29, starting transfers between devices, shift(): return lax.ppermute(x, axis, [(i, (i + by) % n) for i in range(n)])  38.7 us
    pallas_call x15, Pallas kernels, call(): pl.pallas_call(functools.partial(kernel, **static), out_shape=tuple((jax....  23.6 us
    ppermute x29, waiting for transfers between devices, shift(): return lax.ppermute(x, axis, [(i, (i + by) % n) for i in range(n)])  9.52 us
    ppermute x4, waiting for transfers between devices, turn(): return lax.ppermute(x, ('core', axis), pairs)  7.88 us
    ppermute x4, starting transfers between devices, turn(): return lax.ppermute(x, ('core', axis), pairs)  4.78 us
    unnamed x16, local copies, waits for them, and re-layouts  1.9 us
  transfers between devices with their start and end apart: 33, of which 8 were waited for; matrix products, arithmetic and copies ran while one was open for 0% of the time, Pallas kernels for 25%

profile of v8, /device:TPU:24, one launch (start us, length us, event | category | flops | bytes accessed | tf_op | source)
XLA Modules:
  0.0 88.3 jit_solution(9025132891316569910)
XLA Ops:
  5.8 1.7 %collective-permute-start.4 = (bf16[272,768]{1,0:T(8,128)(2,1)S(1)}, bf16[272,768]{1,0:T(8,128)(2,1)S(1)}, u32[]{:S(2)}, u32[]{:S(2)}) collective-permute-start(bf16[272,768]{1,0:T(8,128)(2,1)S(1)} %get-tuple-element.61), channel_id=1, source_target_pairs={{0,3},{1,0},{2,1},{3,2},{4,7},{5,4},{6,5},{7,6},{8,11},{9,8},{10,9... | collective-permute-start | bytes 1253384 | tf_op jit(solution)/shard_map/weights/ppermute | solution.py:62
  8.9 3.3 %collective-permute-start.6 = (bf16[144,768]{1,0:T(8,128)(2,1)S(1)}, bf16[144,768]{1,0:T(8,128)(2,1)S(1)}, u32[]{:S(2)}, u32[]{:S(2)}) collective-permute-start(bf16[144,768]{1,0:T(8,128)(2,1)S(1)} %get-tuple-element.62), channel_id=1, source_target_pairs={{0,8},{4,12},{8,16},{12,20},{16,24},{20,28},{24,0},{28,4},{1,9},{5... | collective-permute-start | bytes 663560 | tf_op jit(solution)/shard_map/rows/ppermute | solution.py:62
  12.2 3.1 %collective-permute-start.7 = (bf16[144,768]{1,0:T(8,128)(2,1)S(1)}, bf16[144,768]{1,0:T(8,128)(2,1)S(1)}, u32[]{:S(2)}, u32[]{:S(2)}) collective-permute-start(bf16[144,768]{1,0:T(8,128)(2,1)S(1)} %get-tuple-element.63), channel_id=1, source_target_pairs={{0,24},{4,28},{8,0},{12,4},{16,8},{20,12},{24,16},{28,20},{1,25},{... | collective-permute-start | bytes 663560 | tf_op jit(solution)/shard_map/rows/ppermute | solution.py:62
  17.3 3.0 %collective-permute-start.5 = (bf16[128,768]{1,0:T(8,128)(2,1)S(1)}, bf16[128,768]{1,0:T(8,128)(2,1)S(1)}, u32[]{:S(2)}, u32[]{:S(2)}) collective-permute-start(bf16[128,768]{1,0:T(8,128)(2,1)S(1)} %slice.33), channel_id=1, source_target_pairs={{0,3},{1,0},{2,1},{3,2},{4,7},{5,4},{6,5},{7,6},{8,11},{9,8},{10,9... | collective-permute-start | bytes 589832 | tf_op jit(solution)/shard_map/weights/ppermute | solution.py:62
  20.3 1.9 %collective-permute-start = (bf16[96,768]{1,0:T(8,128)(2,1)S(1)}, bf16[96,768]{1,0:T(8,128)(2,1)S(1)}, u32[]{:S(2)}, u32[]{:S(2)}) collective-permute-start(bf16[96,768]{1,0:T(8,128)(2,1)S(1)} %get-tuple-element.59), channel_id=1, source_target_pairs={{0,4},{4,8},{8,12},{12,16},{16,20},{20,24},{24,28},{28,0},{1,5},{5... | collective-permute-start | bytes 442376 | tf_op jit(solution)/shard_map/rows/ppermute | solution.py:62
  22.2 4.5 %collective-permute-start.1 = (bf16[96,768]{1,0:T(8,128)(2,1)S(1)}, bf16[96,768]{1,0:T(8,128)(2,1)S(1)}, u32[]{:S(2)}, u32[]{:S(2)}) collective-permute-start(bf16[96,768]{1,0:T(8,128)(2,1)S(1)} %get-tuple-element.60), channel_id=1, source_target_pairs={{0,28},{4,0},{8,4},{12,8},{16,12},{20,16},{24,20},{28,24},{1,29},{... | collective-permute-start | bytes 442376 | tf_op jit(solution)/shard_map/rows/ppermute | solution.py:62
  26.8 4.1 %collective-permute-start.11 = (bf16[48,768]{1,0:T(8,128)(2,1)S(1)}, bf16[48,768]{1,0:T(8,128)(2,1)S(1)}, u32[]{:S(2)}, u32[]{:S(2)}) collective-permute-start(bf16[48,768]{1,0:T(8,128)(2,1)S(1)} %slice.29), channel_id=1, source_target_pairs={{0,24},{4,28},{8,0},{12,4},{16,8},{20,12},{24,16},{28,20},{1,25},{... | collective-permute-start | bytes 221192 | tf_op jit(solution)/shard_map/rows/ppermute | solution.py:62
  30.9 3.7 %collective-permute-start.9 = (bf16[96,768]{1,0:T(8,128)(2,1)S(1)}, bf16[96,768]{1,0:T(8,128)(2,1)S(1)}, u32[]{:S(2)}, u32[]{:S(2)}) collective-permute-start(bf16[96,768]{1,0:T(8,128)(2,1)S(1)} %slice.27), channel_id=1, source_target_pairs={{0,28},{4,0},{8,4},{12,8},{16,12},{20,16},{24,20},{28,24},{1,29},{... | collective-permute-start | bytes 442376 | tf_op jit(solution)/shard_map/rows/ppermute | solution.py:62
  34.6 2.1 %shard_map.103.refs_13_.refs_2_.refs_3_ = f32[4,528,256]{2,1,0:T(8,128)S(1)} custom-call(s32[4]{0:T(128)S(1)} %pad_add_fusion.place, bf16[32,768]{1,0:T(8,128)(2,1)S(1)} %get-tuple-element.68.refs_0_, bf16[96,768]{1,0:T(8,128)(2,1)S(1)} %collective-permute-done.refs_1_, bf16[96,768]{1,0:T(8,128)(2,1)S(1)} %collective-permute-done.1.refs_2_, ...), custom_call_target="tpu_custom_call" | custom-call | flops 2000000000 | bytes 1048576 | tf_op jit(solution)/shard_map/pallas_call | solution.py:49
  38.5 2.4 %collective-permute-done.8.refs_1_.refs_5_ = bf16[96,768]{1,0:T(8,128)(2,1)S(1)} collective-permute-done((bf16[96,768]{1,0:T(8,128)(2,1)S(1)}, bf16[96,768]{1,0:T(8,128)(2,1)S(1)}, u32[]{:S(2)}, u32[]{:S(2)}) %collective-permute-start.8) | collective-permute-done | bytes 147488 | tf_op jit(solution)/shard_map/rows/ppermute | solution.py:62
  41.0 2.1 %shard_map.104.refs_14_.refs_3_.refs_4_ = f32[4,528,256]{2,1,0:T(8,128)S(1)} custom-call(s32[4]{0:T(128)S(1)} %pad_add_fusion.place, bf16[144,768]{1,0:T(8,128)(2,1)S(1)} %collective-permute-done.7.refs_0_.refs_4_, bf16[96,768]{1,0:T(8,128)(2,1)S(1)} %collective-permute-done.8.refs_1_.refs_5_, bf16[96,768]{1,0:T(8,128)(2,1)S(1)} %collective-permute-done.9.refs_2_.refs_6_, ...), custom_call_target="tpu_custom_call" | custom-call | flops 2000000000 | bytes 1048576 | tf_op jit(solution)/shard_map/pallas_call | solution.py:49
  43.1 2.1 %shard_map.105 = (f32[272,768]{1,0:T(8,128)S(1)}, bf16[272,768]{1,0:T(8,128)(2,1)S(1)}, bf16[528,512]{1,0:T(8,128)(2,1)S(1)}, bf16[512,768]{1,0:T(8,128)(2,1)S(1)}, bf16[528,768]{1,0:T(8,128)(2,1)S(1)}) custom-call(s32[4]{0:T(128)S(1)} %pad_add_fusion.place, bf16[64,768]{1,0:T(8,128)(2,1)S(1)} %copy-done.2, ...), custom_call_target="tpu_custom_call" | custom-call | flops 2000000000 | bytes 1048576 | tf_op jit(solution)/shard_map/pallas_call | solution.py:49
  45.8 2.1 %shard_map.107 = (f32[272,768]{1,0:T(8,128)S(1)}, bf16[272,768]{1,0:T(8,128)(2,1)S(1)}, bf16[528,512]{1,0:T(8,128)(2,1)S(1)}, bf16[528,768]{1,0:T(8,128)(2,1)S(1)}) custom-call(s32[4]{0:T(128)S(1)} %pad_add_fusion.place, bf16[512,768]{1,0:T(8,128)(2,1)S(1)} %get-tuple-element.79.refs_0_, bf16[272,768]{1,0:T(8,128)(2,1)S(1)} %collective-permute-done.2.refs_1_, ...), custom_call_target="tpu_custom_call" | custom-call | flops 2000000000 | bytes 1048576 | tf_op jit(solution)/shard_map/pallas_call | solution.py:49
  48.8 3.2 %collective-permute-start.22 = (bf16[144,768]{1,0:T(8,128)(2,1)S(1)}, bf16[144,768]{1,0:T(8,128)(2,1)S(1)}, u32[]{:S(2)}, u32[]{:S(2)}) collective-permute-start(bf16[144,768]{1,0:T(8,128)(2,1)S(1)} %get-tuple-element.94), channel_id=1, source_target_pairs={{0,3},{1,0},{2,1},{3,2},{4,7},{5,4},{6,5},{7,6},{8,11},{9,8},{10,9... | collective-permute-start | bytes 663560 | tf_op jit(solution)/shard_map/ppermute | solution.py:62
  52.0 2.1 %shard_map.108 = (f32[272,768]{1,0:T(8,128)S(1)}, bf16[272,768]{1,0:T(8,128)(2,1)S(1)}, bf16[528,512]{1,0:T(8,128)(2,1)S(1)}, bf16[528,768]{1,0:T(8,128)(2,1)S(1)}) custom-call(s32[4]{0:T(128)S(1)} %pad_add_fusion.place, bf16[512,768]{1,0:T(8,128)(2,1)S(1)} %get-tuple-element.79.refs_0_, bf16[272,768]{1,0:T(8,128)(2,1)S(1)} %collective-permute-done.4.refs_1_, ...), custom_call_target="tpu_custom_call" | custom-call | flops 2000000000 | bytes 1048576 | tf_op jit(solution)/shard_map/pallas_call | solution.py:49
  54.2 2.1 %shard_map.106 = (bf16[272,768]{1,0:T(8,128)(2,1)S(1)}, bf16[272,768]{1,0:T(8,128)(2,1)S(1)}, bf16[528,512]{1,0:T(8,128)(2,1)S(1)}) custom-call(s32[4]{0:T(128)S(1)} %pad_add_fusion.place, bf16[512,768]{1,0:T(8,128)(2,1)S(1)} %get-tuple-element.79.refs_0_, bf16[528,768]{1,0:T(8,128)(2,1)S(1)} %get-tuple-element.80.refs_1_.refs_4_, ...), custom_call_target="tpu_custom_call" | custom-call | flops 2000000000 | bytes 1048576 | tf_op jit(solution)/shard_map/pallas_call | solution.py:49
  56.3 3.4 %shard_map.109 = (bf16[192,768]{1,0:T(8,128)(2,1)S(1)}, bf16[64,768]{1,0:T(8,128)(2,1)S(1)}, bf16[192,768]{1,0:T(8,128)(2,1)S(1)}, f32[64,768]{1,0:T(8,128)S(1)}) custom-call(s32[4]{0:T(128)S(1)} %pad_add_fusion.place, bf16[528,512]{1,0:T(8,128)(2,1)S(1)} %get-tuple-element.81.refs_0_, bf16[528,512]{1,0:T(8,128)(2,1)S(1)} %get-tuple-element.82.refs_1_, ...), custom_call_target="tpu_custom_call" | custom-call | flops 2000000000 | bytes 1048576 | tf_op jit(solution)/shard_map/pallas_call | solution.py:49
  61.4 1.6 %collective-permute-start.27 = (bf16[272,768]{1,0:T(8,128)(2,1)S(1)}, bf16[272,768]{1,0:T(8,128)(2,1)S(1)}, u32[]{:S(2)}, u32[]{:S(2)}) collective-permute-start(bf16[272,768]{1,0:T(8,128)(2,1)S(1)} %get-tuple-element.104), channel_id=1, source_target_pairs={{0,3},{1,0},{2,1},{3,2},{4,7},{5,4},{6,5},{7,6},{8,11},{9,8},{10,9... | collective-permute-start | bytes 1253384 | tf_op jit(solution)/shard_map/weights_x/ppermute | solution.py:62
  65.0 5.8 %collective-permute-done.20.got4 = bf16[64,768]{1,0:T(8,128)(2,1)S(1)} collective-permute-done((bf16[64,768]{1,0:T(8,128)(2,1)S(1)}, bf16[64,768]{1,0:T(8,128)(2,1)S(1)}, u32[]{:S(2)}, u32[]{:S(2)}) %collective-permute-start.20) | collective-permute-done | bytes 98336 | tf_op jit(solution)/shard_map/rows_back/ppermute | solution.py:72
  70.9 3.8 %collective-permute-start.18 = (bf16[128,768]{1,0:T(8,128)(2,1)S(1)}, bf16[128,768]{1,0:T(8,128)(2,1)S(1)}, u32[]{:S(2)}, u32[]{:S(2)}) collective-permute-start(bf16[128,768]{1,0:T(8,128)(2,1)S(1)} %get-tuple-element.91), channel_id=1, source_target_pairs={{0,28},{4,0},{8,4},{12,8},{16,12},{20,16},{24,20},{28,24},{32,36},... | collective-permute-start | bytes 589832 | tf_op jit(solution)/shard_map/rows_back/ppermute | solution.py:72
  78.0 2.2 %collective-permute-start.31 = (bf16[80,768]{1,0:T(8,128)(2,1)S(1)}, bf16[80,768]{1,0:T(8,128)(2,1)S(1)}, u32[]{:S(2)}, u32[]{:S(2)}) collective-permute-start(bf16[80,768]{1,0:T(8,128)(2,1)S(1)} %get-tuple-element.110), channel_id=1, source_target_pairs={{0,64},{64,128},{128,192},{192,0},{1,65},{65,129},{129,193},{193,1... | collective-permute-start | bytes 368648 | tf_op jit(solution)/shard_map/weights_y/ppermute | solution.py:62
  80.2 2.1 %collective-permute-done.21 = bf16[128,768]{1,0:T(8,128)(2,1)S(1)} collective-permute-done((bf16[128,768]{1,0:T(8,128)(2,1)S(1)}, bf16[128,768]{1,0:T(8,128)(2,1)S(1)}, u32[]{:S(2)}, u32[]{:S(2)}) %collective-permute-start.21) | collective-permute-done | bytes 196640 | tf_op jit(solution)/shard_map/rows_back/ppermute | solution.py:72
  82.2 1.9 %collective-permute-done.29.g2 = bf16[80,768]{1,0:T(8,128)(2,1)S(1)} collective-permute-done((bf16[80,768]{1,0:T(8,128)(2,1)S(1)}, bf16[80,768]{1,0:T(8,128)(2,1)S(1)}, u32[]{:S(2)}, u32[]{:S(2)}) %collective-permute-start.29) | collective-permute-done | bytes 122912 | tf_op jit(solution)/shard_map/weights_y/ppermute | solution.py:62
  84.3 2.0 %collective-permute-done.32.g3 = bf16[80,768]{1,0:T(8,128)(2,1)S(1)} collective-permute-done((bf16[80,768]{1,0:T(8,128)(2,1)S(1)}, bf16[80,768]{1,0:T(8,128)(2,1)S(1)}, u32[]{:S(2)}, u32[]{:S(2)}) %collective-permute-start.32) | collective-permute-done | bytes 122912 | tf_op jit(solution)/shard_map/weights_y/ppermute | solution.py:62
  (83 shorter events, 21.1 us)
Async XLA Ops:
  4.2 12.7 %collective-permute-start.2 = (bf16[272,768]{1,0:T(8,128)(2,1)S(1)}, bf16[272,768]{1,0:T(8,128)(2,1)S(1)}, u32[]{:S(2)}, u32[]{:S(2)}) collective-permute-start(bf16[272,768]{1,0:T(8,128)(2,1)S(1)} %get-tuple-element.61), channel_id=1, source_target_pairs={{0,1},{1,2},{2,3},{3,0},{4,5},{5,6},{6,7},{7,4},{8,9},{9,10},{10,1... | collective-permute-start | bytes 1253384 | tf_op jit(solution)/shard_map/weights/ppermute | solution.py:62
  5.8 11.5 %collective-permute-start.4 = (bf16[272,768]{1,0:T(8,128)(2,1)S(1)}, bf16[272,768]{1,0:T(8,128)(2,1)S(1)}, u32[]{:S(2)}, u32[]{:S(2)}) collective-permute-start(bf16[272,768]{1,0:T(8,128)(2,1)S(1)} %get-tuple-element.61), channel_id=1, source_target_pairs={{0,3},{1,0},{2,1},{3,2},{4,7},{5,4},{6,5},{7,6},{8,11},{9,8},{10,9... | collective-permute-start | bytes 1253384 | tf_op jit(solution)/shard_map/weights/ppermute | solution.py:62
  8.9 13.4 %collective-permute-start.6 = (bf16[144,768]{1,0:T(8,128)(2,1)S(1)}, bf16[144,768]{1,0:T(8,128)(2,1)S(1)}, u32[]{:S(2)}, u32[]{:S(2)}) collective-permute-start(bf16[144,768]{1,0:T(8,128)(2,1)S(1)} %get-tuple-element.62), channel_id=1, source_target_pairs={{0,8},{4,12},{8,16},{12,20},{16,24},{20,28},{24,0},{28,4},{1,9},{5... | collective-permute-start | bytes 663560 | tf_op jit(solution)/shard_map/rows/ppermute | solution.py:62
  12.2 14.5 %collective-permute-start.7 = (bf16[144,768]{1,0:T(8,128)(2,1)S(1)}, bf16[144,768]{1,0:T(8,128)(2,1)S(1)}, u32[]{:S(2)}, u32[]{:S(2)}) collective-permute-start(bf16[144,768]{1,0:T(8,128)(2,1)S(1)} %get-tuple-element.63), channel_id=1, source_target_pairs={{0,24},{4,28},{8,0},{12,4},{16,8},{20,12},{24,16},{28,20},{1,25},{... | collective-permute-start | bytes 663560 | tf_op jit(solution)/shard_map/rows/ppermute | solution.py:62
  16.9 9.9 %collective-permute-start.3 = (bf16[144,768]{1,0:T(8,128)(2,1)S(1)}, bf16[144,768]{1,0:T(8,128)(2,1)S(1)}, u32[]{:S(2)}, u32[]{:S(2)}) collective-permute-start(bf16[144,768]{1,0:T(8,128)(2,1)S(1)} %slice.32), channel_id=1, source_target_pairs={{0,1},{1,2},{2,3},{3,0},{4,5},{5,6},{6,7},{7,4},{8,9},{9,10},{10,1... | collective-permute-start | bytes 663560 | tf_op jit(solution)/shard_map/weights/ppermute | solution.py:62
  17.3 9.5 %collective-permute-start.5 = (bf16[128,768]{1,0:T(8,128)(2,1)S(1)}, bf16[128,768]{1,0:T(8,128)(2,1)S(1)}, u32[]{:S(2)}, u32[]{:S(2)}) collective-permute-start(bf16[128,768]{1,0:T(8,128)(2,1)S(1)} %slice.33), channel_id=1, source_target_pairs={{0,3},{1,0},{2,1},{3,2},{4,7},{5,4},{6,5},{7,6},{8,11},{9,8},{10,9... | collective-permute-start | bytes 589832 | tf_op jit(solution)/shard_map/weights/ppermute | solution.py:62
  20.3 14.3 %collective-permute-start = (bf16[96,768]{1,0:T(8,128)(2,1)S(1)}, bf16[96,768]{1,0:T(8,128)(2,1)S(1)}, u32[]{:S(2)}, u32[]{:S(2)}) collective-permute-start(bf16[96,768]{1,0:T(8,128)(2,1)S(1)} %get-tuple-element.59), channel_id=1, source_target_pairs={{0,4},{4,8},{8,12},{12,16},{16,20},{20,24},{24,28},{28,0},{1,5},{5... | collective-permute-start | bytes 442376 | tf_op jit(solution)/shard_map/rows/ppermute | solution.py:62
  22.2 12.4 %collective-permute-start.1 = (bf16[96,768]{1,0:T(8,128)(2,1)S(1)}, bf16[96,768]{1,0:T(8,128)(2,1)S(1)}, u32[]{:S(2)}, u32[]{:S(2)}) collective-permute-start(bf16[96,768]{1,0:T(8,128)(2,1)S(1)} %get-tuple-element.60), channel_id=1, source_target_pairs={{0,28},{4,0},{8,4},{12,8},{16,12},{20,16},{24,20},{28,24},{1,29},{... | collective-permute-start | bytes 442376 | tf_op jit(solution)/shard_map/rows/ppermute | solution.py:62
  26.8 9.9 %collective-permute-start.11 = (bf16[48,768]{1,0:T(8,128)(2,1)S(1)}, bf16[48,768]{1,0:T(8,128)(2,1)S(1)}, u32[]{:S(2)}, u32[]{:S(2)}) collective-permute-start(bf16[48,768]{1,0:T(8,128)(2,1)S(1)} %slice.29), channel_id=1, source_target_pairs={{0,24},{4,28},{8,0},{12,4},{16,8},{20,12},{24,16},{28,20},{1,25},{... | collective-permute-start | bytes 221192 | tf_op jit(solution)/shard_map/rows/ppermute | solution.py:62
  30.9 7.1 %collective-permute-start.10 = (bf16[48,768]{1,0:T(8,128)(2,1)S(1)}, bf16[48,768]{1,0:T(8,128)(2,1)S(1)}, u32[]{:S(2)}, u32[]{:S(2)}) collective-permute-start(bf16[48,768]{1,0:T(8,128)(2,1)S(1)} %slice.28), channel_id=1, source_target_pairs={{0,8},{4,12},{8,16},{12,20},{16,24},{20,28},{24,0},{28,4},{1,9},{5... | collective-permute-start | bytes 221192 | tf_op jit(solution)/shard_map/rows/ppermute | solution.py:62
  30.9 7.6 %collective-permute-start.9 = (bf16[96,768]{1,0:T(8,128)(2,1)S(1)}, bf16[96,768]{1,0:T(8,128)(2,1)S(1)}, u32[]{:S(2)}, u32[]{:S(2)}) collective-permute-start(bf16[96,768]{1,0:T(8,128)(2,1)S(1)} %slice.27), channel_id=1, source_target_pairs={{0,28},{4,0},{8,4},{12,8},{16,12},{20,16},{24,20},{28,24},{1,29},{... | collective-permute-start | bytes 442376 | tf_op jit(solution)/shard_map/rows/ppermute | solution.py:62
  38.5 7.2 %collective-permute-start.15 = (bf16[272,768]{1,0:T(8,128)(2,1)S(1)}, bf16[272,768]{1,0:T(8,128)(2,1)S(1)}, u32[]{:S(2)}, u32[]{:S(2)}) collective-permute-start(bf16[272,768]{1,0:T(8,128)(2,1)S(1)} %collective-permute-done.2.refs_1_), channel_id=1, source_target_pairs={{0,32},{32,0},{1,33},{33,1},{2,34},{34,2},{3,35},{35,3},{4,36},{36... | collective-permute-start | bytes 1253384 | tf_op jit(solution)/shard_map/weights/ppermute | solution.py:62
  45.3 6.7 %collective-permute-start.16 = (bf16[272,768]{1,0:T(8,128)(2,1)S(1)}, bf16[272,768]{1,0:T(8,128)(2,1)S(1)}, u32[]{:S(2)}, u32[]{:S(2)}) collective-permute-start(bf16[272,768]{1,0:T(8,128)(2,1)S(1)} %collective-permute-done.4.refs_1_), channel_id=1, source_target_pairs={{0,32},{32,0},{1,33},{33,1},{2,34},{34,2},{3,35},{35,3},{4,36},{36... | collective-permute-start | bytes 1253384 | tf_op jit(solution)/shard_map/weights/ppermute | solution.py:62
  47.9 12.8 %collective-permute-start.24 = (bf16[272,768]{1,0:T(8,128)(2,1)S(1)}, bf16[272,768]{1,0:T(8,128)(2,1)S(1)}, u32[]{:S(2)}, u32[]{:S(2)}) collective-permute-start(bf16[272,768]{1,0:T(8,128)(2,1)S(1)} %get-tuple-element.99), channel_id=1, source_target_pairs={{0,32},{32,0},{1,33},{33,1},{2,34},{34,2},{3,35},{35,3},{4,36},{36... | collective-permute-start | bytes 1253384 | tf_op jit(solution)/shard_map/ppermute | solution.py:62
  48.7 11.9 %collective-permute-start.26 = (bf16[128,768]{1,0:T(8,128)(2,1)S(1)}, bf16[128,768]{1,0:T(8,128)(2,1)S(1)}, u32[]{:S(2)}, u32[]{:S(2)}) collective-permute-start(bf16[128,768]{1,0:T(8,128)(2,1)S(1)} %get-tuple-element.103), channel_id=1, source_target_pairs={{0,1},{1,2},{2,3},{3,0},{4,5},{5,6},{6,7},{7,4},{8,9},{9,10},{10,1... | collective-permute-start | bytes 589832 | tf_op jit(solution)/shard_map/ppermute | solution.py:62
  48.8 11.5 %collective-permute-start.22 = (bf16[144,768]{1,0:T(8,128)(2,1)S(1)}, bf16[144,768]{1,0:T(8,128)(2,1)S(1)}, u32[]{:S(2)}, u32[]{:S(2)}) collective-permute-start(bf16[144,768]{1,0:T(8,128)(2,1)S(1)} %get-tuple-element.94), channel_id=1, source_target_pairs={{0,3},{1,0},{2,1},{3,2},{4,7},{5,4},{6,5},{7,6},{8,11},{9,8},{10,9... | collective-permute-start | bytes 663560 | tf_op jit(solution)/shard_map/ppermute | solution.py:62
  60.3 15.0 %collective-permute-start.23 = (bf16[272,768]{1,0:T(8,128)(2,1)S(1)}, bf16[272,768]{1,0:T(8,128)(2,1)S(1)}, u32[]{:S(2)}, u32[]{:S(2)}) collective-permute-start(bf16[272,768]{1,0:T(8,128)(2,1)S(1)} %get-tuple-element.97), channel_id=1, source_target_pairs={{0,32},{32,0},{1,33},{33,1},{2,34},{34,2},{3,35},{35,3},{4,36},{36... | collective-permute-start | bytes 1253384 | tf_op jit(solution)/shard_map/ppermute | solution.py:62
  61.4 13.9 %collective-permute-start.27 = (bf16[272,768]{1,0:T(8,128)(2,1)S(1)}, bf16[272,768]{1,0:T(8,128)(2,1)S(1)}, u32[]{:S(2)}, u32[]{:S(2)}) collective-permute-start(bf16[272,768]{1,0:T(8,128)(2,1)S(1)} %get-tuple-element.104), channel_id=1, source_target_pairs={{0,3},{1,0},{2,1},{3,2},{4,7},{5,4},{6,5},{7,6},{8,11},{9,8},{10,9... | collective-permute-start | bytes 1253384 | tf_op jit(solution)/shard_map/weights_x/ppermute | solution.py:62
  63.0 12.7 %collective-permute-start.28 = (bf16[272,768]{1,0:T(8,128)(2,1)S(1)}, bf16[272,768]{1,0:T(8,128)(2,1)S(1)}, u32[]{:S(2)}, u32[]{:S(2)}) collective-permute-start(bf16[272,768]{1,0:T(8,128)(2,1)S(1)} %get-tuple-element.105), channel_id=1, source_target_pairs={{0,1},{1,2},{2,3},{3,0},{4,5},{5,6},{6,7},{7,4},{8,9},{9,10},{10,1... | collective-permute-start | bytes 1253384 | tf_op jit(solution)/shard_map/weights_x/ppermute | solution.py:62
  64.1 10.5 %collective-permute-start.19 = (bf16[128,768]{1,0:T(8,128)(2,1)S(1)}, bf16[128,768]{1,0:T(8,128)(2,1)S(1)}, u32[]{:S(2)}, u32[]{:S(2)}) collective-permute-start(bf16[128,768]{1,0:T(8,128)(2,1)S(1)} %get-tuple-element.92), channel_id=1, source_target_pairs={{0,28},{4,0},{8,4},{12,8},{16,12},{20,16},{24,20},{28,24},{32,36},... | collective-permute-start | bytes 589832 | tf_op jit(solution)/shard_map/rows_back/ppermute | solution.py:72
  64.2 6.6 %collective-permute-start.20 = (bf16[64,768]{1,0:T(8,128)(2,1)S(1)}, bf16[64,768]{1,0:T(8,128)(2,1)S(1)}, u32[]{:S(2)}, u32[]{:S(2)}) collective-permute-start(bf16[64,768]{1,0:T(8,128)(2,1)S(1)} %get-tuple-element.93), channel_id=1, source_target_pairs={{0,24},{4,28},{8,0},{12,4},{16,8},{20,12},{24,16},{28,20},{32,40},... | collective-permute-start | bytes 294920 | tf_op jit(solution)/shard_map/rows_back/ppermute | solution.py:72
  70.9 13.2 %collective-permute-start.18 = (bf16[128,768]{1,0:T(8,128)(2,1)S(1)}, bf16[128,768]{1,0:T(8,128)(2,1)S(1)}, u32[]{:S(2)}, u32[]{:S(2)}) collective-permute-start(bf16[128,768]{1,0:T(8,128)(2,1)S(1)} %get-tuple-element.91), channel_id=1, source_target_pairs={{0,28},{4,0},{8,4},{12,8},{16,12},{20,16},{24,20},{28,24},{32,36},... | collective-permute-start | bytes 589832 | tf_op jit(solution)/shard_map/rows_back/ppermute | solution.py:72
  75.3 7.0 %collective-permute-start.21 = (bf16[128,768]{1,0:T(8,128)(2,1)S(1)}, bf16[128,768]{1,0:T(8,128)(2,1)S(1)}, u32[]{:S(2)}, u32[]{:S(2)}) collective-permute-start(bf16[128,768]{1,0:T(8,128)(2,1)S(1)} %rows_back.3), channel_id=1, source_target_pairs={{0,24},{4,28},{8,0},{12,4},{16,8},{20,12},{24,16},{28,20},{32,40},... | collective-permute-start | bytes 589832 | tf_op jit(solution)/shard_map/rows_back/ppermute | solution.py:72
  76.7 7.4 %collective-permute-start.29 = (bf16[80,768]{1,0:T(8,128)(2,1)S(1)}, bf16[80,768]{1,0:T(8,128)(2,1)S(1)}, u32[]{:S(2)}, u32[]{:S(2)}) collective-permute-start(bf16[80,768]{1,0:T(8,128)(2,1)S(1)} %get-tuple-element.106), channel_id=1, source_target_pairs={{0,128},{64,192},{128,0},{192,64},{1,129},{65,193},{129,1},{193,65... | collective-permute-start | bytes 368648 | tf_op jit(solution)/shard_map/weights_y/ppermute | solution.py:62
  (17 other events, 77.0 us)

commit v9 on v8

--- a/solution.py
+++ b/solution.py
@@ -52,7 +52,7 @@
         in_specs=specs,
         out_specs=(VMEM,) * len(out),
         scratch_shapes=[s if t is None else pltpu.VMEM(s, t) for s, t in scratch],
-        compiler_params=pltpu.CompilerParams(vmem_limit_bytes=16 * 1024 * 1024),
+        compiler_params=pltpu.CompilerParams(vmem_limit_bytes=18 * 1024 * 1024),
         cost_estimate=pl.CostEstimate(flops=2 * 10**9, bytes_accessed=1 << 20, transcendentals=0),
     )(*args)
 
@@ -72,18 +72,18 @@
     return lax.ppermute(x, ("core", axis), pairs)
 
 
-def prepare_kernel(place, lw, cw, w, part, raw, top, kids, sems):
-    copies = [
-        pltpu.make_async_copy(lw, raw, sems.at[0]),
-        pltpu.make_async_copy(cw, top, sems.at[1]),
-    ]
-    for c in copies:
-        c.start()
-    for c in copies:
-        c.wait()
-    for c in range(CL):
+def prepare_kernel(place, counts, inst, clus, prefix, e, want, lw, cw, *refs):
+    (w, part, up1, dn1, up2, dn2, s0), refs = refs[:7], refs[7:]
+    n, i, c, a, ev, wv, raw, top, kids, rows, side, sems = refs
+    pairs = ((counts, n), (inst, i), (clus, c), (prefix, a), (e, ev), (want, wv), (lw, raw), (cw, top))
+    copies = [pltpu.make_async_copy(x, v, sems.at[k]) for k, (x, v) in enumerate(pairs)]
+    for copy in copies:
+        copy.start()
+    for copy in copies:
+        copy.wait()
+    for k in range(CL):
         for j in range(D // 128):
-            kids[j, pl.ds(c, KIDS, stride=CL)] = raw[c, :, j * 128 : j * 128 + 128].astype(F32)
+            kids[j, pl.ds(k, KIDS, stride=CL)] = raw[k, :, j * 128 : j * 128 + 128].astype(F32)
     for y in range(NY):
         for core in range(NC):
             to, at = core * PART + y * 64, (y * NC + core) * 64
@@ -91,16 +91,6 @@
                 w[to : to + 64, j * 128 : j * 128 + 128] = kids[j, at : at + 64].astype(BF16)
     w[TOP : TOP + CL] = top[...]
     part[...] = w[pl.ds(pl.multiple_of(place[1] * TOP, 16), PART)]
-
-
-def load_kernel(place, counts, inst, clus, prefix, e, want, *refs):
-    (up1, dn1, up2, dn2, s0), (n, i, c, a, ev, wv, rows, side, sems) = refs[:5], refs[5:]
-    pairs = ((counts, n), (inst, i), (clus, c), (prefix, a), (e, ev), (want, wv))
-    copies = [pltpu.make_async_copy(x, v, sems.at[k]) for k, (x, v) in enumerate(pairs)]
-    for copy in copies:
-        copy.start()
-    for copy in copies:
-        copy.wait()
     cap = inst.shape[1]
     rows[...] = jnp.zeros(rows.shape, F32)
     lane = lax.broadcasted_iota(jnp.int32, (1, cap), 1)
@@ -166,48 +156,69 @@
     lax.fori_loop(0, NX, step, 0)
 
 
-def owner_kernel(place, *refs, r):
-    core = place[1]
-    mine = pl.ds(pl.multiple_of(core * TOP, 16), PART)
-    other = pl.ds(pl.multiple_of((1 - core) * TOP, 16), PART)
-    if r == 2:
-        blocks, (n1, n2, f1, f2, ay1, ay2, a, b, dzs, e, w, z) = refs[:9], refs[9:]
-        for d in range(NZ):
-            to = d * INST
-            for ref, lo, n in ROW_AT[d]:
-                e[to : to + n] = blocks[ref][lo : lo + n]
-                to += n
-        for at, p1, p2 in ((core, n1, n2), (1 - core, f1, f2)):
-            w[pl.ds(pl.multiple_of(at * TOP, 16), CUT)] = p1[...]
-            w[pl.ds(pl.multiple_of(at * TOP + CUT, 16), PART - CUT)] = p2[...]
-    elif r == 0:
-        e, w, ay1, ay2, a, b, dzs, z = refs
-    else:
-        e, near, far, ay1, ay2, a, b, dzs, w, z = refs
-        w[mine] = near[...]
-        w[other] = far[...]
-    z[...] = dot(w[...], e[...], NT)
+def owner_terms(r, e, w, ay1, ay2, dzs, z):
     top = pl.ds(TOP, CL)
-    for ay, lanes in ((ay1, pl.ds(0, 256)), (ay2, pl.ds(256, 256))):
-        s1 = jax.nn.sigmoid(z[top, lanes])
+    halves = ((ay1, pl.ds(0, 256)), (ay2, pl.ds(256, 256)))
+    for (ay, lanes), zh in zip(halves, z):
+        zh[...] = dot(w[...], e[lanes], NT)
+    for (ay, lanes), zh in zip(halves, z):
+        s1 = jax.nn.sigmoid(zh[top])
         s1a = s1 * ay[r, top]
         total = jnp.zeros((CL, 256), F32)
         for k in range(KIDS + 1):
             if k * CL == TOP:
                 continue
             at = pl.ds(k * CL, CL)
-            s2 = jax.nn.sigmoid(z[at, lanes])
+            s2 = jax.nn.sigmoid(zh[at])
             t = s2 * (s1a * s2 - ay[r, at])
             total = total + t
             dzs[at, lanes] = (s1 * (1.0 - s2) * t).astype(BF16)
         dzs[top, lanes] = (total * s1 * (1.0 - s1)).astype(BF16)
+
+
+def weight_terms(core, e, dzs, a, b):
+    mine = pl.ds(pl.multiple_of(core * TOP, 16), PART)
+    other = pl.ds(pl.multiple_of((1 - core) * TOP, 16), PART)
     b[...] = dot(dzs[other], e[...], NN).astype(BF16)
     a[...] = dot(dzs[mine], e[...], NN).astype(a.dtype)
 
 
+def across_kernel(place, *refs):
+    blocks, (n1, n2, f1, f2, ay1, ay2, a, b, dzs, e, w), z = refs[:9], refs[9:20], refs[20:]
+    for d in range(NZ):
+        to = d * INST
+        for ref, lo, n in ROW_AT[d]:
+            e[to : to + n] = blocks[ref][lo : lo + n]
+            to += n
+    core = place[1]
+    for at, p1, p2 in ((core, n1, n2), (1 - core, f1, f2)):
+        w[pl.ds(pl.multiple_of(at * TOP, 16), CUT)] = p1[...]
+        w[pl.ds(pl.multiple_of(at * TOP + CUT, 16), PART - CUT)] = p2[...]
+    owner_terms(2, e, w, ay1, ay2, dzs, z)
+    weight_terms(core, e, dzs, a, b)
+
+
+def beside_kernel(place, e, n1, f1, n3, f3, ay1, ay2, a1, a3, b, dz1, dz3, w1, w3, *z):
+    core = place[1]
+    for r, near, far, a, lo, dzs, w in ((1, n1, f1, a1, 0, dz1, w1), (3, n3, f3, a3, PART, dz3, w3)):
+        w[pl.ds(pl.multiple_of(core * TOP, 16), PART)] = near[...]
+        w[pl.ds(pl.multiple_of((1 - core) * TOP, 16), PART)] = far[...]
+        owner_terms(r, e, w, ay1, ay2, dzs, z)
+        weight_terms(core, e, dzs, a, b.at[pl.ds(lo, PART)])
+
+
+def own_kernel(place, e, w, ay1, ay2, dz1, dz2, dz3, w1, w2, w3, a, b, near, last, far, own, *refs):
+    z, dz0, ge = refs[:2], refs[2], refs[3]
+    owner_terms(0, e, w, ay1, ay2, dz0, z)
+    weight_terms(place[1], e, dz0, a, b)
+    rows_kernel(place, dz0, dz1, dz2, dz3, w, w1, w2, w3, near, last, far, own, ge)
+
+
 def rows_kernel(place, *refs):
     dzs, ws, (near, last, far, own, ge) = refs[:NX], refs[NX : 2 * NX], refs[2 * NX :]
-    ge[...] = sum(dot(dzs[r][...], ws[r][...], TN) for r in range(NX))
+    kids = (pl.ds(0, TOP), pl.ds(TOP + CL, TOP))
+    tops = [jnp.concatenate([v[TOP : TOP + CL] for v in vs], axis=0) for vs in (dzs, ws)]
+    ge[...] = dot(*tops, TN) + sum(dot(dzs[r][k], ws[r][k], TN) for r in range(NX) for k in kids)
 
     def block(d):
         at = jnp.where(place[1] == 0, ORDER.index(d), ORDER.index(-d % NZ))
@@ -237,7 +248,8 @@
     high[...] = (a[CUT:] + b[CUT:].astype(F32)).astype(BF16)
 
 
-def merge_kernel(place, a1, b1, a3, b3, low, high, t1, t3):
+def merge_kernel(place, a1, a3, b, low, high, t1, t3):
+    b1, b3 = b.at[pl.ds(0, PART)], b.at[pl.ds(PART, PART)]
     t1[:CUT] = (a1[:CUT] + b1[:CUT].astype(F32) + low[...].astype(F32)).astype(BF16)
     t1[CUT:] = (a1[CUT:] + b1[CUT:].astype(F32)).astype(BF16)
     t3[:CUT] = (a3[:CUT] + b3[:CUT].astype(F32)).astype(BF16)
@@ -276,44 +288,35 @@
     iy, ic, iz, ix = (lax.axis_index(n) for n in ("y", "core", "z", "x"))
     place = jnp.stack([ix, ic, iz, iy]).astype(jnp.int32)
 
+    cap = prefix.shape[-1]
+    owners = NZ * NX
+    want = jnp.swapaxes(targets.reshape(owners, cap, KIDS), 1, 2)
+    flat = tuple(v.reshape(owners, cap) for v in (inst, clus, prefix))
+    w, part, up1, dn1, up2, dn2, s0 = call(
+        prepare_kernel,
+        [((n, D), BF16) for n in (WIDE, PART, 96, 96, 144, 144, 32)],
+        (place, counts.reshape(owners)) + flat + (e, want, lw, cw),
+        [
+            (pltpu.SMEM((owners,), jnp.int32), None),
+            ((owners, cap), jnp.int32),
+            ((owners, cap), jnp.int32),
+            ((owners, cap), BF16),
+            ((INST, D), BF16),
+            ((owners, KIDS, cap), BF16),
+            ((CL, KIDS, D), BF16),
+            ((CL, D), BF16),
+            ((D // 128, KIDS * CL, 128), F32),
+            ((owners * 8, 128), F32),
+            ((NZ, 32, 128), BF16),
+            (pltpu.SemaphoreType.DMA((8,)), None),
+        ],
+        own=8,
+    )
     with jax.named_scope("weights"):
-        w, part = call(
-            prepare_kernel,
-            [((WIDE, D), BF16), ((PART, D), BF16)],
-            (place, lw, cw),
-            [
-                ((CL, KIDS, D), BF16),
-                ((CL, D), BF16),
-                ((D // 128, KIDS * CL, 128), F32),
-                (pltpu.SemaphoreType.DMA((2,)), None),
-            ],
-            own=2,
-        )
         low, high = shift(part, "x", 1), shift(part, "x", -1)
         low2, high2 = shift(low[:CUT], "x", 1), shift(high[CUT:], "x", -1)
 
     with jax.named_scope("rows"):
-        cap = prefix.shape[-1]
-        owners = NZ * NX
-        want = jnp.swapaxes(targets.reshape(owners, cap, KIDS), 1, 2)
-        flat = tuple(v.reshape(owners, cap) for v in (inst, clus, prefix))
-        up1, dn1, up2, dn2, s0 = call(
-            load_kernel,
-            [((n, D), BF16) for n in (96, 96, 144, 144, 32)],
-            (place, counts.reshape(owners)) + flat + (e, want),
-            [
-                (pltpu.SMEM((owners,), jnp.int32), None),
-                ((owners, cap), jnp.int32),
-                ((owners, cap), jnp.int32),
-                ((owners, cap), BF16),
-                ((INST, D), BF16),
-                ((owners, KIDS, cap), BF16),
-                ((owners * 8, 128), F32),
-                ((NZ, 32, 128), BF16),
-                (pltpu.SemaphoreType.DMA((6,)), None),
-            ],
-            own=6,
-        )
         up2, dn2 = shift(up2, "z", 2), shift(dn2, "z", -2)
         up1, dn1 = shift(up1, "z", 1), shift(dn1, "z", -1)
         low2, high2, up2, dn2 = lax.optimization_barrier((low2, high2, up2, dn2))
@@ -334,38 +337,38 @@
         low2, high2, up4, dn4, ay1 = lax.optimization_barrier((low2, high2, up4, dn4, ay1))
         low_o, high_o, low2_o, high2_o = (swap(p) for p in (low, high, low2, high2))
     ay2 = sum_slots((dn2, up3, dn3, up4, dn4), SLOT_AT[1])
-    blocks, ay = (e, up1, dn1, up2, dn2, up3, dn3, up4, dn4), (ay1, ay2)
-
     wide, dzs = ((WIDE, D), BF16), ((WIDE, ROWS), BF16)
     half, half32 = ((PART, D), BF16), ((PART, D), F32)
-    z = [((WIDE, ROWS), F32)]
+    z = [((WIDE, 256), F32)] * 2
 
     a2, b2, dz2, rows, w2 = call(
-        owner_kernel,
+        across_kernel,
         [half32, half, dzs, ((ROWS, D), BF16), wide],
-        (place,) + blocks + (low2, high2, low2_o, high2_o) + ay,
+        (place, e, up1, dn1, up2, dn2, up3, dn3, up4, dn4, low2, high2, low2_o, high2_o, ay1, ay2),
         z,
-        r=2,
     )
     with jax.named_scope("weights_x"):
         down, up = call(
             cut_kernel, [((CUT, D), BF16), ((PART - CUT, D), BF16)], (place, a2, swap(b2))
         )
-    outs = [half32, half, dzs, wide]
-    a1, b1, dz1, w1 = call(owner_kernel, outs, (place, rows, low, low_o) + ay, z, r=1)
-    b1 = swap(b1)
+    a1, a3, b13, dz1, dz3, w1, w3 = call(
+        beside_kernel,
+        [half32, half32, ((2 * PART, D), BF16), dzs, dzs, wide, wide],
+        (place, rows, low, low_o, high, high_o, ay1, ay2),
+        z,
+    )
+    b13 = swap(b13)
     rows, down, up = lax.optimization_barrier((rows, down, up))
     down, up = shift(down, "x", -1), shift(up, "x", 1)
-    a3, b3, dz3, w3 = call(owner_kernel, outs, (place, rows, high, high_o) + ay, z, r=3)
-    b3 = swap(b3)
-    a0, b0, dz0 = call(owner_kernel, [half, half, dzs], (place, rows, w) + ay, z, r=0)
+    block = ((INST, D), BF16)
+    three = ((3 * INST, D), BF16)
+    a0, b0, near, last, far, own = call(
+        own_kernel,
+        [half, half, three, block, three, ((INST, D), F32)],
+        (place, rows, w, ay1, ay2, dz1, dz2, dz3, w1, w2, w3),
+        z + [dzs, ((ROWS, D), F32)],
+    )
     b0 = swap(b0)
-    near, last, far, own = call(
-        rows_kernel,
-        [((3 * INST, D), BF16), ((INST, D), BF16), ((3 * INST, D), BF16), ((INST, D), F32)],
-        (place, dz0, dz1, dz2, dz3, w, w1, w2, w3),
-        [((ROWS, D), F32)],
-    )
 
     with jax.named_scope("rows_back"):
         last = turn(last, "z", -2)
@@ -376,7 +379,7 @@
 
     with jax.named_scope("weights_x"):
         down, a0 = lax.optimization_barrier((down, a0))
-        t1, t3 = call(merge_kernel, [half, half], (place, a1, b1, a3, b3, down, up))
+        t1, t3 = call(merge_kernel, [half, half], (place, a1, a3, b13, down, up))
         t1, t3 = shift(t1, "x", -1), shift(t3, "x", 1)
 
     with jax.named_scope("rows_back"):

time: 88.5 us -> 94.1 us (1.063)
  local copies, waits for them, and re-layouts: 1.98 us -> 6.58 us
  Pallas kernels: 23.6 us -> 21.6 us
  waiting for transfers between devices: 17.4 us -> 18.9 us
    unnamed x16 -> x18, local copies, waits for them, and re-layouts: 1.9 us -> 6.5 us
    pallas_call x15 -> x12, Pallas kernels: 23.6 us -> 21.6 us  [call(): pl.pallas_call(functools.partial(kernel, **static), out_shape=tuple((jax....]
    ppermute x29 -> x28, waiting for transfers between devices: 9.52 us -> 10.7 us  [shift(): return lax.ppermute(x, axis, [(i, (i + by) % n) for i in range(n)])]
    ppermute x29 -> x28, starting transfers between devices: 38.7 us -> 39.4 us  [shift(): return lax.ppermute(x, axis, [(i, (i + by) % n) for i in range(n)])]
  transfers between devices with their start and end apart: 33 -> 32, of which waited for: 8 -> 7; matrix products, arithmetic and copies ran while one was open for 0% -> 0% of each run, Pallas kernels for 25% -> 21%
where the time goes in v9:
time: 94.1 us; the launch traced here: 93.2 us
  starting transfers between devices  44.3 us (47%)
  Pallas kernels  21.6 us (23%)
  waiting for transfers between devices  18.9 us (20%)
  local copies, waits for them, and re-layouts  6.58 us (7%)
    ppermute x28, starting transfers between devices, shift(): return lax.ppermute(x, axis, [(i, (i + by) % n) for i in range(n)])  39.4 us
    pallas_call x12, Pallas kernels, call(): pl.pallas_call(functools.partial(kernel, **static), out_shape=tuple((jax....  21.6 us
    ppermute x28, waiting for transfers between devices, shift(): return lax.ppermute(x, axis, [(i, (i + by) % n) for i in range(n)])  10.7 us
    ppermute x4, waiting for transfers between devices, turn(): return lax.ppermute(x, ('core', axis), pairs)  8.2 us
    unnamed x18, local copies, waits for them, and re-layouts  6.5 us
    ppermute x4, starting transfers between devices, turn(): return lax.ppermute(x, ('core', axis), pairs)  4.97 us
  transfers between devices with their start and end apart: 32, of which 7 were waited for; matrix products, arithmetic and copies ran while one was open for 0% of the time, Pallas kernels for 21%

profile of v9, /device:TPU:24, one launch (start us, length us, event | category | flops | bytes accessed | tf_op | source)
XLA Modules:
  0.0 93.2 jit_solution(17487335697440647565)
XLA Ops:
  7.2 2.2 %shard_map.103 = (bf16[528,768]{1,0:T(8,128)(2,1)S(1)}, bf16[272,768]{1,0:T(8,128)(2,1)S(1)}, bf16[96,768]{1,0:T(8,128)(2,1)S(1)}, bf16[96,768]{1,0:T(8,128)(2,1...) custom-call(s32[4]{0:T(128)S(1)} %pad_add_fusion.place, ...), custom_call_target="tpu_custom_call" | custom-call | flops 2000000000 | bytes 1048576 | tf_op jit(solution)/shard_map/pallas_call | solution.py:49
  11.0 1.7 %collective-permute-start.4 = (bf16[272,768]{1,0:T(8,128)(2,1)S(1)}, bf16[272,768]{1,0:T(8,128)(2,1)S(1)}, u32[]{:S(2)}, u32[]{:S(2)}) collective-permute-start(bf16[272,768]{1,0:T(8,128)(2,1)S(1)} %get-tuple-element.59), channel_id=1, source_target_pairs={{0,3},{1,0},{2,1},{3,2},{4,7},{5,4},{6,5},{7,6},{8,11},{9,8},{10,9... | collective-permute-start | bytes 1253384 | tf_op jit(solution)/shard_map/weights/ppermute | solution.py:62
  12.8 3.3 %collective-permute-start.6 = (bf16[144,768]{1,0:T(8,128)(2,1)S(1)}, bf16[144,768]{1,0:T(8,128)(2,1)S(1)}, u32[]{:S(2)}, u32[]{:S(2)}) collective-permute-start(bf16[144,768]{1,0:T(8,128)(2,1)S(1)} %get-tuple-element.60), channel_id=1, source_target_pairs={{0,8},{4,12},{8,16},{12,20},{16,24},{20,28},{24,0},{28,4},{1,9},{5... | collective-permute-start | bytes 663560 | tf_op jit(solution)/shard_map/rows/ppermute | solution.py:62
  16.1 3.0 %collective-permute-start.7 = (bf16[144,768]{1,0:T(8,128)(2,1)S(1)}, bf16[144,768]{1,0:T(8,128)(2,1)S(1)}, u32[]{:S(2)}, u32[]{:S(2)}) collective-permute-start(bf16[144,768]{1,0:T(8,128)(2,1)S(1)} %get-tuple-element.61), channel_id=1, source_target_pairs={{0,24},{4,28},{8,0},{12,4},{16,8},{20,12},{24,16},{28,20},{1,25},{... | collective-permute-start | bytes 663560 | tf_op jit(solution)/shard_map/rows/ppermute | solution.py:62
  19.1 3.1 %collective-permute-done.2.n1 = bf16[272,768]{1,0:T(8,128)(2,1)S(1)} collective-permute-done((bf16[272,768]{1,0:T(8,128)(2,1)S(1)}, bf16[272,768]{1,0:T(8,128)(2,1)S(1)}, u32[]{:S(2)}, u32[]{:S(2)}) %collective-permute-start.2) | collective-permute-done | bytes 417824 | tf_op jit(solution)/shard_map/weights/ppermute | solution.py:62
  22.5 3.0 %collective-permute-start.5 = (bf16[128,768]{1,0:T(8,128)(2,1)S(1)}, bf16[128,768]{1,0:T(8,128)(2,1)S(1)}, u32[]{:S(2)}, u32[]{:S(2)}) collective-permute-start(bf16[128,768]{1,0:T(8,128)(2,1)S(1)} %slice.33), channel_id=1, source_target_pairs={{0,3},{1,0},{2,1},{3,2},{4,7},{5,4},{6,5},{7,6},{8,11},{9,8},{10,9... | collective-permute-start | bytes 589832 | tf_op jit(solution)/shard_map/weights/ppermute | solution.py:62
  25.6 1.9 %collective-permute-start = (bf16[96,768]{1,0:T(8,128)(2,1)S(1)}, bf16[96,768]{1,0:T(8,128)(2,1)S(1)}, u32[]{:S(2)}, u32[]{:S(2)}) collective-permute-start(bf16[96,768]{1,0:T(8,128)(2,1)S(1)} %get-tuple-element.57), channel_id=1, source_target_pairs={{0,4},{4,8},{8,12},{12,16},{16,20},{20,24},{24,28},{28,0},{1,5},{5... | collective-permute-start | bytes 442376 | tf_op jit(solution)/shard_map/rows/ppermute | solution.py:62
  27.5 3.9 %collective-permute-start.1 = (bf16[96,768]{1,0:T(8,128)(2,1)S(1)}, bf16[96,768]{1,0:T(8,128)(2,1)S(1)}, u32[]{:S(2)}, u32[]{:S(2)}) collective-permute-start(bf16[96,768]{1,0:T(8,128)(2,1)S(1)} %get-tuple-element.58), channel_id=1, source_target_pairs={{0,28},{4,0},{8,4},{12,8},{16,12},{20,16},{24,20},{28,24},{1,29},{... | collective-permute-start | bytes 442376 | tf_op jit(solution)/shard_map/rows/ppermute | solution.py:62
  31.5 4.6 %collective-permute-start.11 = (bf16[48,768]{1,0:T(8,128)(2,1)S(1)}, bf16[48,768]{1,0:T(8,128)(2,1)S(1)}, u32[]{:S(2)}, u32[]{:S(2)}) collective-permute-start(bf16[48,768]{1,0:T(8,128)(2,1)S(1)} %slice.29), channel_id=1, source_target_pairs={{0,24},{4,28},{8,0},{12,4},{16,8},{20,12},{24,16},{28,20},{1,25},{... | collective-permute-start | bytes 221192 | tf_op jit(solution)/shard_map/rows/ppermute | solution.py:62
  36.7 3.7 %collective-permute-start.9 = (bf16[96,768]{1,0:T(8,128)(2,1)S(1)}, bf16[96,768]{1,0:T(8,128)(2,1)S(1)}, u32[]{:S(2)}, u32[]{:S(2)}) collective-permute-start(bf16[96,768]{1,0:T(8,128)(2,1)S(1)} %slice.27), channel_id=1, source_target_pairs={{0,28},{4,0},{8,4},{12,8},{16,12},{20,16},{24,20},{28,24},{1,29},{... | collective-permute-start | bytes 442376 | tf_op jit(solution)/shard_map/rows/ppermute | solution.py:62
  40.4 2.1 %shard_map.104.refs_13_.ay1 = f32[4,528,256]{2,1,0:T(8,128)S(1)} custom-call(s32[4]{0:T(128)S(1)} %pad_add_fusion.place, bf16[32,768]{1,0:T(8,128)(2,1)S(1)} %get-tuple-element.66.refs_0_, bf16[96,768]{1,0:T(8,128)(2,1)S(1)} %collective-permute-done.refs_1_, bf16[96,768]{1,0:T(8,128)(2,1)S(1)} %collective-permute-done.1.refs_2_, ...), custom_call_target="tpu_custom_call" | custom-call | flops 2000000000 | bytes 1048576 | tf_op jit(solution)/shard_map/pallas_call | solution.py:49
  42.5 2.1 %collective-permute-done.10.refs_3_.refs_7_ = bf16[48,768]{1,0:T(8,128)(2,1)S(1)} collective-permute-done((bf16[48,768]{1,0:T(8,128)(2,1)S(1)}, bf16[48,768]{1,0:T(8,128)(2,1)S(1)}, u32[]{:S(2)}, u32[]{:S(2)}) %collective-permute-start.10) | collective-permute-done | bytes 73760 | tf_op jit(solution)/shard_map/rows/ppermute | solution.py:62
  45.1 2.2 %collective-permute-done.8.refs_1_.refs_5_ = bf16[96,768]{1,0:T(8,128)(2,1)S(1)} collective-permute-done((bf16[96,768]{1,0:T(8,128)(2,1)S(1)}, bf16[96,768]{1,0:T(8,128)(2,1)S(1)}, u32[]{:S(2)}, u32[]{:S(2)}) %collective-permute-start.8) | collective-permute-done | bytes 147488 | tf_op jit(solution)/shard_map/rows/ppermute | solution.py:62
  47.3 2.1 %shard_map.105.refs_14_.ay2 = f32[4,528,256]{2,1,0:T(8,128)S(1)} custom-call(s32[4]{0:T(128)S(1)} %pad_add_fusion.place, bf16[144,768]{1,0:T(8,128)(2,1)S(1)} %collective-permute-done.7.refs_0_.refs_4_, bf16[96,768]{1,0:T(8,128)(2,1)S(1)} %collective-permute-done.8.refs_1_.refs_5_, bf16[96,768]{1,0:T(8,128)(2,1)S(1)} %collective-permute-done.9.refs_2_.refs_6_, ...), custom_call_target="tpu_custom_call" | custom-call | flops 2000000000 | bytes 1048576 | tf_op jit(solution)/shard_map/pallas_call | solution.py:49
  49.4 2.1 %shard_map.106 = (f32[272,768]{1,0:T(8,128)S(1)}, bf16[272,768]{1,0:T(8,128)(2,1)S(1)}, bf16[528,512]{1,0:T(8,128)(2,1)S(1)}, bf16[512,768]{1,0:T(8,128)(2,1)S(1)}, bf16[528,768]{1,0:T(8,128)(2,1)S(1)}) custom-call(s32[4]{0:T(128)S(1)} %pad_add_fusion.place, bf16[64,768]{1,0:T(8,128)(2,1)S(1)} %copy-done.3, ...), custom_call_target="tpu_custom_call" | custom-call | flops 2000000000 | bytes 1048576 | tf_op jit(solution)/shard_map/pallas_call | solution.py:49
  51.6 3.5 %shard_map.107 = (f32[272,768]{1,0:T(8,128)S(1)}, f32[272,768]{1,0:T(8,128)S(1)}, bf16[544,768]{1,0:T(8,128)(2,1)S(1)}, bf16[528,512]{1,0:T(8,128)(2,1)S(1)}, bf...) custom-call(s32[4]{0:T(128)S(1)} %pad_add_fusion.place, ...), custom_call_target="tpu_custom_call" | custom-call | flops 2000000000 | bytes 1048576 | tf_op jit(solution)/shard_map/pallas_call | solution.py:49
  56.5 3.1 %collective-permute-start.22 = (bf16[144,768]{1,0:T(8,128)(2,1)S(1)}, bf16[144,768]{1,0:T(8,128)(2,1)S(1)}, u32[]{:S(2)}, u32[]{:S(2)}) collective-permute-start(bf16[144,768]{1,0:T(8,128)(2,1)S(1)} %get-tuple-element.91), channel_id=1, source_target_pairs={{0,3},{1,0},{2,1},{3,2},{4,7},{5,4},{6,5},{7,6},{8,11},{9,8},{10,9... | collective-permute-start | bytes 663560 | tf_op jit(solution)/shard_map/ppermute | solution.py:62
  59.7 4.8 %shard_map.108 = (bf16[272,768]{1,0:T(8,128)(2,1)S(1)}, bf16[272,768]{1,0:T(8,128)(2,1)S(1)}, bf16[192,768]{1,0:T(8,128)(2,1)S(1)}, bf16[64,768]{1,0:T(8,128)(2,...) custom-call(s32[4]{0:T(128)S(1)} %pad_add_fusion.place, bf16[512,768]{1,0:T(8,128)(2,1)S(1)} %get-tuple-element.77.e, ...), custom_call_target="tpu_custom_call" | custom-call | flops 2000000000 | bytes 1048576 | tf_op jit(solution)/shard_map/pallas_call | solution.py:49
  65.8 3.0 %collective-permute-start.26 = (bf16[272,768]{1,0:T(8,128)(2,1)S(1)}, bf16[272,768]{1,0:T(8,128)(2,1)S(1)}, u32[]{:S(2)}, u32[]{:S(2)}) collective-permute-start(bf16[272,768]{1,0:T(8,128)(2,1)S(1)} %get-tuple-element.100), channel_id=1, source_target_pairs={{0,3},{1,0},{2,1},{3,2},{4,7},{5,4},{6,5},{7,6},{8,11},{9,8},{10,9... | collective-permute-start | bytes 1253384 | tf_op jit(solution)/shard_map/weights_x/ppermute | solution.py:62
  70.7 5.6 %collective-permute-done.20.got4 = bf16[64,768]{1,0:T(8,128)(2,1)S(1)} collective-permute-done((bf16[64,768]{1,0:T(8,128)(2,1)S(1)}, bf16[64,768]{1,0:T(8,128)(2,1)S(1)}, u32[]{:S(2)}, u32[]{:S(2)}) %collective-permute-start.20) | collective-permute-done | bytes 98336 | tf_op jit(solution)/shard_map/rows_back/ppermute | solution.py:72
  76.4 3.5 %collective-permute-start.18 = (bf16[128,768]{1,0:T(8,128)(2,1)S(1)}, bf16[128,768]{1,0:T(8,128)(2,1)S(1)}, u32[]{:S(2)}, u32[]{:S(2)}) collective-permute-start(bf16[128,768]{1,0:T(8,128)(2,1)S(1)} %get-tuple-element.88), channel_id=1, source_target_pairs={{0,28},{4,0},{8,4},{12,8},{16,12},{20,16},{24,20},{28,24},{32,36},... | collective-permute-start | bytes 589832 | tf_op jit(solution)/shard_map/rows_back/ppermute | solution.py:72
  82.9 2.2 %collective-permute-start.30 = (bf16[80,768]{1,0:T(8,128)(2,1)S(1)}, bf16[80,768]{1,0:T(8,128)(2,1)S(1)}, u32[]{:S(2)}, u32[]{:S(2)}) collective-permute-start(bf16[80,768]{1,0:T(8,128)(2,1)S(1)} %get-tuple-element.106), channel_id=1, source_target_pairs={{0,64},{64,128},{128,192},{192,0},{1,65},{65,129},{129,193},{193,1... | collective-permute-start | bytes 368648 | tf_op jit(solution)/shard_map/weights_y/ppermute | solution.py:62
  85.1 2.6 %collective-permute-done.21 = bf16[128,768]{1,0:T(8,128)(2,1)S(1)} collective-permute-done((bf16[128,768]{1,0:T(8,128)(2,1)S(1)}, bf16[128,768]{1,0:T(8,128)(2,1)S(1)}, u32[]{:S(2)}, u32[]{:S(2)}) %collective-permute-start.21) | collective-permute-done | bytes 196640 | tf_op jit(solution)/shard_map/rows_back/ppermute | solution.py:72
  88.4 2.8 %collective-permute-done.31.g3 = bf16[80,768]{1,0:T(8,128)(2,1)S(1)} collective-permute-done((bf16[80,768]{1,0:T(8,128)(2,1)S(1)}, bf16[80,768]{1,0:T(8,128)(2,1)S(1)}, u32[]{:S(2)}, u32[]{:S(2)}) %collective-permute-start.31) | collective-permute-done | bytes 122912 | tf_op jit(solution)/shard_map/weights_y/ppermute | solution.py:62
  (80 shorter events, 20.2 us)
Async XLA Ops:
  9.5 12.7 %collective-permute-start.2 = (bf16[272,768]{1,0:T(8,128)(2,1)S(1)}, bf16[272,768]{1,0:T(8,128)(2,1)S(1)}, u32[]{:S(2)}, u32[]{:S(2)}) collective-permute-start(bf16[272,768]{1,0:T(8,128)(2,1)S(1)} %get-tuple-element.59), channel_id=1, source_target_pairs={{0,1},{1,2},{2,3},{3,0},{4,5},{5,6},{6,7},{7,4},{8,9},{9,10},{10,1... | collective-permute-start | bytes 1253384 | tf_op jit(solution)/shard_map/weights/ppermute | solution.py:62
  11.0 11.5 %collective-permute-start.4 = (bf16[272,768]{1,0:T(8,128)(2,1)S(1)}, bf16[272,768]{1,0:T(8,128)(2,1)S(1)}, u32[]{:S(2)}, u32[]{:S(2)}) collective-permute-start(bf16[272,768]{1,0:T(8,128)(2,1)S(1)} %get-tuple-element.59), channel_id=1, source_target_pairs={{0,3},{1,0},{2,1},{3,2},{4,7},{5,4},{6,5},{7,6},{8,11},{9,8},{10,9... | collective-permute-start | bytes 1253384 | tf_op jit(solution)/shard_map/weights/ppermute | solution.py:62
  12.8 14.7 %collective-permute-start.6 = (bf16[144,768]{1,0:T(8,128)(2,1)S(1)}, bf16[144,768]{1,0:T(8,128)(2,1)S(1)}, u32[]{:S(2)}, u32[]{:S(2)}) collective-permute-start(bf16[144,768]{1,0:T(8,128)(2,1)S(1)} %get-tuple-element.60), channel_id=1, source_target_pairs={{0,8},{4,12},{8,16},{12,20},{16,24},{20,28},{24,0},{28,4},{1,9},{5... | collective-permute-start | bytes 663560 | tf_op jit(solution)/shard_map/rows/ppermute | solution.py:62
  16.1 15.4 %collective-permute-start.7 = (bf16[144,768]{1,0:T(8,128)(2,1)S(1)}, bf16[144,768]{1,0:T(8,128)(2,1)S(1)}, u32[]{:S(2)}, u32[]{:S(2)}) collective-permute-start(bf16[144,768]{1,0:T(8,128)(2,1)S(1)} %get-tuple-element.61), channel_id=1, source_target_pairs={{0,24},{4,28},{8,0},{12,4},{16,8},{20,12},{24,16},{28,20},{1,25},{... | collective-permute-start | bytes 663560 | tf_op jit(solution)/shard_map/rows/ppermute | solution.py:62
  22.2 9.3 %collective-permute-start.3 = (bf16[144,768]{1,0:T(8,128)(2,1)S(1)}, bf16[144,768]{1,0:T(8,128)(2,1)S(1)}, u32[]{:S(2)}, u32[]{:S(2)}) collective-permute-start(bf16[144,768]{1,0:T(8,128)(2,1)S(1)} %slice.32), channel_id=1, source_target_pairs={{0,1},{1,2},{2,3},{3,0},{4,5},{5,6},{6,7},{7,4},{8,9},{9,10},{10,1... | collective-permute-start | bytes 663560 | tf_op jit(solution)/shard_map/weights/ppermute | solution.py:62
  22.5 8.9 %collective-permute-start.5 = (bf16[128,768]{1,0:T(8,128)(2,1)S(1)}, bf16[128,768]{1,0:T(8,128)(2,1)S(1)}, u32[]{:S(2)}, u32[]{:S(2)}) collective-permute-start(bf16[128,768]{1,0:T(8,128)(2,1)S(1)} %slice.33), channel_id=1, source_target_pairs={{0,3},{1,0},{2,1},{3,2},{4,7},{5,4},{6,5},{7,6},{8,11},{9,8},{10,9... | collective-permute-start | bytes 589832 | tf_op jit(solution)/shard_map/weights/ppermute | solution.py:62
  25.6 11.0 %collective-permute-start = (bf16[96,768]{1,0:T(8,128)(2,1)S(1)}, bf16[96,768]{1,0:T(8,128)(2,1)S(1)}, u32[]{:S(2)}, u32[]{:S(2)}) collective-permute-start(bf16[96,768]{1,0:T(8,128)(2,1)S(1)} %get-tuple-element.57), channel_id=1, source_target_pairs={{0,4},{4,8},{8,12},{12,16},{16,20},{20,24},{24,28},{28,0},{1,5},{5... | collective-permute-start | bytes 442376 | tf_op jit(solution)/shard_map/rows/ppermute | solution.py:62
  27.5 9.2 %collective-permute-start.1 = (bf16[96,768]{1,0:T(8,128)(2,1)S(1)}, bf16[96,768]{1,0:T(8,128)(2,1)S(1)}, u32[]{:S(2)}, u32[]{:S(2)}) collective-permute-start(bf16[96,768]{1,0:T(8,128)(2,1)S(1)} %get-tuple-element.58), channel_id=1, source_target_pairs={{0,28},{4,0},{8,4},{12,8},{16,12},{20,16},{24,20},{28,24},{1,29},{... | collective-permute-start | bytes 442376 | tf_op jit(solution)/shard_map/rows/ppermute | solution.py:62
  31.5 8.9 %collective-permute-start.11 = (bf16[48,768]{1,0:T(8,128)(2,1)S(1)}, bf16[48,768]{1,0:T(8,128)(2,1)S(1)}, u32[]{:S(2)}, u32[]{:S(2)}) collective-permute-start(bf16[48,768]{1,0:T(8,128)(2,1)S(1)} %slice.29), channel_id=1, source_target_pairs={{0,24},{4,28},{8,0},{12,4},{16,8},{20,12},{24,16},{28,20},{1,25},{... | collective-permute-start | bytes 221192 | tf_op jit(solution)/shard_map/rows/ppermute | solution.py:62
  36.1 15.5 %collective-permute-start.16 = (bf16[272,768]{1,0:T(8,128)(2,1)S(1)}, bf16[272,768]{1,0:T(8,128)(2,1)S(1)}, u32[]{:S(2)}, u32[]{:S(2)}) collective-permute-start(bf16[272,768]{1,0:T(8,128)(2,1)S(1)} %collective-permute-done.4.n3), channel_id=1, source_target_pairs={{0,32},{32,0},{1,33},{33,1},{2,34},{34,2},{3,35},{35,3},{4,36},{36... | collective-permute-start | bytes 1253384 | tf_op jit(solution)/shard_map/weights/ppermute | solution.py:62
  36.1 15.6 %collective-permute-start.15 = (bf16[272,768]{1,0:T(8,128)(2,1)S(1)}, bf16[272,768]{1,0:T(8,128)(2,1)S(1)}, u32[]{:S(2)}, u32[]{:S(2)}) collective-permute-start(bf16[272,768]{1,0:T(8,128)(2,1)S(1)} %collective-permute-done.2.n1), channel_id=1, source_target_pairs={{0,32},{32,0},{1,33},{33,1},{2,34},{34,2},{3,35},{35,3},{4,36},{36... | collective-permute-start | bytes 1253384 | tf_op jit(solution)/shard_map/weights/ppermute | solution.py:62
  36.6 8.0 %collective-permute-start.10 = (bf16[48,768]{1,0:T(8,128)(2,1)S(1)}, bf16[48,768]{1,0:T(8,128)(2,1)S(1)}, u32[]{:S(2)}, u32[]{:S(2)}) collective-permute-start(bf16[48,768]{1,0:T(8,128)(2,1)S(1)} %slice.28), channel_id=1, source_target_pairs={{0,8},{4,12},{8,16},{12,20},{16,24},{20,28},{24,0},{28,4},{1,9},{5... | collective-permute-start | bytes 221192 | tf_op jit(solution)/shard_map/rows/ppermute | solution.py:62
  36.7 7.9 %collective-permute-start.9 = (bf16[96,768]{1,0:T(8,128)(2,1)S(1)}, bf16[96,768]{1,0:T(8,128)(2,1)S(1)}, u32[]{:S(2)}, u32[]{:S(2)}) collective-permute-start(bf16[96,768]{1,0:T(8,128)(2,1)S(1)} %slice.27), channel_id=1, source_target_pairs={{0,28},{4,0},{8,4},{12,8},{16,12},{20,16},{24,20},{28,24},{1,29},{... | collective-permute-start | bytes 442376 | tf_op jit(solution)/shard_map/rows/ppermute | solution.py:62
  40.4 6.9 %collective-permute-start.8 = (bf16[96,768]{1,0:T(8,128)(2,1)S(1)}, bf16[96,768]{1,0:T(8,128)(2,1)S(1)}, u32[]{:S(2)}, u32[]{:S(2)}) collective-permute-start(bf16[96,768]{1,0:T(8,128)(2,1)S(1)} %slice.26), channel_id=1, source_target_pairs={{0,4},{4,8},{8,12},{12,16},{16,20},{20,24},{24,28},{28,0},{1,5},{5... | collective-permute-start | bytes 442376 | tf_op jit(solution)/shard_map/rows/ppermute | solution.py:62
  55.1 10.0 %collective-permute-start.24 = (bf16[544,768]{1,0:T(8,128)(2,1)S(1)}, bf16[544,768]{1,0:T(8,128)(2,1)S(1)}, u32[]{:S(2)}, u32[]{:S(2)}) collective-permute-start(bf16[544,768]{1,0:T(8,128)(2,1)S(1)} %get-tuple-element.97), channel_id=1, source_target_pairs={{0,32},{32,0},{1,33},{33,1},{2,34},{34,2},{3,35},{35,3},{4,36},{36... | collective-permute-start | bytes 2506760 | tf_op jit(solution)/shard_map/ppermute | solution.py:62
  56.3 8.7 %collective-permute-start.25 = (bf16[128,768]{1,0:T(8,128)(2,1)S(1)}, bf16[128,768]{1,0:T(8,128)(2,1)S(1)}, u32[]{:S(2)}, u32[]{:S(2)}) collective-permute-start(bf16[128,768]{1,0:T(8,128)(2,1)S(1)} %get-tuple-element.99), channel_id=1, source_target_pairs={{0,1},{1,2},{2,3},{3,0},{4,5},{5,6},{6,7},{7,4},{8,9},{9,10},{10,1... | collective-permute-start | bytes 589832 | tf_op jit(solution)/shard_map/ppermute | solution.py:62
  56.5 8.5 %collective-permute-start.22 = (bf16[144,768]{1,0:T(8,128)(2,1)S(1)}, bf16[144,768]{1,0:T(8,128)(2,1)S(1)}, u32[]{:S(2)}, u32[]{:S(2)}) collective-permute-start(bf16[144,768]{1,0:T(8,128)(2,1)S(1)} %get-tuple-element.91), channel_id=1, source_target_pairs={{0,3},{1,0},{2,1},{3,2},{4,7},{5,4},{6,5},{7,6},{8,11},{9,8},{10,9... | collective-permute-start | bytes 663560 | tf_op jit(solution)/shard_map/ppermute | solution.py:62
  64.6 16.0 %collective-permute-start.23 = (bf16[272,768]{1,0:T(8,128)(2,1)S(1)}, bf16[272,768]{1,0:T(8,128)(2,1)S(1)}, u32[]{:S(2)}, u32[]{:S(2)}) collective-permute-start(bf16[272,768]{1,0:T(8,128)(2,1)S(1)} %get-tuple-element.94), channel_id=1, source_target_pairs={{0,32},{32,0},{1,33},{33,1},{2,34},{34,2},{3,35},{35,3},{4,36},{36... | collective-permute-start | bytes 1253384 | tf_op jit(solution)/shard_map/ppermute | solution.py:62
  65.8 14.8 %collective-permute-start.26 = (bf16[272,768]{1,0:T(8,128)(2,1)S(1)}, bf16[272,768]{1,0:T(8,128)(2,1)S(1)}, u32[]{:S(2)}, u32[]{:S(2)}) collective-permute-start(bf16[272,768]{1,0:T(8,128)(2,1)S(1)} %get-tuple-element.100), channel_id=1, source_target_pairs={{0,3},{1,0},{2,1},{3,2},{4,7},{5,4},{6,5},{7,6},{8,11},{9,8},{10,9... | collective-permute-start | bytes 1253384 | tf_op jit(solution)/shard_map/weights_x/ppermute | solution.py:62
  68.8 11.8 %collective-permute-start.27 = (bf16[272,768]{1,0:T(8,128)(2,1)S(1)}, bf16[272,768]{1,0:T(8,128)(2,1)S(1)}, u32[]{:S(2)}, u32[]{:S(2)}) collective-permute-start(bf16[272,768]{1,0:T(8,128)(2,1)S(1)} %get-tuple-element.101), channel_id=1, source_target_pairs={{0,1},{1,2},{2,3},{3,0},{4,5},{5,6},{6,7},{7,4},{8,9},{9,10},{10,1... | collective-permute-start | bytes 1253384 | tf_op jit(solution)/shard_map/weights_x/ppermute | solution.py:62
  69.4 10.5 %collective-permute-start.19 = (bf16[128,768]{1,0:T(8,128)(2,1)S(1)}, bf16[128,768]{1,0:T(8,128)(2,1)S(1)}, u32[]{:S(2)}, u32[]{:S(2)}) collective-permute-start(bf16[128,768]{1,0:T(8,128)(2,1)S(1)} %get-tuple-element.89), channel_id=1, source_target_pairs={{0,28},{4,0},{8,4},{12,8},{16,12},{20,16},{24,20},{28,24},{32,36},... | collective-permute-start | bytes 589832 | tf_op jit(solution)/shard_map/rows_back/ppermute | solution.py:72
  76.4 11.8 %collective-permute-start.18 = (bf16[128,768]{1,0:T(8,128)(2,1)S(1)}, bf16[128,768]{1,0:T(8,128)(2,1)S(1)}, u32[]{:S(2)}, u32[]{:S(2)}) collective-permute-start(bf16[128,768]{1,0:T(8,128)(2,1)S(1)} %get-tuple-element.88), channel_id=1, source_target_pairs={{0,28},{4,0},{8,4},{12,8},{16,12},{20,16},{24,20},{28,24},{32,36},... | collective-permute-start | bytes 589832 | tf_op jit(solution)/shard_map/rows_back/ppermute | solution.py:72
  80.5 7.2 %collective-permute-start.21 = (bf16[128,768]{1,0:T(8,128)(2,1)S(1)}, bf16[128,768]{1,0:T(8,128)(2,1)S(1)}, u32[]{:S(2)}, u32[]{:S(2)}) collective-permute-start(bf16[128,768]{1,0:T(8,128)(2,1)S(1)} %rows_back.3), channel_id=1, source_target_pairs={{0,24},{4,28},{8,0},{12,4},{16,8},{20,12},{24,16},{28,20},{32,40},... | collective-permute-start | bytes 589832 | tf_op jit(solution)/shard_map/rows_back/ppermute | solution.py:72
  81.6 6.6 %collective-permute-start.28 = (bf16[80,768]{1,0:T(8,128)(2,1)S(1)}, bf16[80,768]{1,0:T(8,128)(2,1)S(1)}, u32[]{:S(2)}, u32[]{:S(2)}) collective-permute-start(bf16[80,768]{1,0:T(8,128)(2,1)S(1)} %get-tuple-element.102), channel_id=1, source_target_pairs={{0,128},{64,192},{128,0},{192,64},{1,129},{65,193},{129,1},{193,65... | collective-permute-start | bytes 368648 | tf_op jit(solution)/shard_map/weights_y/ppermute | solution.py:62
  (17 other events, 53.7 us)

commit v10 on v9

--- a/solution.py
+++ b/solution.py
@@ -72,18 +72,18 @@
     return lax.ppermute(x, ("core", axis), pairs)
 
 
-def prepare_kernel(place, counts, inst, clus, prefix, e, want, lw, cw, *refs):
-    (w, part, up1, dn1, up2, dn2, s0), refs = refs[:7], refs[7:]
-    n, i, c, a, ev, wv, raw, top, kids, rows, side, sems = refs
-    pairs = ((counts, n), (inst, i), (clus, c), (prefix, a), (e, ev), (want, wv), (lw, raw), (cw, top))
-    copies = [pltpu.make_async_copy(x, v, sems.at[k]) for k, (x, v) in enumerate(pairs)]
-    for copy in copies:
-        copy.start()
-    for copy in copies:
-        copy.wait()
-    for k in range(CL):
+def prepare_kernel(place, lw, cw, w, part, raw, top, kids, sems):
+    copies = [
+        pltpu.make_async_copy(lw, raw, sems.at[0]),
+        pltpu.make_async_copy(cw, top, sems.at[1]),
+    ]
+    for c in copies:
+        c.start()
+    for c in copies:
+        c.wait()
+    for c in range(CL):
         for j in range(D // 128):
-            kids[j, pl.ds(k, KIDS, stride=CL)] = raw[k, :, j * 128 : j * 128 + 128].astype(F32)
+            kids[j, pl.ds(c, KIDS, stride=CL)] = raw[c, :, j * 128 : j * 128 + 128].astype(F32)
     for y in range(NY):
         for core in range(NC):
             to, at = core * PART + y * 64, (y * NC + core) * 64
@@ -91,6 +91,16 @@
                 w[to : to + 64, j * 128 : j * 128 + 128] = kids[j, at : at + 64].astype(BF16)
     w[TOP : TOP + CL] = top[...]
     part[...] = w[pl.ds(pl.multiple_of(place[1] * TOP, 16), PART)]
+
+
+def load_kernel(place, counts, inst, clus, prefix, e, want, *refs):
+    (up1, dn1, up2, dn2, s0), (n, i, c, a, ev, wv, rows, side, sems) = refs[:5], refs[5:]
+    pairs = ((counts, n), (inst, i), (clus, c), (prefix, a), (e, ev), (want, wv))
+    copies = [pltpu.make_async_copy(x, v, sems.at[k]) for k, (x, v) in enumerate(pairs)]
+    for copy in copies:
+        copy.start()
+    for copy in copies:
+        copy.wait()
     cap = inst.shape[1]
     rows[...] = jnp.zeros(rows.shape, F32)
     lane = lax.broadcasted_iota(jnp.int32, (1, cap), 1)
@@ -288,35 +298,44 @@
     iy, ic, iz, ix = (lax.axis_index(n) for n in ("y", "core", "z", "x"))
     place = jnp.stack([ix, ic, iz, iy]).astype(jnp.int32)
 
-    cap = prefix.shape[-1]
-    owners = NZ * NX
-    want = jnp.swapaxes(targets.reshape(owners, cap, KIDS), 1, 2)
-    flat = tuple(v.reshape(owners, cap) for v in (inst, clus, prefix))
-    w, part, up1, dn1, up2, dn2, s0 = call(
-        prepare_kernel,
-        [((n, D), BF16) for n in (WIDE, PART, 96, 96, 144, 144, 32)],
-        (place, counts.reshape(owners)) + flat + (e, want, lw, cw),
-        [
-            (pltpu.SMEM((owners,), jnp.int32), None),
-            ((owners, cap), jnp.int32),
-            ((owners, cap), jnp.int32),
-            ((owners, cap), BF16),
-            ((INST, D), BF16),
-            ((owners, KIDS, cap), BF16),
-            ((CL, KIDS, D), BF16),
-            ((CL, D), BF16),
-            ((D // 128, KIDS * CL, 128), F32),
-            ((owners * 8, 128), F32),
-            ((NZ, 32, 128), BF16),
-            (pltpu.SemaphoreType.DMA((8,)), None),
-        ],
-        own=8,
-    )
     with jax.named_scope("weights"):
+        w, part = call(
+            prepare_kernel,
+            [((WIDE, D), BF16), ((PART, D), BF16)],
+            (place, lw, cw),
+            [
+                ((CL, KIDS, D), BF16),
+                ((CL, D), BF16),
+                ((D // 128, KIDS * CL, 128), F32),
+                (pltpu.SemaphoreType.DMA((2,)), None),
+            ],
+            own=2,
+        )
         low, high = shift(part, "x", 1), shift(part, "x", -1)
         low2, high2 = shift(low[:CUT], "x", 1), shift(high[CUT:], "x", -1)
 
     with jax.named_scope("rows"):
+        cap = prefix.shape[-1]
+        owners = NZ * NX
+        want = jnp.swapaxes(targets.reshape(owners, cap, KIDS), 1, 2)
+        flat = tuple(v.reshape(owners, cap) for v in (inst, clus, prefix))
+        up1, dn1, up2, dn2, s0 = call(
+            load_kernel,
+            [((n, D), BF16) for n in (96, 96, 144, 144, 32)],
+            (place, counts.reshape(owners)) + flat + (e, want),
+            [
+                (pltpu.SMEM((owners,), jnp.int32), None),
+                ((owners, cap), jnp.int32),
+                ((owners, cap), jnp.int32),
+                ((owners, cap), BF16),
+                ((INST, D), BF16),
+                ((owners, KIDS, cap), BF16),
+                ((owners * 8, 128), F32),
+                ((NZ, 32, 128), BF16),
+                (pltpu.SemaphoreType.DMA((6,)), None),
+            ],
+            own=6,
+        )
         up2, dn2 = shift(up2, "z", 2), shift(dn2, "z", -2)
         up1, dn1 = shift(up1, "z", 1), shift(dn1, "z", -1)
         low2, high2, up2, dn2 = lax.optimization_barrier((low2, high2, up2, dn2))
@@ -383,6 +402,7 @@
         t1, t3 = shift(t1, "x", -1), shift(t3, "x", 1)
 
     with jax.named_scope("rows_back"):
+        h3, last, h1 = lax.optimization_barrier((h3, last, h1))
         (h2,) = call(pass_kernel, [pair], (place, near, far, h3, last))
         h2 = turn(h2, "z", -2)
 

time: 94.1 us -> 89.5 us (0.951)
  local copies, waits for them, and re-layouts: 6.58 us -> 1.98 us
  starting transfers between devices: 44.3 us -> 46.5 us
  waiting for transfers between devices: 18.9 us -> 16.8 us
    unnamed x18 -> x16, local copies, waits for them, and re-layouts: 6.5 us -> 1.9 us
    ppermute x4, waiting for transfers between devices: 8.2 us -> 4.67 us  [turn(): return lax.ppermute(x, ('core', axis), pairs)]
    ppermute x4, starting transfers between devices: 4.97 us -> 7.96 us  [turn(): return lax.ppermute(x, ('core', axis), pairs)]
    ppermute x28, waiting for transfers between devices: 10.7 us -> 12.2 us  [shift(): return lax.ppermute(x, axis, [(i, (i + by) % n) for i in range(n)])]
    pallas_call x12 -> x13, Pallas kernels: 21.6 us -> 22.3 us  [call(): pl.pallas_call(functools.partial(kernel, **static), out_shape=tuple((jax....]
  transfers between devices with their start and end apart: 32 -> 32, of which waited for: 7 -> 9; matrix products, arithmetic and copies ran while one was open for 0% -> 0% of each run, Pallas kernels for 21% -> 23%
where the time goes in v10:
time: 89.5 us; the launch traced here: 89.3 us
  starting transfers between devices  46.5 us (52%)
  Pallas kernels  22.3 us (25%)
  waiting for transfers between devices  16.8 us (19%)
  local copies, waits for them, and re-layouts  1.98 us (2%)
  between operations  0.92 us (1%)
    ppermute x28, starting transfers between devices, shift(): return lax.ppermute(x, axis, [(i, (i + by) % n) for i in range(n)])  38.5 us
    pallas_call x13, Pallas kernels, call(): pl.pallas_call(functools.partial(kernel, **static), out_shape=tuple((jax....  22.3 us
    ppermute x28, waiting for transfers between devices, shift(): return lax.ppermute(x, axis, [(i, (i + by) % n) for i in range(n)])  12.2 us
    ppermute x4, starting transfers between devices, turn(): return lax.ppermute(x, ('core', axis), pairs)  7.96 us
    ppermute x4, waiting for transfers between devices, turn(): return lax.ppermute(x, ('core', axis), pairs)  4.67 us
    unnamed x16, local copies, waits for them, and re-layouts  1.9 us
  transfers between devices with their start and end apart: 32, of which 9 were waited for; matrix products, arithmetic and copies ran while one was open for 0% of the time, Pallas kernels for 23%

profile of v10, /device:TPU:24, one launch (start us, length us, event | category | flops | bytes accessed | tf_op | source)
XLA Modules:
  0.0 89.3 jit_solution(2550704477826177065)
XLA Ops:
  5.8 1.7 %collective-permute-start.4 = (bf16[272,768]{1,0:T(8,128)(2,1)S(1)}, bf16[272,768]{1,0:T(8,128)(2,1)S(1)}, u32[]{:S(2)}, u32[]{:S(2)}) collective-permute-start(bf16[272,768]{1,0:T(8,128)(2,1)S(1)} %get-tuple-element.62), channel_id=1, source_target_pairs={{0,3},{1,0},{2,1},{3,2},{4,7},{5,4},{6,5},{7,6},{8,11},{9,8},{10,9... | collective-permute-start | bytes 1253384 | tf_op jit(solution)/shard_map/weights/ppermute | solution.py:62
  8.9 3.3 %collective-permute-start.6 = (bf16[144,768]{1,0:T(8,128)(2,1)S(1)}, bf16[144,768]{1,0:T(8,128)(2,1)S(1)}, u32[]{:S(2)}, u32[]{:S(2)}) collective-permute-start(bf16[144,768]{1,0:T(8,128)(2,1)S(1)} %get-tuple-element.63), channel_id=1, source_target_pairs={{0,8},{4,12},{8,16},{12,20},{16,24},{20,28},{24,0},{28,4},{1,9},{5... | collective-permute-start | bytes 663560 | tf_op jit(solution)/shard_map/rows/ppermute | solution.py:62
  12.2 3.1 %collective-permute-start.7 = (bf16[144,768]{1,0:T(8,128)(2,1)S(1)}, bf16[144,768]{1,0:T(8,128)(2,1)S(1)}, u32[]{:S(2)}, u32[]{:S(2)}) collective-permute-start(bf16[144,768]{1,0:T(8,128)(2,1)S(1)} %get-tuple-element.64), channel_id=1, source_target_pairs={{0,24},{4,28},{8,0},{12,4},{16,8},{20,12},{24,16},{28,20},{1,25},{... | collective-permute-start | bytes 663560 | tf_op jit(solution)/shard_map/rows/ppermute | solution.py:62
  17.3 3.0 %collective-permute-start.5 = (bf16[128,768]{1,0:T(8,128)(2,1)S(1)}, bf16[128,768]{1,0:T(8,128)(2,1)S(1)}, u32[]{:S(2)}, u32[]{:S(2)}) collective-permute-start(bf16[128,768]{1,0:T(8,128)(2,1)S(1)} %slice.33), channel_id=1, source_target_pairs={{0,3},{1,0},{2,1},{3,2},{4,7},{5,4},{6,5},{7,6},{8,11},{9,8},{10,9... | collective-permute-start | bytes 589832 | tf_op jit(solution)/shard_map/weights/ppermute | solution.py:62
  20.3 1.9 %collective-permute-start = (bf16[96,768]{1,0:T(8,128)(2,1)S(1)}, bf16[96,768]{1,0:T(8,128)(2,1)S(1)}, u32[]{:S(2)}, u32[]{:S(2)}) collective-permute-start(bf16[96,768]{1,0:T(8,128)(2,1)S(1)} %get-tuple-element.60), channel_id=1, source_target_pairs={{0,4},{4,8},{8,12},{12,16},{16,20},{20,24},{24,28},{28,0},{1,5},{5... | collective-permute-start | bytes 442376 | tf_op jit(solution)/shard_map/rows/ppermute | solution.py:62
  22.2 4.5 %collective-permute-start.1 = (bf16[96,768]{1,0:T(8,128)(2,1)S(1)}, bf16[96,768]{1,0:T(8,128)(2,1)S(1)}, u32[]{:S(2)}, u32[]{:S(2)}) collective-permute-start(bf16[96,768]{1,0:T(8,128)(2,1)S(1)} %get-tuple-element.61), channel_id=1, source_target_pairs={{0,28},{4,0},{8,4},{12,8},{16,12},{20,16},{24,20},{28,24},{1,29},{... | collective-permute-start | bytes 442376 | tf_op jit(solution)/shard_map/rows/ppermute | solution.py:62
  26.8 4.0 %collective-permute-start.11 = (bf16[48,768]{1,0:T(8,128)(2,1)S(1)}, bf16[48,768]{1,0:T(8,128)(2,1)S(1)}, u32[]{:S(2)}, u32[]{:S(2)}) collective-permute-start(bf16[48,768]{1,0:T(8,128)(2,1)S(1)} %slice.29), channel_id=1, source_target_pairs={{0,24},{4,28},{8,0},{12,4},{16,8},{20,12},{24,16},{28,20},{1,25},{... | collective-permute-start | bytes 221192 | tf_op jit(solution)/shard_map/rows/ppermute | solution.py:62
  31.5 3.7 %collective-permute-start.9 = (bf16[96,768]{1,0:T(8,128)(2,1)S(1)}, bf16[96,768]{1,0:T(8,128)(2,1)S(1)}, u32[]{:S(2)}, u32[]{:S(2)}) collective-permute-start(bf16[96,768]{1,0:T(8,128)(2,1)S(1)} %slice.27), channel_id=1, source_target_pairs={{0,28},{4,0},{8,4},{12,8},{16,12},{20,16},{24,20},{28,24},{1,29},{... | collective-permute-start | bytes 442376 | tf_op jit(solution)/shard_map/rows/ppermute | solution.py:62
  35.2 2.1 %shard_map.103.refs_13_.ay1 = f32[4,528,256]{2,1,0:T(8,128)S(1)} custom-call(s32[4]{0:T(128)S(1)} %pad_add_fusion.place, bf16[32,768]{1,0:T(8,128)(2,1)S(1)} %get-tuple-element.69.refs_0_, bf16[96,768]{1,0:T(8,128)(2,1)S(1)} %collective-permute-done.refs_1_, bf16[96,768]{1,0:T(8,128)(2,1)S(1)} %collective-permute-done.1.refs_2_, ...), custom_call_target="tpu_custom_call" | custom-call | flops 2000000000 | bytes 1048576 | tf_op jit(solution)/shard_map/pallas_call | solution.py:49
  37.3 2.1 %collective-permute-done.10.refs_3_.refs_7_ = bf16[48,768]{1,0:T(8,128)(2,1)S(1)} collective-permute-done((bf16[48,768]{1,0:T(8,128)(2,1)S(1)}, bf16[48,768]{1,0:T(8,128)(2,1)S(1)}, u32[]{:S(2)}, u32[]{:S(2)}) %collective-permute-start.10) | collective-permute-done | bytes 73760 | tf_op jit(solution)/shard_map/rows/ppermute | solution.py:62
  39.9 2.1 %collective-permute-done.8.refs_1_.refs_5_ = bf16[96,768]{1,0:T(8,128)(2,1)S(1)} collective-permute-done((bf16[96,768]{1,0:T(8,128)(2,1)S(1)}, bf16[96,768]{1,0:T(8,128)(2,1)S(1)}, u32[]{:S(2)}, u32[]{:S(2)}) %collective-permute-start.8) | collective-permute-done | bytes 147488 | tf_op jit(solution)/shard_map/rows/ppermute | solution.py:62
  42.0 2.1 %shard_map.104.refs_14_.ay2 = f32[4,528,256]{2,1,0:T(8,128)S(1)} custom-call(s32[4]{0:T(128)S(1)} %pad_add_fusion.place, bf16[144,768]{1,0:T(8,128)(2,1)S(1)} %collective-permute-done.7.refs_0_.refs_4_, bf16[96,768]{1,0:T(8,128)(2,1)S(1)} %collective-permute-done.8.refs_1_.refs_5_, bf16[96,768]{1,0:T(8,128)(2,1)S(1)} %collective-permute-done.9.refs_2_.refs_6_, ...), custom_call_target="tpu_custom_call" | custom-call | flops 2000000000 | bytes 1048576 | tf_op jit(solution)/shard_map/pallas_call | solution.py:49
  44.1 2.1 %shard_map.105 = (f32[272,768]{1,0:T(8,128)S(1)}, bf16[272,768]{1,0:T(8,128)(2,1)S(1)}, bf16[528,512]{1,0:T(8,128)(2,1)S(1)}, bf16[512,768]{1,0:T(8,128)(2,1)S(1)}, bf16[528,768]{1,0:T(8,128)(2,1)S(1)}) custom-call(s32[4]{0:T(128)S(1)} %pad_add_fusion.place, bf16[64,768]{1,0:T(8,128)(2,1)S(1)} %copy-done.2, ...), custom_call_target="tpu_custom_call" | custom-call | flops 2000000000 | bytes 1048576 | tf_op jit(solution)/shard_map/pallas_call | solution.py:49
  46.4 3.5 %shard_map.106 = (f32[272,768]{1,0:T(8,128)S(1)}, f32[272,768]{1,0:T(8,128)S(1)}, bf16[544,768]{1,0:T(8,128)(2,1)S(1)}, bf16[528,512]{1,0:T(8,128)(2,1)S(1)}, bf...) custom-call(s32[4]{0:T(128)S(1)} %pad_add_fusion.place, ...), custom_call_target="tpu_custom_call" | custom-call | flops 2000000000 | bytes 1048576 | tf_op jit(solution)/shard_map/pallas_call | solution.py:49
  51.2 3.1 %collective-permute-start.22 = (bf16[144,768]{1,0:T(8,128)(2,1)S(1)}, bf16[144,768]{1,0:T(8,128)(2,1)S(1)}, u32[]{:S(2)}, u32[]{:S(2)}) collective-permute-start(bf16[144,768]{1,0:T(8,128)(2,1)S(1)} %get-tuple-element.97), channel_id=1, source_target_pairs={{0,3},{1,0},{2,1},{3,2},{4,7},{5,4},{6,5},{7,6},{8,11},{9,8},{10,9... | collective-permute-start | bytes 663560 | tf_op jit(solution)/shard_map/ppermute | solution.py:62
  54.4 4.8 %shard_map.107 = (bf16[272,768]{1,0:T(8,128)(2,1)S(1)}, bf16[272,768]{1,0:T(8,128)(2,1)S(1)}, bf16[192,768]{1,0:T(8,128)(2,1)S(1)}, bf16[64,768]{1,0:T(8,128)(2,...) custom-call(s32[4]{0:T(128)S(1)} %pad_add_fusion.place, bf16[512,768]{1,0:T(8,128)(2,1)S(1)} %get-tuple-element.80.e, ...), custom_call_target="tpu_custom_call" | custom-call | flops 2000000000 | bytes 1048576 | tf_op jit(solution)/shard_map/pallas_call | solution.py:49
  61.4 2.4 %collective-permute-start.26 = (bf16[272,768]{1,0:T(8,128)(2,1)S(1)}, bf16[272,768]{1,0:T(8,128)(2,1)S(1)}, u32[]{:S(2)}, u32[]{:S(2)}) collective-permute-start(bf16[272,768]{1,0:T(8,128)(2,1)S(1)} %get-tuple-element.106), channel_id=1, source_target_pairs={{0,3},{1,0},{2,1},{3,2},{4,7},{5,4},{6,5},{7,6},{8,11},{9,8},{10,9... | collective-permute-start | bytes 1253384 | tf_op jit(solution)/shard_map/weights_x/ppermute | solution.py:62
  65.8 2.1 %collective-permute-start.20 = (bf16[128,768]{1,0:T(8,128)(2,1)S(1)}, bf16[128,768]{1,0:T(8,128)(2,1)S(1)}, u32[]{:S(2)}, u32[]{:S(2)}) collective-permute-start(bf16[128,768]{1,0:T(8,128)(2,1)S(1)} %get-tuple-element.93), channel_id=1, source_target_pairs={{0,28},{4,0},{8,4},{12,8},{16,12},{20,16},{24,20},{28,24},{32,36},... | collective-permute-start | bytes 589832 | tf_op jit(solution)/shard_map/rows_back/ppermute | solution.py:72
  68.0 2.1 %collective-permute-done.18.got3 = bf16[128,768]{1,0:T(8,128)(2,1)S(1)} collective-permute-done((bf16[128,768]{1,0:T(8,128)(2,1)S(1)}, bf16[128,768]{1,0:T(8,128)(2,1)S(1)}, u32[]{:S(2)}, u32[]{:S(2)}) %collective-permute-start.18) | collective-permute-done | bytes 196640 | tf_op jit(solution)/shard_map/rows_back/ppermute | solution.py:72
  70.1 2.1 %collective-permute-done.20 = bf16[128,768]{1,0:T(8,128)(2,1)S(1)} collective-permute-done((bf16[128,768]{1,0:T(8,128)(2,1)S(1)}, bf16[128,768]{1,0:T(8,128)(2,1)S(1)}, u32[]{:S(2)}, u32[]{:S(2)}) %collective-permute-start.20) | collective-permute-done | bytes 196640 | tf_op jit(solution)/shard_map/rows_back/ppermute | solution.py:72
  72.8 3.1 %collective-permute-start.21 = (bf16[128,768]{1,0:T(8,128)(2,1)S(1)}, bf16[128,768]{1,0:T(8,128)(2,1)S(1)}, u32[]{:S(2)}, u32[]{:S(2)}) collective-permute-start(bf16[128,768]{1,0:T(8,128)(2,1)S(1)} %rows_back.3), channel_id=1, source_target_pairs={{0,24},{4,28},{8,0},{12,4},{16,8},{20,12},{24,16},{28,20},{32,40},... | collective-permute-start | bytes 589832 | tf_op jit(solution)/shard_map/rows_back/ppermute | solution.py:72
  79.0 2.2 %collective-permute-start.30 = (bf16[80,768]{1,0:T(8,128)(2,1)S(1)}, bf16[80,768]{1,0:T(8,128)(2,1)S(1)}, u32[]{:S(2)}, u32[]{:S(2)}) collective-permute-start(bf16[80,768]{1,0:T(8,128)(2,1)S(1)} %get-tuple-element.112), channel_id=1, source_target_pairs={{0,64},{64,128},{128,192},{192,0},{1,65},{65,129},{129,193},{193,1... | collective-permute-start | bytes 368648 | tf_op jit(solution)/shard_map/weights_y/ppermute | solution.py:62
  81.7 3.8 %collective-permute-done.28.g2 = bf16[80,768]{1,0:T(8,128)(2,1)S(1)} collective-permute-done((bf16[80,768]{1,0:T(8,128)(2,1)S(1)}, bf16[80,768]{1,0:T(8,128)(2,1)S(1)}, u32[]{:S(2)}, u32[]{:S(2)}) %collective-permute-start.28) | collective-permute-done | bytes 122912 | tf_op jit(solution)/shard_map/weights_y/ppermute | solution.py:62
  85.7 1.6 %collective-permute-done.31.g3 = bf16[80,768]{1,0:T(8,128)(2,1)S(1)} collective-permute-done((bf16[80,768]{1,0:T(8,128)(2,1)S(1)}, bf16[80,768]{1,0:T(8,128)(2,1)S(1)}, u32[]{:S(2)}, u32[]{:S(2)}) %collective-permute-start.31) | collective-permute-done | bytes 122912 | tf_op jit(solution)/shard_map/weights_y/ppermute | solution.py:62
  (79 shorter events, 21.8 us)
Async XLA Ops:
  4.2 12.7 %collective-permute-start.2 = (bf16[272,768]{1,0:T(8,128)(2,1)S(1)}, bf16[272,768]{1,0:T(8,128)(2,1)S(1)}, u32[]{:S(2)}, u32[]{:S(2)}) collective-permute-start(bf16[272,768]{1,0:T(8,128)(2,1)S(1)} %get-tuple-element.62), channel_id=1, source_target_pairs={{0,1},{1,2},{2,3},{3,0},{4,5},{5,6},{6,7},{7,4},{8,9},{9,10},{10,1... | collective-permute-start | bytes 1253384 | tf_op jit(solution)/shard_map/weights/ppermute | solution.py:62
  5.8 11.5 %collective-permute-start.4 = (bf16[272,768]{1,0:T(8,128)(2,1)S(1)}, bf16[272,768]{1,0:T(8,128)(2,1)S(1)}, u32[]{:S(2)}, u32[]{:S(2)}) collective-permute-start(bf16[272,768]{1,0:T(8,128)(2,1)S(1)} %get-tuple-element.62), channel_id=1, source_target_pairs={{0,3},{1,0},{2,1},{3,2},{4,7},{5,4},{6,5},{7,6},{8,11},{9,8},{10,9... | collective-permute-start | bytes 1253384 | tf_op jit(solution)/shard_map/weights/ppermute | solution.py:62
  8.9 13.4 %collective-permute-start.6 = (bf16[144,768]{1,0:T(8,128)(2,1)S(1)}, bf16[144,768]{1,0:T(8,128)(2,1)S(1)}, u32[]{:S(2)}, u32[]{:S(2)}) collective-permute-start(bf16[144,768]{1,0:T(8,128)(2,1)S(1)} %get-tuple-element.63), channel_id=1, source_target_pairs={{0,8},{4,12},{8,16},{12,20},{16,24},{20,28},{24,0},{28,4},{1,9},{5... | collective-permute-start | bytes 663560 | tf_op jit(solution)/shard_map/rows/ppermute | solution.py:62
  12.2 14.5 %collective-permute-start.7 = (bf16[144,768]{1,0:T(8,128)(2,1)S(1)}, bf16[144,768]{1,0:T(8,128)(2,1)S(1)}, u32[]{:S(2)}, u32[]{:S(2)}) collective-permute-start(bf16[144,768]{1,0:T(8,128)(2,1)S(1)} %get-tuple-element.64), channel_id=1, source_target_pairs={{0,24},{4,28},{8,0},{12,4},{16,8},{20,12},{24,16},{28,20},{1,25},{... | collective-permute-start | bytes 663560 | tf_op jit(solution)/shard_map/rows/ppermute | solution.py:62
  16.9 9.9 %collective-permute-start.3 = (bf16[144,768]{1,0:T(8,128)(2,1)S(1)}, bf16[144,768]{1,0:T(8,128)(2,1)S(1)}, u32[]{:S(2)}, u32[]{:S(2)}) collective-permute-start(bf16[144,768]{1,0:T(8,128)(2,1)S(1)} %slice.32), channel_id=1, source_target_pairs={{0,1},{1,2},{2,3},{3,0},{4,5},{5,6},{6,7},{7,4},{8,9},{9,10},{10,1... | collective-permute-start | bytes 663560 | tf_op jit(solution)/shard_map/weights/ppermute | solution.py:62
  17.3 9.5 %collective-permute-start.5 = (bf16[128,768]{1,0:T(8,128)(2,1)S(1)}, bf16[128,768]{1,0:T(8,128)(2,1)S(1)}, u32[]{:S(2)}, u32[]{:S(2)}) collective-permute-start(bf16[128,768]{1,0:T(8,128)(2,1)S(1)} %slice.33), channel_id=1, source_target_pairs={{0,3},{1,0},{2,1},{3,2},{4,7},{5,4},{6,5},{7,6},{8,11},{9,8},{10,9... | collective-permute-start | bytes 589832 | tf_op jit(solution)/shard_map/weights/ppermute | solution.py:62
  20.3 11.0 %collective-permute-start = (bf16[96,768]{1,0:T(8,128)(2,1)S(1)}, bf16[96,768]{1,0:T(8,128)(2,1)S(1)}, u32[]{:S(2)}, u32[]{:S(2)}) collective-permute-start(bf16[96,768]{1,0:T(8,128)(2,1)S(1)} %get-tuple-element.60), channel_id=1, source_target_pairs={{0,4},{4,8},{8,12},{12,16},{16,20},{20,24},{24,28},{28,0},{1,5},{5... | collective-permute-start | bytes 442376 | tf_op jit(solution)/shard_map/rows/ppermute | solution.py:62
  22.2 9.2 %collective-permute-start.1 = (bf16[96,768]{1,0:T(8,128)(2,1)S(1)}, bf16[96,768]{1,0:T(8,128)(2,1)S(1)}, u32[]{:S(2)}, u32[]{:S(2)}) collective-permute-start(bf16[96,768]{1,0:T(8,128)(2,1)S(1)} %get-tuple-element.61), channel_id=1, source_target_pairs={{0,28},{4,0},{8,4},{12,8},{16,12},{20,16},{24,20},{28,24},{1,29},{... | collective-permute-start | bytes 442376 | tf_op jit(solution)/shard_map/rows/ppermute | solution.py:62
  26.8 8.4 %collective-permute-start.11 = (bf16[48,768]{1,0:T(8,128)(2,1)S(1)}, bf16[48,768]{1,0:T(8,128)(2,1)S(1)}, u32[]{:S(2)}, u32[]{:S(2)}) collective-permute-start(bf16[48,768]{1,0:T(8,128)(2,1)S(1)} %slice.29), channel_id=1, source_target_pairs={{0,24},{4,28},{8,0},{12,4},{16,8},{20,12},{24,16},{28,20},{1,25},{... | collective-permute-start | bytes 221192 | tf_op jit(solution)/shard_map/rows/ppermute | solution.py:62
  30.8 15.5 %collective-permute-start.16 = (bf16[272,768]{1,0:T(8,128)(2,1)S(1)}, bf16[272,768]{1,0:T(8,128)(2,1)S(1)}, u32[]{:S(2)}, u32[]{:S(2)}) collective-permute-start(bf16[272,768]{1,0:T(8,128)(2,1)S(1)} %collective-permute-done.4.n3), channel_id=1, source_target_pairs={{0,32},{32,0},{1,33},{33,1},{2,34},{34,2},{3,35},{35,3},{4,36},{36... | collective-permute-start | bytes 1253384 | tf_op jit(solution)/shard_map/weights/ppermute | solution.py:62
  30.8 15.5 %collective-permute-start.15 = (bf16[272,768]{1,0:T(8,128)(2,1)S(1)}, bf16[272,768]{1,0:T(8,128)(2,1)S(1)}, u32[]{:S(2)}, u32[]{:S(2)}) collective-permute-start(bf16[272,768]{1,0:T(8,128)(2,1)S(1)} %collective-permute-done.2.n1), channel_id=1, source_target_pairs={{0,32},{32,0},{1,33},{33,1},{2,34},{34,2},{3,35},{35,3},{4,36},{36... | collective-permute-start | bytes 1253384 | tf_op jit(solution)/shard_map/weights/ppermute | solution.py:62
  31.4 8.0 %collective-permute-start.10 = (bf16[48,768]{1,0:T(8,128)(2,1)S(1)}, bf16[48,768]{1,0:T(8,128)(2,1)S(1)}, u32[]{:S(2)}, u32[]{:S(2)}) collective-permute-start(bf16[48,768]{1,0:T(8,128)(2,1)S(1)} %slice.28), channel_id=1, source_target_pairs={{0,8},{4,12},{8,16},{12,20},{16,24},{20,28},{24,0},{28,4},{1,9},{5... | collective-permute-start | bytes 221192 | tf_op jit(solution)/shard_map/rows/ppermute | solution.py:62
  31.5 7.9 %collective-permute-start.9 = (bf16[96,768]{1,0:T(8,128)(2,1)S(1)}, bf16[96,768]{1,0:T(8,128)(2,1)S(1)}, u32[]{:S(2)}, u32[]{:S(2)}) collective-permute-start(bf16[96,768]{1,0:T(8,128)(2,1)S(1)} %slice.27), channel_id=1, source_target_pairs={{0,28},{4,0},{8,4},{12,8},{16,12},{20,16},{24,20},{28,24},{1,29},{... | collective-permute-start | bytes 442376 | tf_op jit(solution)/shard_map/rows/ppermute | solution.py:62
  35.1 6.9 %collective-permute-start.8 = (bf16[96,768]{1,0:T(8,128)(2,1)S(1)}, bf16[96,768]{1,0:T(8,128)(2,1)S(1)}, u32[]{:S(2)}, u32[]{:S(2)}) collective-permute-start(bf16[96,768]{1,0:T(8,128)(2,1)S(1)} %slice.26), channel_id=1, source_target_pairs={{0,4},{4,8},{8,12},{12,16},{16,20},{20,24},{24,28},{28,0},{1,5},{5... | collective-permute-start | bytes 442376 | tf_op jit(solution)/shard_map/rows/ppermute | solution.py:62
  49.8 10.7 %collective-permute-start.24 = (bf16[544,768]{1,0:T(8,128)(2,1)S(1)}, bf16[544,768]{1,0:T(8,128)(2,1)S(1)}, u32[]{:S(2)}, u32[]{:S(2)}) collective-permute-start(bf16[544,768]{1,0:T(8,128)(2,1)S(1)} %get-tuple-element.103), channel_id=1, source_target_pairs={{0,32},{32,0},{1,33},{33,1},{2,34},{34,2},{3,35},{35,3},{4,36},{36... | collective-permute-start | bytes 2506760 | tf_op jit(solution)/shard_map/ppermute | solution.py:62
  51.0 9.5 %collective-permute-start.25 = (bf16[128,768]{1,0:T(8,128)(2,1)S(1)}, bf16[128,768]{1,0:T(8,128)(2,1)S(1)}, u32[]{:S(2)}, u32[]{:S(2)}) collective-permute-start(bf16[128,768]{1,0:T(8,128)(2,1)S(1)} %get-tuple-element.105), channel_id=1, source_target_pairs={{0,1},{1,2},{2,3},{3,0},{4,5},{5,6},{6,7},{7,4},{8,9},{9,10},{10,1... | collective-permute-start | bytes 589832 | tf_op jit(solution)/shard_map/ppermute | solution.py:62
  51.2 9.3 %collective-permute-start.22 = (bf16[144,768]{1,0:T(8,128)(2,1)S(1)}, bf16[144,768]{1,0:T(8,128)(2,1)S(1)}, u32[]{:S(2)}, u32[]{:S(2)}) collective-permute-start(bf16[144,768]{1,0:T(8,128)(2,1)S(1)} %get-tuple-element.97), channel_id=1, source_target_pairs={{0,3},{1,0},{2,1},{3,2},{4,7},{5,4},{6,5},{7,6},{8,11},{9,8},{10,9... | collective-permute-start | bytes 663560 | tf_op jit(solution)/shard_map/ppermute | solution.py:62
  59.3 6.6 %collective-permute-start.19 = (bf16[64,768]{1,0:T(8,128)(2,1)S(1)}, bf16[64,768]{1,0:T(8,128)(2,1)S(1)}, u32[]{:S(2)}, u32[]{:S(2)}) collective-permute-start(bf16[64,768]{1,0:T(8,128)(2,1)S(1)} %get-tuple-element.92), channel_id=1, source_target_pairs={{0,24},{4,28},{8,0},{12,4},{16,8},{20,12},{24,16},{28,20},{32,40},... | collective-permute-start | bytes 294920 | tf_op jit(solution)/shard_map/rows_back/ppermute | solution.py:72
  60.5 15.3 %collective-permute-start.23 = (bf16[272,768]{1,0:T(8,128)(2,1)S(1)}, bf16[272,768]{1,0:T(8,128)(2,1)S(1)}, u32[]{:S(2)}, u32[]{:S(2)}) collective-permute-start(bf16[272,768]{1,0:T(8,128)(2,1)S(1)} %get-tuple-element.100), channel_id=1, source_target_pairs={{0,32},{32,0},{1,33},{33,1},{2,34},{34,2},{3,35},{35,3},{4,36},{36... | collective-permute-start | bytes 1253384 | tf_op jit(solution)/shard_map/ppermute | solution.py:62
  61.4 14.5 %collective-permute-start.26 = (bf16[272,768]{1,0:T(8,128)(2,1)S(1)}, bf16[272,768]{1,0:T(8,128)(2,1)S(1)}, u32[]{:S(2)}, u32[]{:S(2)}) collective-permute-start(bf16[272,768]{1,0:T(8,128)(2,1)S(1)} %get-tuple-element.106), channel_id=1, source_target_pairs={{0,3},{1,0},{2,1},{3,2},{4,7},{5,4},{6,5},{7,6},{8,11},{9,8},{10,9... | collective-permute-start | bytes 1253384 | tf_op jit(solution)/shard_map/weights_x/ppermute | solution.py:62
  63.8 13.0 %collective-permute-start.27 = (bf16[272,768]{1,0:T(8,128)(2,1)S(1)}, bf16[272,768]{1,0:T(8,128)(2,1)S(1)}, u32[]{:S(2)}, u32[]{:S(2)}) collective-permute-start(bf16[272,768]{1,0:T(8,128)(2,1)S(1)} %get-tuple-element.107), channel_id=1, source_target_pairs={{0,1},{1,2},{2,3},{3,0},{4,5},{5,6},{6,7},{7,4},{8,9},{9,10},{10,1... | collective-permute-start | bytes 1253384 | tf_op jit(solution)/shard_map/weights_x/ppermute | solution.py:62
  72.8 8.9 %collective-permute-start.21 = (bf16[128,768]{1,0:T(8,128)(2,1)S(1)}, bf16[128,768]{1,0:T(8,128)(2,1)S(1)}, u32[]{:S(2)}, u32[]{:S(2)}) collective-permute-start(bf16[128,768]{1,0:T(8,128)(2,1)S(1)} %rows_back.3), channel_id=1, source_target_pairs={{0,24},{4,28},{8,0},{12,4},{16,8},{20,12},{24,16},{28,20},{32,40},... | collective-permute-start | bytes 589832 | tf_op jit(solution)/shard_map/rows_back/ppermute | solution.py:72
  77.7 7.8 %collective-permute-start.28 = (bf16[80,768]{1,0:T(8,128)(2,1)S(1)}, bf16[80,768]{1,0:T(8,128)(2,1)S(1)}, u32[]{:S(2)}, u32[]{:S(2)}) collective-permute-start(bf16[80,768]{1,0:T(8,128)(2,1)S(1)} %get-tuple-element.108), channel_id=1, source_target_pairs={{0,128},{64,192},{128,0},{192,64},{1,129},{65,193},{129,1},{193,65... | collective-permute-start | bytes 368648 | tf_op jit(solution)/shard_map/weights_y/ppermute | solution.py:62
  79.0 6.6 %collective-permute-start.30 = (bf16[80,768]{1,0:T(8,128)(2,1)S(1)}, bf16[80,768]{1,0:T(8,128)(2,1)S(1)}, u32[]{:S(2)}, u32[]{:S(2)}) collective-permute-start(bf16[80,768]{1,0:T(8,128)(2,1)S(1)} %get-tuple-element.112), channel_id=1, source_target_pairs={{0,64},{64,128},{128,192},{192,0},{1,65},{65,129},{129,193},{193,1... | collective-permute-start | bytes 368648 | tf_op jit(solution)/shard_map/weights_y/ppermute | solution.py:62
  (16 other events, 71.0 us)

commit v11 on v10

--- a/solution.py
+++ b/solution.py
@@ -17,20 +17,20 @@
 TOP = 256
 PART = 272
 CUT = 144
-ORDER = (0, 1, 7, 2, 6, 3, 5, 4)
+ORDER = (0, 2, 6, 4, 1, 7, 3, 5)
 ROW_AT = (
     ((0, 0, 64),),
-    ((1, 0, 64),),
-    ((2, 0, 64),),
-    ((3, 16, 64),),
-    ((4, 48, 32), (4, 16, 32)),
+    ((1, 16, 64),),
+    ((2, 48, 32), (2, 16, 32)),
+    ((3, 16, 32), (4, 16, 32)),
     ((5, 0, 64),),
-    ((6, 32, 32), (6, 0, 32)),
-    ((7, 16, 32), (8, 16, 32)),
+    ((6, 0, 64),),
+    ((7, 0, 64),),
+    ((8, 32, 32), (8, 0, 32)),
 )
 SLOT_AT = (
-    (((0, 0, 32),), ((1, 64, 32),), ((2, 64, 32),), ((3, 112, 32),)),
-    (((0, 112, 32),), ((1, 64, 32),), ((2, 64, 32),), ((3, 0, 16), (4, 0, 16))),
+    (((0, 0, 32),), ((1, 112, 32),), ((2, 112, 32),), ((3, 0, 16), (4, 0, 16))),
+    (((0, 64, 32),), ((1, 64, 32),), ((2, 64, 32),), ((3, 64, 32),)),
 )
 NT = (((1,), (1,)), ((), ()))
 NN = (((1,), (0,)), ((), ()))
@@ -43,7 +43,7 @@
     return lax.dot_general(a, b, dims, preferred_element_type=F32)
 
 
-def call(kernel, out, args, scratch=(), own=0, **static):
+def call(kernel, out, args, scratch=(), own=0, flops=2 * 10**9, **static):
     specs = [SMEM] + [VMEM] * (len(args) - 1 - own)
     specs += [pl.BlockSpec(memory_space=pltpu.HBM)] * own
     return pl.pallas_call(
@@ -53,7 +53,7 @@
         out_specs=(VMEM,) * len(out),
         scratch_shapes=[s if t is None else pltpu.VMEM(s, t) for s, t in scratch],
         compiler_params=pltpu.CompilerParams(vmem_limit_bytes=18 * 1024 * 1024),
-        cost_estimate=pl.CostEstimate(flops=2 * 10**9, bytes_accessed=1 << 20, transcendentals=0),
+        cost_estimate=pl.CostEstimate(flops=flops, bytes_accessed=1 << 20, transcendentals=0),
     )(*args)
 
 
@@ -208,13 +208,12 @@
     weight_terms(core, e, dzs, a, b)
 
 
-def beside_kernel(place, e, n1, f1, n3, f3, ay1, ay2, a1, a3, b, dz1, dz3, w1, w3, *z):
+def beside_kernel(place, e, near, far, ay1, ay2, a, b, dzs, w, *z, r):
     core = place[1]
-    for r, near, far, a, lo, dzs, w in ((1, n1, f1, a1, 0, dz1, w1), (3, n3, f3, a3, PART, dz3, w3)):
-        w[pl.ds(pl.multiple_of(core * TOP, 16), PART)] = near[...]
-        w[pl.ds(pl.multiple_of((1 - core) * TOP, 16), PART)] = far[...]
-        owner_terms(r, e, w, ay1, ay2, dzs, z)
-        weight_terms(core, e, dzs, a, b.at[pl.ds(lo, PART)])
+    w[pl.ds(pl.multiple_of(core * TOP, 16), PART)] = near[...]
+    w[pl.ds(pl.multiple_of((1 - core) * TOP, 16), PART)] = far[...]
+    owner_terms(r, e, w, ay1, ay2, dzs, z)
+    weight_terms(core, e, dzs, a, b)
 
 
 def own_kernel(place, e, w, ay1, ay2, dz1, dz2, dz3, w1, w2, w3, a, b, near, last, far, own, *refs):
@@ -258,8 +257,7 @@
     high[...] = (a[CUT:] + b[CUT:].astype(F32)).astype(BF16)
 
 
-def merge_kernel(place, a1, a3, b, low, high, t1, t3):
-    b1, b3 = b.at[pl.ds(0, PART)], b.at[pl.ds(PART, PART)]
+def merge_kernel(place, a1, b1, a3, b3, low, high, t1, t3):
     t1[:CUT] = (a1[:CUT] + b1[:CUT].astype(F32) + low[...].astype(F32)).astype(BF16)
     t1[CUT:] = (a1[CUT:] + b1[CUT:].astype(F32)).astype(BF16)
     t3[:CUT] = (a3[:CUT] + b3[:CUT].astype(F32)).astype(BF16)
@@ -337,10 +335,11 @@
             own=6,
         )
         up2, dn2 = shift(up2, "z", 2), shift(dn2, "z", -2)
-        up1, dn1 = shift(up1, "z", 1), shift(dn1, "z", -1)
         low2, high2, up2, dn2 = lax.optimization_barrier((low2, high2, up2, dn2))
         up3, dn3 = shift(up2[16:112], "z", 1), shift(dn2[16:112], "z", -1)
         up4, dn4 = shift(up2[:48], "z", 2), shift(dn2[:48], "z", -2)
+        up1, dn1, _, _ = lax.optimization_barrier((up1, dn1, up2, dn2))
+        up1, dn1 = shift(up1, "z", 1), shift(dn1, "z", -1)
 
     def sum_slots(blocks, spots):
         return call(
@@ -351,11 +350,11 @@
             spots=spots,
         )[0]
 
-    ay1 = sum_slots((s0, up1, dn1, up2), SLOT_AT[0])
+    ay1 = sum_slots((s0, up2, dn2, up4, dn4), SLOT_AT[0])
     with jax.named_scope("weights"):
-        low2, high2, up4, dn4, ay1 = lax.optimization_barrier((low2, high2, up4, dn4, ay1))
+        low2, high2, ay1 = lax.optimization_barrier((low2, high2, ay1))
         low_o, high_o, low2_o, high2_o = (swap(p) for p in (low, high, low2, high2))
-    ay2 = sum_slots((dn2, up3, dn3, up4, dn4), SLOT_AT[1])
+    ay2 = sum_slots((up1, dn1, up3, dn3), SLOT_AT[1])
     wide, dzs = ((WIDE, D), BF16), ((WIDE, ROWS), BF16)
     half, half32 = ((PART, D), BF16), ((PART, D), F32)
     z = [((WIDE, 256), F32)] * 2
@@ -363,22 +362,20 @@
     a2, b2, dz2, rows, w2 = call(
         across_kernel,
         [half32, half, dzs, ((ROWS, D), BF16), wide],
-        (place, e, up1, dn1, up2, dn2, up3, dn3, up4, dn4, low2, high2, low2_o, high2_o, ay1, ay2),
+        (place, e, up2, dn2, up4, dn4, up1, dn1, up3, dn3, low2, high2, low2_o, high2_o, ay1, ay2),
         z,
     )
     with jax.named_scope("weights_x"):
         down, up = call(
             cut_kernel, [((CUT, D), BF16), ((PART - CUT, D), BF16)], (place, a2, swap(b2))
         )
-    a1, a3, b13, dz1, dz3, w1, w3 = call(
-        beside_kernel,
-        [half32, half32, ((2 * PART, D), BF16), dzs, dzs, wide, wide],
-        (place, rows, low, low_o, high, high_o, ay1, ay2),
-        z,
-    )
-    b13 = swap(b13)
+    outs = [half32, half, dzs, wide]
+    a1, b1, dz1, w1 = call(beside_kernel, outs, (place, rows, low, low_o, ay1, ay2), z, r=1)
+    b1 = swap(b1)
     rows, down, up = lax.optimization_barrier((rows, down, up))
     down, up = shift(down, "x", -1), shift(up, "x", 1)
+    a3, b3, dz3, w3 = call(beside_kernel, outs, (place, rows, high, high_o, ay1, ay2), z, r=3)
+    b3 = swap(b3)
     block = ((INST, D), BF16)
     three = ((3 * INST, D), BF16)
     a0, b0, near, last, far, own = call(
@@ -386,6 +383,7 @@
         [half, half, three, block, three, ((INST, D), F32)],
         (place, rows, w, ay1, ay2, dz1, dz2, dz3, w1, w2, w3),
         z + [dzs, ((ROWS, D), F32)],
+        flops=4 * 10**9,
     )
     b0 = swap(b0)
 
@@ -398,7 +396,7 @@
 
     with jax.named_scope("weights_x"):
         down, a0 = lax.optimization_barrier((down, a0))
-        t1, t3 = call(merge_kernel, [half, half], (place, a1, a3, b13, down, up))
+        t1, t3 = call(merge_kernel, [half, half], (place, a1, b1, a3, b3, down, up))
         t1, t3 = shift(t1, "x", -1), shift(t3, "x", 1)
 
     with jax.named_scope("rows_back"):

time: 89.5 us -> 91.2 us (1.019)
  waiting for transfers between devices: 16.8 us -> 20.5 us
  starting transfers between devices: 46.5 us -> 44 us
    ppermute x28 -> x29, waiting for transfers between devices: 12.2 us -> 15.8 us  [shift(): return lax.ppermute(x, axis, [(i, (i + by) % n) for i in range(n)])]
    ppermute x28 -> x29, starting transfers between devices: 38.5 us -> 36 us  [shift(): return lax.ppermute(x, axis, [(i, (i + by) % n) for i in range(n)])]
    pallas_call x13 -> x14, Pallas kernels: 22.3 us -> 22.9 us  [call(): pl.pallas_call(functools.partial(kernel, **static), out_shape=tuple((jax....]
  transfers between devices with their start and end apart: 32 -> 33, of which waited for: 9 -> 13; matrix products, arithmetic and copies ran while one was open for 0% -> 0% of each run, Pallas kernels for 23% -> 23%
where the time goes in v11:
time: 91.2 us; the launch traced here: 91.1 us
  starting transfers between devices  44 us (48%)
  Pallas kernels  22.9 us (25%)
  waiting for transfers between devices  20.5 us (22%)
  local copies, waits for them, and re-layouts  1.98 us (2%)
  between operations  0.92 us (1%)
    ppermute x29, starting transfers between devices, shift(): return lax.ppermute(x, axis, [(i, (i + by) % n) for i in range(n)])  36 us
    pallas_call x14, Pallas kernels, call(): pl.pallas_call(functools.partial(kernel, **static), out_shape=tuple((jax....  22.9 us
    ppermute x29, waiting for transfers between devices, shift(): return lax.ppermute(x, axis, [(i, (i + by) % n) for i in range(n)])  15.8 us
    ppermute x4, starting transfers between devices, turn(): return lax.ppermute(x, ('core', axis), pairs)  7.97 us
    ppermute x4, waiting for transfers between devices, turn(): return lax.ppermute(x, ('core', axis), pairs)  4.7 us
    unnamed x16, local copies, waits for them, and re-layouts  1.9 us
  transfers between devices with their start and end apart: 33, of which 13 were waited for; matrix products, arithmetic and copies ran while one was open for 0% of the time, Pallas kernels for 23%

profile of v11, /device:TPU:24, one launch (start us, length us, event | category | flops | bytes accessed | tf_op | source)
XLA Modules:
  0.0 91.1 jit_solution(5568437866614296640)
XLA Ops:
  2.6 1.6 %weights.1 = (bf16[528,768]{1,0:T(8,128)(2,1)S(1)}, bf16[272,768]{1,0:T(8,128)(2,1)S(1)}) custom-call(s32[4]{0:T(128)S(1)} %pad_add_fusion.place, bf16[16,32,768]{2,1,0:T(8,128)(2,1)S(1)} %copy-done, bf16[16,768]{1,0:T(8,128)(2,1)S(1)} %copy-done.3), custom_call_target="tpu_custom_call" | custom-call | flops 2000000000 | bytes 1048576 | tf_op jit(solution)/shard_map/weights/pallas_call | solution.py:49
  5.8 1.7 %collective-permute-start.2 = (bf16[272,768]{1,0:T(8,128)(2,1)S(1)}, bf16[272,768]{1,0:T(8,128)(2,1)S(1)}, u32[]{:S(2)}, u32[]{:S(2)}) collective-permute-start(bf16[272,768]{1,0:T(8,128)(2,1)S(1)} %get-tuple-element.61), channel_id=1, source_target_pairs={{0,3},{1,0},{2,1},{3,2},{4,7},{5,4},{6,5},{7,6},{8,11},{9,8},{10,9... | collective-permute-start | bytes 1253384 | tf_op jit(solution)/shard_map/weights/ppermute | solution.py:62
  8.9 3.3 %collective-permute-start.4 = (bf16[144,768]{1,0:T(8,128)(2,1)S(1)}, bf16[144,768]{1,0:T(8,128)(2,1)S(1)}, u32[]{:S(2)}, u32[]{:S(2)}) collective-permute-start(bf16[144,768]{1,0:T(8,128)(2,1)S(1)} %get-tuple-element.62), channel_id=1, source_target_pairs={{0,8},{4,12},{8,16},{12,20},{16,24},{20,28},{24,0},{28,4},{1,9},{5... | collective-permute-start | bytes 663560 | tf_op jit(solution)/shard_map/rows/ppermute | solution.py:62
  12.2 3.1 %collective-permute-start.5 = (bf16[144,768]{1,0:T(8,128)(2,1)S(1)}, bf16[144,768]{1,0:T(8,128)(2,1)S(1)}, u32[]{:S(2)}, u32[]{:S(2)}) collective-permute-start(bf16[144,768]{1,0:T(8,128)(2,1)S(1)} %get-tuple-element.63), channel_id=1, source_target_pairs={{0,24},{4,28},{8,0},{12,4},{16,8},{20,12},{24,16},{28,20},{1,25},{... | collective-permute-start | bytes 663560 | tf_op jit(solution)/shard_map/rows/ppermute | solution.py:62
  17.3 3.0 %collective-permute-start.3 = (bf16[128,768]{1,0:T(8,128)(2,1)S(1)}, bf16[128,768]{1,0:T(8,128)(2,1)S(1)}, u32[]{:S(2)}, u32[]{:S(2)}) collective-permute-start(bf16[128,768]{1,0:T(8,128)(2,1)S(1)} %slice.33), channel_id=1, source_target_pairs={{0,3},{1,0},{2,1},{3,2},{4,7},{5,4},{6,5},{7,6},{8,11},{9,8},{10,9... | collective-permute-start | bytes 589832 | tf_op jit(solution)/shard_map/weights/ppermute | solution.py:62
  21.7 4.3 %collective-permute-done.5.refs_2_ = bf16[144,768]{1,0:T(8,128)(2,1)S(1)} collective-permute-done((bf16[144,768]{1,0:T(8,128)(2,1)S(1)}, bf16[144,768]{1,0:T(8,128)(2,1)S(1)}, u32[]{:S(2)}, u32[]{:S(2)}) %collective-permute-start.5) | collective-permute-done | bytes 221216 | tf_op jit(solution)/shard_map/rows/ppermute | solution.py:62
  26.1 4.7 %collective-permute-start.7 = (bf16[48,768]{1,0:T(8,128)(2,1)S(1)}, bf16[48,768]{1,0:T(8,128)(2,1)S(1)}, u32[]{:S(2)}, u32[]{:S(2)}) collective-permute-start(bf16[48,768]{1,0:T(8,128)(2,1)S(1)} %slice.27), channel_id=1, source_target_pairs={{0,24},{4,28},{8,0},{12,4},{16,8},{20,12},{24,16},{28,20},{1,25},{... | collective-permute-start | bytes 221192 | tf_op jit(solution)/shard_map/rows/ppermute | solution.py:62
  30.9 3.8 %collective-permute-start.11 = (bf16[96,768]{1,0:T(8,128)(2,1)S(1)}, bf16[96,768]{1,0:T(8,128)(2,1)S(1)}, u32[]{:S(2)}, u32[]{:S(2)}) collective-permute-start(bf16[96,768]{1,0:T(8,128)(2,1)S(1)} %slice.29), channel_id=1, source_target_pairs={{0,28},{4,0},{8,4},{12,8},{16,12},{20,16},{24,20},{28,24},{1,29},{... | collective-permute-start | bytes 442376 | tf_op jit(solution)/shard_map/rows/ppermute | solution.py:62
  34.8 3.1 %collective-permute-start.9 = (bf16[96,768]{1,0:T(8,128)(2,1)S(1)}, bf16[96,768]{1,0:T(8,128)(2,1)S(1)}, u32[]{:S(2)}, u32[]{:S(2)}) collective-permute-start(bf16[96,768]{1,0:T(8,128)(2,1)S(1)} %get-tuple-element.69), channel_id=1, source_target_pairs={{0,28},{4,0},{8,4},{12,8},{16,12},{20,16},{24,20},{28,24},{1,29},{... | collective-permute-start | bytes 442376 | tf_op jit(solution)/shard_map/rows/ppermute | solution.py:62
  38.6 2.1 %shard_map.103.refs_13_.ay1 = f32[4,528,256]{2,1,0:T(8,128)S(1)} custom-call(s32[4]{0:T(128)S(1)} %pad_add_fusion.place, bf16[32,768]{1,0:T(8,128)(2,1)S(1)} %get-tuple-element.72.refs_0_, bf16[144,768]{1,0:T(8,128)(2,1)S(1)} %collective-permute-done.4.refs_1_, bf16[144,768]{1,0:T(8,128)(2,1)S(1)} %collective-permute-done.5.refs_2_, ...), custom_call_target="tpu_custom_call" | custom-call | flops 2000000000 | bytes 1048576 | tf_op jit(solution)/shard_map/pallas_call | solution.py:49
  43.5 2.1 %shard_map.104.refs_14_.ay2 = f32[4,528,256]{2,1,0:T(8,128)S(1)} custom-call(s32[4]{0:T(128)S(1)} %pad_add_fusion.place, bf16[96,768]{1,0:T(8,128)(2,1)S(1)} %collective-permute-done.8.refs_0_.refs_5_, bf16[96,768]{1,0:T(8,128)(2,1)S(1)} %collective-permute-done.9.refs_1_.refs_6_, bf16[96,768]{1,0:T(8,128)(2,1)S(1)} %collective-permute-done.10.refs_2_.refs_7_, ...), custom_call_target="tpu_custom_call" | custom-call | flops 2000000000 | bytes 1048576 | tf_op jit(solution)/shard_map/pallas_call | solution.py:49
  45.6 2.1 %shard_map.105 = (f32[272,768]{1,0:T(8,128)S(1)}, bf16[272,768]{1,0:T(8,128)(2,1)S(1)}, bf16[528,512]{1,0:T(8,128)(2,1)S(1)}, bf16[512,768]{1,0:T(8,128)(2,1)S(1)}, bf16[528,768]{1,0:T(8,128)(2,1)S(1)}) custom-call(s32[4]{0:T(128)S(1)} %pad_add_fusion.place, bf16[64,768]{1,0:T(8,128)(2,1)S(1)} %copy-done.2, ...), custom_call_target="tpu_custom_call" | custom-call | flops 2000000000 | bytes 1048576 | tf_op jit(solution)/shard_map/pallas_call | solution.py:49
  48.3 2.1 %shard_map.106 = (f32[272,768]{1,0:T(8,128)S(1)}, bf16[272,768]{1,0:T(8,128)(2,1)S(1)}, bf16[528,512]{1,0:T(8,128)(2,1)S(1)}, bf16[528,768]{1,0:T(8,128)(2,1)S(1)}) custom-call(s32[4]{0:T(128)S(1)} %pad_add_fusion.place, bf16[512,768]{1,0:T(8,128)(2,1)S(1)} %get-tuple-element.81.e, bf16[272,768]{1,0:T(8,128)(2,1)S(1)} %collective-permute-done.near, ...), custom_call_target="tpu_custom_call" | custom-call | flops 2000000000 | bytes 1048576 | tf_op jit(solution)/shard_map/pallas_call | solution.py:49
  51.3 3.2 %collective-permute-start.22 = (bf16[144,768]{1,0:T(8,128)(2,1)S(1)}, bf16[144,768]{1,0:T(8,128)(2,1)S(1)}, u32[]{:S(2)}, u32[]{:S(2)}) collective-permute-start(bf16[144,768]{1,0:T(8,128)(2,1)S(1)} %get-tuple-element.98), channel_id=1, source_target_pairs={{0,3},{1,0},{2,1},{3,2},{4,7},{5,4},{6,5},{7,6},{8,11},{9,8},{10,9... | collective-permute-start | bytes 663560 | tf_op jit(solution)/shard_map/ppermute | solution.py:62
  54.5 2.1 %shard_map.107 = (f32[272,768]{1,0:T(8,128)S(1)}, bf16[272,768]{1,0:T(8,128)(2,1)S(1)}, bf16[528,512]{1,0:T(8,128)(2,1)S(1)}, bf16[528,768]{1,0:T(8,128)(2,1)S(1)}) custom-call(s32[4]{0:T(128)S(1)} %pad_add_fusion.place, bf16[512,768]{1,0:T(8,128)(2,1)S(1)} %get-tuple-element.81.e, bf16[272,768]{1,0:T(8,128)(2,1)S(1)} %collective-permute-done.2.near, ...), custom_call_target="tpu_custom_call" | custom-call | flops 2000000000 | bytes 1048576 | tf_op jit(solution)/shard_map/pallas_call | solution.py:49
  56.7 4.8 %shard_map.108 = (bf16[272,768]{1,0:T(8,128)(2,1)S(1)}, bf16[272,768]{1,0:T(8,128)(2,1)S(1)}, bf16[192,768]{1,0:T(8,128)(2,1)S(1)}, bf16[64,768]{1,0:T(8,128)(2,...) custom-call(s32[4]{0:T(128)S(1)} %pad_add_fusion.place, bf16[512,768]{1,0:T(8,128)(2,1)S(1)} %get-tuple-element.81.e, ...), custom_call_target="tpu_custom_call" | custom-call | flops 4000000000 | bytes 1048576 | tf_op jit(solution)/shard_map/pallas_call | solution.py:49
  63.8 1.6 %collective-permute-start.27 = (bf16[272,768]{1,0:T(8,128)(2,1)S(1)}, bf16[272,768]{1,0:T(8,128)(2,1)S(1)}, u32[]{:S(2)}, u32[]{:S(2)}) collective-permute-start(bf16[272,768]{1,0:T(8,128)(2,1)S(1)} %get-tuple-element.108), channel_id=1, source_target_pairs={{0,3},{1,0},{2,1},{3,2},{4,7},{5,4},{6,5},{7,6},{8,11},{9,8},{10,9... | collective-permute-start | bytes 1253384 | tf_op jit(solution)/shard_map/weights_x/ppermute | solution.py:62
  67.7 2.9 %collective-permute-start.20 = (bf16[128,768]{1,0:T(8,128)(2,1)S(1)}, bf16[128,768]{1,0:T(8,128)(2,1)S(1)}, u32[]{:S(2)}, u32[]{:S(2)}) collective-permute-start(bf16[128,768]{1,0:T(8,128)(2,1)S(1)} %get-tuple-element.94), channel_id=1, source_target_pairs={{0,28},{4,0},{8,4},{12,8},{16,12},{20,16},{24,20},{28,24},{32,36},... | collective-permute-start | bytes 589832 | tf_op jit(solution)/shard_map/rows_back/ppermute | solution.py:72
  70.6 1.7 %collective-permute-done.18.got3 = bf16[128,768]{1,0:T(8,128)(2,1)S(1)} collective-permute-done((bf16[128,768]{1,0:T(8,128)(2,1)S(1)}, bf16[128,768]{1,0:T(8,128)(2,1)S(1)}, u32[]{:S(2)}, u32[]{:S(2)}) %collective-permute-start.18) | collective-permute-done | bytes 196640 | tf_op jit(solution)/shard_map/rows_back/ppermute | solution.py:72
  72.3 2.1 %collective-permute-done.20 = bf16[128,768]{1,0:T(8,128)(2,1)S(1)} collective-permute-done((bf16[128,768]{1,0:T(8,128)(2,1)S(1)}, bf16[128,768]{1,0:T(8,128)(2,1)S(1)}, u32[]{:S(2)}, u32[]{:S(2)}) %collective-permute-start.20) | collective-permute-done | bytes 196640 | tf_op jit(solution)/shard_map/rows_back/ppermute | solution.py:72
  75.0 3.1 %collective-permute-start.21 = (bf16[128,768]{1,0:T(8,128)(2,1)S(1)}, bf16[128,768]{1,0:T(8,128)(2,1)S(1)}, u32[]{:S(2)}, u32[]{:S(2)}) collective-permute-start(bf16[128,768]{1,0:T(8,128)(2,1)S(1)} %rows_back.3), channel_id=1, source_target_pairs={{0,24},{4,28},{8,0},{12,4},{16,8},{20,12},{24,16},{28,20},{32,40},... | collective-permute-start | bytes 589832 | tf_op jit(solution)/shard_map/rows_back/ppermute | solution.py:72
  80.8 2.2 %collective-permute-start.31 = (bf16[80,768]{1,0:T(8,128)(2,1)S(1)}, bf16[80,768]{1,0:T(8,128)(2,1)S(1)}, u32[]{:S(2)}, u32[]{:S(2)}) collective-permute-start(bf16[80,768]{1,0:T(8,128)(2,1)S(1)} %get-tuple-element.114), channel_id=1, source_target_pairs={{0,64},{64,128},{128,192},{192,0},{1,65},{65,129},{129,193},{193,1... | collective-permute-start | bytes 368648 | tf_op jit(solution)/shard_map/weights_y/ppermute | solution.py:62
  83.7 3.5 %collective-permute-done.29.g2 = bf16[80,768]{1,0:T(8,128)(2,1)S(1)} collective-permute-done((bf16[80,768]{1,0:T(8,128)(2,1)S(1)}, bf16[80,768]{1,0:T(8,128)(2,1)S(1)}, u32[]{:S(2)}, u32[]{:S(2)}) %collective-permute-start.29) | collective-permute-done | bytes 122912 | tf_op jit(solution)/shard_map/weights_y/ppermute | solution.py:62
  87.4 1.6 %collective-permute-done.32.g3 = bf16[80,768]{1,0:T(8,128)(2,1)S(1)} collective-permute-done((bf16[80,768]{1,0:T(8,128)(2,1)S(1)}, bf16[80,768]{1,0:T(8,128)(2,1)S(1)}, u32[]{:S(2)}, u32[]{:S(2)}) %collective-permute-start.32) | collective-permute-done | bytes 122912 | tf_op jit(solution)/shard_map/weights_y/ppermute | solution.py:62
  (82 shorter events, 24.3 us)
Async XLA Ops:
  4.2 12.7 %collective-permute-start = (bf16[272,768]{1,0:T(8,128)(2,1)S(1)}, bf16[272,768]{1,0:T(8,128)(2,1)S(1)}, u32[]{:S(2)}, u32[]{:S(2)}) collective-permute-start(bf16[272,768]{1,0:T(8,128)(2,1)S(1)} %get-tuple-element.61), channel_id=1, source_target_pairs={{0,1},{1,2},{2,3},{3,0},{4,5},{5,6},{6,7},{7,4},{8,9},{9,10},{10,1... | collective-permute-start | bytes 1253384 | tf_op jit(solution)/shard_map/weights/ppermute | solution.py:62
  5.8 11.5 %collective-permute-start.2 = (bf16[272,768]{1,0:T(8,128)(2,1)S(1)}, bf16[272,768]{1,0:T(8,128)(2,1)S(1)}, u32[]{:S(2)}, u32[]{:S(2)}) collective-permute-start(bf16[272,768]{1,0:T(8,128)(2,1)S(1)} %get-tuple-element.61), channel_id=1, source_target_pairs={{0,3},{1,0},{2,1},{3,2},{4,7},{5,4},{6,5},{7,6},{8,11},{9,8},{10,9... | collective-permute-start | bytes 1253384 | tf_op jit(solution)/shard_map/weights/ppermute | solution.py:62
  8.9 12.8 %collective-permute-start.4 = (bf16[144,768]{1,0:T(8,128)(2,1)S(1)}, bf16[144,768]{1,0:T(8,128)(2,1)S(1)}, u32[]{:S(2)}, u32[]{:S(2)}) collective-permute-start(bf16[144,768]{1,0:T(8,128)(2,1)S(1)} %get-tuple-element.62), channel_id=1, source_target_pairs={{0,8},{4,12},{8,16},{12,20},{16,24},{20,28},{24,0},{28,4},{1,9},{5... | collective-permute-start | bytes 663560 | tf_op jit(solution)/shard_map/rows/ppermute | solution.py:62
  12.2 13.8 %collective-permute-start.5 = (bf16[144,768]{1,0:T(8,128)(2,1)S(1)}, bf16[144,768]{1,0:T(8,128)(2,1)S(1)}, u32[]{:S(2)}, u32[]{:S(2)}) collective-permute-start(bf16[144,768]{1,0:T(8,128)(2,1)S(1)} %get-tuple-element.63), channel_id=1, source_target_pairs={{0,24},{4,28},{8,0},{12,4},{16,8},{20,12},{24,16},{28,20},{1,25},{... | collective-permute-start | bytes 663560 | tf_op jit(solution)/shard_map/rows/ppermute | solution.py:62
  16.9 9.1 %collective-permute-start.1 = (bf16[144,768]{1,0:T(8,128)(2,1)S(1)}, bf16[144,768]{1,0:T(8,128)(2,1)S(1)}, u32[]{:S(2)}, u32[]{:S(2)}) collective-permute-start(bf16[144,768]{1,0:T(8,128)(2,1)S(1)} %slice.32), channel_id=1, source_target_pairs={{0,1},{1,2},{2,3},{3,0},{4,5},{5,6},{6,7},{7,4},{8,9},{9,10},{10,1... | collective-permute-start | bytes 663560 | tf_op jit(solution)/shard_map/weights/ppermute | solution.py:62
  17.3 8.7 %collective-permute-start.3 = (bf16[128,768]{1,0:T(8,128)(2,1)S(1)}, bf16[128,768]{1,0:T(8,128)(2,1)S(1)}, u32[]{:S(2)}, u32[]{:S(2)}) collective-permute-start(bf16[128,768]{1,0:T(8,128)(2,1)S(1)} %slice.33), channel_id=1, source_target_pairs={{0,3},{1,0},{2,1},{3,2},{4,7},{5,4},{6,5},{7,6},{8,11},{9,8},{10,9... | collective-permute-start | bytes 589832 | tf_op jit(solution)/shard_map/weights/ppermute | solution.py:62
  26.1 8.7 %collective-permute-start.7 = (bf16[48,768]{1,0:T(8,128)(2,1)S(1)}, bf16[48,768]{1,0:T(8,128)(2,1)S(1)}, u32[]{:S(2)}, u32[]{:S(2)}) collective-permute-start(bf16[48,768]{1,0:T(8,128)(2,1)S(1)} %slice.27), channel_id=1, source_target_pairs={{0,24},{4,28},{8,0},{12,4},{16,8},{20,12},{24,16},{28,20},{1,25},{... | collective-permute-start | bytes 221192 | tf_op jit(solution)/shard_map/rows/ppermute | solution.py:62
  30.8 7.8 %collective-permute-start.6 = (bf16[48,768]{1,0:T(8,128)(2,1)S(1)}, bf16[48,768]{1,0:T(8,128)(2,1)S(1)}, u32[]{:S(2)}, u32[]{:S(2)}) collective-permute-start(bf16[48,768]{1,0:T(8,128)(2,1)S(1)} %slice.26), channel_id=1, source_target_pairs={{0,8},{4,12},{8,16},{12,20},{16,24},{20,28},{24,0},{28,4},{1,9},{5... | collective-permute-start | bytes 221192 | tf_op jit(solution)/shard_map/rows/ppermute | solution.py:62
  30.9 9.9 %collective-permute-start.11 = (bf16[96,768]{1,0:T(8,128)(2,1)S(1)}, bf16[96,768]{1,0:T(8,128)(2,1)S(1)}, u32[]{:S(2)}, u32[]{:S(2)}) collective-permute-start(bf16[96,768]{1,0:T(8,128)(2,1)S(1)} %slice.29), channel_id=1, source_target_pairs={{0,28},{4,0},{8,4},{12,8},{16,12},{20,16},{24,20},{28,24},{1,29},{... | collective-permute-start | bytes 442376 | tf_op jit(solution)/shard_map/rows/ppermute | solution.py:62
  34.6 7.3 %collective-permute-start.10 = (bf16[96,768]{1,0:T(8,128)(2,1)S(1)}, bf16[96,768]{1,0:T(8,128)(2,1)S(1)}, u32[]{:S(2)}, u32[]{:S(2)}) collective-permute-start(bf16[96,768]{1,0:T(8,128)(2,1)S(1)} %slice.28), channel_id=1, source_target_pairs={{0,4},{4,8},{8,12},{12,16},{16,20},{20,24},{24,28},{28,0},{1,5},{5... | collective-permute-start | bytes 442376 | tf_op jit(solution)/shard_map/rows/ppermute | solution.py:62
  34.6 8.9 %collective-permute-start.8 = (bf16[96,768]{1,0:T(8,128)(2,1)S(1)}, bf16[96,768]{1,0:T(8,128)(2,1)S(1)}, u32[]{:S(2)}, u32[]{:S(2)}) collective-permute-start(bf16[96,768]{1,0:T(8,128)(2,1)S(1)} %get-tuple-element.68), channel_id=1, source_target_pairs={{0,4},{4,8},{8,12},{12,16},{16,20},{20,24},{24,28},{28,0},{1,5},{5... | collective-permute-start | bytes 442376 | tf_op jit(solution)/shard_map/rows/ppermute | solution.py:62
  34.8 8.8 %collective-permute-start.9 = (bf16[96,768]{1,0:T(8,128)(2,1)S(1)}, bf16[96,768]{1,0:T(8,128)(2,1)S(1)}, u32[]{:S(2)}, u32[]{:S(2)}) collective-permute-start(bf16[96,768]{1,0:T(8,128)(2,1)S(1)} %get-tuple-element.69), channel_id=1, source_target_pairs={{0,28},{4,0},{8,4},{12,8},{16,12},{20,16},{24,20},{28,24},{1,29},{... | collective-permute-start | bytes 442376 | tf_op jit(solution)/shard_map/rows/ppermute | solution.py:62
  47.8 6.7 %collective-permute-start.16 = (bf16[272,768]{1,0:T(8,128)(2,1)S(1)}, bf16[272,768]{1,0:T(8,128)(2,1)S(1)}, u32[]{:S(2)}, u32[]{:S(2)}) collective-permute-start(bf16[272,768]{1,0:T(8,128)(2,1)S(1)} %collective-permute-done.2.near), channel_id=1, source_target_pairs={{0,32},{32,0},{1,33},{33,1},{2,34},{34,2},{3,35},{35,3},{4,36},{36... | collective-permute-start | bytes 1253384 | tf_op jit(solution)/shard_map/weights/ppermute | solution.py:62
  50.4 12.6 %collective-permute-start.24 = (bf16[272,768]{1,0:T(8,128)(2,1)S(1)}, bf16[272,768]{1,0:T(8,128)(2,1)S(1)}, u32[]{:S(2)}, u32[]{:S(2)}) collective-permute-start(bf16[272,768]{1,0:T(8,128)(2,1)S(1)} %get-tuple-element.103), channel_id=1, source_target_pairs={{0,32},{32,0},{1,33},{33,1},{2,34},{34,2},{3,35},{35,3},{4,36},{36... | collective-permute-start | bytes 1253384 | tf_op jit(solution)/shard_map/ppermute | solution.py:62
  51.2 11.8 %collective-permute-start.26 = (bf16[128,768]{1,0:T(8,128)(2,1)S(1)}, bf16[128,768]{1,0:T(8,128)(2,1)S(1)}, u32[]{:S(2)}, u32[]{:S(2)}) collective-permute-start(bf16[128,768]{1,0:T(8,128)(2,1)S(1)} %get-tuple-element.107), channel_id=1, source_target_pairs={{0,1},{1,2},{2,3},{3,0},{4,5},{5,6},{6,7},{7,4},{8,9},{9,10},{10,1... | collective-permute-start | bytes 589832 | tf_op jit(solution)/shard_map/ppermute | solution.py:62
  51.3 10.8 %collective-permute-start.22 = (bf16[144,768]{1,0:T(8,128)(2,1)S(1)}, bf16[144,768]{1,0:T(8,128)(2,1)S(1)}, u32[]{:S(2)}, u32[]{:S(2)}) collective-permute-start(bf16[144,768]{1,0:T(8,128)(2,1)S(1)} %get-tuple-element.98), channel_id=1, source_target_pairs={{0,3},{1,0},{2,1},{3,2},{4,7},{5,4},{6,5},{7,6},{8,11},{9,8},{10,9... | collective-permute-start | bytes 663560 | tf_op jit(solution)/shard_map/ppermute | solution.py:62
  56.6 6.4 %collective-permute-start.25 = (bf16[272,768]{1,0:T(8,128)(2,1)S(1)}, bf16[272,768]{1,0:T(8,128)(2,1)S(1)}, u32[]{:S(2)}, u32[]{:S(2)}) collective-permute-start(bf16[272,768]{1,0:T(8,128)(2,1)S(1)} %get-tuple-element.105), channel_id=1, source_target_pairs={{0,32},{32,0},{1,33},{33,1},{2,34},{34,2},{3,35},{35,3},{4,36},{36... | collective-permute-start | bytes 1253384 | tf_op jit(solution)/shard_map/ppermute | solution.py:62
  63.0 15.1 %collective-permute-start.23 = (bf16[272,768]{1,0:T(8,128)(2,1)S(1)}, bf16[272,768]{1,0:T(8,128)(2,1)S(1)}, u32[]{:S(2)}, u32[]{:S(2)}) collective-permute-start(bf16[272,768]{1,0:T(8,128)(2,1)S(1)} %get-tuple-element.101), channel_id=1, source_target_pairs={{0,32},{32,0},{1,33},{33,1},{2,34},{34,2},{3,35},{35,3},{4,36},{36... | collective-permute-start | bytes 1253384 | tf_op jit(solution)/shard_map/ppermute | solution.py:62
  63.8 14.2 %collective-permute-start.27 = (bf16[272,768]{1,0:T(8,128)(2,1)S(1)}, bf16[272,768]{1,0:T(8,128)(2,1)S(1)}, u32[]{:S(2)}, u32[]{:S(2)}) collective-permute-start(bf16[272,768]{1,0:T(8,128)(2,1)S(1)} %get-tuple-element.108), channel_id=1, source_target_pairs={{0,3},{1,0},{2,1},{3,2},{4,7},{5,4},{6,5},{7,6},{8,11},{9,8},{10,9... | collective-permute-start | bytes 1253384 | tf_op jit(solution)/shard_map/weights_x/ppermute | solution.py:62
  65.5 13.0 %collective-permute-start.28 = (bf16[272,768]{1,0:T(8,128)(2,1)S(1)}, bf16[272,768]{1,0:T(8,128)(2,1)S(1)}, u32[]{:S(2)}, u32[]{:S(2)}) collective-permute-start(bf16[272,768]{1,0:T(8,128)(2,1)S(1)} %get-tuple-element.109), channel_id=1, source_target_pairs={{0,1},{1,2},{2,3},{3,0},{4,5},{5,6},{6,7},{7,4},{8,9},{9,10},{10,1... | collective-permute-start | bytes 1253384 | tf_op jit(solution)/shard_map/weights_x/ppermute | solution.py:62
  67.7 6.7 %collective-permute-start.20 = (bf16[128,768]{1,0:T(8,128)(2,1)S(1)}, bf16[128,768]{1,0:T(8,128)(2,1)S(1)}, u32[]{:S(2)}, u32[]{:S(2)}) collective-permute-start(bf16[128,768]{1,0:T(8,128)(2,1)S(1)} %get-tuple-element.94), channel_id=1, source_target_pairs={{0,28},{4,0},{8,4},{12,8},{16,12},{20,16},{24,20},{28,24},{32,36},... | collective-permute-start | bytes 589832 | tf_op jit(solution)/shard_map/rows_back/ppermute | solution.py:72
  75.0 8.8 %collective-permute-start.21 = (bf16[128,768]{1,0:T(8,128)(2,1)S(1)}, bf16[128,768]{1,0:T(8,128)(2,1)S(1)}, u32[]{:S(2)}, u32[]{:S(2)}) collective-permute-start(bf16[128,768]{1,0:T(8,128)(2,1)S(1)} %rows_back.3), channel_id=1, source_target_pairs={{0,24},{4,28},{8,0},{12,4},{16,8},{20,12},{24,16},{28,20},{32,40},... | collective-permute-start | bytes 589832 | tf_op jit(solution)/shard_map/rows_back/ppermute | solution.py:72
  79.4 7.8 %collective-permute-start.29 = (bf16[80,768]{1,0:T(8,128)(2,1)S(1)}, bf16[80,768]{1,0:T(8,128)(2,1)S(1)}, u32[]{:S(2)}, u32[]{:S(2)}) collective-permute-start(bf16[80,768]{1,0:T(8,128)(2,1)S(1)} %get-tuple-element.110), channel_id=1, source_target_pairs={{0,128},{64,192},{128,0},{192,64},{1,129},{65,193},{129,1},{193,65... | collective-permute-start | bytes 368648 | tf_op jit(solution)/shard_map/weights_y/ppermute | solution.py:62
  80.8 6.6 %collective-permute-start.31 = (bf16[80,768]{1,0:T(8,128)(2,1)S(1)}, bf16[80,768]{1,0:T(8,128)(2,1)S(1)}, u32[]{:S(2)}, u32[]{:S(2)}) collective-permute-start(bf16[80,768]{1,0:T(8,128)(2,1)S(1)} %get-tuple-element.114), channel_id=1, source_target_pairs={{0,64},{64,128},{128,192},{192,0},{1,65},{65,129},{129,193},{193,1... | collective-permute-start | bytes 368648 | tf_op jit(solution)/shard_map/weights_y/ppermute | solution.py:62
  (17 other events, 75.5 us)

commit v12 on v8

--- a/solution.py
+++ b/solution.py
@@ -72,24 +72,16 @@
     return lax.ppermute(x, ("core", axis), pairs)
 
 
-def prepare_kernel(place, lw, cw, w, part, raw, top, kids, sems):
-    copies = [
-        pltpu.make_async_copy(lw, raw, sems.at[0]),
-        pltpu.make_async_copy(cw, top, sems.at[1]),
-    ]
-    for c in copies:
-        c.start()
-    for c in copies:
-        c.wait()
+def prepare_kernel(place, lw, cw, w, part, kids):
     for c in range(CL):
         for j in range(D // 128):
-            kids[j, pl.ds(c, KIDS, stride=CL)] = raw[c, :, j * 128 : j * 128 + 128].astype(F32)
+            kids[j, pl.ds(c, KIDS, stride=CL)] = lw[c, :, j * 128 : j * 128 + 128].astype(F32)
     for y in range(NY):
         for core in range(NC):
             to, at = core * PART + y * 64, (y * NC + core) * 64
             for j in range(D // 128):
                 w[to : to + 64, j * 128 : j * 128 + 128] = kids[j, at : at + 64].astype(BF16)
-    w[TOP : TOP + CL] = top[...]
+    w[TOP : TOP + CL] = cw[...]
     part[...] = w[pl.ds(pl.multiple_of(place[1] * TOP, 16), PART)]
 
 
@@ -207,7 +199,9 @@
 
 def rows_kernel(place, *refs):
     dzs, ws, (near, last, far, own, ge) = refs[:NX], refs[NX : 2 * NX], refs[2 * NX :]
-    ge[...] = sum(dot(dzs[r][...], ws[r][...], TN) for r in range(NX))
+    kids = (pl.ds(0, TOP), pl.ds(TOP + CL, TOP))
+    tops = [jnp.concatenate([v[TOP : TOP + CL] for v in vs], axis=0) for vs in (dzs, ws)]
+    ge[...] = dot(*tops, TN) + sum(dot(dzs[r][k], ws[r][k], TN) for r in range(NX) for k in kids)
 
     def block(d):
         at = jnp.where(place[1] == 0, ORDER.index(d), ORDER.index(-d % NZ))
@@ -281,13 +275,7 @@
             prepare_kernel,
             [((WIDE, D), BF16), ((PART, D), BF16)],
             (place, lw, cw),
-            [
-                ((CL, KIDS, D), BF16),
-                ((CL, D), BF16),
-                ((D // 128, KIDS * CL, 128), F32),
-                (pltpu.SemaphoreType.DMA((2,)), None),
-            ],
-            own=2,
+            [((D // 128, KIDS * CL, 128), F32)],
         )
         low, high = shift(part, "x", 1), shift(part, "x", -1)
         low2, high2 = shift(low[:CUT], "x", 1), shift(high[CUT:], "x", -1)

time: 88.5 us -> 88 us (level)
  transfers between devices with their start and end apart: 33 -> 33, of which waited for: 8 -> 8; matrix products, arithmetic and copies ran while one was open for 0% -> 0% of each run, Pallas kernels for 25% -> 24%
where the time goes in v12:
time: 88 us; the launch traced here: 87.8 us
  starting transfers between devices  44 us (50%)
  Pallas kernels  22.9 us (26%)
  waiting for transfers between devices  17.1 us (19%)
  local copies, waits for them, and re-layouts  1.98 us (2%)
  between operations  0.95 us (1%)
    ppermute x29, starting transfers between devices, shift(): return lax.ppermute(x, axis, [(i, (i + by) % n) for i in range(n)])  38.7 us
    pallas_call x15, Pallas kernels, call(): pl.pallas_call(functools.partial(kernel, **static), out_shape=tuple((jax....  22.9 us
    ppermute x29, waiting for transfers between devices, shift(): return lax.ppermute(x, axis, [(i, (i + by) % n) for i in range(n)])  10 us
    ppermute x4, waiting for transfers between devices, turn(): return lax.ppermute(x, ('core', axis), pairs)  7.11 us
    ppermute x4, starting transfers between devices, turn(): return lax.ppermute(x, ('core', axis), pairs)  5.3 us
    unnamed x16, local copies, waits for them, and re-layouts  1.9 us
  transfers between devices with their start and end apart: 33, of which 8 were waited for; matrix products, arithmetic and copies ran while one was open for 0% of the time, Pallas kernels for 24%

profile of v12, /device:TPU:24, one launch (start us, length us, event | category | flops | bytes accessed | tf_op | source)
XLA Modules:
  0.0 87.8 jit_solution(15062224791817761703)
XLA Ops:
  5.7 1.7 %collective-permute-start.4 = (bf16[272,768]{1,0:T(8,128)(2,1)S(1)}, bf16[272,768]{1,0:T(8,128)(2,1)S(1)}, u32[]{:S(2)}, u32[]{:S(2)}) collective-permute-start(bf16[272,768]{1,0:T(8,128)(2,1)S(1)} %get-tuple-element.61), channel_id=1, source_target_pairs={{0,3},{1,0},{2,1},{3,2},{4,7},{5,4},{6,5},{7,6},{8,11},{9,8},{10,9... | collective-permute-start | bytes 1253384 | tf_op jit(solution)/shard_map/weights/ppermute | solution.py:62
  8.8 3.3 %collective-permute-start.6 = (bf16[144,768]{1,0:T(8,128)(2,1)S(1)}, bf16[144,768]{1,0:T(8,128)(2,1)S(1)}, u32[]{:S(2)}, u32[]{:S(2)}) collective-permute-start(bf16[144,768]{1,0:T(8,128)(2,1)S(1)} %get-tuple-element.62), channel_id=1, source_target_pairs={{0,8},{4,12},{8,16},{12,20},{16,24},{20,28},{24,0},{28,4},{1,9},{5... | collective-permute-start | bytes 663560 | tf_op jit(solution)/shard_map/rows/ppermute | solution.py:62
  12.1 3.1 %collective-permute-start.7 = (bf16[144,768]{1,0:T(8,128)(2,1)S(1)}, bf16[144,768]{1,0:T(8,128)(2,1)S(1)}, u32[]{:S(2)}, u32[]{:S(2)}) collective-permute-start(bf16[144,768]{1,0:T(8,128)(2,1)S(1)} %get-tuple-element.63), channel_id=1, source_target_pairs={{0,24},{4,28},{8,0},{12,4},{16,8},{20,12},{24,16},{28,20},{1,25},{... | collective-permute-start | bytes 663560 | tf_op jit(solution)/shard_map/rows/ppermute | solution.py:62
  17.2 3.0 %collective-permute-start.5 = (bf16[128,768]{1,0:T(8,128)(2,1)S(1)}, bf16[128,768]{1,0:T(8,128)(2,1)S(1)}, u32[]{:S(2)}, u32[]{:S(2)}) collective-permute-start(bf16[128,768]{1,0:T(8,128)(2,1)S(1)} %slice.33), channel_id=1, source_target_pairs={{0,3},{1,0},{2,1},{3,2},{4,7},{5,4},{6,5},{7,6},{8,11},{9,8},{10,9... | collective-permute-start | bytes 589832 | tf_op jit(solution)/shard_map/weights/ppermute | solution.py:62
  20.2 1.9 %collective-permute-start = (bf16[96,768]{1,0:T(8,128)(2,1)S(1)}, bf16[96,768]{1,0:T(8,128)(2,1)S(1)}, u32[]{:S(2)}, u32[]{:S(2)}) collective-permute-start(bf16[96,768]{1,0:T(8,128)(2,1)S(1)} %get-tuple-element.59), channel_id=1, source_target_pairs={{0,4},{4,8},{8,12},{12,16},{16,20},{20,24},{24,28},{28,0},{1,5},{5... | collective-permute-start | bytes 442376 | tf_op jit(solution)/shard_map/rows/ppermute | solution.py:62
  22.1 4.5 %collective-permute-start.1 = (bf16[96,768]{1,0:T(8,128)(2,1)S(1)}, bf16[96,768]{1,0:T(8,128)(2,1)S(1)}, u32[]{:S(2)}, u32[]{:S(2)}) collective-permute-start(bf16[96,768]{1,0:T(8,128)(2,1)S(1)} %get-tuple-element.60), channel_id=1, source_target_pairs={{0,28},{4,0},{8,4},{12,8},{16,12},{20,16},{24,20},{28,24},{1,29},{... | collective-permute-start | bytes 442376 | tf_op jit(solution)/shard_map/rows/ppermute | solution.py:62
  26.7 4.1 %collective-permute-start.11 = (bf16[48,768]{1,0:T(8,128)(2,1)S(1)}, bf16[48,768]{1,0:T(8,128)(2,1)S(1)}, u32[]{:S(2)}, u32[]{:S(2)}) collective-permute-start(bf16[48,768]{1,0:T(8,128)(2,1)S(1)} %slice.29), channel_id=1, source_target_pairs={{0,24},{4,28},{8,0},{12,4},{16,8},{20,12},{24,16},{28,20},{1,25},{... | collective-permute-start | bytes 221192 | tf_op jit(solution)/shard_map/rows/ppermute | solution.py:62
  30.8 3.7 %collective-permute-start.9 = (bf16[96,768]{1,0:T(8,128)(2,1)S(1)}, bf16[96,768]{1,0:T(8,128)(2,1)S(1)}, u32[]{:S(2)}, u32[]{:S(2)}) collective-permute-start(bf16[96,768]{1,0:T(8,128)(2,1)S(1)} %slice.27), channel_id=1, source_target_pairs={{0,28},{4,0},{8,4},{12,8},{16,12},{20,16},{24,20},{28,24},{1,29},{... | collective-permute-start | bytes 442376 | tf_op jit(solution)/shard_map/rows/ppermute | solution.py:62
  34.5 2.1 %shard_map.103.refs_13_.refs_2_.refs_3_ = f32[4,528,256]{2,1,0:T(8,128)S(1)} custom-call(s32[4]{0:T(128)S(1)} %pad_add_fusion.place, bf16[32,768]{1,0:T(8,128)(2,1)S(1)} %get-tuple-element.68.refs_0_, bf16[96,768]{1,0:T(8,128)(2,1)S(1)} %collective-permute-done.refs_1_, bf16[96,768]{1,0:T(8,128)(2,1)S(1)} %collective-permute-done.1.refs_2_, ...), custom_call_target="tpu_custom_call" | custom-call | flops 2000000000 | bytes 1048576 | tf_op jit(solution)/shard_map/pallas_call | solution.py:49
  38.4 2.4 %collective-permute-done.8.refs_1_.refs_5_ = bf16[96,768]{1,0:T(8,128)(2,1)S(1)} collective-permute-done((bf16[96,768]{1,0:T(8,128)(2,1)S(1)}, bf16[96,768]{1,0:T(8,128)(2,1)S(1)}, u32[]{:S(2)}, u32[]{:S(2)}) %collective-permute-start.8) | collective-permute-done | bytes 147488 | tf_op jit(solution)/shard_map/rows/ppermute | solution.py:62
  40.9 2.1 %shard_map.104.refs_14_.refs_3_.refs_4_ = f32[4,528,256]{2,1,0:T(8,128)S(1)} custom-call(s32[4]{0:T(128)S(1)} %pad_add_fusion.place, bf16[144,768]{1,0:T(8,128)(2,1)S(1)} %collective-permute-done.7.refs_0_.refs_4_, bf16[96,768]{1,0:T(8,128)(2,1)S(1)} %collective-permute-done.8.refs_1_.refs_5_, bf16[96,768]{1,0:T(8,128)(2,1)S(1)} %collective-permute-done.9.refs_2_.refs_6_, ...), custom_call_target="tpu_custom_call" | custom-call | flops 2000000000 | bytes 1048576 | tf_op jit(solution)/shard_map/pallas_call | solution.py:49
  43.0 2.1 %shard_map.105 = (f32[272,768]{1,0:T(8,128)S(1)}, bf16[272,768]{1,0:T(8,128)(2,1)S(1)}, bf16[528,512]{1,0:T(8,128)(2,1)S(1)}, bf16[512,768]{1,0:T(8,128)(2,1)S(1)}, bf16[528,768]{1,0:T(8,128)(2,1)S(1)}) custom-call(s32[4]{0:T(128)S(1)} %pad_add_fusion.place, bf16[64,768]{1,0:T(8,128)(2,1)S(1)} %copy-done.2, ...), custom_call_target="tpu_custom_call" | custom-call | flops 2000000000 | bytes 1048576 | tf_op jit(solution)/shard_map/pallas_call | solution.py:49
  45.7 2.1 %shard_map.107 = (f32[272,768]{1,0:T(8,128)S(1)}, bf16[272,768]{1,0:T(8,128)(2,1)S(1)}, bf16[528,512]{1,0:T(8,128)(2,1)S(1)}, bf16[528,768]{1,0:T(8,128)(2,1)S(1)}) custom-call(s32[4]{0:T(128)S(1)} %pad_add_fusion.place, bf16[512,768]{1,0:T(8,128)(2,1)S(1)} %get-tuple-element.79.refs_0_, bf16[272,768]{1,0:T(8,128)(2,1)S(1)} %collective-permute-done.2.refs_1_, ...), custom_call_target="tpu_custom_call" | custom-call | flops 2000000000 | bytes 1048576 | tf_op jit(solution)/shard_map/pallas_call | solution.py:49
  48.7 3.2 %collective-permute-start.22 = (bf16[144,768]{1,0:T(8,128)(2,1)S(1)}, bf16[144,768]{1,0:T(8,128)(2,1)S(1)}, u32[]{:S(2)}, u32[]{:S(2)}) collective-permute-start(bf16[144,768]{1,0:T(8,128)(2,1)S(1)} %get-tuple-element.94), channel_id=1, source_target_pairs={{0,3},{1,0},{2,1},{3,2},{4,7},{5,4},{6,5},{7,6},{8,11},{9,8},{10,9... | collective-permute-start | bytes 663560 | tf_op jit(solution)/shard_map/ppermute | solution.py:62
  51.9 2.1 %shard_map.108 = (f32[272,768]{1,0:T(8,128)S(1)}, bf16[272,768]{1,0:T(8,128)(2,1)S(1)}, bf16[528,512]{1,0:T(8,128)(2,1)S(1)}, bf16[528,768]{1,0:T(8,128)(2,1)S(1)}) custom-call(s32[4]{0:T(128)S(1)} %pad_add_fusion.place, bf16[512,768]{1,0:T(8,128)(2,1)S(1)} %get-tuple-element.79.refs_0_, bf16[272,768]{1,0:T(8,128)(2,1)S(1)} %collective-permute-done.4.refs_1_, ...), custom_call_target="tpu_custom_call" | custom-call | flops 2000000000 | bytes 1048576 | tf_op jit(solution)/shard_map/pallas_call | solution.py:49
  54.1 2.1 %shard_map.106 = (bf16[272,768]{1,0:T(8,128)(2,1)S(1)}, bf16[272,768]{1,0:T(8,128)(2,1)S(1)}, bf16[528,512]{1,0:T(8,128)(2,1)S(1)}) custom-call(s32[4]{0:T(128)S(1)} %pad_add_fusion.place, bf16[512,768]{1,0:T(8,128)(2,1)S(1)} %get-tuple-element.79.refs_0_, bf16[528,768]{1,0:T(8,128)(2,1)S(1)} %get-tuple-element.80.refs_1_.refs_4_, ...), custom_call_target="tpu_custom_call" | custom-call | flops 2000000000 | bytes 1048576 | tf_op jit(solution)/shard_map/pallas_call | solution.py:49
  56.2 2.8 %shard_map.109 = (bf16[192,768]{1,0:T(8,128)(2,1)S(1)}, bf16[64,768]{1,0:T(8,128)(2,1)S(1)}, bf16[192,768]{1,0:T(8,128)(2,1)S(1)}, f32[64,768]{1,0:T(8,128)S(1)}) custom-call(s32[4]{0:T(128)S(1)} %pad_add_fusion.place, bf16[528,512]{1,0:T(8,128)(2,1)S(1)} %get-tuple-element.81.refs_0_, bf16[528,512]{1,0:T(8,128)(2,1)S(1)} %get-tuple-element.82.refs_1_, ...), custom_call_target="tpu_custom_call" | custom-call | flops 2000000000 | bytes 1048576 | tf_op jit(solution)/shard_map/pallas_call | solution.py:49
  60.5 1.8 %collective-permute-start.27 = (bf16[272,768]{1,0:T(8,128)(2,1)S(1)}, bf16[272,768]{1,0:T(8,128)(2,1)S(1)}, u32[]{:S(2)}, u32[]{:S(2)}) collective-permute-start(bf16[272,768]{1,0:T(8,128)(2,1)S(1)} %get-tuple-element.104), channel_id=1, source_target_pairs={{0,3},{1,0},{2,1},{3,2},{4,7},{5,4},{6,5},{7,6},{8,11},{9,8},{10,9... | collective-permute-start | bytes 1253384 | tf_op jit(solution)/shard_map/weights_x/ppermute | solution.py:62
  64.3 5.3 %collective-permute-done.20.got4 = bf16[64,768]{1,0:T(8,128)(2,1)S(1)} collective-permute-done((bf16[64,768]{1,0:T(8,128)(2,1)S(1)}, bf16[64,768]{1,0:T(8,128)(2,1)S(1)}, u32[]{:S(2)}, u32[]{:S(2)}) %collective-permute-start.20) | collective-permute-done | bytes 98336 | tf_op jit(solution)/shard_map/rows_back/ppermute | solution.py:72
  69.6 4.3 %collective-permute-start.18 = (bf16[128,768]{1,0:T(8,128)(2,1)S(1)}, bf16[128,768]{1,0:T(8,128)(2,1)S(1)}, u32[]{:S(2)}, u32[]{:S(2)}) collective-permute-start(bf16[128,768]{1,0:T(8,128)(2,1)S(1)} %get-tuple-element.91), channel_id=1, source_target_pairs={{0,28},{4,0},{8,4},{12,8},{16,12},{20,16},{24,20},{28,24},{32,36},... | collective-permute-start | bytes 589832 | tf_op jit(solution)/shard_map/rows_back/ppermute | solution.py:72
  77.5 2.2 %collective-permute-start.31 = (bf16[80,768]{1,0:T(8,128)(2,1)S(1)}, bf16[80,768]{1,0:T(8,128)(2,1)S(1)}, u32[]{:S(2)}, u32[]{:S(2)}) collective-permute-start(bf16[80,768]{1,0:T(8,128)(2,1)S(1)} %get-tuple-element.110), channel_id=1, source_target_pairs={{0,64},{64,128},{128,192},{192,0},{1,65},{65,129},{129,193},{193,1... | collective-permute-start | bytes 368648 | tf_op jit(solution)/shard_map/weights_y/ppermute | solution.py:62
  79.7 1.8 %collective-permute-done.21 = bf16[128,768]{1,0:T(8,128)(2,1)S(1)} collective-permute-done((bf16[128,768]{1,0:T(8,128)(2,1)S(1)}, bf16[128,768]{1,0:T(8,128)(2,1)S(1)}, u32[]{:S(2)}, u32[]{:S(2)}) %collective-permute-start.21) | collective-permute-done | bytes 196640 | tf_op jit(solution)/shard_map/rows_back/ppermute | solution.py:72
  81.5 2.4 %collective-permute-done.29.g2 = bf16[80,768]{1,0:T(8,128)(2,1)S(1)} collective-permute-done((bf16[80,768]{1,0:T(8,128)(2,1)S(1)}, bf16[80,768]{1,0:T(8,128)(2,1)S(1)}, u32[]{:S(2)}, u32[]{:S(2)}) %collective-permute-start.29) | collective-permute-done | bytes 122912 | tf_op jit(solution)/shard_map/weights_y/ppermute | solution.py:62
  84.1 1.7 %collective-permute-done.32.g3 = bf16[80,768]{1,0:T(8,128)(2,1)S(1)} collective-permute-done((bf16[80,768]{1,0:T(8,128)(2,1)S(1)}, bf16[80,768]{1,0:T(8,128)(2,1)S(1)}, u32[]{:S(2)}, u32[]{:S(2)}) %collective-permute-start.32) | collective-permute-done | bytes 122912 | tf_op jit(solution)/shard_map/weights_y/ppermute | solution.py:62
  (83 shorter events, 21.0 us)
Async XLA Ops:
  4.1 12.7 %collective-permute-start.2 = (bf16[272,768]{1,0:T(8,128)(2,1)S(1)}, bf16[272,768]{1,0:T(8,128)(2,1)S(1)}, u32[]{:S(2)}, u32[]{:S(2)}) collective-permute-start(bf16[272,768]{1,0:T(8,128)(2,1)S(1)} %get-tuple-element.61), channel_id=1, source_target_pairs={{0,1},{1,2},{2,3},{3,0},{4,5},{5,6},{6,7},{7,4},{8,9},{9,10},{10,1... | collective-permute-start | bytes 1253384 | tf_op jit(solution)/shard_map/weights/ppermute | solution.py:62
  5.7 11.5 %collective-permute-start.4 = (bf16[272,768]{1,0:T(8,128)(2,1)S(1)}, bf16[272,768]{1,0:T(8,128)(2,1)S(1)}, u32[]{:S(2)}, u32[]{:S(2)}) collective-permute-start(bf16[272,768]{1,0:T(8,128)(2,1)S(1)} %get-tuple-element.61), channel_id=1, source_target_pairs={{0,3},{1,0},{2,1},{3,2},{4,7},{5,4},{6,5},{7,6},{8,11},{9,8},{10,9... | collective-permute-start | bytes 1253384 | tf_op jit(solution)/shard_map/weights/ppermute | solution.py:62
  8.8 13.4 %collective-permute-start.6 = (bf16[144,768]{1,0:T(8,128)(2,1)S(1)}, bf16[144,768]{1,0:T(8,128)(2,1)S(1)}, u32[]{:S(2)}, u32[]{:S(2)}) collective-permute-start(bf16[144,768]{1,0:T(8,128)(2,1)S(1)} %get-tuple-element.62), channel_id=1, source_target_pairs={{0,8},{4,12},{8,16},{12,20},{16,24},{20,28},{24,0},{28,4},{1,9},{5... | collective-permute-start | bytes 663560 | tf_op jit(solution)/shard_map/rows/ppermute | solution.py:62
  12.1 14.5 %collective-permute-start.7 = (bf16[144,768]{1,0:T(8,128)(2,1)S(1)}, bf16[144,768]{1,0:T(8,128)(2,1)S(1)}, u32[]{:S(2)}, u32[]{:S(2)}) collective-permute-start(bf16[144,768]{1,0:T(8,128)(2,1)S(1)} %get-tuple-element.63), channel_id=1, source_target_pairs={{0,24},{4,28},{8,0},{12,4},{16,8},{20,12},{24,16},{28,20},{1,25},{... | collective-permute-start | bytes 663560 | tf_op jit(solution)/shard_map/rows/ppermute | solution.py:62
  16.8 9.9 %collective-permute-start.3 = (bf16[144,768]{1,0:T(8,128)(2,1)S(1)}, bf16[144,768]{1,0:T(8,128)(2,1)S(1)}, u32[]{:S(2)}, u32[]{:S(2)}) collective-permute-start(bf16[144,768]{1,0:T(8,128)(2,1)S(1)} %slice.32), channel_id=1, source_target_pairs={{0,1},{1,2},{2,3},{3,0},{4,5},{5,6},{6,7},{7,4},{8,9},{9,10},{10,1... | collective-permute-start | bytes 663560 | tf_op jit(solution)/shard_map/weights/ppermute | solution.py:62
  17.2 9.5 %collective-permute-start.5 = (bf16[128,768]{1,0:T(8,128)(2,1)S(1)}, bf16[128,768]{1,0:T(8,128)(2,1)S(1)}, u32[]{:S(2)}, u32[]{:S(2)}) collective-permute-start(bf16[128,768]{1,0:T(8,128)(2,1)S(1)} %slice.33), channel_id=1, source_target_pairs={{0,3},{1,0},{2,1},{3,2},{4,7},{5,4},{6,5},{7,6},{8,11},{9,8},{10,9... | collective-permute-start | bytes 589832 | tf_op jit(solution)/shard_map/weights/ppermute | solution.py:62
  20.2 14.3 %collective-permute-start = (bf16[96,768]{1,0:T(8,128)(2,1)S(1)}, bf16[96,768]{1,0:T(8,128)(2,1)S(1)}, u32[]{:S(2)}, u32[]{:S(2)}) collective-permute-start(bf16[96,768]{1,0:T(8,128)(2,1)S(1)} %get-tuple-element.59), channel_id=1, source_target_pairs={{0,4},{4,8},{8,12},{12,16},{16,20},{20,24},{24,28},{28,0},{1,5},{5... | collective-permute-start | bytes 442376 | tf_op jit(solution)/shard_map/rows/ppermute | solution.py:62
  22.1 12.4 %collective-permute-start.1 = (bf16[96,768]{1,0:T(8,128)(2,1)S(1)}, bf16[96,768]{1,0:T(8,128)(2,1)S(1)}, u32[]{:S(2)}, u32[]{:S(2)}) collective-permute-start(bf16[96,768]{1,0:T(8,128)(2,1)S(1)} %get-tuple-element.60), channel_id=1, source_target_pairs={{0,28},{4,0},{8,4},{12,8},{16,12},{20,16},{24,20},{28,24},{1,29},{... | collective-permute-start | bytes 442376 | tf_op jit(solution)/shard_map/rows/ppermute | solution.py:62
  26.7 9.9 %collective-permute-start.11 = (bf16[48,768]{1,0:T(8,128)(2,1)S(1)}, bf16[48,768]{1,0:T(8,128)(2,1)S(1)}, u32[]{:S(2)}, u32[]{:S(2)}) collective-permute-start(bf16[48,768]{1,0:T(8,128)(2,1)S(1)} %slice.29), channel_id=1, source_target_pairs={{0,24},{4,28},{8,0},{12,4},{16,8},{20,12},{24,16},{28,20},{1,25},{... | collective-permute-start | bytes 221192 | tf_op jit(solution)/shard_map/rows/ppermute | solution.py:62
  30.8 7.1 %collective-permute-start.10 = (bf16[48,768]{1,0:T(8,128)(2,1)S(1)}, bf16[48,768]{1,0:T(8,128)(2,1)S(1)}, u32[]{:S(2)}, u32[]{:S(2)}) collective-permute-start(bf16[48,768]{1,0:T(8,128)(2,1)S(1)} %slice.28), channel_id=1, source_target_pairs={{0,8},{4,12},{8,16},{12,20},{16,24},{20,28},{24,0},{28,4},{1,9},{5... | collective-permute-start | bytes 221192 | tf_op jit(solution)/shard_map/rows/ppermute | solution.py:62
  30.8 7.6 %collective-permute-start.9 = (bf16[96,768]{1,0:T(8,128)(2,1)S(1)}, bf16[96,768]{1,0:T(8,128)(2,1)S(1)}, u32[]{:S(2)}, u32[]{:S(2)}) collective-permute-start(bf16[96,768]{1,0:T(8,128)(2,1)S(1)} %slice.27), channel_id=1, source_target_pairs={{0,28},{4,0},{8,4},{12,8},{16,12},{20,16},{24,20},{28,24},{1,29},{... | collective-permute-start | bytes 442376 | tf_op jit(solution)/shard_map/rows/ppermute | solution.py:62
  38.4 7.2 %collective-permute-start.15 = (bf16[272,768]{1,0:T(8,128)(2,1)S(1)}, bf16[272,768]{1,0:T(8,128)(2,1)S(1)}, u32[]{:S(2)}, u32[]{:S(2)}) collective-permute-start(bf16[272,768]{1,0:T(8,128)(2,1)S(1)} %collective-permute-done.2.refs_1_), channel_id=1, source_target_pairs={{0,32},{32,0},{1,33},{33,1},{2,34},{34,2},{3,35},{35,3},{4,36},{36... | collective-permute-start | bytes 1253384 | tf_op jit(solution)/shard_map/weights/ppermute | solution.py:62
  45.2 6.7 %collective-permute-start.16 = (bf16[272,768]{1,0:T(8,128)(2,1)S(1)}, bf16[272,768]{1,0:T(8,128)(2,1)S(1)}, u32[]{:S(2)}, u32[]{:S(2)}) collective-permute-start(bf16[272,768]{1,0:T(8,128)(2,1)S(1)} %collective-permute-done.4.refs_1_), channel_id=1, source_target_pairs={{0,32},{32,0},{1,33},{33,1},{2,34},{34,2},{3,35},{35,3},{4,36},{36... | collective-permute-start | bytes 1253384 | tf_op jit(solution)/shard_map/weights/ppermute | solution.py:62
  47.8 11.9 %collective-permute-start.24 = (bf16[272,768]{1,0:T(8,128)(2,1)S(1)}, bf16[272,768]{1,0:T(8,128)(2,1)S(1)}, u32[]{:S(2)}, u32[]{:S(2)}) collective-permute-start(bf16[272,768]{1,0:T(8,128)(2,1)S(1)} %get-tuple-element.99), channel_id=1, source_target_pairs={{0,32},{32,0},{1,33},{33,1},{2,34},{34,2},{3,35},{35,3},{4,36},{36... | collective-permute-start | bytes 1253384 | tf_op jit(solution)/shard_map/ppermute | solution.py:62
  48.6 11.1 %collective-permute-start.26 = (bf16[128,768]{1,0:T(8,128)(2,1)S(1)}, bf16[128,768]{1,0:T(8,128)(2,1)S(1)}, u32[]{:S(2)}, u32[]{:S(2)}) collective-permute-start(bf16[128,768]{1,0:T(8,128)(2,1)S(1)} %get-tuple-element.103), channel_id=1, source_target_pairs={{0,1},{1,2},{2,3},{3,0},{4,5},{5,6},{6,7},{7,4},{8,9},{9,10},{10,1... | collective-permute-start | bytes 589832 | tf_op jit(solution)/shard_map/ppermute | solution.py:62
  48.7 10.8 %collective-permute-start.22 = (bf16[144,768]{1,0:T(8,128)(2,1)S(1)}, bf16[144,768]{1,0:T(8,128)(2,1)S(1)}, u32[]{:S(2)}, u32[]{:S(2)}) collective-permute-start(bf16[144,768]{1,0:T(8,128)(2,1)S(1)} %get-tuple-element.94), channel_id=1, source_target_pairs={{0,3},{1,0},{2,1},{3,2},{4,7},{5,4},{6,5},{7,6},{8,11},{9,8},{10,9... | collective-permute-start | bytes 663560 | tf_op jit(solution)/shard_map/ppermute | solution.py:62
  59.6 15.0 %collective-permute-start.23 = (bf16[272,768]{1,0:T(8,128)(2,1)S(1)}, bf16[272,768]{1,0:T(8,128)(2,1)S(1)}, u32[]{:S(2)}, u32[]{:S(2)}) collective-permute-start(bf16[272,768]{1,0:T(8,128)(2,1)S(1)} %get-tuple-element.97), channel_id=1, source_target_pairs={{0,32},{32,0},{1,33},{33,1},{2,34},{34,2},{3,35},{35,3},{4,36},{36... | collective-permute-start | bytes 1253384 | tf_op jit(solution)/shard_map/ppermute | solution.py:62
  60.5 14.1 %collective-permute-start.27 = (bf16[272,768]{1,0:T(8,128)(2,1)S(1)}, bf16[272,768]{1,0:T(8,128)(2,1)S(1)}, u32[]{:S(2)}, u32[]{:S(2)}) collective-permute-start(bf16[272,768]{1,0:T(8,128)(2,1)S(1)} %get-tuple-element.104), channel_id=1, source_target_pairs={{0,3},{1,0},{2,1},{3,2},{4,7},{5,4},{6,5},{7,6},{8,11},{9,8},{10,9... | collective-permute-start | bytes 1253384 | tf_op jit(solution)/shard_map/weights_x/ppermute | solution.py:62
  62.3 12.9 %collective-permute-start.28 = (bf16[272,768]{1,0:T(8,128)(2,1)S(1)}, bf16[272,768]{1,0:T(8,128)(2,1)S(1)}, u32[]{:S(2)}, u32[]{:S(2)}) collective-permute-start(bf16[272,768]{1,0:T(8,128)(2,1)S(1)} %get-tuple-element.105), channel_id=1, source_target_pairs={{0,1},{1,2},{2,3},{3,0},{4,5},{5,6},{6,7},{7,4},{8,9},{9,10},{10,1... | collective-permute-start | bytes 1253384 | tf_op jit(solution)/shard_map/weights_x/ppermute | solution.py:62
  63.4 10.5 %collective-permute-start.19 = (bf16[128,768]{1,0:T(8,128)(2,1)S(1)}, bf16[128,768]{1,0:T(8,128)(2,1)S(1)}, u32[]{:S(2)}, u32[]{:S(2)}) collective-permute-start(bf16[128,768]{1,0:T(8,128)(2,1)S(1)} %get-tuple-element.92), channel_id=1, source_target_pairs={{0,28},{4,0},{8,4},{12,8},{16,12},{20,16},{24,20},{28,24},{32,36},... | collective-permute-start | bytes 589832 | tf_op jit(solution)/shard_map/rows_back/ppermute | solution.py:72
  69.6 14.3 %collective-permute-start.18 = (bf16[128,768]{1,0:T(8,128)(2,1)S(1)}, bf16[128,768]{1,0:T(8,128)(2,1)S(1)}, u32[]{:S(2)}, u32[]{:S(2)}) collective-permute-start(bf16[128,768]{1,0:T(8,128)(2,1)S(1)} %get-tuple-element.91), channel_id=1, source_target_pairs={{0,28},{4,0},{8,4},{12,8},{16,12},{20,16},{24,20},{28,24},{32,36},... | collective-permute-start | bytes 589832 | tf_op jit(solution)/shard_map/rows_back/ppermute | solution.py:72
  74.5 7.0 %collective-permute-start.21 = (bf16[128,768]{1,0:T(8,128)(2,1)S(1)}, bf16[128,768]{1,0:T(8,128)(2,1)S(1)}, u32[]{:S(2)}, u32[]{:S(2)}) collective-permute-start(bf16[128,768]{1,0:T(8,128)(2,1)S(1)} %rows_back.3), channel_id=1, source_target_pairs={{0,24},{4,28},{8,0},{12,4},{16,8},{20,12},{24,16},{28,20},{32,40},... | collective-permute-start | bytes 589832 | tf_op jit(solution)/shard_map/rows_back/ppermute | solution.py:72
  76.2 7.7 %collective-permute-start.29 = (bf16[80,768]{1,0:T(8,128)(2,1)S(1)}, bf16[80,768]{1,0:T(8,128)(2,1)S(1)}, u32[]{:S(2)}, u32[]{:S(2)}) collective-permute-start(bf16[80,768]{1,0:T(8,128)(2,1)S(1)} %get-tuple-element.106), channel_id=1, source_target_pairs={{0,128},{64,192},{128,0},{192,64},{1,129},{65,193},{129,1},{193,65... | collective-permute-start | bytes 368648 | tf_op jit(solution)/shard_map/weights_y/ppermute | solution.py:62
  77.5 6.6 %collective-permute-start.31 = (bf16[80,768]{1,0:T(8,128)(2,1)S(1)}, bf16[80,768]{1,0:T(8,128)(2,1)S(1)}, u32[]{:S(2)}, u32[]{:S(2)}) collective-permute-start(bf16[80,768]{1,0:T(8,128)(2,1)S(1)} %get-tuple-element.110), channel_id=1, source_target_pairs={{0,64},{64,128},{128,192},{192,0},{1,65},{65,129},{129,193},{193,1... | collective-permute-start | bytes 368648 | tf_op jit(solution)/shard_map/weights_y/ppermute | solution.py:62
  (17 other events, 75.1 us)

commit v13 on v12

--- a/solution.py
+++ b/solution.py
@@ -368,6 +368,7 @@
         t1, t3 = shift(t1, "x", -1), shift(t3, "x", 1)
 
     with jax.named_scope("rows_back"):
+        h3, last, h1 = lax.optimization_barrier((h3, last, h1))
         (h2,) = call(pass_kernel, [pair], (place, near, far, h3, last))
         h2 = turn(h2, "z", -2)
 

time: 88 us -> 87.7 us (level)
  starting transfers between devices: 44 us -> 42.1 us
  waiting for transfers between devices: 17.1 us -> 18.8 us
    ppermute x4, waiting for transfers between devices: 7.11 us -> 9.28 us  [turn(): return lax.ppermute(x, ('core', axis), pairs)]
    ppermute x4, starting transfers between devices: 5.3 us -> 3.6 us  [turn(): return lax.ppermute(x, ('core', axis), pairs)]
  transfers between devices with their start and end apart: 33 -> 33, of which waited for: 8 -> 10; matrix products, arithmetic and copies ran while one was open for 0% -> 0% of each run, Pallas kernels for 24% -> 24%
where the time goes in v13:
time: 87.7 us; the launch traced here: 87.6 us
  starting transfers between devices  42.1 us (48%)
  Pallas kernels  22.9 us (26%)
  waiting for transfers between devices  18.8 us (21%)
  local copies, waits for them, and re-layouts  1.98 us (2%)
  between operations  0.94 us (1%)
    ppermute x29, starting transfers between devices, shift(): return lax.ppermute(x, axis, [(i, (i + by) % n) for i in range(n)])  38.5 us
    pallas_call x15, Pallas kernels, call(): pl.pallas_call(functools.partial(kernel, **static), out_shape=tuple((jax....  22.9 us
    ppermute x29, waiting for transfers between devices, shift(): return lax.ppermute(x, axis, [(i, (i + by) % n) for i in range(n)])  9.55 us
    ppermute x4, waiting for transfers between devices, turn(): return lax.ppermute(x, ('core', axis), pairs)  9.28 us
    ppermute x4, starting transfers between devices, turn(): return lax.ppermute(x, ('core', axis), pairs)  3.6 us
    unnamed x16, local copies, waits for them, and re-layouts  1.9 us
  transfers between devices with their start and end apart: 33, of which 10 were waited for; matrix products, arithmetic and copies ran while one was open for 0% of the time, Pallas kernels for 24%

profile of v13, /device:TPU:24, one launch (start us, length us, event | category | flops | bytes accessed | tf_op | source)
XLA Modules:
  0.0 87.6 jit_solution(13043739928367886661)
XLA Ops:
  8.8 3.3 %collective-permute-start.6 = (bf16[144,768]{1,0:T(8,128)(2,1)S(1)}, bf16[144,768]{1,0:T(8,128)(2,1)S(1)}, u32[]{:S(2)}, u32[]{:S(2)}) collective-permute-start(bf16[144,768]{1,0:T(8,128)(2,1)S(1)} %get-tuple-element.65), channel_id=1, source_target_pairs={{0,8},{4,12},{8,16},{12,20},{16,24},{20,28},{24,0},{28,4},{1,9},{5... | collective-permute-start | bytes 663560 | tf_op jit(solution)/shard_map/rows/ppermute | solution.py:62
  12.1 3.1 %collective-permute-start.7 = (bf16[144,768]{1,0:T(8,128)(2,1)S(1)}, bf16[144,768]{1,0:T(8,128)(2,1)S(1)}, u32[]{:S(2)}, u32[]{:S(2)}) collective-permute-start(bf16[144,768]{1,0:T(8,128)(2,1)S(1)} %get-tuple-element.66), channel_id=1, source_target_pairs={{0,24},{4,28},{8,0},{12,4},{16,8},{20,12},{24,16},{28,20},{1,25},{... | collective-permute-start | bytes 663560 | tf_op jit(solution)/shard_map/rows/ppermute | solution.py:62
  17.2 3.0 %collective-permute-start.5 = (bf16[128,768]{1,0:T(8,128)(2,1)S(1)}, bf16[128,768]{1,0:T(8,128)(2,1)S(1)}, u32[]{:S(2)}, u32[]{:S(2)}) collective-permute-start(bf16[128,768]{1,0:T(8,128)(2,1)S(1)} %slice.33), channel_id=1, source_target_pairs={{0,3},{1,0},{2,1},{3,2},{4,7},{5,4},{6,5},{7,6},{8,11},{9,8},{10,9... | collective-permute-start | bytes 589832 | tf_op jit(solution)/shard_map/weights/ppermute | solution.py:62
  20.2 1.9 %collective-permute-start = (bf16[96,768]{1,0:T(8,128)(2,1)S(1)}, bf16[96,768]{1,0:T(8,128)(2,1)S(1)}, u32[]{:S(2)}, u32[]{:S(2)}) collective-permute-start(bf16[96,768]{1,0:T(8,128)(2,1)S(1)} %get-tuple-element.62), channel_id=1, source_target_pairs={{0,4},{4,8},{8,12},{12,16},{16,20},{20,24},{24,28},{28,0},{1,5},{5... | collective-permute-start | bytes 442376 | tf_op jit(solution)/shard_map/rows/ppermute | solution.py:62
  22.1 4.5 %collective-permute-start.1 = (bf16[96,768]{1,0:T(8,128)(2,1)S(1)}, bf16[96,768]{1,0:T(8,128)(2,1)S(1)}, u32[]{:S(2)}, u32[]{:S(2)}) collective-permute-start(bf16[96,768]{1,0:T(8,128)(2,1)S(1)} %get-tuple-element.63), channel_id=1, source_target_pairs={{0,28},{4,0},{8,4},{12,8},{16,12},{20,16},{24,20},{28,24},{1,29},{... | collective-permute-start | bytes 442376 | tf_op jit(solution)/shard_map/rows/ppermute | solution.py:62
  26.7 4.1 %collective-permute-start.11 = (bf16[48,768]{1,0:T(8,128)(2,1)S(1)}, bf16[48,768]{1,0:T(8,128)(2,1)S(1)}, u32[]{:S(2)}, u32[]{:S(2)}) collective-permute-start(bf16[48,768]{1,0:T(8,128)(2,1)S(1)} %slice.29), channel_id=1, source_target_pairs={{0,24},{4,28},{8,0},{12,4},{16,8},{20,12},{24,16},{28,20},{1,25},{... | collective-permute-start | bytes 221192 | tf_op jit(solution)/shard_map/rows/ppermute | solution.py:62
  30.8 3.7 %collective-permute-start.9 = (bf16[96,768]{1,0:T(8,128)(2,1)S(1)}, bf16[96,768]{1,0:T(8,128)(2,1)S(1)}, u32[]{:S(2)}, u32[]{:S(2)}) collective-permute-start(bf16[96,768]{1,0:T(8,128)(2,1)S(1)} %slice.27), channel_id=1, source_target_pairs={{0,28},{4,0},{8,4},{12,8},{16,12},{20,16},{24,20},{28,24},{1,29},{... | collective-permute-start | bytes 442376 | tf_op jit(solution)/shard_map/rows/ppermute | solution.py:62
  34.5 2.1 %shard_map.103.refs_13_.refs_2_.refs_3_ = f32[4,528,256]{2,1,0:T(8,128)S(1)} custom-call(s32[4]{0:T(128)S(1)} %pad_add_fusion.place, bf16[32,768]{1,0:T(8,128)(2,1)S(1)} %get-tuple-element.71.refs_0_, bf16[96,768]{1,0:T(8,128)(2,1)S(1)} %collective-permute-done.refs_1_, bf16[96,768]{1,0:T(8,128)(2,1)S(1)} %collective-permute-done.1.refs_2_, ...), custom_call_target="tpu_custom_call" | custom-call | flops 2000000000 | bytes 1048576 | tf_op jit(solution)/shard_map/pallas_call | solution.py:49
  38.4 2.4 %collective-permute-done.8.refs_1_.refs_5_ = bf16[96,768]{1,0:T(8,128)(2,1)S(1)} collective-permute-done((bf16[96,768]{1,0:T(8,128)(2,1)S(1)}, bf16[96,768]{1,0:T(8,128)(2,1)S(1)}, u32[]{:S(2)}, u32[]{:S(2)}) %collective-permute-start.8) | collective-permute-done | bytes 147488 | tf_op jit(solution)/shard_map/rows/ppermute | solution.py:62
  40.9 2.1 %shard_map.104.refs_14_.refs_3_.refs_4_ = f32[4,528,256]{2,1,0:T(8,128)S(1)} custom-call(s32[4]{0:T(128)S(1)} %pad_add_fusion.place, bf16[144,768]{1,0:T(8,128)(2,1)S(1)} %collective-permute-done.7.refs_0_.refs_4_, bf16[96,768]{1,0:T(8,128)(2,1)S(1)} %collective-permute-done.8.refs_1_.refs_5_, bf16[96,768]{1,0:T(8,128)(2,1)S(1)} %collective-permute-done.9.refs_2_.refs_6_, ...), custom_call_target="tpu_custom_call" | custom-call | flops 2000000000 | bytes 1048576 | tf_op jit(solution)/shard_map/pallas_call | solution.py:49
  43.0 2.1 %shard_map.105 = (f32[272,768]{1,0:T(8,128)S(1)}, bf16[272,768]{1,0:T(8,128)(2,1)S(1)}, bf16[528,512]{1,0:T(8,128)(2,1)S(1)}, bf16[512,768]{1,0:T(8,128)(2,1)S(1)}, bf16[528,768]{1,0:T(8,128)(2,1)S(1)}) custom-call(s32[4]{0:T(128)S(1)} %pad_add_fusion.place, bf16[64,768]{1,0:T(8,128)(2,1)S(1)} %copy-done.2, ...), custom_call_target="tpu_custom_call" | custom-call | flops 2000000000 | bytes 1048576 | tf_op jit(solution)/shard_map/pallas_call | solution.py:49
  45.7 2.1 %shard_map.107 = (f32[272,768]{1,0:T(8,128)S(1)}, bf16[272,768]{1,0:T(8,128)(2,1)S(1)}, bf16[528,512]{1,0:T(8,128)(2,1)S(1)}, bf16[528,768]{1,0:T(8,128)(2,1)S(1)}) custom-call(s32[4]{0:T(128)S(1)} %pad_add_fusion.place, bf16[512,768]{1,0:T(8,128)(2,1)S(1)} %get-tuple-element.82.refs_0_, bf16[272,768]{1,0:T(8,128)(2,1)S(1)} %collective-permute-done.2.refs_1_, ...), custom_call_target="tpu_custom_call" | custom-call | flops 2000000000 | bytes 1048576 | tf_op jit(solution)/shard_map/pallas_call | solution.py:49
  48.7 3.2 %collective-permute-start.22 = (bf16[144,768]{1,0:T(8,128)(2,1)S(1)}, bf16[144,768]{1,0:T(8,128)(2,1)S(1)}, u32[]{:S(2)}, u32[]{:S(2)}) collective-permute-start(bf16[144,768]{1,0:T(8,128)(2,1)S(1)} %get-tuple-element.100), channel_id=1, source_target_pairs={{0,3},{1,0},{2,1},{3,2},{4,7},{5,4},{6,5},{7,6},{8,11},{9,8},{10,9... | collective-permute-start | bytes 663560 | tf_op jit(solution)/shard_map/ppermute | solution.py:62
  51.9 2.1 %shard_map.108 = (f32[272,768]{1,0:T(8,128)S(1)}, bf16[272,768]{1,0:T(8,128)(2,1)S(1)}, bf16[528,512]{1,0:T(8,128)(2,1)S(1)}, bf16[528,768]{1,0:T(8,128)(2,1)S(1)}) custom-call(s32[4]{0:T(128)S(1)} %pad_add_fusion.place, bf16[512,768]{1,0:T(8,128)(2,1)S(1)} %get-tuple-element.82.refs_0_, bf16[272,768]{1,0:T(8,128)(2,1)S(1)} %collective-permute-done.4.refs_1_, ...), custom_call_target="tpu_custom_call" | custom-call | flops 2000000000 | bytes 1048576 | tf_op jit(solution)/shard_map/pallas_call | solution.py:49
  54.1 2.1 %shard_map.106 = (bf16[272,768]{1,0:T(8,128)(2,1)S(1)}, bf16[272,768]{1,0:T(8,128)(2,1)S(1)}, bf16[528,512]{1,0:T(8,128)(2,1)S(1)}) custom-call(s32[4]{0:T(128)S(1)} %pad_add_fusion.place, bf16[512,768]{1,0:T(8,128)(2,1)S(1)} %get-tuple-element.82.refs_0_, bf16[528,768]{1,0:T(8,128)(2,1)S(1)} %get-tuple-element.83.refs_1_.refs_4_, ...), custom_call_target="tpu_custom_call" | custom-call | flops 2000000000 | bytes 1048576 | tf_op jit(solution)/shard_map/pallas_call | solution.py:49
  56.2 2.8 %shard_map.109 = (bf16[192,768]{1,0:T(8,128)(2,1)S(1)}, bf16[64,768]{1,0:T(8,128)(2,1)S(1)}, bf16[192,768]{1,0:T(8,128)(2,1)S(1)}, f32[64,768]{1,0:T(8,128)S(1)}) custom-call(s32[4]{0:T(128)S(1)} %pad_add_fusion.place, bf16[528,512]{1,0:T(8,128)(2,1)S(1)} %get-tuple-element.84.refs_0_, bf16[528,512]{1,0:T(8,128)(2,1)S(1)} %get-tuple-element.85.refs_1_, ...), custom_call_target="tpu_custom_call" | custom-call | flops 2000000000 | bytes 1048576 | tf_op jit(solution)/shard_map/pallas_call | solution.py:49
  64.3 2.1 %collective-permute-done.19.got4 = bf16[64,768]{1,0:T(8,128)(2,1)S(1)} collective-permute-done((bf16[64,768]{1,0:T(8,128)(2,1)S(1)}, bf16[64,768]{1,0:T(8,128)(2,1)S(1)}, u32[]{:S(2)}, u32[]{:S(2)}) %collective-permute-start.19) | collective-permute-done | bytes 98336 | tf_op jit(solution)/shard_map/rows_back/ppermute | solution.py:72
  66.8 2.3 %collective-permute-done.18.got3 = bf16[128,768]{1,0:T(8,128)(2,1)S(1)} collective-permute-done((bf16[128,768]{1,0:T(8,128)(2,1)S(1)}, bf16[128,768]{1,0:T(8,128)(2,1)S(1)}, u32[]{:S(2)}, u32[]{:S(2)}) %collective-permute-start.18) | collective-permute-done | bytes 196640 | tf_op jit(solution)/shard_map/rows_back/ppermute | solution.py:72
  69.1 2.9 %collective-permute-done.20 = bf16[128,768]{1,0:T(8,128)(2,1)S(1)} collective-permute-done((bf16[128,768]{1,0:T(8,128)(2,1)S(1)}, bf16[128,768]{1,0:T(8,128)(2,1)S(1)}, u32[]{:S(2)}, u32[]{:S(2)}) %collective-permute-start.20) | collective-permute-done | bytes 196640 | tf_op jit(solution)/shard_map/rows_back/ppermute | solution.py:72
  72.6 2.1 %collective-permute-start.21 = (bf16[128,768]{1,0:T(8,128)(2,1)S(1)}, bf16[128,768]{1,0:T(8,128)(2,1)S(1)}, u32[]{:S(2)}, u32[]{:S(2)}) collective-permute-start(bf16[128,768]{1,0:T(8,128)(2,1)S(1)} %rows_back.3), channel_id=1, source_target_pairs={{0,24},{4,28},{8,0},{12,4},{16,8},{20,12},{24,16},{28,20},{32,40},... | collective-permute-start | bytes 589832 | tf_op jit(solution)/shard_map/rows_back/ppermute | solution.py:72
  77.2 2.2 %collective-permute-start.31 = (bf16[80,768]{1,0:T(8,128)(2,1)S(1)}, bf16[80,768]{1,0:T(8,128)(2,1)S(1)}, u32[]{:S(2)}, u32[]{:S(2)}) collective-permute-start(bf16[80,768]{1,0:T(8,128)(2,1)S(1)} %get-tuple-element.116), channel_id=1, source_target_pairs={{0,64},{64,128},{128,192},{192,0},{1,65},{65,129},{129,193},{193,1... | collective-permute-start | bytes 368648 | tf_op jit(solution)/shard_map/weights_y/ppermute | solution.py:62
  79.4 2.0 %collective-permute-done.21 = bf16[128,768]{1,0:T(8,128)(2,1)S(1)} collective-permute-done((bf16[128,768]{1,0:T(8,128)(2,1)S(1)}, bf16[128,768]{1,0:T(8,128)(2,1)S(1)}, u32[]{:S(2)}, u32[]{:S(2)}) %collective-permute-start.21) | collective-permute-done | bytes 196640 | tf_op jit(solution)/shard_map/rows_back/ppermute | solution.py:72
  81.4 1.9 %collective-permute-done.29.g2 = bf16[80,768]{1,0:T(8,128)(2,1)S(1)} collective-permute-done((bf16[80,768]{1,0:T(8,128)(2,1)S(1)}, bf16[80,768]{1,0:T(8,128)(2,1)S(1)}, u32[]{:S(2)}, u32[]{:S(2)}) %collective-permute-start.29) | collective-permute-done | bytes 122912 | tf_op jit(solution)/shard_map/weights_y/ppermute | solution.py:62
  83.5 2.0 %collective-permute-done.32.g3 = bf16[80,768]{1,0:T(8,128)(2,1)S(1)} collective-permute-done((bf16[80,768]{1,0:T(8,128)(2,1)S(1)}, bf16[80,768]{1,0:T(8,128)(2,1)S(1)}, u32[]{:S(2)}, u32[]{:S(2)}) %collective-permute-start.32) | collective-permute-done | bytes 122912 | tf_op jit(solution)/shard_map/weights_y/ppermute | solution.py:62
  (83 shorter events, 24.6 us)
Async XLA Ops:
  4.1 12.7 %collective-permute-start.2 = (bf16[272,768]{1,0:T(8,128)(2,1)S(1)}, bf16[272,768]{1,0:T(8,128)(2,1)S(1)}, u32[]{:S(2)}, u32[]{:S(2)}) collective-permute-start(bf16[272,768]{1,0:T(8,128)(2,1)S(1)} %get-tuple-element.64), channel_id=1, source_target_pairs={{0,1},{1,2},{2,3},{3,0},{4,5},{5,6},{6,7},{7,4},{8,9},{9,10},{10,1... | collective-permute-start | bytes 1253384 | tf_op jit(solution)/shard_map/weights/ppermute | solution.py:62
  5.7 11.5 %collective-permute-start.4 = (bf16[272,768]{1,0:T(8,128)(2,1)S(1)}, bf16[272,768]{1,0:T(8,128)(2,1)S(1)}, u32[]{:S(2)}, u32[]{:S(2)}) collective-permute-start(bf16[272,768]{1,0:T(8,128)(2,1)S(1)} %get-tuple-element.64), channel_id=1, source_target_pairs={{0,3},{1,0},{2,1},{3,2},{4,7},{5,4},{6,5},{7,6},{8,11},{9,8},{10,9... | collective-permute-start | bytes 1253384 | tf_op jit(solution)/shard_map/weights/ppermute | solution.py:62
  8.8 13.4 %collective-permute-start.6 = (bf16[144,768]{1,0:T(8,128)(2,1)S(1)}, bf16[144,768]{1,0:T(8,128)(2,1)S(1)}, u32[]{:S(2)}, u32[]{:S(2)}) collective-permute-start(bf16[144,768]{1,0:T(8,128)(2,1)S(1)} %get-tuple-element.65), channel_id=1, source_target_pairs={{0,8},{4,12},{8,16},{12,20},{16,24},{20,28},{24,0},{28,4},{1,9},{5... | collective-permute-start | bytes 663560 | tf_op jit(solution)/shard_map/rows/ppermute | solution.py:62
  12.1 14.5 %collective-permute-start.7 = (bf16[144,768]{1,0:T(8,128)(2,1)S(1)}, bf16[144,768]{1,0:T(8,128)(2,1)S(1)}, u32[]{:S(2)}, u32[]{:S(2)}) collective-permute-start(bf16[144,768]{1,0:T(8,128)(2,1)S(1)} %get-tuple-element.66), channel_id=1, source_target_pairs={{0,24},{4,28},{8,0},{12,4},{16,8},{20,12},{24,16},{28,20},{1,25},{... | collective-permute-start | bytes 663560 | tf_op jit(solution)/shard_map/rows/ppermute | solution.py:62
  16.8 9.9 %collective-permute-start.3 = (bf16[144,768]{1,0:T(8,128)(2,1)S(1)}, bf16[144,768]{1,0:T(8,128)(2,1)S(1)}, u32[]{:S(2)}, u32[]{:S(2)}) collective-permute-start(bf16[144,768]{1,0:T(8,128)(2,1)S(1)} %slice.32), channel_id=1, source_target_pairs={{0,1},{1,2},{2,3},{3,0},{4,5},{5,6},{6,7},{7,4},{8,9},{9,10},{10,1... | collective-permute-start | bytes 663560 | tf_op jit(solution)/shard_map/weights/ppermute | solution.py:62
  17.2 9.5 %collective-permute-start.5 = (bf16[128,768]{1,0:T(8,128)(2,1)S(1)}, bf16[128,768]{1,0:T(8,128)(2,1)S(1)}, u32[]{:S(2)}, u32[]{:S(2)}) collective-permute-start(bf16[128,768]{1,0:T(8,128)(2,1)S(1)} %slice.33), channel_id=1, source_target_pairs={{0,3},{1,0},{2,1},{3,2},{4,7},{5,4},{6,5},{7,6},{8,11},{9,8},{10,9... | collective-permute-start | bytes 589832 | tf_op jit(solution)/shard_map/weights/ppermute | solution.py:62
  20.2 14.3 %collective-permute-start = (bf16[96,768]{1,0:T(8,128)(2,1)S(1)}, bf16[96,768]{1,0:T(8,128)(2,1)S(1)}, u32[]{:S(2)}, u32[]{:S(2)}) collective-permute-start(bf16[96,768]{1,0:T(8,128)(2,1)S(1)} %get-tuple-element.62), channel_id=1, source_target_pairs={{0,4},{4,8},{8,12},{12,16},{16,20},{20,24},{24,28},{28,0},{1,5},{5... | collective-permute-start | bytes 442376 | tf_op jit(solution)/shard_map/rows/ppermute | solution.py:62
  22.1 12.4 %collective-permute-start.1 = (bf16[96,768]{1,0:T(8,128)(2,1)S(1)}, bf16[96,768]{1,0:T(8,128)(2,1)S(1)}, u32[]{:S(2)}, u32[]{:S(2)}) collective-permute-start(bf16[96,768]{1,0:T(8,128)(2,1)S(1)} %get-tuple-element.63), channel_id=1, source_target_pairs={{0,28},{4,0},{8,4},{12,8},{16,12},{20,16},{24,20},{28,24},{1,29},{... | collective-permute-start | bytes 442376 | tf_op jit(solution)/shard_map/rows/ppermute | solution.py:62
  26.7 9.9 %collective-permute-start.11 = (bf16[48,768]{1,0:T(8,128)(2,1)S(1)}, bf16[48,768]{1,0:T(8,128)(2,1)S(1)}, u32[]{:S(2)}, u32[]{:S(2)}) collective-permute-start(bf16[48,768]{1,0:T(8,128)(2,1)S(1)} %slice.29), channel_id=1, source_target_pairs={{0,24},{4,28},{8,0},{12,4},{16,8},{20,12},{24,16},{28,20},{1,25},{... | collective-permute-start | bytes 221192 | tf_op jit(solution)/shard_map/rows/ppermute | solution.py:62
  30.8 7.1 %collective-permute-start.10 = (bf16[48,768]{1,0:T(8,128)(2,1)S(1)}, bf16[48,768]{1,0:T(8,128)(2,1)S(1)}, u32[]{:S(2)}, u32[]{:S(2)}) collective-permute-start(bf16[48,768]{1,0:T(8,128)(2,1)S(1)} %slice.28), channel_id=1, source_target_pairs={{0,8},{4,12},{8,16},{12,20},{16,24},{20,28},{24,0},{28,4},{1,9},{5... | collective-permute-start | bytes 221192 | tf_op jit(solution)/shard_map/rows/ppermute | solution.py:62
  30.8 7.6 %collective-permute-start.9 = (bf16[96,768]{1,0:T(8,128)(2,1)S(1)}, bf16[96,768]{1,0:T(8,128)(2,1)S(1)}, u32[]{:S(2)}, u32[]{:S(2)}) collective-permute-start(bf16[96,768]{1,0:T(8,128)(2,1)S(1)} %slice.27), channel_id=1, source_target_pairs={{0,28},{4,0},{8,4},{12,8},{16,12},{20,16},{24,20},{28,24},{1,29},{... | collective-permute-start | bytes 442376 | tf_op jit(solution)/shard_map/rows/ppermute | solution.py:62
  34.5 6.4 %collective-permute-start.8 = (bf16[96,768]{1,0:T(8,128)(2,1)S(1)}, bf16[96,768]{1,0:T(8,128)(2,1)S(1)}, u32[]{:S(2)}, u32[]{:S(2)}) collective-permute-start(bf16[96,768]{1,0:T(8,128)(2,1)S(1)} %slice.26), channel_id=1, source_target_pairs={{0,4},{4,8},{8,12},{12,16},{16,20},{20,24},{24,28},{28,0},{1,5},{5... | collective-permute-start | bytes 442376 | tf_op jit(solution)/shard_map/rows/ppermute | solution.py:62
  38.4 7.2 %collective-permute-start.15 = (bf16[272,768]{1,0:T(8,128)(2,1)S(1)}, bf16[272,768]{1,0:T(8,128)(2,1)S(1)}, u32[]{:S(2)}, u32[]{:S(2)}) collective-permute-start(bf16[272,768]{1,0:T(8,128)(2,1)S(1)} %collective-permute-done.2.refs_1_), channel_id=1, source_target_pairs={{0,32},{32,0},{1,33},{33,1},{2,34},{34,2},{3,35},{35,3},{4,36},{36... | collective-permute-start | bytes 1253384 | tf_op jit(solution)/shard_map/weights/ppermute | solution.py:62
  45.2 6.7 %collective-permute-start.16 = (bf16[272,768]{1,0:T(8,128)(2,1)S(1)}, bf16[272,768]{1,0:T(8,128)(2,1)S(1)}, u32[]{:S(2)}, u32[]{:S(2)}) collective-permute-start(bf16[272,768]{1,0:T(8,128)(2,1)S(1)} %collective-permute-done.4.refs_1_), channel_id=1, source_target_pairs={{0,32},{32,0},{1,33},{33,1},{2,34},{34,2},{3,35},{35,3},{4,36},{36... | collective-permute-start | bytes 1253384 | tf_op jit(solution)/shard_map/weights/ppermute | solution.py:62
  47.8 11.9 %collective-permute-start.24 = (bf16[272,768]{1,0:T(8,128)(2,1)S(1)}, bf16[272,768]{1,0:T(8,128)(2,1)S(1)}, u32[]{:S(2)}, u32[]{:S(2)}) collective-permute-start(bf16[272,768]{1,0:T(8,128)(2,1)S(1)} %get-tuple-element.105), channel_id=1, source_target_pairs={{0,32},{32,0},{1,33},{33,1},{2,34},{34,2},{3,35},{35,3},{4,36},{36... | collective-permute-start | bytes 1253384 | tf_op jit(solution)/shard_map/ppermute | solution.py:62
  48.6 11.3 %collective-permute-start.26 = (bf16[128,768]{1,0:T(8,128)(2,1)S(1)}, bf16[128,768]{1,0:T(8,128)(2,1)S(1)}, u32[]{:S(2)}, u32[]{:S(2)}) collective-permute-start(bf16[128,768]{1,0:T(8,128)(2,1)S(1)} %get-tuple-element.109), channel_id=1, source_target_pairs={{0,1},{1,2},{2,3},{3,0},{4,5},{5,6},{6,7},{7,4},{8,9},{9,10},{10,1... | collective-permute-start | bytes 589832 | tf_op jit(solution)/shard_map/ppermute | solution.py:62
  48.7 10.8 %collective-permute-start.22 = (bf16[144,768]{1,0:T(8,128)(2,1)S(1)}, bf16[144,768]{1,0:T(8,128)(2,1)S(1)}, u32[]{:S(2)}, u32[]{:S(2)}) collective-permute-start(bf16[144,768]{1,0:T(8,128)(2,1)S(1)} %get-tuple-element.100), channel_id=1, source_target_pairs={{0,3},{1,0},{2,1},{3,2},{4,7},{5,4},{6,5},{7,6},{8,11},{9,8},{10,9... | collective-permute-start | bytes 663560 | tf_op jit(solution)/shard_map/ppermute | solution.py:62
  59.6 15.1 %collective-permute-start.23 = (bf16[272,768]{1,0:T(8,128)(2,1)S(1)}, bf16[272,768]{1,0:T(8,128)(2,1)S(1)}, u32[]{:S(2)}, u32[]{:S(2)}) collective-permute-start(bf16[272,768]{1,0:T(8,128)(2,1)S(1)} %get-tuple-element.103), channel_id=1, source_target_pairs={{0,32},{32,0},{1,33},{33,1},{2,34},{34,2},{3,35},{35,3},{4,36},{36... | collective-permute-start | bytes 1253384 | tf_op jit(solution)/shard_map/ppermute | solution.py:62
  59.7 6.7 %collective-permute-start.19 = (bf16[64,768]{1,0:T(8,128)(2,1)S(1)}, bf16[64,768]{1,0:T(8,128)(2,1)S(1)}, u32[]{:S(2)}, u32[]{:S(2)}) collective-permute-start(bf16[64,768]{1,0:T(8,128)(2,1)S(1)} %get-tuple-element.95), channel_id=1, source_target_pairs={{0,24},{4,28},{8,0},{12,4},{16,8},{20,12},{24,16},{28,20},{32,40},... | collective-permute-start | bytes 294920 | tf_op jit(solution)/shard_map/rows_back/ppermute | solution.py:72
  60.7 14.0 %collective-permute-start.27 = (bf16[272,768]{1,0:T(8,128)(2,1)S(1)}, bf16[272,768]{1,0:T(8,128)(2,1)S(1)}, u32[]{:S(2)}, u32[]{:S(2)}) collective-permute-start(bf16[272,768]{1,0:T(8,128)(2,1)S(1)} %get-tuple-element.110), channel_id=1, source_target_pairs={{0,3},{1,0},{2,1},{3,2},{4,7},{5,4},{6,5},{7,6},{8,11},{9,8},{10,9... | collective-permute-start | bytes 1253384 | tf_op jit(solution)/shard_map/weights_x/ppermute | solution.py:62
  62.3 12.7 %collective-permute-start.28 = (bf16[272,768]{1,0:T(8,128)(2,1)S(1)}, bf16[272,768]{1,0:T(8,128)(2,1)S(1)}, u32[]{:S(2)}, u32[]{:S(2)}) collective-permute-start(bf16[272,768]{1,0:T(8,128)(2,1)S(1)} %get-tuple-element.111), channel_id=1, source_target_pairs={{0,1},{1,2},{2,3},{3,0},{4,5},{5,6},{6,7},{7,4},{8,9},{9,10},{10,1... | collective-permute-start | bytes 1253384 | tf_op jit(solution)/shard_map/weights_x/ppermute | solution.py:62
  72.6 8.8 %collective-permute-start.21 = (bf16[128,768]{1,0:T(8,128)(2,1)S(1)}, bf16[128,768]{1,0:T(8,128)(2,1)S(1)}, u32[]{:S(2)}, u32[]{:S(2)}) collective-permute-start(bf16[128,768]{1,0:T(8,128)(2,1)S(1)} %rows_back.3), channel_id=1, source_target_pairs={{0,24},{4,28},{8,0},{12,4},{16,8},{20,12},{24,16},{28,20},{32,40},... | collective-permute-start | bytes 589832 | tf_op jit(solution)/shard_map/rows_back/ppermute | solution.py:72
  75.9 7.4 %collective-permute-start.29 = (bf16[80,768]{1,0:T(8,128)(2,1)S(1)}, bf16[80,768]{1,0:T(8,128)(2,1)S(1)}, u32[]{:S(2)}, u32[]{:S(2)}) collective-permute-start(bf16[80,768]{1,0:T(8,128)(2,1)S(1)} %get-tuple-element.112), channel_id=1, source_target_pairs={{0,128},{64,192},{128,0},{192,64},{1,129},{65,193},{129,1},{193,65... | collective-permute-start | bytes 368648 | tf_op jit(solution)/shard_map/weights_y/ppermute | solution.py:62
  77.2 6.3 %collective-permute-start.31 = (bf16[80,768]{1,0:T(8,128)(2,1)S(1)}, bf16[80,768]{1,0:T(8,128)(2,1)S(1)}, u32[]{:S(2)}, u32[]{:S(2)}) collective-permute-start(bf16[80,768]{1,0:T(8,128)(2,1)S(1)} %get-tuple-element.116), channel_id=1, source_target_pairs={{0,64},{64,128},{128,192},{192,0},{1,65},{65,129},{129,193},{193,1... | collective-permute-start | bytes 368648 | tf_op jit(solution)/shard_map/weights_y/ppermute | solution.py:62
  (17 other events, 74.5 us)
